TPU v7x, 32 devices: a whole 2x2x4 slice. The times are simulated.
32 devices in a mesh: dp: 16 (over z, y, core), mp: 2 (over x).
Axes of the slice: x: 2, y: 2, z: 4, core: 2. Of those that a mesh axis runs over, the one named last changes fastest.
Arguments:
- tokens: bfloat16 [40960, 1024], P(('dp', 'mp')), may hold values from -6 to 6
- ln1_gain: float32 [1024], replicated, may hold values from 0.5 to 1.5
- ln1_bias: float32 [1024], replicated, may hold values from -1 to 1
- w_qkv: bfloat16 [1024, 3, 1024], P(None, None, 'mp'), may hold values from -0.1875 to 0.1875
- qv_bias: float32 [2, 1024], P(None, 'mp'), may hold values from -1.5 to 1.5
- w_out: bfloat16 [1024, 1024], P('mp'), may hold values from -0.1875 to 0.1875
- out_bias: float32 [1024], replicated, may hold values from -1.5 to 1.5
- ln2_gain: float32 [1024], replicated, may hold values from 0.5 to 1.5
- ln2_bias: float32 [1024], replicated, may hold values from -1 to 1
- ln3_gain: float32 [1024], replicated, may hold values from 0.5 to 1.5
- ln3_bias: float32 [1024], replicated, may hold values from -1 to 1
- w_up: bfloat16 [1024, 4096], P(None, 'mp'), may hold values from -0.1875 to 0.1875
- up_bias: float32 [4096], P('mp'), may hold values from -1.5 to 1.5
- w_down: bfloat16 [4096, 1024], P('mp'), may hold values from -0.09375 to 0.09375
- down_bias: float32 [1024], replicated, may hold values from -1.5 to 1.5
- ln4_gain: float32 [1024], replicated, may hold values from 0.5 to 1.5
- ln4_bias: float32 [1024], replicated, may hold values from -1 to 1
- row_grid: int32 [16, 8], P('dp'), may hold values from 0 to 48, as said below
- pad_mask: int32 [40960], P('dp'), may hold values from 0 to 1, as said below
- cotangent: bfloat16 [40960, 1024], P(('dp', 'mp')), may hold values from -6 to 6
Outputs:
- layer_out: bfloat16 [40960, 1024], P(('dp', 'mp'))
- grad_in: float32 [40960, 1024], P(('dp', 'mp'))
- g_ln1_gain: float32 [1024], replicated
- g_ln1_bias: float32 [1024], replicated
- g_w_qkv: float32 [1024, 3, 1024], P(None, None, 'mp')
- g_qv_bias: float32 [2, 1024], P(None, 'mp')
- g_w_out: float32 [1024, 1024], P('mp')
- g_out_bias: float32 [1024], replicated
- g_ln2_gain: float32 [1024], replicated
- g_ln2_bias: float32 [1024], replicated
- g_ln3_gain: float32 [1024], replicated
- g_ln3_bias: float32 [1024], replicated
- g_w_up: float32 [1024, 4096], P(None, 'mp')
- g_up_bias: float32 [4096], P('mp')
- g_w_down: float32 [4096, 1024], P('mp')
- g_down_bias: float32 [1024], replicated
- g_ln4_gain: float32 [1024], replicated
- g_ln4_bias: float32 [1024], replicated
Inputs may be any that keep to these rules, and one draw needn't show every extreme that they name: `row_grid`: in each group all nonzero entries are the same side, 16, 32 or 48; the first 2560 // (64 + side^2) slots of a group hold it and the rest are 0; some group has side 3 * 16. `pad_mask`: in each row the first few text tokens (at least one, fewer than 64) and all image tokens are 1, the rest of its text tokens 0; slots after a group's last row are 0.
All inputs are finite; a program needn't handle non-finite values.
Results may differ from a plain program's by a relative error of at most 0.022.
Values may be sent and summed in bfloat16 or wider, within the bound.
No kernel may reach another device: no remote copies, remote signals or barrier semaphores. Data moves between devices by JAX's collectives and lax.ppermute only.
A program may use at most 320 MiB of HBM per device.

v0:
```python
import jax
import jax.numpy as jnp
from jax import lax
from jax.sharding import PartitionSpec as P

HDIM = 64
TEXT = 64
QBLK = 512


epsilon = 1e-05
masked_score = -1e30


def norm_parts(values, ln_gain, ln_bias):
    centred = values - jnp.mean(values, -1, keepdims=True)
    inv_std = lax.rsqrt(jnp.mean(centred * centred, -1, keepdims=True) + epsilon)
    normed = centred * inv_std
    return (normed * ln_gain + ln_bias, normed, inv_std)


def norm_back(upstream, normed, inv_std, ln_gain):
    scaled = upstream * ln_gain
    return inv_std * (
        scaled
        - jnp.mean(scaled, -1, keepdims=True)
        - normed * jnp.mean(scaled * normed, -1, keepdims=True)
    )


def gelu_tanh(values):
    return jax.nn.gelu(values, approximate=True)


def segment_ids(grid_row, group_rows):
    position = jnp.arange(group_rows, dtype=jnp.int32)
    lengths = jnp.where(grid_row > 0, TEXT + grid_row * grid_row, 0)
    row_ends = jnp.cumsum(lengths)
    return jnp.sum((position[:, None] >= row_ends[None, :]).astype(jnp.int32), axis=1)


def permitted(seg_all, keep_all, row_start, row_count):
    key_pos = jnp.arange(seg_all.shape[0], dtype=jnp.int32)
    row_pos = row_start + jnp.arange(row_count, dtype=jnp.int32)
    seg_rows = lax.dynamic_slice_in_dim(seg_all, row_start, row_count, 0)
    same_row = seg_rows[:, None] == seg_all[None, :]
    causal = key_pos[None, :] <= row_pos[:, None]
    visible = (keep_all[None, :] == 1) | (key_pos[None, :] == row_pos[:, None])
    return same_row & causal & visible


def contract_rows(left, right):
    return lax.dot_general(
        left, right, (((0,), (0,)), ((), ())), preferred_element_type=jnp.float32
    )


def contract_cols(left, right):
    return lax.dot_general(
        left, right, (((1,), (1,)), ((), ())), preferred_element_type=jnp.float32
    )


def masked_scores(query_blk, keys_all, seg_all, keep_all, row_start, head_scale):
    scores = (
        jnp.einsum("qhd,khd->hqk", query_blk, keys_all, preferred_element_type=jnp.float32)
        * head_scale
    )
    return jnp.where(permitted(seg_all, keep_all, row_start, QBLK)[None], scores, masked_score)


def attend_forward(query, keys_all, values_all, seg_all, keep_all):
    group_rows = query.shape[0]
    head_scale = query.shape[2] ** (-0.5)

    def score_block(block_idx):
        row_start = block_idx * QBLK
        query_blk = lax.dynamic_slice_in_dim(query, row_start, QBLK, 0)
        scores = masked_scores(query_blk, keys_all, seg_all, keep_all, row_start, head_scale)
        row_top = jnp.max(scores, -1, keepdims=True)
        exp_scores = jnp.exp(scores - row_top)
        row_total = jnp.sum(exp_scores, -1, keepdims=True)
        probs = (exp_scores / row_total).astype(jnp.bfloat16)
        context = jnp.einsum(
            "hqk,khd->qhd", probs, values_all, preferred_element_type=jnp.float32
        ).astype(jnp.bfloat16)
        return (context, (row_top + jnp.log(row_total))[:, :, 0])

    context, log_total = lax.map(score_block, jnp.arange(group_rows // QBLK, dtype=jnp.int32))
    return (context.reshape(group_rows, -1), log_total)


def attend_backward(query, keys_all, values_all, grad_ctx, log_total, seg_all, keep_all):
    group_rows = query.shape[0]
    head_scale = query.shape[2] ** (-0.5)

    def step_block(carry, block_idx):
        acc_keys, acc_values = carry
        row_start = block_idx * QBLK
        query_blk = lax.dynamic_slice_in_dim(query, row_start, QBLK, 0)
        grad_blk = lax.dynamic_slice_in_dim(grad_ctx, row_start, QBLK, 0)
        scores = masked_scores(query_blk, keys_all, seg_all, keep_all, row_start, head_scale)
        probs = jnp.exp(scores - log_total[block_idx][:, :, None])
        grad_probs = jnp.einsum(
            "qhd,khd->hqk", grad_blk, values_all, preferred_element_type=jnp.float32
        )
        acc_values = acc_values + jnp.einsum(
            "hqk,qhd->khd", probs.astype(jnp.bfloat16), grad_blk, preferred_element_type=jnp.float32
        )
        inner = jnp.sum(probs * grad_probs, -1, keepdims=True)
        grad_scores = (probs * (grad_probs - inner) * head_scale).astype(jnp.bfloat16)
        grad_query = jnp.einsum(
            "hqk,khd->qhd", grad_scores, keys_all, preferred_element_type=jnp.float32
        )
        acc_keys = acc_keys + jnp.einsum(
            "hqk,qhd->khd", grad_scores, query_blk, preferred_element_type=jnp.float32
        )
        return ((acc_keys, acc_values), grad_query)

    zero_acc = jnp.zeros(keys_all.shape, jnp.float32)
    (acc_keys, acc_values), grad_query = lax.scan(
        step_block, (zero_acc, zero_acc), jnp.arange(group_rows // QBLK, dtype=jnp.int32)
    )
    return (grad_query.reshape(keys_all.shape), acc_keys, acc_values)


def body(
    tokens,
    ln1_gain,
    ln1_bias,
    w_qkv,
    qv_bias,
    w_out,
    out_bias,
    ln2_gain,
    ln2_bias,
    ln3_gain,
    ln3_bias,
    w_up,
    up_bias,
    w_down,
    down_bias,
    ln4_gain,
    ln4_bias,
    row_grid,
    pad_mask,
    cotangent,
):
    model_dim = tokens.shape[1]
    group_rows = pad_mask.shape[0]
    local_width = w_qkv.shape[2]
    local_heads = local_width // HDIM
    head_shape = (group_rows, local_heads, HDIM)
    seg_all = segment_ids(row_grid[0], group_rows)
    flat_qkv = w_qkv.reshape(model_dim, 3 * local_width)
    resid_in = tokens.astype(jnp.float32)
    norm1_out, normed1, inv1 = norm_parts(resid_in, ln1_gain, ln1_bias)
    attn_full = lax.all_gather(norm1_out.astype(jnp.bfloat16), "mp", axis=0, tiled=True)
    qkv_raw = jnp.dot(attn_full, flat_qkv, preferred_element_type=jnp.float32).reshape(
        group_rows, 3, local_width
    )
    query = (qkv_raw[:, 0] + qv_bias[0]).astype(jnp.bfloat16).reshape(head_shape)
    keys_all = qkv_raw[:, 1].astype(jnp.bfloat16).reshape(head_shape)
    values_all = (qkv_raw[:, 2] + qv_bias[1]).astype(jnp.bfloat16).reshape(head_shape)
    context, log_total = attend_forward(query, keys_all, values_all, seg_all, pad_mask)
    proj_sum = lax.psum_scatter(
        jnp.dot(context, w_out, preferred_element_type=jnp.float32).astype(jnp.bfloat16),
        "mp",
        scatter_dimension=0,
        tiled=True,
    ).astype(jnp.float32)
    branch_z = proj_sum + out_bias
    norm2_out, normed2, inv2 = norm_parts(branch_z, ln2_gain, ln2_bias)
    resid_mid = resid_in + norm2_out
    norm3_out, normed3, inv3 = norm_parts(resid_mid, ln3_gain, ln3_bias)
    ffn_full = lax.all_gather(norm3_out.astype(jnp.bfloat16), "mp", axis=0, tiled=True)
    hidden_pre = jnp.dot(ffn_full, w_up, preferred_element_type=jnp.float32) + up_bias
    hidden_act = gelu_tanh(hidden_pre).astype(jnp.bfloat16)
    branch_f = (
        lax.psum_scatter(
            jnp.dot(hidden_act, w_down, preferred_element_type=jnp.float32).astype(jnp.bfloat16),
            "mp",
            scatter_dimension=0,
            tiled=True,
        ).astype(jnp.float32)
        + down_bias
    )
    norm4_out, normed4, inv4 = norm_parts(branch_f, ln4_gain, ln4_bias)
    layer_out = (resid_mid + norm4_out).astype(jnp.bfloat16)
    upstream = cotangent.astype(jnp.float32)
    grad_f = norm_back(upstream, normed4, inv4, ln4_gain).astype(jnp.bfloat16)
    grad_f_full = lax.all_gather(grad_f, "mp", axis=0, tiled=True)
    g_w_down = contract_rows(hidden_act, grad_f_full)
    grad_act = contract_cols(grad_f_full, w_down)
    grad_pre = jax.vjp(gelu_tanh, hidden_pre)[1](grad_act)[0].astype(jnp.bfloat16)
    g_up_bias = jnp.sum(grad_pre.astype(jnp.float32), 0)
    g_w_up = contract_rows(ffn_full, grad_pre)
    grad_a3 = lax.psum_scatter(
        contract_cols(grad_pre, w_up).astype(jnp.bfloat16), "mp", scatter_dimension=0, tiled=True
    ).astype(jnp.float32)
    grad_mid = upstream + norm_back(grad_a3, normed3, inv3, ln3_gain)
    grad_z = norm_back(grad_mid, normed2, inv2, ln2_gain).astype(jnp.bfloat16)
    grad_z_full = lax.all_gather(grad_z, "mp", axis=0, tiled=True)
    g_w_out = contract_rows(context, grad_z_full)
    grad_ctx = contract_cols(grad_z_full, w_out).astype(jnp.bfloat16)
    grad_query, acc_keys, acc_values = attend_backward(
        query, keys_all, values_all, grad_ctx.reshape(head_shape), log_total, seg_all, pad_mask
    )
    grad_q_low = grad_query.astype(jnp.bfloat16).reshape(group_rows, local_width)
    grad_k_low = acc_keys.astype(jnp.bfloat16).reshape(group_rows, local_width)
    grad_v_low = acc_values.astype(jnp.bfloat16).reshape(group_rows, local_width)
    grad_qkv = jnp.stack([grad_q_low, grad_k_low, grad_v_low], 1).reshape(
        group_rows, 3 * local_width
    )
    g_qv_bias = jnp.stack(
        [jnp.sum(grad_q_low.astype(jnp.float32), 0), jnp.sum(grad_v_low.astype(jnp.float32), 0)], 0
    )
    g_w_qkv = contract_rows(attn_full, grad_qkv).reshape(model_dim, 3, local_width)
    grad_a1 = lax.psum_scatter(
        contract_cols(grad_qkv, flat_qkv).astype(jnp.bfloat16),
        "mp",
        scatter_dimension=0,
        tiled=True,
    ).astype(jnp.float32)
    grad_input = grad_mid + norm_back(grad_a1, normed1, inv1, ln1_gain)
    norm_terms = jnp.stack(
        [
            jnp.sum(grad_a1 * normed1, 0),
            jnp.sum(grad_a1, 0),
            jnp.sum(grad_z.astype(jnp.float32), 0),
            jnp.sum(grad_mid * normed2, 0),
            jnp.sum(grad_mid, 0),
            jnp.sum(grad_a3 * normed3, 0),
            jnp.sum(grad_a3, 0),
            jnp.sum(grad_f.astype(jnp.float32), 0),
            jnp.sum(upstream * normed4, 0),
            jnp.sum(upstream, 0),
        ],
        0,
    )
    weight_grads = (
        lax.psum(g_w_qkv.astype(jnp.bfloat16), "dp").astype(jnp.float32),
        lax.psum(g_qv_bias.astype(jnp.bfloat16), "dp").astype(jnp.float32),
        lax.psum(g_w_out.astype(jnp.bfloat16), "dp").astype(jnp.float32),
        lax.psum(g_w_up.astype(jnp.bfloat16), "dp").astype(jnp.float32),
        lax.psum(g_up_bias.astype(jnp.bfloat16), "dp").astype(jnp.float32),
        lax.psum(g_w_down.astype(jnp.bfloat16), "dp").astype(jnp.float32),
    )
    norm_grads = lax.psum(norm_terms, ("dp", "mp"))
    return (
        layer_out,
        grad_input,
        norm_grads[0],
        norm_grads[1],
        weight_grads[0],
        weight_grads[1],
        weight_grads[2],
        norm_grads[2],
        norm_grads[3],
        norm_grads[4],
        norm_grads[5],
        norm_grads[6],
        weight_grads[3],
        weight_grads[4],
        weight_grads[5],
        norm_grads[7],
        norm_grads[8],
        norm_grads[9],
    )


def solution(mesh):
    in_specs = (
        P(("dp", "mp"), None),
        P(),
        P(),
        P(None, None, "mp"),
        P(None, "mp"),
        P("mp", None),
        P(),
        P(),
        P(),
        P(),
        P(),
        P(None, "mp"),
        P("mp"),
        P("mp", None),
        P(),
        P(),
        P(),
        P("dp", None),
        P("dp"),
        P(("dp", "mp"), None),
    )
    out_specs = (
        P(("dp", "mp"), None),
        P(("dp", "mp"), None),
        P(),
        P(),
        P(None, None, "mp"),
        P(None, "mp"),
        P("mp", None),
        P(),
        P(),
        P(),
        P(),
        P(),
        P(None, "mp"),
        P("mp"),
        P("mp", None),
        P(),
        P(),
        P(),
    )
    return jax.shard_map(body, mesh=mesh, in_specs=in_specs, out_specs=out_specs, check_vma=False)
```

profile of v0, /device:TPU:0, one launch (start us, length us, event | category | flops | bytes accessed | tf_op | source)
XLA Modules:
  0.0 2276.4 jit_solution(3043264382986382878)
XLA Ops:
  20.4 66.2 %all-gather.5.cloned.1.call-done = bf16[2560,1024]{1,0:T(8,128)(2,1)} async-done(((bf16[1280,1024]{1,0:T(8,128)(2,1)}), bf16[2560,1024]{1,0:T(8,128)(2,1)}) %all-gather.5.cloned.1.call-update) | async-done | bytes 5242896 | tf_op jit(solution)/shard_map/all_gather | solution.py:158
  113.1 312.6 %while.27 = (s32[]{:T(128)}, bf16[5,512,8,64]{1,3,2,0:T(8,128)(2,1)}, f32[5,8,512]{2,1,0:T(8,128)}, s32[5]{0:T(128)S(1)}, s32[2560]{0:T(1024)S(1)}, /*index=5*/s...) while((s32[]{:T(128)}, ...), condition=%wide.region_7.8_spmd, body=%wide.region_4.7_spmd.sunk | while | flops 2818309120 | bytes 148016368 | solution.py:89
  119.0 18.6 fusion.159
  137.6 18.8 fusion.160
  156.5 18.6 fusion.161
  181.4 18.6 fusion.159
  200.0 18.8 fusion.160
  218.9 18.6 fusion.161
  243.8 18.6 fusion.159
  262.4 18.8 fusion.160
  281.3 18.6 fusion.161
  306.2 18.6 fusion.159
  324.8 18.8 fusion.160
  343.7 18.6 fusion.161
  368.6 18.6 fusion.159
  387.2 18.8 fusion.160
  436.9 65.8 %reduce-scatter.5.cloned.1.call-done = bf16[1280,1024]{1,0:T(8,128)(2,1)} async-done(((bf16[2560,1024]{1,0:T(8,128)(2,1)}), bf16[1280,1024]{1,0:T(8,128)(2,1)}) %reduce-scatter.5.cloned.1.call-update) | async-done | bytes 2621456 | tf_op jit(solution)/shard_map/reduce_scatter | solution.py:166
  519.6 68.7 %all-gather.7.cloned.1.call-done = bf16[2560,1024]{1,0:T(8,128)(2,1)} async-done(((bf16[1280,1024]{1,0:T(8,128)(2,1)}), bf16[2560,1024]{1,0:T(8,128)(2,1)}) %all-gather.7.cloned.1.call-update) | async-done | bytes 5242896 | tf_op jit(solution)/shard_map/all_gather | solution.py:176
  588.3 24.2 %multiply_convert_fusion.1 = (bf16[2560,2048]{1,0:T(8,128)(2,1)}, f32[2560,2048]{1,0:T(8,128)}) fusion(f32[2048]{0:T(1024)S(1)} %copy-done.51, bf16[2560,1024]{1,0:T(8,128)(2,1)} %all-gather.7.cloned.1.call-done, bf16[1024,2048]{1,0:T(8,128)(2,1)} %param.35), kind=kOutput, calls=%fused_computation.65 | convolution fusion | flops 10789847040 | bytes 40902656 | tf_op jit(solution)/shard_map/dot_general | solution.py:177
  627.8 65.8 %reduce-scatter.7.cloned.1.call-done = bf16[1280,1024]{1,0:T(8,128)(2,1)} async-done(((bf16[2560,1024]{1,0:T(8,128)(2,1)}), bf16[1280,1024]{1,0:T(8,128)(2,1)}) %reduce-scatter.7.cloned.1.call-update) | async-done | bytes 2621456 | tf_op jit(solution)/shard_map/reduce_scatter | solution.py:180
  706.9 68.3 %all-gather.9.cloned.1.call-done = bf16[2560,1024]{1,0:T(8,128)(2,1)} async-done(((bf16[1280,1024]{1,0:T(8,128)(2,1)}), bf16[2560,1024]{1,0:T(8,128)(2,1)}) %all-gather.9.cloned.1.call-update) | async-done | bytes 5242896 | tf_op jit(solution)/shard_map/all_gather | solution.py:192
  775.1 30.8 %fusion.112 = (bf16[2048]{0:T(1024)(128)(2,1)}, bf16[2560,2048]{1,0:T(8,128)(2,1)}) fusion(f32[2560,2048]{1,0:T(8,128)} %get-tuple-element.263, f32[2048]{0:T(1024)S(1)} %copy-done.51, bf16[2560,1024]{1,0:T(8,128)(2,1)} %all-gather.9.cloned.1.call-done, bf16[2048,1024]{1,0:T(8,128)(2,1)} %param.37), kind=kOutput, calls=%fused_computation.175 | convolution fusion | flops 10852759552 | bytes 40906752 | tf_op jit(solution)/shard_map/dot_general | solution.py:59
  821.7 65.6 %reduce-scatter.9.cloned.1.call-done = bf16[1280,1024]{1,0:T(8,128)(2,1)} async-done(((bf16[2560,1024]{1,0:T(8,128)(2,1)}), bf16[1280,1024]{1,0:T(8,128)(2,1)}) %reduce-scatter.9.cloned.1.call-update) | async-done | bytes 2621456 | tf_op jit(solution)/shard_map/reduce_scatter | solution.py:198
  943.4 35.0 %all-gather.11.cloned.1.call-done = bf16[2560,1024]{1,0:T(8,128)(2,1)} async-done(((bf16[1280,1024]{1,0:T(8,128)(2,1)}), bf16[2560,1024]{1,0:T(8,128)(2,1)}) %all-gather.11.cloned.1.call-update) | async-done | bytes 5242896 | tf_op jit(solution)/shard_map/all_gather | solution.py:203
  985.1 862.8 %while.28 = (s32[]{:T(128)}, f32[2560,8,64]{0,2,1:T(8,128)}, f32[2560,8,64]{0,2,1:T(8,128)}, bf16[5,512,8,64]{1,3,2,0:T(8,128)(2,1)}, s32[5]{0:T(128)S(1)}, /*in...) while((s32[]{:T(128)}, f32[2560,8,64]{0,2,1:T(8,128)}, ...), condition=%wide.region_25.26_spmd.clone, body=%wide.region_23.25_spmd.clone.sunk | while | flops 6870810624 | bytes 506547488 | solution.py:121
  994.0 20.6 subtract_exponential_fusion.3
  1049.2 53.0 %fusion.174 = bf16[5,512,8,64]{1,3,2,0:T(8,128)(2,1)} fusion(bf16[5,512,8,64]{1,3,2,0:T(8,128)(2,1)} %get-tuple-element.459, s32[]{:T(128)S(6)} %copy.79, bf16[2560,8,64]{0,2,1:T(8,128)(2,1)} %get-tuple-element.481, f32[8,512,2560]{2,1,0:T(8,128)} %subtract_exponential_fusion.3, f32[8,512,2560]{2,1,0:T(8,128)} %fusion.173), kind=kOutput, calls=%fused_computation.39.clone.1 | convolution fusion | flops 1394612736 | bytes 171442176 | tf_op jit(solution)/shard_map/while/body/eval_jaxpr/hqk,khd->qhd/dot_general | solution.py:112
  1102.2 53.5 %bitcast_add_fusion.4 = f32[2560,8,64]{0,2,1:T(8,128)} fusion(f32[2560,8,64]{0,2,1:T(8,128)} %get-tuple-element.457, f32[8,512,2560]{2,1,0:T(8,128)} %subtract_exponential_fusion.3, f32[8,512,2560]{2,1,0:T(8,128)} %fusion.173, pred[]{:T(512)S(6)} %compare.3, bf16[2560,8,64]{0,2,1:T(8,128)(2,1)} %get-tuple-element.478, s32[]{:T(128)S(6)} %select_n.64), kind=kOutput, calls=%fused_computation.32.clone.1 | convolution fusion | flops 1397234176 | bytes 178782208 | tf_op jit(solution)/shard_map/while/body/eval_jaxpr/hqk,qhd->khd/dot_general | solution.py:115
  1164.0 20.6 subtract_exponential_fusion.3
  1184.6 18.8 bitcast_add_fusion.5
  1220.7 52.9 %fusion.174 = bf16[5,512,8,64]{1,3,2,0:T(8,128)(2,1)} fusion(bf16[5,512,8,64]{1,3,2,0:T(8,128)(2,1)} %get-tuple-element.459, s32[]{:T(128)S(6)} %copy.79, bf16[2560,8,64]{0,2,1:T(8,128)(2,1)} %get-tuple-element.481, f32[8,512,2560]{2,1,0:T(8,128)} %subtract_exponential_fusion.3, f32[8,512,2560]{2,1,0:T(8,128)} %fusion.173), kind=kOutput, calls=%fused_computation.39.clone.1 | convolution fusion | flops 1394612736 | bytes 171442176 | tf_op jit(solution)/shard_map/while/body/eval_jaxpr/hqk,khd->qhd/dot_general | solution.py:112
  1273.7 55.0 %bitcast_add_fusion.4 = f32[2560,8,64]{0,2,1:T(8,128)} fusion(f32[2560,8,64]{0,2,1:T(8,128)} %get-tuple-element.457, f32[8,512,2560]{2,1,0:T(8,128)} %subtract_exponential_fusion.3, f32[8,512,2560]{2,1,0:T(8,128)} %fusion.173, pred[]{:T(512)S(6)} %compare.3, bf16[2560,8,64]{0,2,1:T(8,128)(2,1)} %get-tuple-element.478, s32[]{:T(128)S(6)} %select_n.64), kind=kOutput, calls=%fused_computation.32.clone.1 | convolution fusion | flops 1397234176 | bytes 178782208 | tf_op jit(solution)/shard_map/while/body/eval_jaxpr/hqk,qhd->khd/dot_general | solution.py:115
  1337.1 20.6 subtract_exponential_fusion.3
  1357.7 18.8 bitcast_add_fusion.5
  1393.8 52.9 %fusion.174 = bf16[5,512,8,64]{1,3,2,0:T(8,128)(2,1)} fusion(bf16[5,512,8,64]{1,3,2,0:T(8,128)(2,1)} %get-tuple-element.459, s32[]{:T(128)S(6)} %copy.79, bf16[2560,8,64]{0,2,1:T(8,128)(2,1)} %get-tuple-element.481, f32[8,512,2560]{2,1,0:T(8,128)} %subtract_exponential_fusion.3, f32[8,512,2560]{2,1,0:T(8,128)} %fusion.173), kind=kOutput, calls=%fused_computation.39.clone.1 | convolution fusion | flops 1394612736 | bytes 171442176 | tf_op jit(solution)/shard_map/while/body/eval_jaxpr/hqk,khd->qhd/dot_general | solution.py:112
  1446.7 54.9 %bitcast_add_fusion.4 = f32[2560,8,64]{0,2,1:T(8,128)} fusion(f32[2560,8,64]{0,2,1:T(8,128)} %get-tuple-element.457, f32[8,512,2560]{2,1,0:T(8,128)} %subtract_exponential_fusion.3, f32[8,512,2560]{2,1,0:T(8,128)} %fusion.173, pred[]{:T(512)S(6)} %compare.3, bf16[2560,8,64]{0,2,1:T(8,128)(2,1)} %get-tuple-element.478, s32[]{:T(128)S(6)} %select_n.64), kind=kOutput, calls=%fused_computation.32.clone.1 | convolution fusion | flops 1397234176 | bytes 178782208 | tf_op jit(solution)/shard_map/while/body/eval_jaxpr/hqk,qhd->khd/dot_general | solution.py:115
  1510.1 20.6 subtract_exponential_fusion.3
  1530.6 18.8 bitcast_add_fusion.5
  1566.8 52.9 %fusion.174 = bf16[5,512,8,64]{1,3,2,0:T(8,128)(2,1)} fusion(bf16[5,512,8,64]{1,3,2,0:T(8,128)(2,1)} %get-tuple-element.459, s32[]{:T(128)S(6)} %copy.79, bf16[2560,8,64]{0,2,1:T(8,128)(2,1)} %get-tuple-element.481, f32[8,512,2560]{2,1,0:T(8,128)} %subtract_exponential_fusion.3, f32[8,512,2560]{2,1,0:T(8,128)} %fusion.173), kind=kOutput, calls=%fused_computation.39.clone.1 | convolution fusion | flops 1394612736 | bytes 171442176 | tf_op jit(solution)/shard_map/while/body/eval_jaxpr/hqk,khd->qhd/dot_general | solution.py:112
  1619.7 55.0 %bitcast_add_fusion.4 = f32[2560,8,64]{0,2,1:T(8,128)} fusion(f32[2560,8,64]{0,2,1:T(8,128)} %get-tuple-element.457, f32[8,512,2560]{2,1,0:T(8,128)} %subtract_exponential_fusion.3, f32[8,512,2560]{2,1,0:T(8,128)} %fusion.173, pred[]{:T(512)S(6)} %compare.3, bf16[2560,8,64]{0,2,1:T(8,128)(2,1)} %get-tuple-element.478, s32[]{:T(128)S(6)} %select_n.64), kind=kOutput, calls=%fused_computation.32.clone.1 | convolution fusion | flops 1397234176 | bytes 178782208 | tf_op jit(solution)/shard_map/while/body/eval_jaxpr/hqk,qhd->khd/dot_general | solution.py:115
  1683.1 20.6 subtract_exponential_fusion.3
  1703.7 18.8 bitcast_add_fusion.5
  1739.8 52.9 %fusion.174 = bf16[5,512,8,64]{1,3,2,0:T(8,128)(2,1)} fusion(bf16[5,512,8,64]{1,3,2,0:T(8,128)(2,1)} %get-tuple-element.459, s32[]{:T(128)S(6)} %copy.79, bf16[2560,8,64]{0,2,1:T(8,128)(2,1)} %get-tuple-element.481, f32[8,512,2560]{2,1,0:T(8,128)} %subtract_exponential_fusion.3, f32[8,512,2560]{2,1,0:T(8,128)} %fusion.173), kind=kOutput, calls=%fused_computation.39.clone.1 | convolution fusion | flops 1394612736 | bytes 171442176 | tf_op jit(solution)/shard_map/while/body/eval_jaxpr/hqk,khd->qhd/dot_general | solution.py:112
  1792.7 55.0 %bitcast_add_fusion.4 = f32[2560,8,64]{0,2,1:T(8,128)} fusion(f32[2560,8,64]{0,2,1:T(8,128)} %get-tuple-element.457, f32[8,512,2560]{2,1,0:T(8,128)} %subtract_exponential_fusion.3, f32[8,512,2560]{2,1,0:T(8,128)} %fusion.173, pred[]{:T(512)S(6)} %compare.3, bf16[2560,8,64]{0,2,1:T(8,128)(2,1)} %get-tuple-element.478, s32[]{:T(128)S(6)} %select_n.64), kind=kOutput, calls=%fused_computation.32.clone.1 | convolution fusion | flops 1397234176 | bytes 178782208 | tf_op jit(solution)/shard_map/while/body/eval_jaxpr/hqk,qhd->khd/dot_general | solution.py:115
  1931.4 36.0 %all-reduce = (bf16[2,512]{1,0:T(2,128)(2,1)S(1)}, bf16[2048]{0:T(1024)(128)(2,1)S(1)}) all-reduce(bf16[2,512]{1,0:T(2,128)(2,1)S(1)} %pad_maximum_fusion.1, bf16[2048]{0:T(1024)(128)(2,1)S(1)} %copy-done.47), channel_id=1, replica_groups=mesh['dp'=16,'mp'=2] {'dp'}, use_global_device_ids=true, to_apply=%region_43.44 | all-reduce | flops 3072 | bytes 12288 | tf_op jit(solution)/shard_map/psum | solution.py:243
  1968.7 181.6 %all-reduce.4.cloned.1.call-done = (bf16[1024,3,512]{2,0,1:T(8,128)(2,1)}, bf16[512,1024]{1,0:T(8,128)(2,1)}, bf16[1024,2048]{1,0:T(8,128)(2,1)}, bf16[2048,1024]{1,0:T(8,128)(2,1)}) async-done(((bf16[1024,3,512]{2,0,1:T(8,128)(2,1)}, bf16[512,1024]{1,0:T(8,128)(2,1)}, bf16[1024,2048]{1,0:T(8,128)(2,1)}, bf16[2048,1024]{1,0:T(8,128)(2,1)}), (bf16[1024,3,512]{2,0,1:T(8,128)(2,1)}, ...) | async-done | bytes 12582928 | tf_op jit(solution)/shard_map/psum | solution.py:242
  2165.8 52.6 %reduce-scatter.11.cloned.1.call-done = bf16[1280,1024]{1,0:T(8,128)(2,1)} async-done(((bf16[2560,1024]{1,0:T(8,128)(2,1)}), bf16[1280,1024]{1,0:T(8,128)(2,1)}) %reduce-scatter.11.cloned.1.call-update) | async-done | bytes 2621456 | tf_op jit(solution)/shard_map/reduce_scatter | solution.py:219
  2222.9 39.7 %psum.49 = f32[10,1024]{1,0:T(8,128)S(1)} all-reduce(f32[10,1024]{1,0:T(8,128)S(1)} %stack.59), channel_id=1, replica_groups=mesh['dp'=16,'mp'=2] {'dp','mp'}, use_global_device_ids=true, to_apply=%region_39.40 | all-reduce | flops 10240 | bytes 81920 | tf_op jit(solution)/shard_map/psum | solution.py:249
  (294 shorter events, 466.1 us)
Async XLA Ops:
  7.2 424.9 %copy-start = (bf16[512,1024]{1,0:T(8,128)(2,1)S(1)}, bf16[512,1024]{1,0:T(8,128)(2,1)}, u32[]{:S(2)}) copy-start(bf16[512,1024]{1,0:T(8,128)(2,1)} %param.29) | copy-start | bytes 3145732
  7.2 79.4 %all-gather.5.cloned.1.call-start = ((), (), s32[]{:S(2)}) async-start(), calls=%async_computation.4 | async-start | bytes 7864320 | tf_op jit(solution)/shard_map/all_gather | solution.py:158
  15.2 487.4 %reduce-scatter.5.cloned.1.call-start = ((), (), s32[]{:S(2)}) async-start(), calls=%async_computation.5 | async-start | bytes 7864320 | tf_op jit(solution)/shard_map/reduce_scatter | solution.py:166
  137.6 18.8 copy-start.7
  200.0 18.8 copy-start.7
  262.4 18.8 copy-start.7
  324.8 18.8 copy-start.7
  387.2 18.8 copy-start.7
  436.8 65.9 %copy-start.24 = (f32[1024]{0:T(1024)S(1)}, f32[1024]{0:T(1024)}, u32[]{:S(2)}) copy-start(f32[1024]{0:T(1024)} %param.30) | copy-start | bytes 12292
  436.8 71.1 %copy-start.27 = (f32[1024]{0:T(1024)S(1)}, f32[1024]{0:T(1024)}, u32[]{:S(2)}) copy-start(f32[1024]{0:T(1024)} %param.31) | copy-start | bytes 12292
  436.8 71.1 %copy-start.31 = (f32[1024]{0:T(1024)S(1)}, f32[1024]{0:T(1024)}, u32[]{:S(2)}) copy-start(f32[1024]{0:T(1024)} %param.32) | copy-start | bytes 12292
  436.8 151.5 %all-gather.7.cloned.1.call-start = ((), (), s32[]{:S(2)}) async-start(), calls=%async_computation.6 | async-start | bytes 7864320 | tf_op jit(solution)/shard_map/all_gather | solution.py:176
  512.9 75.4 %copy-start.51 = (f32[2048]{0:T(1024)S(1)}, f32[2048]{0:T(1024)}, u32[]{:S(2)}) copy-start(f32[2048]{0:T(1024)} %param.36) | copy-start | bytes 24580
  519.6 174.0 %reduce-scatter.7.cloned.1.call-start = ((), (), s32[]{:S(2)}) async-start(), calls=%async_computation.7 | async-start | bytes 7864320 | tf_op jit(solution)/shard_map/reduce_scatter | solution.py:180
  588.3 24.2 %copy-start.49 = (bf16[2048,1024]{1,0:T(8,128)(2,1)S(1)}, bf16[2048,1024]{1,0:T(8,128)(2,1)}, u32[]{:S(2)}) copy-start(bf16[2048,1024]{1,0:T(8,128)(2,1)} %param.37) | copy-start | bytes 12582916
  627.7 65.9 %copy-start.30 = (f32[1024]{0:T(1024)S(1)}, f32[1024]{0:T(1024)}, u32[]{:S(2)}) copy-start(f32[1024]{0:T(1024)} %param.38) | copy-start | bytes 12292
  627.7 71.1 %copy-start.32 = (f32[1024]{0:T(1024)S(1)}, f32[1024]{0:T(1024)}, u32[]{:S(2)}) copy-start(f32[1024]{0:T(1024)} %param.39) | copy-start | bytes 12292
  627.7 147.4 %all-gather.9.cloned.1.call-start = ((), (), s32[]{:S(2)}) async-start(), calls=%async_computation.8 | async-start | bytes 7864320 | tf_op jit(solution)/shard_map/all_gather | solution.py:192
  706.4 180.9 %reduce-scatter.9.cloned.1.call-start = ((), (), s32[]{:S(2)}) async-start(), calls=%async_computation.9 | async-start | bytes 7864320 | tf_op jit(solution)/shard_map/reduce_scatter | solution.py:198
  775.1 30.8 %copy-start.50 = (bf16[1024,2048]{1,0:T(8,128)(2,1)S(1)}, bf16[1024,2048]{1,0:T(8,128)(2,1)}, u32[]{:S(2)}) copy-start(bf16[1024,2048]{1,0:T(8,128)(2,1)} %param.35) | copy-start | bytes 12582916
  821.5 65.9 %copy-start.46 = (f32[1024]{0:T(1024)S(1)}, f32[1024]{0:T(1024)}, u32[]{:S(2)}) copy-start(f32[1024]{0:T(1024)} %param.40) | copy-start | bytes 12292
  821.5 156.9 %all-gather.11.cloned.1.call-start = ((), (), s32[]{:S(2)}) async-start(), calls=%async_computation.10 | async-start | bytes 7864320 | tf_op jit(solution)/shard_map/all_gather | solution.py:203
  887.3 11.5 copy-start.4
  887.3 11.5 copy-start.6
  887.3 11.5 copy-start.12
  887.3 11.5 copy-start.14
  909.7 1240.5 %all-reduce.4.cloned.1.call-start = ((), (), s32[]{:S(2)}) async-start(), calls=%async_computation.12 | async-start | bytes 25165824 | tf_op jit(solution)/shard_map/psum | solution.py:242
  943.4 41.7 %copy-start.21 = (s32[2560]{0:T(1024)S(1)}, s32[2560]{0:T(1024)}, u32[]{:S(2)}) copy-start(s32[2560]{0:T(1024)} %copy-done.20) | copy-start | bytes 30724
  943.4 41.7 %copy-start.23 = (s32[2560]{0:T(1024)S(1)}, s32[2560]{0:T(1024)}, u32[]{:S(2)}) copy-start(s32[2560]{0:T(1024)} %param.42) | copy-start | bytes 30724
  1014.5 17.4 copy-start.8
  1184.6 18.8 copy-start.8
  1357.7 18.8 copy-start.8
  1530.6 18.8 copy-start.8
  1703.7 18.8 copy-start.8
  1886.9 18.1 slice-start
  1897.8 7.3 slice-start.1
  1914.8 303.6 %reduce-scatter.11.cloned.1.call-start = ((), (), s32[]{:S(2)}) async-start(), calls=%async_computation.11 | async-start | bytes 7864320 | tf_op jit(solution)/shard_map/reduce_scatter | solution.py:219
  2161.3 57.1 %copy-start.26 = (f32[1280]{0:T(1024)S(1)}, f32[1280]{0:T(1024)}, u32[]{:S(2)}) copy-start(f32[1280]{0:T(1024)} %copy-done.25) | copy-start | bytes 15364
  2161.3 57.1 %copy-start.29 = (f32[1280]{0:T(1024)S(1)}, f32[1280]{0:T(1024)}, u32[]{:S(2)}) copy-start(f32[1280]{0:T(1024)} %copy-done.28) | copy-start | bytes 15364
  2161.3 57.1 %copy-start.34 = (f32[1024]{0:T(1024)S(1)}, f32[1024]{0:T(1024)}, u32[]{:S(2)}) copy-start(f32[1024]{0:T(1024)} %param.25) | copy-start | bytes 12292
  2165.7 57.0 %copy-start.36 = (f32[1024]{0:T(1024)S(1)}, f32[1024]{0:T(1024)}, u32[]{:S(2)}) copy-start(f32[1024]{0:T(1024)} %get-tuple-element.178) | copy-start | bytes 12292
  2165.7 57.0 %copy-start.37 = (f32[1024]{0:T(1024)S(1)}, f32[1024]{0:T(1024)}, u32[]{:S(2)}) copy-start(f32[1024]{0:T(1024)} %get-tuple-element.187) | copy-start | bytes 12292
  2165.7 57.0 %copy-start.38 = (f32[1024]{0:T(1024)S(1)}, f32[1024]{0:T(1024)}, u32[]{:S(2)}) copy-start(f32[1024]{0:T(1024)} %get-tuple-element.242) | copy-start | bytes 12292
  2165.7 57.0 %copy-start.39 = (f32[1024]{0:T(1024)S(1)}, f32[1024]{0:T(1024)}, u32[]{:S(2)}) copy-start(f32[1024]{0:T(1024)} %get-tuple-element.174) | copy-start | bytes 12292
  2165.7 57.0 %copy-start.40 = (f32[1024]{0:T(1024)S(1)}, f32[1024]{0:T(1024)}, u32[]{:S(2)}) copy-start(f32[1024]{0:T(1024)} %get-tuple-element.188) | copy-start | bytes 12292
  2165.7 57.0 %copy-start.41 = (f32[1024]{0:T(1024)S(1)}, f32[1024]{0:T(1024)}, u32[]{:S(2)}) copy-start(f32[1024]{0:T(1024)} %get-tuple-element.244) | copy-start | bytes 12292
  2165.7 57.0 %copy-start.42 = (f32[1024]{0:T(1024)S(1)}, f32[1024]{0:T(1024)}, u32[]{:S(2)}) copy-start(f32[1024]{0:T(1024)} %get-tuple-element.176) | copy-start | bytes 12292
  2165.7 57.0 %copy-start.43 = (f32[1024]{0:T(1024)S(1)}, f32[1024]{0:T(1024)}, u32[]{:S(2)}) copy-start(f32[1024]{0:T(1024)} %get-tuple-element.183) | copy-start | bytes 12292
  (24 other events, 109.0 us)
Sparse Core Ops, SparseCore 0:
  15.3 71.2 all-gather.4
  436.9 65.6 reduce-scatter.4
  519.7 68.5 all-gather.6
  627.8 65.6 reduce-scatter.6
  706.5 68.5 all-gather.8
  821.6 65.6 reduce-scatter.8
  909.8 68.5 all-gather.10
  1914.9 235.2 all-reduce.3
  2152.6 65.6 reduce-scatter.10
where the time goes:
time: 2290 us; the launch traced here: 2280 us
  matrix products  1180 us (52%)
  waiting for transfers between devices  670 us (29%)
  other arithmetic  249 us (11%)
  blocking collectives  75.7 us (3%)
  local copies, waits for them, and re-layouts  69.7 us (3%)
    dot_general x5, matrix products, step_block(): jnp.einsum('hqk,qhd->khd', grad_scores, query_blk, preferred_element_type...  273 us
    dot_general x5, matrix products, step_block(): jnp.einsum('hqk,khd->qhd', grad_scores, keys_all, preferred_element_type=...  265 us
    dot_general x10, matrix products, masked_scores(): jnp.einsum('qhd,khd->hqk', query_blk, keys_all, preferred_element_type=jn...  196 us
    psum x1, waiting for transfers between devices, body(): lax.psum(g_w_qkv.astype(jnp.bfloat16), 'dp').astype(jnp.float32)  182 us
    reduce_sum x5, other arithmetic, score_block(): row_total = jnp.sum(exp_scores, -1, keepdims=True)  94 us
    dot_general x5, matrix products, score_block(): jnp.einsum('hqk,khd->qhd', probs, values_all, preferred_element_type=jnp....  92.9 us
    dot_general x5, matrix products, step_block(): jnp.einsum('hqk,qhd->khd', probs.astype(jnp.bfloat16), grad_blk, preferre...  92.6 us
    dot_general x5, matrix products, step_block(): jnp.einsum('qhd,khd->hqk', grad_blk, values_all, preferred_element_type=j...  86.5 us
  transfers between devices with their start and end apart: 9, of which 9 were waited for; matrix products, arithmetic and copies ran while one was open for 3% of the time, Pallas kernels for 0%

commit v1 on v0

v1 whole, which is shorter than its diff:
```python
import functools

import jax
import jax.numpy as jnp
from jax import lax
from jax.experimental import pallas as pl
from jax.experimental.pallas import tpu as pltpu
from jax.sharding import PartitionSpec as P

HDIM = 64
TEXT = 64


epsilon = 1e-05
masked_score = -1e30


def norm_parts(values, ln_gain, ln_bias):
    centred = values - jnp.mean(values, -1, keepdims=True)
    inv_std = lax.rsqrt(jnp.mean(centred * centred, -1, keepdims=True) + epsilon)
    normed = centred * inv_std
    return (normed * ln_gain + ln_bias, normed, inv_std)


def norm_back(upstream, normed, inv_std, ln_gain):
    scaled = upstream * ln_gain
    return inv_std * (
        scaled
        - jnp.mean(scaled, -1, keepdims=True)
        - normed * jnp.mean(scaled * normed, -1, keepdims=True)
    )


def gelu_tanh(values):
    return jax.nn.gelu(values, approximate=True)


def contract_rows(left, right):
    return lax.dot_general(
        left, right, (((0,), (0,)), ((), ())), preferred_element_type=jnp.float32
    )


def contract_cols(left, right):
    return lax.dot_general(
        left, right, (((1,), (1,)), ((), ())), preferred_element_type=jnp.float32
    )


BQ=256; BK=256
F32=jnp.float32; BF16=jnp.bfloat16

def dot(a,b):
    return jnp.dot(a,b,preferred_element_type=F32)

def row_tables(grid_row, tokens):
    side=jnp.max(grid_row)
    length=TEXT+side*side
    rows=tokens//length
    used=rows*length
    position=jnp.arange(tokens,dtype=jnp.int32)
    seg=jnp.minimum(position//length,rows)
    blocks=tokens//BQ
    first=jnp.arange(blocks,dtype=jnp.int32)*BQ
    last=first+BQ-1
    start=jnp.where(first<used,(first//length)*length,first)
    low=start//BK
    diag=first//BK
    row_start=(last//length)*length
    clean=jnp.where(last<used,(row_start+TEXT+BK-1)//BK,diag)
    clean=jnp.clip(clean,low,diag)
    return seg,jnp.stack([low,clean,diag]).astype(jnp.int32)

def allowed(kseg_ref,qseg_ref,i,j):
    qs=qseg_ref[:,pl.ds(pl.multiple_of(i*BQ,BQ),BQ)]
    ks=kseg_ref[pl.ds(pl.multiple_of(j*BK,BK),BK),:]
    ik=j*BK+lax.broadcasted_iota(jnp.int32,(BK,BQ),0)
    iq=i*BQ+lax.broadcasted_iota(jnp.int32,(BK,BQ),1)
    return ((ks==qs)&(ik<=iq))|(ik==iq)

def sweep(tab_ref,i,step,carry):
    low,clean,diag=tab_ref[0,i],tab_ref[1,i],tab_ref[2,i]
    carry=lax.fori_loop(low,clean,functools.partial(step,True),carry)
    carry=lax.fori_loop(clean,diag,functools.partial(step,False),carry)
    return lax.fori_loop(diag,diag+BQ//BK if BQ>BK else diag+1,functools.partial(step,True),carry)

def forward_kernel(tab_ref,kseg_ref,qseg_ref,q_ref,k_ref,v_ref,o_ref,lse_ref,kx,vx):
    tokens=q_ref.shape[1]
    lane=lax.broadcasted_iota(jnp.int32,(BK,128),1)
    def prepare(c,_):
        at=pl.ds(pl.multiple_of(c*BK,BK),BK)
        kt=k_ref[:,at].astype(F32).T
        kx[0,at,:]=jnp.where(lane<HDIM,kt,0.0).astype(BF16)
        kx[1,at,:]=jnp.where(lane<HDIM,0.0,kt).astype(BF16)
        return 0
    lax.fori_loop(0,tokens//BK,prepare,0)
    for h in range(2):
        vx[h,:HDIM,:]=v_ref[h*HDIM:(h+1)*HDIM,:]
        vx[h,HDIM:,:]=jnp.ones((16,tokens),BF16)
    def block(i,_):
        cols=pl.ds(pl.multiple_of(i*BQ,BQ),BQ)
        qb=q_ref[:,cols]
        def step(masked,j,carry):
            at=pl.ds(pl.multiple_of(j*BK,BK),BK)
            if masked: ok=allowed(kseg_ref,qseg_ref,i,j)
            out=[]
            for h in range(2):
                top,acc=carry[h]
                s=dot(kx[h,at,:],qb)
                if masked: s=jnp.where(ok,s,masked_score)
                new=jnp.maximum(top,jnp.max(s,axis=0,keepdims=True))
                p=jnp.exp(s-new).astype(BF16)
                acc=acc*jnp.exp(top-new)+dot(vx[h,:,at],p)
                out.append((new,acc))
            return tuple(out)
        init=tuple((jnp.full((1,BQ),masked_score,F32),jnp.zeros((HDIM+16,BQ),F32)) for _ in range(2))
        res=sweep(tab_ref,i,step,init)
        for h in range(2):
            top,acc=res[h]
            total=acc[HDIM:HDIM+1,:]
            o_ref[h*HDIM:(h+1)*HDIM,cols]=(acc[:HDIM,:]/total).astype(BF16)
            lse_ref[0,h:h+1,cols]=top+jnp.log(total)
        return 0
    lax.fori_loop(0,tokens//BQ,block,0)

def parts3(x):
    hi=x.astype(BF16); r=x-hi.astype(F32)
    mid=r.astype(BF16); lo=(r-mid.astype(F32)).astype(BF16)
    return hi,mid,lo

def backward_kernel(tab_ref,kseg_ref,qseg_ref,q_ref,k_ref,v_ref,o_ref,do_ref,lse_ref,out_ref,
                    kx,vx,qx,dox,qt,dot_,dk,dv):
    tokens=q_ref.shape[1]
    lane=lax.broadcasted_iota(jnp.int32,(BK,128),1)
    sub=lax.broadcasted_iota(jnp.int32,(HDIM,BK),0)
    one0=jnp.where((lane>=HDIM)&(lane<HDIM+3),1.0,0.0)
    one1=jnp.where(lane<3,1.0,0.0)
    def extra(x):
        hi,mid,lo=(e.astype(F32) for e in parts3(x))
        z=jnp.where(sub==0,hi,jnp.where(sub==1,mid,jnp.where(sub==2,lo,0.0)))
        return z.astype(BF16)
    def prepare(c,_):
        at=pl.ds(pl.multiple_of(c*BK,BK),BK)
        kt=k_ref[:,at].astype(F32).T
        kx[0,at,:]=jnp.where(lane<HDIM,kt,one0).astype(BF16)
        kx[1,at,:]=jnp.where(lane<HDIM,one1,kt).astype(BF16)
        vt=v_ref[:,at].astype(F32).T
        vx[0,at,:]=jnp.where(lane<HDIM,vt,one0).astype(BF16)
        vx[1,at,:]=jnp.where(lane<HDIM,one1,vt).astype(BF16)
        q=q_ref[:,at]
        qtt=q.astype(F32).T
        qt[0,at,:]=jnp.where(lane<HDIM,qtt,0.0).astype(BF16)
        qt[1,at,:]=jnp.where(lane<HDIM,0.0,qtt).astype(BF16)
        do=do_ref[:,at]
        dof=do.astype(F32)
        dtt=dof.T
        dot_[0,at,:]=jnp.where(lane<HDIM,dtt,0.0).astype(BF16)
        dot_[1,at,:]=jnp.where(lane<HDIM,0.0,dtt).astype(BF16)
        prod=dof*o_ref[:,at].astype(F32)
        d0=jnp.sum(prod[:HDIM],axis=0,keepdims=True)
        d1=jnp.sum(prod[HDIM:],axis=0,keepdims=True)
        qx[0,:HDIM,at]=q[:HDIM]
        qx[0,HDIM:,at]=extra(-lse_ref[0,0:1,at])
        qx[1,HDIM:,at]=q[HDIM:]
        qx[1,:HDIM,at]=extra(-lse_ref[0,1:2,at])
        dox[0,:HDIM,at]=do[:HDIM]
        dox[0,HDIM:,at]=extra(-d0)
        dox[1,HDIM:,at]=do[HDIM:]
        dox[1,:HDIM,at]=extra(-d1)
        dk[at,:]=jnp.zeros((BK,128),F32)
        dv[at,:]=jnp.zeros((BK,128),F32)
        return 0
    lax.fori_loop(0,tokens//BK,prepare,0)
    def block(i,_):
        cols=pl.ds(pl.multiple_of(i*BQ,BQ),BQ)
        def step(masked,j,carry):
            at=pl.ds(pl.multiple_of(j*BK,BK),BK)
            if masked: ok=allowed(kseg_ref,qseg_ref,i,j)
            new=[]; dvs=dv[at,:]; dks=dk[at,:]
            for h in range(2):
                s=dot(kx[h,at,:],qx[h,:,cols])
                if masked: s=jnp.where(ok,s,masked_score)
                p=jnp.exp(s)
                dp=dot(vx[h,at,:],dox[h,:,cols])
                ds=(p*dp).astype(BF16)
                dvs=dvs+dot(p.astype(BF16),dot_[h,cols,:])
                dks=dks+dot(ds,qt[h,cols,:])
                new.append(carry[h]+dot(k_ref[h*HDIM:(h+1)*HDIM,at],ds))
            dv[at,:]=dvs
            dk[at,:]=dks
            return tuple(new)
        init=tuple(jnp.zeros((HDIM,BQ),F32) for _ in range(2))
        res=sweep(tab_ref,i,step,init)
        for h in range(2):
            out_ref[0,h*HDIM:(h+1)*HDIM,cols]=(res[h]*(HDIM**-0.5)).astype(BF16)
        return 0
    lax.fori_loop(0,tokens//BQ,block,0)
    def finish(c,_):
        at=pl.ds(pl.multiple_of(c*BK,BK),BK)
        out_ref[1,:,at]=dk[at,:].T.astype(BF16)
        out_ref[2,:,at]=dv[at,:].T.astype(BF16)
        return 0
    lax.fori_loop(0,tokens//BK,finish,0)

PAIR=2*HDIM
def specs(tokens,heads):
    pairs=heads//2
    seg_specs=[pl.BlockSpec((tokens,1),lambda g,t:(0,0)),pl.BlockSpec((1,tokens),lambda g,t:(0,0))]
    def part(c): return pl.BlockSpec((PAIR,tokens),lambda g,t,c=c:(c*pairs+g,0))
    return pairs,seg_specs,part

def attend_forward(qkv,seg,keep,tables):
    tokens=qkv.shape[1]; heads=qkv.shape[0]//(3*HDIM)
    pairs,seg_specs,part=specs(tokens,heads)
    kseg=jnp.where(keep==1,seg,-1)[:,None]
    return pl.pallas_call(forward_kernel,
        grid_spec=pltpu.PrefetchScalarGridSpec(num_scalar_prefetch=1,grid=(pairs,),
            in_specs=seg_specs+[part(0),part(1),part(2)],
            out_specs=[part(0),pl.BlockSpec((1,2,tokens),lambda g,t:(g,0,0))],
            scratch_shapes=[pltpu.VMEM((2,tokens,128),BF16),pltpu.VMEM((2,HDIM+16,tokens),BF16)]),
        out_shape=[jax.ShapeDtypeStruct((heads*HDIM,tokens),BF16),jax.ShapeDtypeStruct((pairs,2,tokens),F32)],
        compiler_params=pltpu.CompilerParams(vmem_limit_bytes=48*2**20),
        name="attend_forward",
    )(tables,kseg,seg[None,:],qkv,qkv,qkv)

def attend_backward(qkv,context,grad_ctx,lse,seg,keep,tables):
    tokens=qkv.shape[1]; heads=qkv.shape[0]//(3*HDIM)
    pairs,seg_specs,part=specs(tokens,heads)
    kseg=jnp.where(keep==1,seg,-1)[:,None]
    out=pl.pallas_call(backward_kernel,
        grid_spec=pltpu.PrefetchScalarGridSpec(num_scalar_prefetch=1,grid=(pairs,),
            in_specs=seg_specs+[part(0),part(1),part(2),part(0),part(0),pl.BlockSpec((1,2,tokens),lambda g,t:(g,0,0))],
            out_specs=pl.BlockSpec((3,PAIR,tokens),lambda g,t:(0,g,0)),
            scratch_shapes=[pltpu.VMEM((2,tokens,128),BF16),pltpu.VMEM((2,tokens,128),BF16),
                pltpu.VMEM((2,128,tokens),BF16),pltpu.VMEM((2,128,tokens),BF16),
                pltpu.VMEM((2,tokens,128),BF16),pltpu.VMEM((2,tokens,128),BF16),
                pltpu.VMEM((tokens,128),F32),pltpu.VMEM((tokens,128),F32)]),
        out_shape=jax.ShapeDtypeStruct((3,heads*HDIM,tokens),BF16),
        compiler_params=pltpu.CompilerParams(vmem_limit_bytes=48*2**20),
        name="attend_backward",
    )(tables,kseg,seg[None,:],qkv,qkv,qkv,context,grad_ctx,lse)
    return out.reshape(3*heads*HDIM,tokens)


def body(
    tokens,
    ln1_gain,
    ln1_bias,
    w_qkv,
    qv_bias,
    w_out,
    out_bias,
    ln2_gain,
    ln2_bias,
    ln3_gain,
    ln3_bias,
    w_up,
    up_bias,
    w_down,
    down_bias,
    ln4_gain,
    ln4_bias,
    row_grid,
    pad_mask,
    cotangent,
):
    model_dim = tokens.shape[1]
    group_rows = pad_mask.shape[0]
    local_width = w_qkv.shape[2]
    seg_all, tables = row_tables(row_grid[0], group_rows)
    flat_qkv = w_qkv.reshape(model_dim, 3 * local_width)
    resid_in = tokens.astype(jnp.float32)
    norm1_out, normed1, inv1 = norm_parts(resid_in, ln1_gain, ln1_bias)
    attn_full = lax.all_gather(norm1_out.astype(jnp.bfloat16), "mp", axis=0, tiled=True)
    qkv_raw = lax.dot_general(
        flat_qkv, attn_full, (((0,), (1,)), ((), ())), preferred_element_type=jnp.float32
    ).reshape(3, local_width, group_rows)
    query = (qkv_raw[0] + qv_bias[0][:, None]).astype(jnp.bfloat16) * HDIM ** (-0.5)
    values_all = (qkv_raw[2] + qv_bias[1][:, None]).astype(jnp.bfloat16)
    qkv = jnp.concatenate([query, qkv_raw[1].astype(jnp.bfloat16), values_all], 0)
    context, log_total = attend_forward(qkv, seg_all, pad_mask, tables)
    proj_sum = lax.psum_scatter(
        contract_rows(context, w_out).astype(jnp.bfloat16),
        "mp",
        scatter_dimension=0,
        tiled=True,
    ).astype(jnp.float32)
    branch_z = proj_sum + out_bias
    norm2_out, normed2, inv2 = norm_parts(branch_z, ln2_gain, ln2_bias)
    resid_mid = resid_in + norm2_out
    norm3_out, normed3, inv3 = norm_parts(resid_mid, ln3_gain, ln3_bias)
    ffn_full = lax.all_gather(norm3_out.astype(jnp.bfloat16), "mp", axis=0, tiled=True)
    hidden_pre = jnp.dot(ffn_full, w_up, preferred_element_type=jnp.float32) + up_bias
    hidden_act = gelu_tanh(hidden_pre).astype(jnp.bfloat16)
    branch_f = (
        lax.psum_scatter(
            jnp.dot(hidden_act, w_down, preferred_element_type=jnp.float32).astype(jnp.bfloat16),
            "mp",
            scatter_dimension=0,
            tiled=True,
        ).astype(jnp.float32)
        + down_bias
    )
    norm4_out, normed4, inv4 = norm_parts(branch_f, ln4_gain, ln4_bias)
    layer_out = (resid_mid + norm4_out).astype(jnp.bfloat16)
    upstream = cotangent.astype(jnp.float32)
    grad_f = norm_back(upstream, normed4, inv4, ln4_gain).astype(jnp.bfloat16)
    grad_f_full = lax.all_gather(grad_f, "mp", axis=0, tiled=True)
    g_w_down = contract_rows(hidden_act, grad_f_full)
    grad_act = contract_cols(grad_f_full, w_down)
    grad_pre = jax.vjp(gelu_tanh, hidden_pre)[1](grad_act)[0].astype(jnp.bfloat16)
    g_up_bias = jnp.sum(grad_pre.astype(jnp.float32), 0)
    g_w_up = contract_rows(ffn_full, grad_pre)
    grad_a3 = lax.psum_scatter(
        contract_cols(grad_pre, w_up).astype(jnp.bfloat16), "mp", scatter_dimension=0, tiled=True
    ).astype(jnp.float32)
    grad_mid = upstream + norm_back(grad_a3, normed3, inv3, ln3_gain)
    grad_z = norm_back(grad_mid, normed2, inv2, ln2_gain).astype(jnp.bfloat16)
    grad_z_full = lax.all_gather(grad_z, "mp", axis=0, tiled=True)
    g_w_out = jnp.dot(context, grad_z_full, preferred_element_type=jnp.float32)
    grad_ctx = contract_cols(w_out, grad_z_full).astype(jnp.bfloat16)
    grad_qkv = attend_backward(
        qkv, context, grad_ctx, log_total, seg_all, pad_mask, tables
    )
    sums = jnp.sum(grad_qkv.astype(jnp.float32).reshape(3, local_width, group_rows), 2)
    g_qv_bias = jnp.stack([sums[0], sums[2]], 0)
    g_w_qkv = lax.dot_general(
        attn_full, grad_qkv, (((0,), (1,)), ((), ())), preferred_element_type=jnp.float32
    ).reshape(model_dim, 3, local_width)
    grad_a1 = lax.psum_scatter(
        lax.dot_general(
            grad_qkv, flat_qkv, (((0,), (1,)), ((), ())), preferred_element_type=jnp.float32
        ).astype(jnp.bfloat16),
        "mp",
        scatter_dimension=0,
        tiled=True,
    ).astype(jnp.float32)
    grad_input = grad_mid + norm_back(grad_a1, normed1, inv1, ln1_gain)
    norm_terms = jnp.stack(
        [
            jnp.sum(grad_a1 * normed1, 0),
            jnp.sum(grad_a1, 0),
            jnp.sum(grad_z.astype(jnp.float32), 0),
            jnp.sum(grad_mid * normed2, 0),
            jnp.sum(grad_mid, 0),
            jnp.sum(grad_a3 * normed3, 0),
            jnp.sum(grad_a3, 0),
            jnp.sum(grad_f.astype(jnp.float32), 0),
            jnp.sum(upstream * normed4, 0),
            jnp.sum(upstream, 0),
        ],
        0,
    )
    weight_grads = (
        lax.psum(g_w_qkv.astype(jnp.bfloat16), "dp").astype(jnp.float32),
        lax.psum(g_qv_bias.astype(jnp.bfloat16), "dp").astype(jnp.float32),
        lax.psum(g_w_out.astype(jnp.bfloat16), "dp").astype(jnp.float32),
        lax.psum(g_w_up.astype(jnp.bfloat16), "dp").astype(jnp.float32),
        lax.psum(g_up_bias.astype(jnp.bfloat16), "dp").astype(jnp.float32),
        lax.psum(g_w_down.astype(jnp.bfloat16), "dp").astype(jnp.float32),
    )
    norm_grads = lax.psum(norm_terms, ("dp", "mp"))
    return (
        layer_out,
        grad_input,
        norm_grads[0],
        norm_grads[1],
        weight_grads[0],
        weight_grads[1],
        weight_grads[2],
        norm_grads[2],
        norm_grads[3],
        norm_grads[4],
        norm_grads[5],
        norm_grads[6],
        weight_grads[3],
        weight_grads[4],
        weight_grads[5],
        norm_grads[7],
        norm_grads[8],
        norm_grads[9],
    )


def solution(mesh):
    in_specs = (
        P(("dp", "mp"), None),
        P(),
        P(),
        P(None, None, "mp"),
        P(None, "mp"),
        P("mp", None),
        P(),
        P(),
        P(),
        P(),
        P(),
        P(None, "mp"),
        P("mp"),
        P("mp", None),
        P(),
        P(),
        P(),
        P("dp", None),
        P("dp"),
        P(("dp", "mp"), None),
    )
    out_specs = (
        P(("dp", "mp"), None),
        P(("dp", "mp"), None),
        P(),
        P(),
        P(None, None, "mp"),
        P(None, "mp"),
        P("mp", None),
        P(),
        P(),
        P(),
        P(),
        P(),
        P(None, "mp"),
        P("mp"),
        P("mp", None),
        P(),
        P(),
        P(),
    )
    return jax.shard_map(body, mesh=mesh, in_specs=in_specs, out_specs=out_specs, check_vma=False)
```

time: 2290 us -> 1340 us (0.59)
  matrix products: 1180 us -> 169 us
  Pallas kernels: 0 us -> 300 us
  other arithmetic: 249 us -> 98.7 us
  local copies, waits for them, and re-layouts: 69.7 us -> 9.65 us
    dot_general x37 -> x4, matrix products: 1020 us -> 39.2 us  [the longest x1 14.1 us: body(): lax.dot_general(grad_qkv, flat_qkv, (((0,), (1,)), ((), ())), preferred_e...]
    pallas_call x0 -> x2, Pallas kernels: none -> 300 us  [the longest x1 154 us: attend_forward(): pl.pallas_call(forward_kernel, grid_spec=pltpu.PrefetchScalarGridSpec(num...]
    reduce_sum x8 -> x1, other arithmetic: 101 us -> 4.44 us  [body(): jnp.sum(grad_qkv.astype(jnp.float32).reshape(3, local_width, group_rows), 2)]
    and x10 -> x0, other arithmetic: 44.1 us -> none  [permitted(): return same_row & causal & visible]
    dot_general x4 -> x3, matrix products: 67.2 us -> 52.5 us  [contract_cols(): lax.dot_general(left, right, (((1,), (1,)), ((), ())), preferred_element_...]
    dot_general x4 -> x3, matrix products: 50.6 us -> 38.4 us  [contract_rows(): lax.dot_general(left, right, (((0,), (0,)), ((), ())), preferred_element_...]
  transfers between devices with their start and end apart: 9 -> 9, of which waited for: 9 -> 9; matrix products, arithmetic and copies ran while one was open for 3% -> 6% of each run, Pallas kernels for 0% -> 0%
where the time goes in v1:
time: 1340 us; the launch traced here: 1330 us
  waiting for transfers between devices  653 us (49%)
  Pallas kernels  300 us (22%)
  matrix products  169 us (13%)
  other arithmetic  98.7 us (7%)
  blocking collectives  72.1 us (5%)
  between operations  15.9 us (1%)
    psum x1, waiting for transfers between devices, body(): lax.psum(g_w_qkv.astype(jnp.bfloat16), 'dp').astype(jnp.float32)  183 us
    pallas_call x1, Pallas kernels, attend_forward(): pl.pallas_call(forward_kernel, grid_spec=pltpu.PrefetchScalarGridSpec(num...  154 us
    pallas_call x1, Pallas kernels, attend_backward(): pl.pallas_call(backward_kernel, grid_spec=pltpu.PrefetchScalarGridSpec(nu...  147 us
    all_gather x1, waiting for transfers between devices, body(): lax.all_gather(norm3_out.astype(jnp.bfloat16), 'mp', axis=0, tiled=True)  68.7 us
    all_gather x1, waiting for transfers between devices, body(): grad_f_full = lax.all_gather(grad_f, 'mp', axis=0, tiled=True)  68.7 us
    reduce_scatter x1, waiting for transfers between devices, body(): lax.psum_scatter(contract_cols(grad_pre, w_up).astype(jnp.bfloat16), 'mp'...  65.8 us
    reduce_scatter x1, waiting for transfers between devices, body(): lax.psum_scatter(jnp.dot(hidden_act, w_down, preferred_element_type=jnp.f...  65.4 us
    all_gather x1, waiting for transfers between devices, body(): lax.all_gather(norm1_out.astype(jnp.bfloat16), 'mp', axis=0, tiled=True)  63.2 us
  transfers between devices with their start and end apart: 9, of which 9 were waited for; matrix products, arithmetic and copies ran while one was open for 6% of the time, Pallas kernels for 0%

profile of v1, /device:TPU:0, one launch (start us, length us, event | category | flops | bytes accessed | tf_op | source)
XLA Modules:
  0.0 1332.7 jit_solution(12112146208101333800)
XLA Ops:
  9.6 2.6 fusion.25
  12.3 2.3 fusion.21
  17.2 4.6 copy.41
  22.9 63.2 %all-gather.5.cloned.1.call-done = bf16[2560,1024]{1,0:T(8,128)(2,1)} async-done(((bf16[1280,1024]{1,0:T(8,128)(2,1)}), bf16[2560,1024]{1,0:T(8,128)(2,1)}) %all-gather.5.cloned.1.call-update) | async-done | bytes 5242896 | tf_op jit(solution)/shard_map/all_gather | solution.py:274
  86.1 11.4 convolution_bitcast_fusion
  97.5 3.1 fusion.48
  103.2 3.5 pad_maximum_fusion.q_ref.k_ref.v_ref
  106.7 153.7 %attend_forward.1 = (bf16[512,2560]{1,0:T(8,128)(2,1)S(1)}, f32[4,2,2560]{2,1,0:T(2,128)S(1)}) custom-call(s32[3,10]{1,0:T(4,128)S(1)} %pad_add_fusion.tab_ref, s32[2560,1]{1,0:T(8,128)S(1)} %broadcast_in_dim.6.kseg_ref, s32[1,2560]{1,0:T(1,128)S(1)} %fusion.55.qseg_ref, bf16[1536,2560]{1,0:T(8,128)(2,1)} %pad_maximum_fusion.q_ref.k_ref.v_ref, ...), custom_call_target="tpu_custom_call" | custom-call | tf_op jit(solution)/shard_map/attend_forward/pallas_call | solution.py:216
  260.5 4.7 convolution_convert_fusion.2
  266.7 12.4 all-gather.7.cloned.1.call-start
  279.0 52.5 %reduce-scatter.5.cloned.1.call-done = bf16[1280,1024]{1,0:T(8,128)(2,1)} async-done(((bf16[2560,1024]{1,0:T(8,128)(2,1)}), bf16[1280,1024]{1,0:T(8,128)(2,1)}) %reduce-scatter.5.cloned.1.call-update) | async-done | bytes 2621456 | tf_op jit(solution)/shard_map/reduce_scatter | solution.py:282
  331.6 2.5 fusion.45
  334.1 2.7 multiply_reduce_fusion.4
  339.1 2.6 multiply_reduce_fusion.3
  341.8 6.6 add_convert_fusion.1
  348.5 68.7 %all-gather.7.cloned.1.call-done = bf16[2560,1024]{1,0:T(8,128)(2,1)} async-done(((bf16[1280,1024]{1,0:T(8,128)(2,1)}), bf16[2560,1024]{1,0:T(8,128)(2,1)}) %all-gather.7.cloned.1.call-update) | async-done | bytes 5242896 | tf_op jit(solution)/shard_map/all_gather | solution.py:292
  417.2 24.0 %multiply_convert_fusion = (bf16[2560,2048]{1,0:T(8,128)(2,1)}, f32[2560,2048]{1,0:T(8,128)}) fusion(f32[2048]{0:T(1024)S(1)} %copy-done.41, bf16[2560,1024]{1,0:T(8,128)(2,1)} %all-gather.7.cloned.1.call-done, bf16[1024,2048]{1,0:T(8,128)(2,1)} %param.31), kind=kOutput, calls=%fused_computation.9 | convolution fusion | flops 10789847040 | bytes 40902656 | tf_op jit(solution)/shard_map/dot_general | solution.py:293
  441.3 15.3 %convolution_convert_fusion.1 = bf16[2560,1024]{1,0:T(8,128)(2,1)} fusion(bf16[2560,2048]{1,0:T(8,128)(2,1)} %get-tuple-element.66, bf16[2048,1024]{1,0:T(8,128)(2,1)S(1)} %copy-done.39), kind=kOutput, calls=%fused_computation.40 | convolution fusion | flops 10740039680 | bytes 19922944 | tf_op jit(solution)/shard_map/dot_general | solution.py:297
  457.0 65.4 %reduce-scatter.7.cloned.1.call-done = bf16[1280,1024]{1,0:T(8,128)(2,1)} async-done(((bf16[2560,1024]{1,0:T(8,128)(2,1)}), bf16[1280,1024]{1,0:T(8,128)(2,1)}) %reduce-scatter.7.cloned.1.call-update) | async-done | bytes 2621456 | tf_op jit(solution)/shard_map/reduce_scatter | solution.py:296
  522.4 2.5 fusion.42
  524.9 2.7 multiply_reduce_fusion.2
  527.6 3.8 fusion.36
  531.4 3.8 convert_reduce_fusion.4
  535.3 68.7 %all-gather.9.cloned.1.call-done = bf16[2560,1024]{1,0:T(8,128)(2,1)} async-done(((bf16[1280,1024]{1,0:T(8,128)(2,1)}), bf16[2560,1024]{1,0:T(8,128)(2,1)}) %all-gather.9.cloned.1.call-update) | async-done | bytes 5242896 | tf_op jit(solution)/shard_map/all_gather | solution.py:308
  604.0 30.3 %fusion.64 = (bf16[2048]{0:T(1024)(128)(2,1)S(1)}, bf16[2560,2048]{1,0:T(8,128)(2,1)}) fusion(f32[2560,2048]{1,0:T(8,128)} %get-tuple-element.67, f32[2048]{0:T(1024)S(1)} %copy-done.41, bf16[2560,1024]{1,0:T(8,128)(2,1)} %all-gather.9.cloned.1.call-done, bf16[2048,1024]{1,0:T(8,128)(2,1)} %param.33), kind=kOutput, calls=%fused_computation.143 | convolution fusion | flops 10852759552 | bytes 40906752 | tf_op jit(solution)/shard_map/dot_general | solution.py:45
  634.2 15.4 %convolution_convert_fusion = bf16[2560,1024]{1,0:T(8,128)(2,1)} fusion(bf16[2560,2048]{1,0:T(8,128)(2,1)} %get-tuple-element.69, bf16[1024,2048]{1,0:T(8,128)(2,1)S(1)} %copy-done.40), kind=kOutput, calls=%fused_computation.39 | convolution fusion | flops 10740039680 | bytes 19922944 | tf_op jit(solution)/shard_map/dot_general | solution.py:45
  649.7 65.8 %reduce-scatter.9.cloned.1.call-done = bf16[1280,1024]{1,0:T(8,128)(2,1)} async-done(((bf16[2560,1024]{1,0:T(8,128)(2,1)}), bf16[1280,1024]{1,0:T(8,128)(2,1)}) %reduce-scatter.9.cloned.1.call-update) | async-done | bytes 2621456 | tf_op jit(solution)/shard_map/reduce_scatter | solution.py:314
  715.6 10.8 fusion.34
  726.4 6.3 multiply_reduce_fusion
  732.8 3.1 convert_reduce_fusion.5
  736.0 17.0 %convolution_convert_fusion.4 = bf16[1024,2048]{1,0:T(8,128)(2,1)} fusion(bf16[2560,1024]{1,0:T(8,128)(2,1)} %all-gather.7.cloned.1.call-done, bf16[2560,2048]{1,0:T(8,128)(2,1)} %get-tuple-element.69), kind=kOutput, calls=%fused_computation.88 | convolution fusion | flops 10739515392 | bytes 19922944 | tf_op jit(solution)/shard_map/dot_general | solution.py:39
  753.0 16.8 %convolution_convert_fusion.5 = bf16[2048,1024]{1,0:T(8,128)(2,1)} fusion(bf16[2560,2048]{1,0:T(8,128)(2,1)} %get-tuple-element.66, bf16[2560,1024]{1,0:T(8,128)(2,1)} %all-gather.9.cloned.1.call-done), kind=kOutput, calls=%fused_computation.89 | convolution fusion | flops 10739515392 | bytes 19922944 | tf_op jit(solution)/shard_map/dot_general | solution.py:39
  769.8 34.9 %all-gather.11.cloned.1.call-done = bf16[2560,1024]{1,0:T(8,128)(2,1)} async-done(((bf16[1280,1024]{1,0:T(8,128)(2,1)}), bf16[2560,1024]{1,0:T(8,128)(2,1)}) %all-gather.11.cloned.1.call-update) | async-done | bytes 5242896 | tf_op jit(solution)/shard_map/all_gather | solution.py:319
  804.7 6.8 fusion.47.do_ref
  811.5 146.6 %attend_backward.1 = bf16[3,512,2560]{2,1,0:T(8,128)(2,1)} custom-call(s32[3,10]{1,0:T(4,128)S(1)} %pad_add_fusion.tab_ref, s32[2560,1]{1,0:T(8,128)S(1)} %broadcast_in_dim.6.kseg_ref, s32[1,2560]{1,0:T(1,128)S(1)} %fusion.55.qseg_ref, bf16[1536,2560]{1,0:T(8,128)(2,1)} %pad_maximum_fusion.q_ref.k_ref.v_ref, ...), custom_call_target="tpu_custom_call" | custom-call | tf_op jit(solution)/shard_map/attend_backward/pallas_call | solution.py:230
  958.2 3.8 convolution_convert_fusion.6
  962.0 9.8 fusion.49
  971.9 14.1 %bitcast_convert_fusion = bf16[2560,1024]{1,0:T(8,128)(2,1)} fusion(bf16[3,512,2560]{2,1,0:T(8,128)(2,1)} %attend_backward.1, bf16[1024,3,512]{2,0,1:T(8,128)(2,1)} %param.23), kind=kOutput, calls=%fused_computation.11 | convolution fusion | flops 8055685120 | bytes 16252928 | tf_op jit(solution)/shard_map/dot_general | solution.py:331
  986.0 4.4 reduce.2
  990.5 32.4 %all-reduce = (bf16[2,512]{1,0:T(2,128)(2,1)S(1)}, bf16[2048]{0:T(1024)(128)(2,1)S(1)}) all-reduce(bf16[2,512]{1,0:T(2,128)(2,1)S(1)} %pad_maximum_fusion.1, bf16[2048]{0:T(1024)(128)(2,1)S(1)} %get-tuple-element.68), channel_id=1, replica_groups=mesh['dp'=16,'mp'=2] {'dp'}, use_global_device_ids=true, to_apply=%region_34.35 | all-reduce | flops 3072 | bytes 12288 | tf_op jit(solution)/shard_map/psum | solution.py:356
  1024.1 182.5 %all-reduce.4.cloned.1.call-done = (bf16[1024,3,512]{2,0,1:T(8,128)(2,1)}, bf16[512,1024]{1,0:T(8,128)(2,1)}, bf16[1024,2048]{1,0:T(8,128)(2,1)}, bf16[2048,1024]{1,0:T(8,128)(2,1)}) async-done(((bf16[1024,3,512]{2,0,1:T(8,128)(2,1)}, bf16[512,1024]{1,0:T(8,128)(2,1)}, bf16[1024,2048]{1,0:T(8,128)(2,1)}, bf16[2048,1024]{1,0:T(8,128)(2,1)}), (bf16[1024,3,512]{2,0,1:T(8,128)(2,1)}, ...) | async-done | bytes 12582928 | tf_op jit(solution)/shard_map/psum | solution.py:355
  1206.6 6.8 convert_element_type.136
  1213.4 4.4 convert_element_type.139
  1217.9 3.6 convert_element_type.130
  1223.1 51.7 %reduce-scatter.11.cloned.1.call-done = bf16[1280,1024]{1,0:T(8,128)(2,1)} async-done(((bf16[2560,1024]{1,0:T(8,128)(2,1)}), bf16[1280,1024]{1,0:T(8,128)(2,1)}) %reduce-scatter.11.cloned.1.call-update) | async-done | bytes 2621456 | tf_op jit(solution)/shard_map/reduce_scatter | solution.py:330
  1274.7 4.3 fusion.35
  1279.2 39.7 %psum.49 = f32[10,1024]{1,0:T(8,128)S(1)} all-reduce(f32[10,1024]{1,0:T(8,128)S(1)} %stack.54), channel_id=1, replica_groups=mesh['dp'=16,'mp'=2] {'dp','mp'}, use_global_device_ids=true, to_apply=%region_31.32 | all-reduce | flops 10240 | bytes 81920 | tf_op jit(solution)/shard_map/psum | solution.py:362
  1319.5 6.5 fusion.24
  (147 shorter events, 15.4 us)
Async XLA Ops:
  7.2 253.3 %copy-start = (bf16[512,1024]{1,0:T(8,128)(2,1)S(1)}, bf16[512,1024]{1,0:T(8,128)(2,1)}, u32[]{:S(2)}) copy-start(bf16[512,1024]{1,0:T(8,128)(2,1)} %param.25) | copy-start | bytes 3145732
  7.2 5.0 copy-start.28
  7.2 5.0 copy-start.36
  7.2 78.9 %all-gather.5.cloned.1.call-start = ((), (), s32[]{:S(2)}) async-start(), calls=%async_computation.4 | async-start | bytes 7864320 | tf_op jit(solution)/shard_map/all_gather | solution.py:274
  7.3 5.0 copy-start.3
  9.6 5.0 copy-start.20
  9.6 5.1 copy-start.42
  9.6 7.1 copy-start.34
  14.6 7.4 copy-start.38
  14.6 316.9 %reduce-scatter.5.cloned.1.call-start = ((), (), s32[]{:S(2)}) async-start(), calls=%async_computation.5 | async-start | bytes 7864320 | tf_op jit(solution)/shard_map/reduce_scatter | solution.py:282
  266.6 64.9 %copy-start.19 = (f32[1024]{0:T(1024)S(1)}, f32[1024]{0:T(1024)}, u32[]{:S(2)}) copy-start(f32[1024]{0:T(1024)} %param.26) | copy-start | bytes 12292
  266.6 70.2 %copy-start.22 = (f32[1024]{0:T(1024)S(1)}, f32[1024]{0:T(1024)}, u32[]{:S(2)}) copy-start(f32[1024]{0:T(1024)} %param.27) | copy-start | bytes 12292
  266.6 70.2 %copy-start.26 = (f32[1024]{0:T(1024)S(1)}, f32[1024]{0:T(1024)}, u32[]{:S(2)}) copy-start(f32[1024]{0:T(1024)} %param.28) | copy-start | bytes 12292
  266.7 150.6 %all-gather.7.cloned.1.call-start = ((), (), s32[]{:S(2)}) async-start(), calls=%async_computation.6 | async-start | bytes 7864320 | tf_op jit(solution)/shard_map/all_gather | solution.py:292
  331.6 5.2 copy-start.4
  331.6 5.2 copy-start.6
  336.8 5.0 copy-start.30
  336.8 5.0 copy-start.35
  341.8 75.4 %copy-start.41 = (f32[2048]{0:T(1024)S(1)}, f32[2048]{0:T(1024)}, u32[]{:S(2)}) copy-start(f32[2048]{0:T(1024)} %param.32) | copy-start | bytes 24580
  348.5 173.9 %reduce-scatter.7.cloned.1.call-start = ((), (), s32[]{:S(2)}) async-start(), calls=%async_computation.7 | async-start | bytes 7864320 | tf_op jit(solution)/shard_map/reduce_scatter | solution.py:296
  417.2 24.0 %copy-start.39 = (bf16[2048,1024]{1,0:T(8,128)(2,1)S(1)}, bf16[2048,1024]{1,0:T(8,128)(2,1)}, u32[]{:S(2)}) copy-start(bf16[2048,1024]{1,0:T(8,128)(2,1)} %param.33) | copy-start | bytes 12582916
  456.5 65.9 %copy-start.25 = (f32[1024]{0:T(1024)S(1)}, f32[1024]{0:T(1024)}, u32[]{:S(2)}) copy-start(f32[1024]{0:T(1024)} %param.34) | copy-start | bytes 12292
  456.5 71.1 %copy-start.27 = (f32[1024]{0:T(1024)S(1)}, f32[1024]{0:T(1024)}, u32[]{:S(2)}) copy-start(f32[1024]{0:T(1024)} %param.35) | copy-start | bytes 12292
  456.6 147.4 %all-gather.9.cloned.1.call-start = ((), (), s32[]{:S(2)}) async-start(), calls=%async_computation.8 | async-start | bytes 7864320 | tf_op jit(solution)/shard_map/all_gather | solution.py:308
  522.4 5.2 copy-start.8
  522.4 5.2 copy-start.11
  535.2 180.3 %reduce-scatter.9.cloned.1.call-start = ((), (), s32[]{:S(2)}) async-start(), calls=%async_computation.9 | async-start | bytes 7864320 | tf_op jit(solution)/shard_map/reduce_scatter | solution.py:314
  604.0 30.3 %copy-start.40 = (bf16[1024,2048]{1,0:T(8,128)(2,1)S(1)}, bf16[1024,2048]{1,0:T(8,128)(2,1)}, u32[]{:S(2)}) copy-start(bf16[1024,2048]{1,0:T(8,128)(2,1)} %param.31) | copy-start | bytes 12582916
  649.7 65.9 %copy-start.37 = (f32[1024]{0:T(1024)S(1)}, f32[1024]{0:T(1024)}, u32[]{:S(2)}) copy-start(f32[1024]{0:T(1024)} %param.36) | copy-start | bytes 12292
  649.7 155.0 %all-gather.11.cloned.1.call-start = ((), (), s32[]{:S(2)}) async-start(), calls=%async_computation.10 | async-start | bytes 7864320 | tf_op jit(solution)/shard_map/all_gather | solution.py:319
  715.5 10.9 copy-start.5
  715.5 10.9 copy-start.7
  715.5 10.9 copy-start.12
  715.5 10.9 copy-start.13
  736.0 470.6 %all-reduce.4.cloned.1.call-start = ((), (), s32[]{:S(2)}) async-start(), calls=%async_computation.12 | async-start | bytes 25165824 | tf_op jit(solution)/shard_map/psum | solution.py:355
  804.7 6.8 copy-start.2
  804.7 153.4 %slice-start.2 = ((s8[5242880]{0:T(1024)(128)(4,1)}), s8[4194304]{0:T(1024)(128)(4,1)S(1)}, s32[]{:S(2)}) async-start(s8[5242880]{0:T(1024)(128)(4,1)} %bitcast.82), calls=%async_computation.15 | async-start | bytes 8388608
  804.7 157.3 %slice-start = ((s8[5242880]{0:T(1024)(128)(4,1)}), s8[4194304]{0:T(1024)(128)(4,1)S(1)}, s32[]{:S(2)}) async-start(s8[5242880]{0:T(1024)(128)(4,1)} %bitcast.80), calls=%async_computation.13 | async-start | bytes 8388608
  811.5 146.6 %slice-start.3 = ((s8[5242880]{0:T(1024)(128)(4,1)}), s8[1048576]{0:T(1024)(128)(4,1)S(1)}, s32[]{:S(2)}) async-start(s8[5242880]{0:T(1024)(128)(4,1)} %bitcast.82), calls=%async_computation.16 | async-start | bytes 2097152
  811.5 150.5 %slice-start.1 = ((s8[5242880]{0:T(1024)(128)(4,1)}), s8[1048576]{0:T(1024)(128)(4,1)S(1)}, s32[]{:S(2)}) async-start(s8[5242880]{0:T(1024)(128)(4,1)} %bitcast.80), calls=%async_computation.14 | async-start | bytes 2097152
  971.8 302.9 %reduce-scatter.11.cloned.1.call-start = ((), (), s32[]{:S(2)}) async-start(), calls=%async_computation.11 | async-start | bytes 7864320 | tf_op jit(solution)/shard_map/reduce_scatter | solution.py:330
  1206.6 6.8 copy-start.16
  1217.9 56.9 %copy-start.21 = (f32[1280]{0:T(1024)S(1)}, f32[1280]{0:T(1024)}, u32[]{:S(2)}) copy-start(f32[1280]{0:T(1024)} %copy-done.20) | copy-start | bytes 15364
  1217.9 56.9 %copy-start.24 = (f32[1280]{0:T(1024)S(1)}, f32[1280]{0:T(1024)}, u32[]{:S(2)}) copy-start(f32[1280]{0:T(1024)} %copy-done.23) | copy-start | bytes 15364
  1217.9 56.9 %copy-start.29 = (f32[1024]{0:T(1024)S(1)}, f32[1024]{0:T(1024)}, u32[]{:S(2)}) copy-start(f32[1024]{0:T(1024)} %param.21) | copy-start | bytes 12292
  1221.5 57.6 %copy-start.31 = (f32[1024]{0:T(1024)S(1)}, f32[1024]{0:T(1024)}, u32[]{:S(2)}) copy-start(f32[1024]{0:T(1024)} %get-tuple-element.26) | copy-start | bytes 12292
  1221.5 57.6 %copy-start.32 = (f32[1024]{0:T(1024)S(1)}, f32[1024]{0:T(1024)}, u32[]{:S(2)}) copy-start(f32[1024]{0:T(1024)} %get-tuple-element.35) | copy-start | bytes 12292
  1221.5 57.6 %copy-start.33 = (f32[1024]{0:T(1024)S(1)}, f32[1024]{0:T(1024)}, u32[]{:S(2)}) copy-start(f32[1024]{0:T(1024)} %get-tuple-element.44) | copy-start | bytes 12292
  (8 other events, 25.3 us)
Sparse Core Ops, SparseCore 0:
  14.8 71.2 all-gather.4
  266.8 64.7 reduce-scatter.4
  348.6 68.5 all-gather.6
  456.7 65.6 reduce-scatter.6
  535.4 68.5 all-gather.8
  649.8 65.6 reduce-scatter.8
  736.1 68.5 all-gather.10
  971.9 234.6 all-reduce.3
  1209.0 65.6 reduce-scatter.10

commit v2 on v0

v2 whole, which is shorter than its diff:
```python
import functools

import jax
import jax.numpy as jnp
from jax import lax
from jax.experimental import pallas as pl
from jax.experimental.pallas import tpu as pltpu
from jax.sharding import PartitionSpec as P

HDIM = 64
TEXT = 64


epsilon = 1e-05
masked_score = -1e30


def norm_parts(values, ln_gain, ln_bias):
    centred = values - jnp.mean(values, -1, keepdims=True)
    inv_std = lax.rsqrt(jnp.mean(centred * centred, -1, keepdims=True) + epsilon)
    normed = centred * inv_std
    return (normed * ln_gain + ln_bias, normed, inv_std)


def norm_back(upstream, normed, inv_std, ln_gain):
    scaled = upstream * ln_gain
    return inv_std * (
        scaled
        - jnp.mean(scaled, -1, keepdims=True)
        - normed * jnp.mean(scaled * normed, -1, keepdims=True)
    )


def contract_rows(left, right):
    return lax.dot_general(
        left, right, (((0,), (0,)), ((), ())), preferred_element_type=jnp.float32
    )


def contract_cols(left, right):
    return lax.dot_general(
        left, right, (((1,), (1,)), ((), ())), preferred_element_type=jnp.float32
    )


BQ = 256
BK = 256
PAIR = 2 * HDIM
F32 = jnp.float32
BF16 = jnp.bfloat16


def matmul(left, right):
    return jnp.dot(left, right, preferred_element_type=F32)


def row_tables(grid_row, tokens, turn):
    side = jnp.max(grid_row)
    length = TEXT + side * side
    rows = tokens // length
    used = rows * length
    position = jnp.arange(tokens, dtype=jnp.int32)
    seg = jnp.minimum(position // length, rows)
    blocks = tokens // BQ
    first = jnp.arange(blocks, dtype=jnp.int32) * BQ
    last = first + BQ - 1
    start = jnp.where(first < used, (first // length) * length, first)
    low = start // BK
    diag = first // BK
    row_start = (last // length) * length
    clean = jnp.where(last < used, (row_start + TEXT + BK - 1) // BK, diag)
    clean = jnp.clip(clean, low, diag)
    turns = jnp.full((blocks,), turn, jnp.int32)
    return seg, jnp.stack([low, clean, diag, turns]).astype(jnp.int32)


def allowed(kseg_ref, qseg_ref, i, j):
    qs = qseg_ref[:, pl.ds(pl.multiple_of(i * BQ, BQ), BQ)]
    ks = kseg_ref[pl.ds(pl.multiple_of(j * BK, BK), BK), :]
    ik = j * BK + lax.broadcasted_iota(jnp.int32, (BK, BQ), 0)
    iq = i * BQ + lax.broadcasted_iota(jnp.int32, (BK, BQ), 1)
    return ((ks == qs) & (ik <= iq)) | (ik == iq)


def sweep(tab_ref, i, step, carry):
    low, clean, diag = tab_ref[0, i], tab_ref[1, i], tab_ref[2, i]
    carry = lax.fori_loop(low, clean, functools.partial(step, True), carry)
    carry = lax.fori_loop(clean, diag, functools.partial(step, False), carry)
    return step(True, diag, carry)


def each_block(tab_ref, parts, width, work):
    blocks = width // BQ
    count = blocks * parts
    for part in range(parts):

        def one(c, _, part=part):
            whole = lax.rem(tab_ref[3, 0] + part * blocks + c, count)
            work(
                part,
                pl.ds(pl.multiple_of(c * BQ, BQ), BQ),
                pl.ds(pl.multiple_of(whole * BQ, BQ), BQ),
            )
            return 0

        lax.fori_loop(0, blocks, one, 0)


def forward_kernel(parts, tab_ref, kseg_ref, qseg_ref, *refs):
    q_refs, k_refs, v_refs, o_refs = (refs[n * parts : (n + 1) * parts] for n in range(4))
    lse_ref, kx, vx, qx, ox = refs[4 * parts :]
    tokens = qx.shape[1]
    width = tokens // parts
    lane = lax.broadcasted_iota(jnp.int32, (BK, 128), 1)

    def prepare(part, here, there):
        kt = k_refs[part][:, here].astype(F32).T
        kx[0, there, :] = jnp.where(lane < HDIM, kt, 0.0).astype(BF16)
        kx[1, there, :] = jnp.where(lane < HDIM, 0.0, kt).astype(BF16)
        qx[:, there] = q_refs[part][:, here]
        for h in range(2):
            vx[h, :HDIM, there] = v_refs[part][h * HDIM : (h + 1) * HDIM, here]
            vx[h, HDIM:, there] = jnp.ones((16, BQ), BF16)

    each_block(tab_ref, parts, width, prepare)

    def block(i, _):
        cols = pl.ds(pl.multiple_of(i * BQ, BQ), BQ)
        qb = qx[:, cols]

        def step(masked, j, carry):
            at = pl.ds(pl.multiple_of(j * BK, BK), BK)
            if masked:
                ok = allowed(kseg_ref, qseg_ref, i, j)
            out = []
            for h in range(2):
                top, acc = carry[h]
                s = matmul(kx[h, at, :], qb)
                if masked:
                    s = jnp.where(ok, s, masked_score)
                new = jnp.maximum(top, jnp.max(s, axis=0, keepdims=True))
                p = jnp.exp(s - new).astype(BF16)
                acc = acc * jnp.exp(top - new) + matmul(vx[h, :, at], p)
                out.append((new, acc))
            return tuple(out)

        init = tuple(
            (jnp.full((1, BQ), masked_score, F32), jnp.zeros((HDIM + 16, BQ), F32))
            for _ in range(2)
        )
        res = sweep(tab_ref, i, step, init)
        for h in range(2):
            top, acc = res[h]
            total = acc[HDIM : HDIM + 1, :]
            ox[h * HDIM : (h + 1) * HDIM, cols] = (acc[:HDIM, :] / total).astype(BF16)
            lse_ref[0, h : h + 1, cols] = top + jnp.log(total)
        return 0

    lax.fori_loop(0, tokens // BQ, block, 0)

    def finish(part, here, there):
        o_refs[part][:, here] = ox[:, there]

    each_block(tab_ref, parts, width, finish)


def three_parts(x):
    high = x.astype(BF16)
    rest = x - high.astype(F32)
    middle = rest.astype(BF16)
    return high, middle, (rest - middle.astype(F32)).astype(BF16)


def backward_kernel(parts, tab_ref, kseg_ref, qseg_ref, *refs):
    q_refs, k_refs, v_refs, o_refs, do_refs = (
        refs[n * parts : (n + 1) * parts] for n in range(5)
    )
    lse_ref = refs[5 * parts]
    out_refs = refs[5 * parts + 1 : 6 * parts + 1]
    kx, vx, kt, qx, dox, qt, dot, dq, dk, dv = refs[6 * parts + 1 :]
    tokens = kt.shape[1]
    width = tokens // parts
    lane = lax.broadcasted_iota(jnp.int32, (BK, 128), 1)
    sub = lax.broadcasted_iota(jnp.int32, (HDIM, BK), 0)
    one0 = jnp.where((lane >= HDIM) & (lane < HDIM + 3), 1.0, 0.0)
    one1 = jnp.where(lane < 3, 1.0, 0.0)

    def extra(x):
        high, middle, low = (e.astype(F32) for e in three_parts(x))
        rows = jnp.where(
            sub == 0, high, jnp.where(sub == 1, middle, jnp.where(sub == 2, low, 0.0))
        )
        return rows.astype(BF16)

    def prepare(part, here, there):
        k = k_refs[part][:, here]
        kt[:, there] = k
        turned = k.astype(F32).T
        kx[0, there, :] = jnp.where(lane < HDIM, turned, one0).astype(BF16)
        kx[1, there, :] = jnp.where(lane < HDIM, one1, turned).astype(BF16)
        turned = v_refs[part][:, here].astype(F32).T
        vx[0, there, :] = jnp.where(lane < HDIM, turned, one0).astype(BF16)
        vx[1, there, :] = jnp.where(lane < HDIM, one1, turned).astype(BF16)
        q = q_refs[part][:, here]
        turned = q.astype(F32).T
        qt[0, there, :] = jnp.where(lane < HDIM, turned, 0.0).astype(BF16)
        qt[1, there, :] = jnp.where(lane < HDIM, 0.0, turned).astype(BF16)
        do = do_refs[part][:, here]
        wide = do.astype(F32)
        turned = wide.T
        dot[0, there, :] = jnp.where(lane < HDIM, turned, 0.0).astype(BF16)
        dot[1, there, :] = jnp.where(lane < HDIM, 0.0, turned).astype(BF16)
        prod = wide * o_refs[part][:, here].astype(F32)
        inner0 = jnp.sum(prod[:HDIM], axis=0, keepdims=True)
        inner1 = jnp.sum(prod[HDIM:], axis=0, keepdims=True)
        qx[0, :HDIM, there] = q[:HDIM]
        qx[0, HDIM:, there] = extra(-lse_ref[0, 0:1, there])
        qx[1, HDIM:, there] = q[HDIM:]
        qx[1, :HDIM, there] = extra(-lse_ref[0, 1:2, there])
        dox[0, :HDIM, there] = do[:HDIM]
        dox[0, HDIM:, there] = extra(-inner0)
        dox[1, HDIM:, there] = do[HDIM:]
        dox[1, :HDIM, there] = extra(-inner1)
        dk[there, :] = jnp.zeros((BK, 128), F32)
        dv[there, :] = jnp.zeros((BK, 128), F32)

    each_block(tab_ref, parts, width, prepare)

    def block(i, _):
        cols = pl.ds(pl.multiple_of(i * BQ, BQ), BQ)

        def step(masked, j, carry):
            at = pl.ds(pl.multiple_of(j * BK, BK), BK)
            if masked:
                ok = allowed(kseg_ref, qseg_ref, i, j)
            new = []
            dvs = dv[at, :]
            dks = dk[at, :]
            for h in range(2):
                s = matmul(kx[h, at, :], qx[h, :, cols])
                if masked:
                    s = jnp.where(ok, s, masked_score)
                p = jnp.exp(s)
                dp = matmul(vx[h, at, :], dox[h, :, cols])
                ds = (p * dp).astype(BF16)
                dvs = dvs + matmul(p.astype(BF16), dot[h, cols, :])
                dks = dks + matmul(ds, qt[h, cols, :])
                new.append(carry[h] + matmul(kt[h * HDIM : (h + 1) * HDIM, at], ds))
            dv[at, :] = dvs
            dk[at, :] = dks
            return tuple(new)

        init = tuple(jnp.zeros((HDIM, BQ), F32) for _ in range(2))
        res = sweep(tab_ref, i, step, init)
        for h in range(2):
            dq[h * HDIM : (h + 1) * HDIM, cols] = (res[h] * (HDIM**-0.5)).astype(BF16)
        return 0

    lax.fori_loop(0, tokens // BQ, block, 0)

    def finish(part, here, there):
        out_refs[part][0, :, here] = dq[:, there]
        out_refs[part][1, :, here] = dk[there, :].T.astype(BF16)
        out_refs[part][2, :, here] = dv[there, :].T.astype(BF16)

    each_block(tab_ref, parts, width, finish)


def rows_of(pairs, which):
    return lambda g, t: (which * pairs + g, 0)


def attend_specs(qkv_parts):
    parts = len(qkv_parts)
    width = qkv_parts[0].shape[1]
    tokens = parts * width
    heads = qkv_parts[0].shape[0] // (3 * HDIM)
    pairs = heads // 2
    seg_specs = [
        pl.BlockSpec((tokens, 1), lambda g, t: (0, 0)),
        pl.BlockSpec((1, tokens), lambda g, t: (0, 0)),
    ]
    per_part = [[pl.BlockSpec((PAIR, width), rows_of(pairs, c))] * parts for c in range(3)]
    lse_spec = pl.BlockSpec((1, 2, tokens), lambda g, t: (g, 0, 0))
    return parts, width, tokens, heads, pairs, seg_specs, per_part, lse_spec


def attend_forward(qkv_parts, seg, keep, tables):
    parts, width, tokens, heads, pairs, seg_specs, per_part, lse_spec = attend_specs(qkv_parts)
    kseg = jnp.where(keep == 1, seg, -1)[:, None]
    *context, log_total = pl.pallas_call(
        functools.partial(forward_kernel, parts),
        grid_spec=pltpu.PrefetchScalarGridSpec(
            num_scalar_prefetch=1,
            grid=(pairs,),
            in_specs=seg_specs + per_part[0] + per_part[1] + per_part[2],
            out_specs=per_part[0] + [lse_spec],
            scratch_shapes=[
                pltpu.VMEM((2, tokens, 128), BF16),
                pltpu.VMEM((2, HDIM + 16, tokens), BF16),
                pltpu.VMEM((PAIR, tokens), BF16),
                pltpu.VMEM((PAIR, tokens), BF16),
            ],
        ),
        out_shape=[jax.ShapeDtypeStruct((heads * HDIM, width), BF16)] * parts
        + [jax.ShapeDtypeStruct((pairs, 2, tokens), F32)],
        compiler_params=pltpu.CompilerParams(vmem_limit_bytes=40 * 2**20),
        cost_estimate=pl.CostEstimate(
            flops=3000 * tokens * tokens * heads, bytes_accessed=2**23, transcendentals=0
        ),
        name="attend_forward",
    )(tables, kseg, seg[None, :], *qkv_parts, *qkv_parts, *qkv_parts)
    return context, log_total


def attend_backward(qkv_parts, context, grad_ctx, lse, seg, keep, tables):
    parts, width, tokens, heads, pairs, seg_specs, per_part, lse_spec = attend_specs(qkv_parts)
    kseg = jnp.where(keep == 1, seg, -1)[:, None]
    out = pl.pallas_call(
        functools.partial(backward_kernel, parts),
        grid_spec=pltpu.PrefetchScalarGridSpec(
            num_scalar_prefetch=1,
            grid=(pairs,),
            in_specs=seg_specs
            + per_part[0]
            + per_part[1]
            + per_part[2]
            + per_part[0]
            + per_part[0]
            + [lse_spec],
            out_specs=[pl.BlockSpec((3, PAIR, width), lambda g, t: (0, g, 0))] * parts,
            scratch_shapes=[
                pltpu.VMEM((2, tokens, 128), BF16),
                pltpu.VMEM((2, tokens, 128), BF16),
                pltpu.VMEM((PAIR, tokens), BF16),
                pltpu.VMEM((2, 128, tokens), BF16),
                pltpu.VMEM((2, 128, tokens), BF16),
                pltpu.VMEM((2, tokens, 128), BF16),
                pltpu.VMEM((2, tokens, 128), BF16),
                pltpu.VMEM((PAIR, tokens), BF16),
                pltpu.VMEM((tokens, 128), F32),
                pltpu.VMEM((tokens, 128), F32),
            ],
        ),
        out_shape=[jax.ShapeDtypeStruct((3, heads * HDIM, width), BF16)] * parts,
        compiler_params=pltpu.CompilerParams(vmem_limit_bytes=48 * 2**20),
        cost_estimate=pl.CostEstimate(
            flops=3000 * tokens * tokens * heads, bytes_accessed=2**24, transcendentals=0
        ),
        name="attend_backward",
    )(
        tables,
        kseg,
        seg[None, :],
        *qkv_parts,
        *qkv_parts,
        *qkv_parts,
        *context,
        *grad_ctx,
        lse,
    )
    return [part.reshape(3 * heads * HDIM, width) for part in out]


def gelu_and_slope(u):
    root = 0.7978845608028654
    square = u * u
    t = jnp.tanh(root * u * (1.0 + 0.044715 * square))
    half = 0.5 * (1.0 + t)
    slope = half + 0.5 * u * (1.0 - t * t) * (root * (1.0 + 0.134145 * square))
    return u * half, slope


def after(value, *others):
    return lax.optimization_barrier((value, *others))[0]


class Layout:
    def __init__(self, mesh):
        self.dp, self.n = mesh.shape["dp"], mesh.shape["mp"]
        self.pairs = self.dp // 2
        self.axes = ("dp", "mp")

    def device(self, pair, core, m):
        return (2 * pair + core) * self.n + m

    def at_rank(self, pair, group, rank):
        return self.device(pair, rank % 2, group * (self.n // 2) + rank // 2)

    def each(self):
        for pair in range(self.pairs):
            for group in range(2):
                for rank in range(self.n):
                    yield pair, group, rank

    def moved(self, value, moves):
        there = lax.ppermute(value, self.axes, [(a, b) for a, b in moves if a != b])
        core, m = lax.axis_index("dp") % 2, lax.axis_index("mp")
        stays = (m // (self.n // 2) == core) & ((m % (self.n // 2)) * 2 + core == m)
        return jnp.where(stays, value, there)

    def regroup(self, value):
        moves = [(self.device(p, g, r), self.at_rank(p, g, r)) for p, g, r in self.each()]
        return self.moved(value, moves)

    def give_back(self, value):
        moves = [(self.at_rank(p, g, r), self.device(p, g, r)) for p, g, r in self.each()]
        return self.moved(value, moves)

    def to_rank(self, value, ahead):
        moves = [
            (self.at_rank(p, g, r), self.at_rank(p, g, (r + ahead) % self.n))
            for p, g, r in self.each()
        ]
        return lax.ppermute(value, self.axes, moves)

    def rank(self):
        core = lax.axis_index("dp") % 2
        return (lax.axis_index("mp") % (self.n // 2)) * 2 + core

    def gather(self, mine):
        return [mine] + [self.to_rank(mine, self.n - k) for k in range(1, self.n)]

    def scatter_sum(self, shares):
        total = shares[0].astype(jnp.float32)
        for k in range(1, self.n):
            total = total + self.to_rank(shares[k].astype(jnp.bfloat16), k).astype(jnp.float32)
        return total

    def sum_all(self, value):
        devices = self.dp * self.n
        step = 1
        while step < devices:
            value = value + lax.ppermute(value, self.axes, [(i, i ^ step) for i in range(devices)])
            step *= 2
        return value

    def weight_sum(self, grad, turn):
        order = [(i + turn) % self.dp for i in range(self.dp)]
        grad = self.give_back(grad.astype(jnp.bfloat16))
        return lax.psum(grad, "dp", axis_index_groups=[order]).astype(jnp.float32)


def for_kernel(columns, rank):
    width = columns[0].shape[1]
    if width % BQ == 0:
        return columns, rank * (width // BQ)
    return [jnp.roll(jnp.concatenate(columns, 1), rank * width, 1)], 0


def from_kernel(columns, rank, shares):
    if len(columns) == shares:
        return columns
    width = columns[0].shape[1] // shares
    return jnp.split(jnp.roll(columns[0], -rank * width, 1), shares, 1)


def cols_by_cols(left, right):
    return lax.dot_general(
        left, right, (((0,), (1,)), ((), ())), preferred_element_type=jnp.float32
    )


def total(terms):
    return functools.reduce(jnp.add, terms)


def body(
    layout,
    tokens,
    ln1_gain,
    ln1_bias,
    w_qkv,
    qv_bias,
    w_out,
    out_bias,
    ln2_gain,
    ln2_bias,
    ln3_gain,
    ln3_bias,
    w_up,
    up_bias,
    w_down,
    down_bias,
    ln4_gain,
    ln4_bias,
    row_grid,
    pad_mask,
    cotangent,
):
    f32, bf16 = jnp.float32, jnp.bfloat16
    model_dim = tokens.shape[1]
    group_rows = pad_mask.shape[0]
    width = w_qkv.shape[2]
    units = w_up.shape[1]
    shares = layout.n
    rank = layout.rank()

    small = jnp.concatenate(
        [
            qv_bias.reshape(-1),
            up_bias,
            pad_mask.astype(f32),
            row_grid[0].astype(f32),
        ]
    )
    small = layout.regroup(small)
    qv_bias = small[: 2 * width].reshape(2, width)
    up_bias = small[2 * width : 2 * width + units]
    keep = small[2 * width + units : 2 * width + units + group_rows].astype(jnp.int32)
    grid_row = small[2 * width + units + group_rows :].astype(jnp.int32)
    tokens = layout.regroup(tokens)
    w_qkv = w_qkv.reshape(model_dim, 3 * width)
    w_qkv = layout.regroup(w_qkv)
    w_out = layout.regroup(after(w_out, w_qkv))
    w_up = layout.regroup(after(w_up, w_qkv))
    w_down = layout.regroup(after(w_down, w_qkv))
    cotangent = layout.regroup(after(cotangent, w_qkv))

    resid_in = tokens.astype(f32)
    norm1_out, normed1, inv1 = norm_parts(resid_in, ln1_gain, ln1_bias)
    a1 = layout.gather(norm1_out.astype(bf16))
    zeros = jnp.zeros((width,), f32)
    qkv_bias = jnp.concatenate([qv_bias[0], zeros, qv_bias[1]])[:, None]
    qkv_scale = jnp.concatenate([zeros + HDIM ** (-0.5), zeros + 1.0, zeros + 1.0])[:, None]
    qkv = [((cols_by_cols(w_qkv, x) + qkv_bias) * qkv_scale).astype(bf16) for x in a1]
    qkv, turn = for_kernel(qkv, rank)
    seg, tables = row_tables(grid_row, group_rows, turn)
    context_in, log_total = attend_forward(qkv, seg, keep, tables)
    context = from_kernel(context_in, rank, shares)
    branch_z = layout.scatter_sum([contract_rows(x, w_out) for x in context]) + out_bias
    norm2_out, normed2, inv2 = norm_parts(branch_z, ln2_gain, ln2_bias)
    resid_mid = resid_in + norm2_out
    norm3_out, normed3, inv3 = norm_parts(resid_mid, ln3_gain, ln3_bias)
    a3 = layout.gather(norm3_out.astype(bf16))
    hidden, slope = [], []
    for x in a3:
        act, der = gelu_and_slope(matmul(x, w_up) + up_bias)
        hidden.append(act.astype(bf16))
        slope.append(der.astype(bf16))
    branch_f = layout.scatter_sum([matmul(x, w_down) for x in hidden]) + down_bias
    norm4_out, normed4, inv4 = norm_parts(branch_f, ln4_gain, ln4_bias)
    layer_out = layout.give_back((resid_mid + norm4_out).astype(bf16))

    upstream = cotangent.astype(f32)
    grad_f = norm_back(upstream, normed4, inv4, ln4_gain).astype(bf16)
    grad_f_all = layout.gather(grad_f)
    grad_pre = [
        (contract_cols(g, w_down) * s.astype(f32)).astype(bf16)
        for g, s in zip(grad_f_all, slope)
    ]
    grad_a3 = layout.scatter_sum([contract_cols(g, w_up) for g in grad_pre])
    g_w_down = layout.weight_sum(total([contract_rows(x, g) for x, g in zip(hidden, grad_f_all)]), 0)
    g_w_up = layout.weight_sum(total([contract_rows(x, g) for x, g in zip(a3, grad_pre)]), 0)
    g_up_bias = total([jnp.sum(g.astype(f32), 0) for g in grad_pre])
    grad_mid = upstream + norm_back(grad_a3, normed3, inv3, ln3_gain)
    grad_z = norm_back(grad_mid, normed2, inv2, ln2_gain).astype(bf16)
    grad_z_all = layout.gather(grad_z)
    grad_ctx = [contract_cols(w_out, g).astype(bf16) for g in grad_z_all]
    g_w_out = layout.weight_sum(total([matmul(x, g) for x, g in zip(context, grad_z_all)]), 1)
    grad_ctx, _ = for_kernel(grad_ctx, rank)
    grad_qkv = attend_backward(qkv, context_in, grad_ctx, log_total, seg, keep, tables)
    grad_qkv = from_kernel(grad_qkv, rank, shares)
    grad_a1 = layout.scatter_sum([cols_by_cols(g, w_qkv) for g in grad_qkv])
    g_w_qkv = layout.weight_sum(
        total([contract_cols(x.T, g) for x, g in zip(a1, grad_qkv)]), 2
    ).reshape(model_dim, 3, width)
    grad_input = grad_mid + norm_back(grad_a1, normed1, inv1, ln1_gain)
    grad_input = layout.give_back(grad_input.astype(bf16)).astype(f32)

    early = jnp.stack(
        [
            jnp.sum(grad_z.astype(f32), 0),
            jnp.sum(grad_mid * normed2, 0),
            jnp.sum(grad_mid, 0),
            jnp.sum(grad_a3 * normed3, 0),
            jnp.sum(grad_a3, 0),
            jnp.sum(grad_f.astype(f32), 0),
            jnp.sum(upstream * normed4, 0),
            jnp.sum(upstream, 0),
        ],
        0,
    )
    all_units = lax.dynamic_update_slice(jnp.zeros((units * shares,), f32), g_up_bias, (rank * units,))
    early = layout.sum_all(jnp.concatenate([early.reshape(-1), all_units]))
    all_units = early[8 * model_dim :]
    early = early[: 8 * model_dim].reshape(8, model_dim)
    sums = total([jnp.sum(g.astype(f32), 1) for g in grad_qkv]).reshape(3, width)
    all_width = lax.dynamic_update_slice(
        jnp.zeros((2, width * shares), f32), jnp.stack([sums[0], sums[2]], 0), (0, rank * width)
    )
    late = layout.sum_all(
        jnp.concatenate(
            [jnp.sum(grad_a1 * normed1, 0), jnp.sum(grad_a1, 0), all_width.reshape(-1)]
        )
    )
    all_width = late[2 * model_dim :].reshape(2, width * shares)
    m = lax.axis_index("mp")
    g_qv_bias = lax.dynamic_slice(all_width, (0, m * width), (2, width))
    g_up_bias = lax.dynamic_slice(all_units, (m * units,), (units,))
    return (
        layer_out,
        grad_input,
        late[:model_dim],
        late[model_dim : 2 * model_dim],
        g_w_qkv,
        g_qv_bias,
        g_w_out,
        early[0],
        early[1],
        early[2],
        early[3],
        early[4],
        g_w_up,
        g_up_bias,
        g_w_down,
        early[5],
        early[6],
        early[7],
    )


def solution(mesh):
    in_specs = (
        P(("dp", "mp"), None),
        P(),
        P(),
        P(None, None, "mp"),
        P(None, "mp"),
        P("mp", None),
        P(),
        P(),
        P(),
        P(),
        P(),
        P(None, "mp"),
        P("mp"),
        P("mp", None),
        P(),
        P(),
        P(),
        P("dp", None),
        P("dp"),
        P(("dp", "mp"), None),
    )
    out_specs = (
        P(("dp", "mp"), None),
        P(("dp", "mp"), None),
        P(),
        P(),
        P(None, None, "mp"),
        P(None, "mp"),
        P("mp", None),
        P(),
        P(),
        P(),
        P(),
        P(),
        P(None, "mp"),
        P("mp"),
        P("mp", None),
        P(),
        P(),
        P(),
    )
    return jax.shard_map(functools.partial(body, Layout(mesh)), mesh=mesh, in_specs=in_specs, out_specs=out_specs, check_vma=False)
```

time: 2290 us -> 1050 us (0.46)
  matrix products: 1180 us -> 199 us
  waiting for transfers between devices: 670 us -> 210 us
  starting transfers between devices: 0.96 us -> 337 us
  other arithmetic: 249 us -> 62.9 us
  Pallas kernels: 0 us -> 173 us
  blocking collectives: 75.7 us -> 0 us
  local copies, waits for them, and re-layouts: 69.7 us -> 40 us
    dot_general x39 -> x10, matrix products: 1060 us -> 73 us  [the longest x6 50.5 us: matmul(): return jnp.dot(left, right, preferred_element_type=F32)]
    ppermute x0 -> x31, starting transfers between devices: none -> 336 us  [the longest x8 240 us: to_rank(): return lax.ppermute(value, self.axes, moves)]
    reduce_scatter x4 -> x0, waiting for transfers between devices: 250 us -> none  [the longest x1 65.8 us: body(): lax.psum_scatter(jnp.dot(context, w_out, preferred_element_type=jnp.float...]
    all_gather x4 -> x0, waiting for transfers between devices: 238 us -> none  [the longest x1 68.7 us: body(): lax.all_gather(norm3_out.astype(jnp.bfloat16), 'mp', axis=0, tiled=True)]
    pallas_call x0 -> x2, Pallas kernels: none -> 173 us  [the longest x1 87.8 us: attend_backward(): pl.pallas_call(functools.partial(backward_kernel, parts), grid_spec=pltpu...]
    reduce_sum x12 -> x4, other arithmetic: 124 us -> 8.29 us  [the longest x1 3.94 us: body(): jnp.sum(grad_f.astype(f32), 0)]
    ppermute x0 -> x31, waiting for transfers between devices: none -> 109 us  [the longest x10 105 us: sum_all(): lax.ppermute(value, self.axes, [(i, i ^ step) for i in range(devices)])]
    psum x1 -> x3, waiting for transfers between devices: 182 us -> 101 us  [weight_sum(): return lax.psum(grad, 'dp', axis_index_groups=[order]).astype(jnp.float32)]
  transfers between devices with their start and end apart: 9 -> 34, of which waited for: 9 -> 8; matrix products, arithmetic and copies ran while one was open for 3% -> 21% of each run, Pallas kernels for 0% -> 8%
where the time goes in v2:
time: 1050 us; the launch traced here: 1040 us
  starting transfers between devices  337 us (32%)
  waiting for transfers between devices  210 us (20%)
  matrix products  199 us (19%)
  Pallas kernels  173 us (16%)
  other arithmetic  62.9 us (6%)
  local copies, waits for them, and re-layouts  40 us (4%)
  between operations  16.8 us (2%)
    ppermute x8, starting transfers between devices, to_rank(): return lax.ppermute(value, self.axes, moves)  240 us
    ppermute x10, waiting for transfers between devices, sum_all(): lax.ppermute(value, self.axes, [(i, i ^ step) for i in range(devices)])  105 us
    psum x3, waiting for transfers between devices, weight_sum(): return lax.psum(grad, 'dp', axis_index_groups=[order]).astype(jnp.float32)  101 us
    pallas_call x1, Pallas kernels, attend_backward(): pl.pallas_call(functools.partial(backward_kernel, parts), grid_spec=pltpu...  87.8 us
    pallas_call x1, Pallas kernels, attend_forward(): pl.pallas_call(functools.partial(forward_kernel, parts), grid_spec=pltpu....  85.5 us
    ppermute x10, starting transfers between devices, sum_all(): lax.ppermute(value, self.axes, [(i, i ^ step) for i in range(devices)])  75.3 us
    dot_general x8, matrix products, contract_cols(): lax.dot_general(left, right, (((1,), (1,)), ((), ())), preferred_element_...  74.5 us
    dot_general x6, matrix products, contract_rows(): lax.dot_general(left, right, (((0,), (0,)), ((), ())), preferred_element_...  51.2 us
  transfers between devices with their start and end apart: 34, of which 8 were waited for; matrix products, arithmetic and copies ran while one was open for 21% of the time, Pallas kernels for 8%

profile of v2, /device:TPU:0, one launch (start us, length us, event | category | flops | bytes accessed | tf_op | source)
XLA Modules:
  0.0 1038.6 jit_solution(6855023038091050631)
XLA Ops:
  7.3 4.4 copy.53
  14.5 3.2 copy.54
  28.4 24.9 %collective-permute-start.3 = (bf16[1280,1024]{0,1:T(8,128)(2,1)S(1)}, bf16[1280,1024]{0,1:T(8,128)(2,1)S(1)}, u32[]{:S(2)}, u32[]{:S(2)}) collective-permute-start(bf16[1280,1024]{0,1:T(8,128)(2,1)S(1)} %fusion.14), channel_id=1, source_target_pairs={{0,2},{2,0},{1,3},{3,1},{4,6},{6,4},{5,7},{7,5},{8,10},{10,8},{9,1... | collective-permute-start | bytes 7864328 | tf_op jit(solution)/shard_map/ppermute | solution.py:415
  56.0 4.8 fusion.2.refs_0_.refs_2_.refs_4_
  62.0 4.8 fusion.3.refs_1_.refs_3_.refs_5_
  66.9 85.5 %attend_forward.1 = (bf16[512,1280]{1,0:T(8,128)(2,1)S(1)}, bf16[512,1280]{1,0:T(8,128)(2,1)S(1)}, f32[4,2,2560]{2,1,0:T(2,128)S(1)}) custom-call(s32[4,10]{1,0:T(4,128)S(1)} %add_add_fusion.2.tab_ref, s32[2560,1]{1,0:T(8,128)S(1)} %broadcast_in_dim.15.kseg_ref, s32[1,2560]{1,0:T(1,128)S(1)} %fusion.31.qseg_ref, ...), custom_call_target="tpu_custom_call" | custom-call | flops 157286400000 | bytes 8388608 | tf_op jit(solution)/shard_map/attend_forward/pallas_call | solution.py:291
  154.1 35.8 %collective-permute-start.5 = (bf16[1280,1024]{0,1:T(8,128)(2,1)S(1)}, bf16[1280,1024]{0,1:T(8,128)(2,1)S(1)}, u32[]{:S(2)}, u32[]{:S(2)}) collective-permute-start(bf16[1280,1024]{0,1:T(8,128)(2,1)S(1)} %convolution_convert_fusion.3), channel_id=1, source_target_pairs={{0,2},{2,0},{1,3},{3,1},{4,6},{6,4},{5,7},{7,5},{8,10},{10,8},{9,1... | collective-permute-start | bytes 7864328 | tf_op jit(solution)/shard_map/ppermute | solution.py:415
  203.9 68.6 %collective-permute-start.8 = (bf16[1280,1024]{0,1:T(8,128)(2,1)S(1)}, bf16[1280,1024]{0,1:T(8,128)(2,1)}, u32[]{:S(2)}, u32[]{:S(2)}) collective-permute-start(bf16[1280,1024]{0,1:T(8,128)(2,1)S(1)} %add_convert_fusion.6), channel_id=1, source_target_pairs={{0,2},{2,0},{1,3},{3,1},{4,6},{6,4},{5,7},{7,5},{8,10},{10,8},{9,1... | collective-permute-start | bytes 7864328 | tf_op jit(solution)/shard_map/ppermute | solution.py:415
  277.2 10.2 fusion.49
  287.3 11.7 %convolution_convert_fusion.1 = bf16[1280,1024]{0,1:T(8,128)(2,1)} fusion(bf16[2048,1024]{1,0:T(8,128)(2,1)S(1)} %broadcast_select_fusion.1, f32[1280,2048]{1,0:T(8,128)} %fusion.49, f32[2048]{0:T(1024)S(1)} %slice.117), kind=kOutput, calls=%fused_computation.80 | convolution fusion | flops 5396234240 | bytes 17309696 | tf_op jit(solution)/shard_map/dot_general | solution.py:54
  299.0 79.1 %collective-permute-start.9 = (bf16[1280,1024]{0,1:T(8,128)(2,1)}, bf16[1280,1024]{0,1:T(8,128)(2,1)}, u32[]{:S(2)}, u32[]{:S(2)}) collective-permute-start(bf16[1280,1024]{0,1:T(8,128)(2,1)} %convolution_convert_fusion.1), channel_id=1, source_target_pairs={{0,2},{2,0},{1,3},{3,1},{4,6},{6,4},{5,7},{7,5},{8,10},{10,8},{9,1... | collective-permute-start | bytes 7864328 | tf_op jit(solution)/shard_map/ppermute | solution.py:415
  382.1 11.3 %fusion.48 = f32[1280,2048]{1,0:T(8,128)} fusion(bf16[1280,1024]{0,1:T(8,128)(2,1)} %copy-done.38, bf16[1024,2048]{1,0:T(8,128)(2,1)} %copy-done.26), kind=kOutput, calls=%fused_computation.165 | convolution fusion | flops 5368709120 | bytes 17301504 | tf_op jit(solution)/shard_map/dot_general | solution.py:54
  393.4 10.7 %fusion.47 = (f32[1280]{0:T(1024)S(1)}, f32[1280,1024]{0,1:T(8,128)S(1)}) fusion(f32[1024]{0:T(1024)S(1)} %copy-done.73, bf16[1280,1024]{0,1:T(8,128)(2,1)} %collective-permute-done.9, bf16[2048,1024]{1,0:T(8,128)(2,1)S(1)} %copy-done.29, f32[1280,2048]{1,0:T(8,128)} %fusion.48, f32[2048]{0:T(1024)S(1)} %slice.117), kind=kOutput, calls=%fused_computation.164 | convolution fusion | flops 5400165376 | bytes 22561792 | tf_op jit(solution)/shard_map/dot_general | solution.py:54
  407.9 3.9 convert_reduce_fusion.6
  411.8 9.6 collective-permute-start.12
  421.4 15.7 %convert_reduce_fusion.1 = (f32[2048]{0:T(1024)S(1)}, bf16[1280,2048]{1,0:T(8,128)(2,1)}) fusion(f32[1280,2048]{1,0:T(8,128)} %fusion.48, f32[2048]{0:T(1024)S(1)} %slice.117, bf16[1280,1024]{0,1:T(8,128)(2,1)S(1)} %get-tuple-element.91, bf16[2048,1024]{1,0:T(8,128)(2,1)S(1)} %copy-done.30), kind=kOutput, calls=%fused_computation.1 | convolution fusion | flops 5429000192 | bytes 22560768 | tf_op jit(solution)/shard_map/dot_general | solution.py:41
  437.1 10.4 %fusion.52 = f32[1024,2048]{1,0:T(8,128)} fusion(bf16[1280,1024]{0,1:T(8,128)(2,1)S(1)} %copy-done.39, bf16[1280,2048]{1,0:T(8,128)(2,1)} %get-tuple-element.122), kind=kOutput, calls=%fused_computation.169 | convolution fusion | flops 5368709120 | bytes 16252928 | tf_op jit(solution)/shard_map/dot_general | solution.py:35
  447.5 16.7 %convert_reduce_fusion = (f32[2048]{0:T(1024)S(1)}, bf16[1280,2048]{1,0:T(8,128)(2,1)}) fusion(f32[1280,2048]{1,0:T(8,128)} %fusion.49, f32[2048]{0:T(1024)S(1)} %slice.117, bf16[1280,1024]{0,1:T(8,128)(2,1)} %collective-permute-done.12, bf16[2048,1024]{1,0:T(8,128)(2,1)S(1)} %copy-done.31), kind=kOutput, calls=%fused_computation | convolution fusion | flops 5429000192 | bytes 22560768 | tf_op jit(solution)/shard_map/dot_general | solution.py:41
  464.2 9.4 convolution_convert_fusion
  473.8 12.9 %fusion.39 = f32[2048,1024]{1,0:T(8,128)} fusion(bf16[1280,1024]{0,1:T(8,128)(2,1)} %collective-permute-done.12, f32[1280,2048]{1,0:T(8,128)} %fusion.49, f32[2048]{0:T(1024)S(1)} %slice.117), kind=kOutput, calls=%fused_computation.157 | convolution fusion | flops 5394923520 | bytes 21504000 | tf_op jit(solution)/shard_map/dot_general | solution.py:35
  486.7 13.2 %add_convert_fusion.2 = bf16[2048,1024]{1,0:T(8,128)(2,1)} fusion(f32[2048,1024]{1,0:T(8,128)} %fusion.39, bf16[1280,1024]{0,1:T(8,128)(2,1)S(1)} %get-tuple-element.91, f32[1280,2048]{1,0:T(8,128)} %fusion.48, f32[2048]{0:T(1024)S(1)} %slice.117), kind=kOutput, calls=%fused_computation.20 | convolution fusion | flops 5399117824 | bytes 25698304 | tf_op jit(solution)/shard_map/dot_general | solution.py:35
  502.8 10.5 %multiply_reduce_fusion = (f32[1024]{0:T(1024)S(1)}, f32[1280]{0:T(1024)S(1)}, f32[1280]{0:T(1024)S(1)}, f32[1024]{0:T(1024)S(1)}, f32[1280,1024]{0,1:T(8,128)S(1)}) fusion(f32[1280,1024]{0,1:T(8,128)S(1)} %bitcast.70, f32[1280]{0:T(1024)S(1)} %copy-done.53, f32[1280]{0:T(1024)S(1)} %copy-done.46, f32[1024]{0:T(1024)S(1)} %copy-done.61, ...), kind=kOutput, calls=%fused_computation.54 | convolution fusion | flops 5383122944 | bytes 22577152 | tf_op jit(solution)/shard_map/dot_general | solution.py:41
  513.4 5.0 multiply_reduce_fusion.1
  523.0 11.2 %add_convert_fusion.3 = bf16[1024,2048]{1,0:T(8,128)(2,1)} fusion(f32[1024,2048]{1,0:T(8,128)} %fusion.52, bf16[1280,1024]{0,1:T(8,128)(2,1)} %collective-permute-done.8, bf16[1280,2048]{1,0:T(8,128)(2,1)} %get-tuple-element.124), kind=kOutput, calls=%fused_computation.21 | convolution fusion | flops 5372903424 | bytes 20447232 | tf_op jit(solution)/shard_map/dot_general | solution.py:35
  540.4 56.3 %collective-permute-done.24 = f32[12288]{0:T(1024)S(1)} collective-permute-done((f32[12288]{0:T(1024)S(1)}, f32[12288]{0:T(1024)S(1)}, u32[]{:S(2)}, u32[]{:S(2)}) %collective-permute-start.24) | collective-permute-done | bytes 49184 | tf_op jit(solution)/shard_map/ppermute | solution.py:434
  596.7 3.3 fusion.51
  600.2 3.4 add_convert_fusion.7
  604.6 4.5 convolution_convert_fusion.5.refs_8_
  616.5 4.6 broadcast_select_fusion.2
  621.3 4.9 convolution_convert_fusion.4.refs_9_
  626.2 87.8 %attend_backward.1 = (bf16[3,512,1280]{2,1,0:T(8,128)(2,1)}, bf16[3,512,1280]{2,1,0:T(8,128)(2,1)}) custom-call(s32[4,10]{1,0:T(4,128)S(1)} %copy-done.5, s32[2560,1]{1,0:T(8,128)S(1)} %copy-done.1, s32[1,2560]{1,0:T(1,128)S(1)} %copy-done.3, bf16[1536,1280]{1,0:T(8,128)(2,1)} %copy-done.12, bf16[1536,1280]{1,0:T(8,128)(2,1)} %copy-done.13, ...), custom_call_target="tpu_custom_call" | custom-call | flops 157286400000 | bytes 16777216 | tf_op jit(solution)/shard_map/attend_backward/pallas_call | solution.py:319
  714.0 7.8 convolution_convert_fusion.2
  721.8 20.4 %collective-permute-start.15 = (bf16[1280,1024]{0,1:T(8,128)(2,1)}, bf16[1280,1024]{0,1:T(8,128)(2,1)S(1)}, u32[]{:S(2)}, u32[]{:S(2)}) collective-permute-start(bf16[1280,1024]{0,1:T(8,128)(2,1)} %convolution_convert_fusion.2), channel_id=1, source_target_pairs={{0,2},{2,0},{1,3},{3,1},{4,6},{6,4},{5,7},{7,5},{8,10},{10,8},{9,1... | collective-permute-start | bytes 7864328 | tf_op jit(solution)/shard_map/ppermute | solution.py:415
  742.8 6.2 fusion.50
  749.0 6.6 add_convert_fusion.4
  757.4 5.2 fusion.20
  762.6 3.3 fusion.19
  768.1 63.9 %collective-permute-start.17 = (f32[4096]{0:T(1024)S(1)}, f32[4096]{0:T(1024)S(1)}, u32[]{:S(2)}, u32[]{:S(2)}) collective-permute-start(f32[4096]{0:T(1024)S(1)} %pad_maximum_fusion.2), channel_id=1, source_target_pairs={{0,1},{1,0},{2,3},{3,2},{4,5},{5,4},{6,7},{7,6},{8,9},{9,8},{10,11... | collective-permute-start | bytes 49160 | tf_op jit(solution)/shard_map/ppermute | solution.py:434
  835.2 47.8 %collective-permute-done.17 = f32[4096]{0:T(1024)S(1)} collective-permute-done((f32[4096]{0:T(1024)S(1)}, f32[4096]{0:T(1024)S(1)}, u32[]{:S(2)}, u32[]{:S(2)}) %collective-permute-start.17) | collective-permute-done | bytes 16416 | tf_op jit(solution)/shard_map/ppermute | solution.py:434
  885.1 4.1 collective-permute-start.28
  892.6 4.4 copy.68
  903.8 4.3 all-reduce.9.cloned.1.call-done
  908.1 6.8 convert_element_type.188
  914.9 4.4 convert_element_type.190
  919.3 96.8 %all-reduce.5.cloned.1.call-done = bf16[1024,3,512]{0,2,1:T(8,128)(2,1)} async-done(((bf16[1024,3,512]{0,2,1:T(8,128)(2,1)}), bf16[1024,3,512]{0,2,1:T(8,128)(2,1)}) %all-reduce.5.cloned.1.call-update) | async-done | bytes 3145744 | tf_op jit(solution)/shard_map/psum | solution.py:441
  1016.2 5.4 copy.70
  1021.6 4.4 select_convert_fusion
  1026.0 5.9 copy.69
  (313 shorter events, 85.8 us)
Async XLA Ops:
  7.2 892.5 %all-reduce.7.cloned.1.call-start = ((), (), s32[]{:S(2)}) async-start(), calls=%async_computation.1 | async-start | bytes 2097152 | tf_op jit(solution)/shard_map/psum | solution.py:441
  11.7 12.3 %collective-permute-start = (bf16[1280,1024]{0,1:T(8,128)(2,1)}, bf16[1280,1024]{0,1:T(8,128)(2,1)}, u32[]{:S(2)}, u32[]{:S(2)}) collective-permute-start(bf16[1280,1024]{0,1:T(8,128)(2,1)} %copy.53), channel_id=1, source_target_pairs={{1,2},{2,1},{5,6},{6,5},{9,10},{10,9},{13,14},{14,13},{17,18},{18,... | collective-permute-start | bytes 7864328 | tf_op jit(solution)/shard_map/ppermute | solution.py:397
  13.9 7.8 collective-permute-start.1
  20.7 33.5 %collective-permute-start.2 = (bf16[1024,1536]{1,0:T(8,128)(2,1)}, bf16[1024,1536]{1,0:T(8,128)(2,1)S(1)}, u32[]{:S(2)}, u32[]{:S(2)}) collective-permute-start(bf16[1024,1536]{1,0:T(8,128)(2,1)} %copy.56), channel_id=1, source_target_pairs={{1,2},{2,1},{5,6},{6,5},{9,10},{10,9},{13,14},{14,13},{17,18},{18,... | collective-permute-start | bytes 9437192 | tf_op jit(solution)/shard_map/ppermute | solution.py:397
  28.4 33.6 %collective-permute-start.3 = (bf16[1280,1024]{0,1:T(8,128)(2,1)S(1)}, bf16[1280,1024]{0,1:T(8,128)(2,1)S(1)}, u32[]{:S(2)}, u32[]{:S(2)}) collective-permute-start(bf16[1280,1024]{0,1:T(8,128)(2,1)S(1)} %fusion.14), channel_id=1, source_target_pairs={{0,2},{2,0},{1,3},{3,1},{4,6},{6,4},{5,7},{7,5},{8,10},{10,8},{9,1... | collective-permute-start | bytes 7864328 | tf_op jit(solution)/shard_map/ppermute | solution.py:415
  54.6 6.2 collective-permute-start.4
  66.8 85.6 %copy-start.13 = (bf16[1536,1280]{1,0:T(8,128)(2,1)}, bf16[1536,1280]{1,0:T(8,128)(2,1)S(1)}, u32[]{:S(2)}) copy-start(bf16[1536,1280]{1,0:T(8,128)(2,1)S(1)} %fusion.3.refs_1_.refs_3_.refs_5_) | copy-start | bytes 11796484
  66.9 85.6 %copy-start.41 = (bf16[512,1024]{1,0:T(8,128)(2,1)S(1)}, bf16[512,1024]{1,0:T(8,128)(2,1)}, u32[]{:S(2)}) copy-start(bf16[512,1024]{1,0:T(8,128)(2,1)} %broadcast_select_fusion.10) | copy-start | bytes 3145732
  152.4 43.9 %copy-start.6 = (bf16[512,1280]{1,0:T(8,128)(2,1)}, bf16[512,1280]{1,0:T(8,128)(2,1)S(1)}, u32[]{:S(2)}) copy-start(bf16[512,1280]{1,0:T(8,128)(2,1)S(1)} %get-tuple-element.29.refs_7_) | copy-start | bytes 3932164
  152.4 43.9 %copy-start.8 = (bf16[512,1280]{1,0:T(8,128)(2,1)}, bf16[512,1280]{1,0:T(8,128)(2,1)S(1)}, u32[]{:S(2)}) copy-start(bf16[512,1280]{1,0:T(8,128)(2,1)S(1)} %get-tuple-element.27.refs_6_) | copy-start | bytes 3932164
  152.4 37.4 %copy-start.23 = (bf16[1024,2048]{1,0:T(8,128)(2,1)S(1)}, bf16[1024,2048]{1,0:T(8,128)(2,1)}, u32[]{:S(2)}) copy-start(bf16[1024,2048]{1,0:T(8,128)(2,1)} %param.31) | copy-start | bytes 12582916
  152.5 38.4 %copy-start.24 = (bf16[2048,1024]{1,0:T(8,128)(2,1)S(1)}, bf16[2048,1024]{1,0:T(8,128)(2,1)}, u32[]{:S(2)}) copy-start(bf16[2048,1024]{1,0:T(8,128)(2,1)} %param.33) | copy-start | bytes 12582916
  152.5 41.9 %copy-start.72 = (f32[1024]{0:T(1024)S(1)}, f32[1024]{0:T(1024)}, u32[]{:S(2)}) copy-start(f32[1024]{0:T(1024)} %param.26) | copy-start | bytes 12292
  154.1 40.3 %collective-permute-start.5 = (bf16[1280,1024]{0,1:T(8,128)(2,1)S(1)}, bf16[1280,1024]{0,1:T(8,128)(2,1)S(1)}, u32[]{:S(2)}, u32[]{:S(2)}) collective-permute-start(bf16[1280,1024]{0,1:T(8,128)(2,1)S(1)} %convolution_convert_fusion.3), channel_id=1, source_target_pairs={{0,2},{2,0},{1,3},{3,1},{4,6},{6,4},{5,7},{7,5},{8,10},{10,8},{9,1... | collective-permute-start | bytes 7864328 | tf_op jit(solution)/shard_map/ppermute | solution.py:415
  189.9 83.3 %collective-permute-start.6 = (bf16[1024,2048]{1,0:T(8,128)(2,1)S(1)}, bf16[1024,2048]{1,0:T(8,128)(2,1)S(1)}, u32[]{:S(2)}, u32[]{:S(2)}) collective-permute-start(bf16[1024,2048]{1,0:T(8,128)(2,1)S(1)} %copy-done.23), channel_id=1, source_target_pairs={{1,2},{2,1},{5,6},{6,5},{9,10},{10,9},{13,14},{14,13},{17,18},{18,... | collective-permute-start | bytes 12582920 | tf_op jit(solution)/shard_map/ppermute | solution.py:397
  190.8 82.9 %collective-permute-start.7 = (bf16[2048,1024]{1,0:T(8,128)(2,1)S(1)}, bf16[2048,1024]{1,0:T(8,128)(2,1)}, u32[]{:S(2)}, u32[]{:S(2)}) collective-permute-start(bf16[2048,1024]{1,0:T(8,128)(2,1)S(1)} %copy-done.24), channel_id=1, source_target_pairs={{1,2},{2,1},{5,6},{6,5},{9,10},{10,9},{13,14},{14,13},{17,18},{18,... | collective-permute-start | bytes 12582920 | tf_op jit(solution)/shard_map/ppermute | solution.py:397
  202.3 71.3 %copy-start.52 = (f32[1280]{0:T(1024)}, f32[1280]{0:T(1024)S(1)}, u32[]{:S(2)}) copy-start(f32[1280]{0:T(1024)S(1)} %add_rsqrt_fusion.1) | copy-start | bytes 15364
  203.9 69.8 %copy-start.38 = (bf16[1280,1024]{0,1:T(8,128)(2,1)}, bf16[1280,1024]{0,1:T(8,128)(2,1)S(1)}, u32[]{:S(2)}) copy-start(bf16[1280,1024]{0,1:T(8,128)(2,1)S(1)} %add_convert_fusion.6) | copy-start | bytes 7864324
  203.9 73.3 %collective-permute-start.8 = (bf16[1280,1024]{0,1:T(8,128)(2,1)S(1)}, bf16[1280,1024]{0,1:T(8,128)(2,1)}, u32[]{:S(2)}, u32[]{:S(2)}) collective-permute-start(bf16[1280,1024]{0,1:T(8,128)(2,1)S(1)} %add_convert_fusion.6), channel_id=1, source_target_pairs={{0,2},{2,0},{1,3},{3,1},{4,6},{6,4},{5,7},{7,5},{8,10},{10,8},{9,1... | collective-permute-start | bytes 7864328 | tf_op jit(solution)/shard_map/ppermute | solution.py:415
  299.0 94.3 %collective-permute-start.9 = (bf16[1280,1024]{0,1:T(8,128)(2,1)}, bf16[1280,1024]{0,1:T(8,128)(2,1)}, u32[]{:S(2)}, u32[]{:S(2)}) collective-permute-start(bf16[1280,1024]{0,1:T(8,128)(2,1)} %convolution_convert_fusion.1), channel_id=1, source_target_pairs={{0,2},{2,0},{1,3},{3,1},{4,6},{6,4},{5,7},{7,5},{8,10},{10,8},{9,1... | collective-permute-start | bytes 7864328 | tf_op jit(solution)/shard_map/ppermute | solution.py:415
  381.1 23.6 %collective-permute-start.11 = (bf16[1280,1024]{0,1:T(8,128)(2,1)S(1)}, bf16[1280,1024]{0,1:T(8,128)(2,1)S(1)}, u32[]{:S(2)}, u32[]{:S(2)}) collective-permute-start(bf16[1280,1024]{0,1:T(8,128)(2,1)S(1)} %copy.61), channel_id=1, source_target_pairs={{1,2},{2,1},{5,6},{6,5},{9,10},{10,9},{13,14},{14,13},{17,18},{18,... | collective-permute-start | bytes 7864328 | tf_op jit(solution)/shard_map/ppermute | solution.py:397
  411.8 35.7 %collective-permute-start.12 = (bf16[1280,1024]{0,1:T(8,128)(2,1)S(1)}, bf16[1280,1024]{0,1:T(8,128)(2,1)}, u32[]{:S(2)}, u32[]{:S(2)}) collective-permute-start(bf16[1280,1024]{0,1:T(8,128)(2,1)S(1)} %get-tuple-element.91), channel_id=1, source_target_pairs={{0,2},{2,0},{1,3},{3,1},{4,6},{6,4},{5,7},{7,5},{8,10},{10,8},{9,1... | collective-permute-start | bytes 7864328 | tf_op jit(solution)/shard_map/ppermute | solution.py:415
  473.6 29.1 %collective-permute-start.13 = (bf16[1280,1024]{0,1:T(8,128)(2,1)}, bf16[1280,1024]{0,1:T(8,128)(2,1)S(1)}, u32[]{:S(2)}, u32[]{:S(2)}) collective-permute-start(bf16[1280,1024]{0,1:T(8,128)(2,1)} %convolution_convert_fusion), channel_id=1, source_target_pairs={{0,2},{2,0},{1,3},{3,1},{4,6},{6,4},{5,7},{7,5},{8,10},{10,8},{9,1... | collective-permute-start | bytes 7864328 | tf_op jit(solution)/shard_map/ppermute | solution.py:415
  473.8 39.5 %slice-start.2 = ((s8[5242880]{0:T(1024)(128)(4,1)}), s8[4194304]{0:T(1024)(128)(4,1)S(1)}, s32[]{:S(2)}) async-start(s8[5242880]{0:T(1024)(128)(4,1)} %bitcast.71), calls=%async_computation.5 | async-start | bytes 8388608
  500.0 112.8 %collective-permute-start.30 = (bf16[2048,1024]{1,0:T(8,128)(2,1)}, bf16[2048,1024]{1,0:T(8,128)(2,1)}, u32[]{:S(2)}, u32[]{:S(2)}) collective-permute-start(bf16[2048,1024]{1,0:T(8,128)(2,1)} %add_convert_fusion.2), channel_id=1, source_target_pairs={{2,1},{1,2},{6,5},{5,6},{10,9},{9,10},{14,13},{13,14},{18,17},{17,... | collective-permute-start | bytes 12582920 | tf_op jit(solution)/shard_map/ppermute | solution.py:397
  521.6 75.1 %copy-start.9 = (bf16[512,1280]{1,0:T(8,128)(2,1)S(1)}, bf16[512,1280]{1,0:T(8,128)(2,1)}, u32[]{:S(2)}) copy-start(bf16[512,1280]{1,0:T(8,128)(2,1)} %copy-done.8) | copy-start | bytes 3932164
  521.6 78.5 %collective-permute-start.14 = (bf16[1280,1024]{0,1:T(8,128)(2,1)}, bf16[1280,1024]{0,1:T(8,128)(2,1)}, u32[]{:S(2)}, u32[]{:S(2)}) collective-permute-start(bf16[1280,1024]{0,1:T(8,128)(2,1)} %get-tuple-element.93), channel_id=1, source_target_pairs={{0,2},{2,0},{1,3},{3,1},{4,6},{6,4},{5,7},{7,5},{8,10},{10,8},{9,1... | collective-permute-start | bytes 7864328 | tf_op jit(solution)/shard_map/ppermute | solution.py:415
  534.2 65.9 %copy-start.7 = (bf16[512,1280]{1,0:T(8,128)(2,1)S(1)}, bf16[512,1280]{1,0:T(8,128)(2,1)}, u32[]{:S(2)}) copy-start(bf16[512,1280]{1,0:T(8,128)(2,1)} %copy-done.6) | copy-start | bytes 3932164
  534.2 82.3 %collective-permute-start.29 = (bf16[1024,2048]{1,0:T(8,128)(2,1)}, bf16[1024,2048]{1,0:T(8,128)(2,1)}, u32[]{:S(2)}, u32[]{:S(2)}) collective-permute-start(bf16[1024,2048]{1,0:T(8,128)(2,1)} %add_convert_fusion.3), channel_id=1, source_target_pairs={{2,1},{1,2},{6,5},{5,6},{10,9},{9,10},{14,13},{13,14},{18,17},{17,... | collective-permute-start | bytes 12582920 | tf_op jit(solution)/shard_map/ppermute | solution.py:397
  537.1 59.6 %collective-permute-start.24 = (f32[12288]{0:T(1024)S(1)}, f32[12288]{0:T(1024)S(1)}, u32[]{:S(2)}, u32[]{:S(2)}) collective-permute-start(f32[12288]{0:T(1024)S(1)} %pad_maximum_fusion), channel_id=1, source_target_pairs={{0,1},{1,0},{2,3},{3,2},{4,5},{5,4},{6,7},{7,6},{8,9},{9,8},{10,11... | collective-permute-start | bytes 147464 | tf_op jit(solution)/shard_map/ppermute | solution.py:434
  538.2 352.7 %collective-permute-start.10 = (bf16[1280,1024]{0,1:T(8,128)(2,1)}, bf16[1280,1024]{0,1:T(8,128)(2,1)}, u32[]{:S(2)}, u32[]{:S(2)}) collective-permute-start(bf16[1280,1024]{0,1:T(8,128)(2,1)} %get-tuple-element.100), channel_id=1, source_target_pairs={{2,1},{1,2},{6,5},{5,6},{10,9},{9,10},{14,13},{13,14},{18,17},{17,... | collective-permute-start | bytes 7864328 | tf_op jit(solution)/shard_map/ppermute | solution.py:397
  596.6 3.4 collective-permute-start.25
  600.1 9.1 collective-permute-start.26
  603.6 11.8 %collective-permute-start.23 = (bf16[512,1024]{1,0:T(8,128)(2,1)S(1)}, bf16[512,1024]{1,0:T(8,128)(2,1)S(1)}, u32[]{:S(2)}, u32[]{:S(2)}) collective-permute-start(bf16[512,1024]{1,0:T(8,128)(2,1)S(1)} %add_convert_fusion.7), channel_id=1, source_target_pairs={{2,1},{1,2},{6,5},{5,6},{10,9},{9,10},{14,13},{13,14},{18,17},{17,... | collective-permute-start | bytes 3145736 | tf_op jit(solution)/shard_map/ppermute | solution.py:397
  609.8 274.5 %collective-permute-start.27 = (f32[12288]{0:T(1024)}, f32[12288]{0:T(1024)}, u32[]{:S(2)}, u32[]{:S(2)}) collective-permute-start(f32[12288]{0:T(1024)} %add.416), channel_id=1, source_target_pairs={{0,8},{1,9},{2,10},{3,11},{4,12},{5,13},{6,14},{7,15},{8,0},{9,1},... | collective-permute-start | bytes 147464 | tf_op jit(solution)/shard_map/ppermute | solution.py:434
  616.5 291.6 %all-reduce.9.cloned.1.call-start = ((), (), s32[]{:S(2)}) async-start(), calls=%async_computation.2 | async-start | bytes 16777216 | tf_op jit(solution)/shard_map/psum | solution.py:441
  621.2 394.9 %all-reduce.5.cloned.1.call-start = ((), (), s32[]{:S(2)}) async-start(), calls=%async_computation | async-start | bytes 6291456 | tf_op jit(solution)/shard_map/psum | solution.py:441
  626.2 87.8 %copy-start.35 = (bf16[1024,1536]{1,0:T(8,128)(2,1)S(1)}, bf16[1024,1536]{1,0:T(8,128)(2,1)}, u32[]{:S(2)}) copy-start(bf16[1024,1536]{1,0:T(8,128)(2,1)} %copy-done.34) | copy-start | bytes 9437188
  721.8 35.5 %collective-permute-start.15 = (bf16[1280,1024]{0,1:T(8,128)(2,1)}, bf16[1280,1024]{0,1:T(8,128)(2,1)S(1)}, u32[]{:S(2)}, u32[]{:S(2)}) collective-permute-start(bf16[1280,1024]{0,1:T(8,128)(2,1)} %convolution_convert_fusion.2), channel_id=1, source_target_pairs={{0,2},{2,0},{1,3},{3,1},{4,6},{6,4},{5,7},{7,5},{8,10},{10,8},{9,1... | collective-permute-start | bytes 7864328 | tf_op jit(solution)/shard_map/ppermute | solution.py:415
  756.2 75.8 %collective-permute-start.22 = (bf16[1024,1536]{1,0:T(8,128)(2,1)S(1)}, bf16[1024,1536]{1,0:T(8,128)(2,1)S(1)}, u32[]{:S(2)}, u32[]{:S(2)}) collective-permute-start(bf16[1024,1536]{1,0:T(8,128)(2,1)S(1)} %add_convert_fusion.4), channel_id=1, source_target_pairs={{2,1},{1,2},{6,5},{5,6},{10,9},{9,10},{14,13},{13,14},{18,17},{17,... | collective-permute-start | bytes 9437192 | tf_op jit(solution)/shard_map/ppermute | solution.py:397
  765.9 255.6 %collective-permute-start.16 = (bf16[1280,1024]{0,1:T(8,128)(2,1)}, bf16[1280,1024]{0,1:T(8,128)(2,1)}, u32[]{:S(2)}, u32[]{:S(2)}) collective-permute-start(bf16[1280,1024]{0,1:T(8,128)(2,1)} %fusion.19), channel_id=1, source_target_pairs={{2,1},{1,2},{6,5},{5,6},{10,9},{9,10},{14,13},{13,14},{18,17},{17,... | collective-permute-start | bytes 7864328 | tf_op jit(solution)/shard_map/ppermute | solution.py:397
  768.1 114.9 %collective-permute-start.17 = (f32[4096]{0:T(1024)S(1)}, f32[4096]{0:T(1024)S(1)}, u32[]{:S(2)}, u32[]{:S(2)}) collective-permute-start(f32[4096]{0:T(1024)S(1)} %pad_maximum_fusion.2), channel_id=1, source_target_pairs={{0,1},{1,0},{2,3},{3,2},{4,5},{5,4},{6,7},{7,6},{8,9},{9,8},{10,11... | collective-permute-start | bytes 49160 | tf_op jit(solution)/shard_map/ppermute | solution.py:434
  835.2 55.7 %copy-start.21 = (bf16[1280,1024]{0,1:T(8,128)(2,1)S(1)}, bf16[1280,1024]{0,1:T(8,128)(2,1)}, u32[]{:S(2)}) copy-start(bf16[1280,1024]{0,1:T(8,128)(2,1)} %get-tuple-element.100) | copy-start | bytes 7864324
  883.0 1.2 collective-permute-start.18
  884.2 5.0 collective-permute-start.19
  885.1 11.9 %collective-permute-start.28 = (f32[12288]{0:T(1024)S(1)}, f32[12288]{0:T(1024)S(1)}, u32[]{:S(2)}, u32[]{:S(2)}) collective-permute-start(f32[12288]{0:T(1024)S(1)} %add.417), channel_id=1, source_target_pairs={{0,16},{1,17},{2,18},{3,19},{4,20},{5,21},{6,22},{7,23},{8,24},{9,... | collective-permute-start | bytes 147464 | tf_op jit(solution)/shard_map/ppermute | solution.py:434
  889.2 7.8 collective-permute-start.20
  897.0 5.5 collective-permute-start.21
  (68 other events, 681.9 us)
Sparse Core Ops, SparseCore 0:
  616.6 115.2 all-reduce.6
  736.8 171.2 all-reduce.8
  912.7 103.4 all-reduce.4

commit v3 on v2

v3 whole, which is shorter than its diff:
```python
import functools

import jax
import jax.numpy as jnp
from jax import lax
from jax.experimental import pallas as pl
from jax.experimental.pallas import tpu as pltpu
from jax.sharding import PartitionSpec as P

HDIM = 64
TEXT = 64


epsilon = 1e-05
masked_score = -1e30


def norm_parts(values, ln_gain, ln_bias):
    centred = values - jnp.mean(values, -1, keepdims=True)
    inv_std = lax.rsqrt(jnp.mean(centred * centred, -1, keepdims=True) + epsilon)
    normed = centred * inv_std
    return (normed * ln_gain + ln_bias, normed, inv_std)


def norm_back(upstream, normed, inv_std, ln_gain):
    scaled = upstream * ln_gain
    return inv_std * (
        scaled
        - jnp.mean(scaled, -1, keepdims=True)
        - normed * jnp.mean(scaled * normed, -1, keepdims=True)
    )


def contract_rows(left, right):
    return lax.dot_general(
        left, right, (((0,), (0,)), ((), ())), preferred_element_type=jnp.float32
    )


def contract_cols(left, right):
    return lax.dot_general(
        left, right, (((1,), (1,)), ((), ())), preferred_element_type=jnp.float32
    )


BQ = 256
BK = 256
MOST = 4
PAIR = 2 * HDIM
F32 = jnp.float32
BF16 = jnp.bfloat16


def matmul(left, right):
    return jnp.dot(left, right, preferred_element_type=F32)


def row_tables(grid_row, tokens, turn):
    side = jnp.max(grid_row)
    length = TEXT + side * side
    rows = tokens // length
    used = rows * length
    position = jnp.arange(tokens, dtype=jnp.int32)
    seg = jnp.minimum(position // length, rows)
    blocks = tokens // BQ
    first = jnp.arange(blocks, dtype=jnp.int32) * BQ
    start = jnp.where(first < used, (first // length) * length, first)
    low = start // BK
    diag = first // BK
    turns = jnp.full((blocks,), turn, jnp.int32)
    return seg, jnp.stack([low, diag, turns]).astype(jnp.int32)


def allowed(kseg_ref, qseg_ref, i, j, blocks):
    qs = qseg_ref[:, pl.ds(pl.multiple_of(i * BQ, BQ), BQ)]
    ks = kseg_ref[pl.ds(pl.multiple_of(j * BK, BK), blocks * BK), :]
    ik = j * BK + lax.broadcasted_iota(jnp.int32, (blocks * BK, BQ), 0)
    iq = i * BQ + lax.broadcasted_iota(jnp.int32, (blocks * BK, BQ), 1)
    return ((ks == qs) & (ik <= iq)) | (ik == iq)


def sweep(tab_ref, i, step, carry):
    return several(tab_ref[0, i], tab_ref[1, i] + 1, step, carry)


def several(first, stop, step, carry, most=MOST):
    while most > 1:
        turns = (stop - first) // most

        def turn(n, carry, first=first, most=most):
            return step(most, first + most * n, carry)

        carry = lax.fori_loop(0, turns, turn, carry)
        first, most = first + most * turns, most // 2
    return lax.fori_loop(first, stop, functools.partial(step, 1), carry)


def each_block(tab_ref, parts, width, work):
    blocks = width // BQ
    count = blocks * parts
    for part in range(parts):

        def one(c, _, part=part):
            whole = lax.rem(tab_ref[2, 0] + part * blocks + c, count)
            work(
                part,
                pl.ds(pl.multiple_of(c * BQ, BQ), BQ),
                pl.ds(pl.multiple_of(whole * BQ, BQ), BQ),
            )
            return 0

        lax.fori_loop(0, blocks, one, 0)


def forward_kernel(parts, tab_ref, kseg_ref, qseg_ref, *refs):
    qkv_refs = refs[:parts]
    *o_refs, ot_ref, lse_ref, kx, vx, qx, scores = refs[-6 - parts :]
    tokens = qx.shape[1]
    width = tokens // parts
    lane = lax.broadcasted_iota(jnp.int32, (BK, 128), 1)
    zero = jnp.zeros((BK, 128), BF16)

    def prepare(part, here, there):
        k = qkv_refs[part][here, PAIR : 2 * PAIR]
        kx[0, there, :] = jnp.where(lane < HDIM, k, zero)
        kx[1, there, :] = jnp.where(lane < HDIM, zero, k)
        qx[:, there] = qkv_refs[part][here, :PAIR].astype(F32).T.astype(BF16)
        v = qkv_refs[part][here, 2 * PAIR :].astype(F32).T.astype(BF16)
        for h in range(2):
            vx[h, :HDIM, there] = v[h * HDIM : (h + 1) * HDIM]
            vx[h, HDIM:, there] = jnp.ones((16, BQ), BF16)

    each_block(tab_ref, parts, width, prepare)

    def block(i, _):
        cols = pl.ds(pl.multiple_of(i * BQ, BQ), BQ)
        qb = qx[:, cols]

        def score(blocks, j, tops):
            at = pl.ds(pl.multiple_of(j * BK, BK), blocks * BK)
            ok = allowed(kseg_ref, qseg_ref, i, j, blocks)
            out = []
            for h in range(2):
                s = matmul(kx[h, at, :], qb)
                s = jnp.where(ok, s, masked_score)
                scores[h, at, :] = s
                out.append(jnp.maximum(tops[h], jnp.max(s.reshape(blocks * BK // 8, 8, BQ), axis=0)))
            return tuple(out)

        tops = sweep(tab_ref, i, score, (jnp.full((8, BQ), masked_score, F32),) * 2)
        tops = [jnp.max(top, axis=0, keepdims=True) for top in tops]

        def weigh(blocks, j, accs):
            at = pl.ds(pl.multiple_of(j * BK, BK), blocks * BK)
            out = []
            for h in range(2):
                p = jnp.exp(scores[h, at, :] - tops[h]).astype(BF16)
                out.append(accs[h] + matmul(vx[h, :, at], p))
            return tuple(out)

        accs = sweep(tab_ref, i, weigh, (jnp.zeros((HDIM + 16, BQ), F32),) * 2)
        for h in range(2):
            total = accs[h][HDIM : HDIM + 1, :]
            ot_ref[h * HDIM : (h + 1) * HDIM, cols] = (accs[h][:HDIM, :] / total).astype(BF16)
            lse_ref[0, h : h + 1, cols] = tops[h] + jnp.log(total)
        return 0

    lax.fori_loop(0, tokens // BQ, block, 0)

    def finish(part, here, there):
        o_refs[part][here, :] = ot_ref[:, there].astype(F32).T.astype(BF16)

    each_block(tab_ref, parts, width, finish)


def three_parts(x):
    high = x.astype(BF16)
    rest = x - high.astype(F32)
    middle = rest.astype(BF16)
    return high, middle, (rest - middle.astype(F32)).astype(BF16)


def backward_kernel(parts, tab_ref, kseg_ref, qseg_ref, *refs):
    qkv_refs, do_refs = refs[:parts], refs[parts : 2 * parts]
    ot_ref, lse_ref = refs[2 * parts : 2 * parts + 2]
    out_refs = refs[2 * parts + 2 : 3 * parts + 2]
    kx, vx, kt, qx, dox, qt, dot, dq, dk, dv = refs[3 * parts + 2 :]
    tokens = kt.shape[1]
    width = tokens // parts
    lane = lax.broadcasted_iota(jnp.int32, (BK, 128), 1)
    sub = lax.broadcasted_iota(jnp.int32, (HDIM, BK), 0)
    one0 = jnp.where((lane >= HDIM) & (lane < HDIM + 3), 1.0, 0.0).astype(BF16)
    one1 = jnp.where(lane < 3, 1.0, 0.0).astype(BF16)
    zero = jnp.zeros((BK, 128), BF16)

    def extra(x):
        high, middle, low = (e.astype(F32) for e in three_parts(x))
        rows = jnp.where(
            sub == 0, high, jnp.where(sub == 1, middle, jnp.where(sub == 2, low, 0.0))
        )
        return rows.astype(BF16)

    def prepare(part, here, there):
        k = qkv_refs[part][here, PAIR : 2 * PAIR]
        kt[:, there] = k.astype(F32).T.astype(BF16)
        kx[0, there, :] = jnp.where(lane < HDIM, k, one0)
        kx[1, there, :] = jnp.where(lane < HDIM, one1, k)
        v = qkv_refs[part][here, 2 * PAIR :]
        vx[0, there, :] = jnp.where(lane < HDIM, v, one0)
        vx[1, there, :] = jnp.where(lane < HDIM, one1, v)
        q = qkv_refs[part][here, :PAIR]
        qt[0, there, :] = jnp.where(lane < HDIM, q, zero)
        qt[1, there, :] = jnp.where(lane < HDIM, zero, q)
        do = do_refs[part][here, :]
        dot[0, there, :] = jnp.where(lane < HDIM, do, zero)
        dot[1, there, :] = jnp.where(lane < HDIM, zero, do)
        turned = do.astype(F32).T
        prod = turned * ot_ref[:, there].astype(F32)
        inner0 = jnp.sum(prod[:HDIM], axis=0, keepdims=True)
        inner1 = jnp.sum(prod[HDIM:], axis=0, keepdims=True)
        turned = turned.astype(BF16)
        dox[0, :HDIM, there] = turned[:HDIM]
        dox[0, HDIM:, there] = extra(-inner0)
        dox[1, HDIM:, there] = turned[HDIM:]
        dox[1, :HDIM, there] = extra(-inner1)
        turned = q.astype(F32).T.astype(BF16)
        qx[0, :HDIM, there] = turned[:HDIM]
        qx[0, HDIM:, there] = extra(-lse_ref[0, 0:1, there])
        qx[1, HDIM:, there] = turned[HDIM:]
        qx[1, :HDIM, there] = extra(-lse_ref[0, 1:2, there])
        dk[there, :] = jnp.zeros((BK, 128), F32)
        dv[there, :] = jnp.zeros((BK, 128), F32)

    each_block(tab_ref, parts, width, prepare)

    def block(i, _):
        cols = pl.ds(pl.multiple_of(i * BQ, BQ), BQ)

        def step(blocks, j, carry):
            at = pl.ds(pl.multiple_of(j * BK, BK), blocks * BK)
            ok = allowed(kseg_ref, qseg_ref, i, j, blocks)
            new = []
            dvs = dv[at, :]
            dks = dk[at, :]
            for h in range(2):
                s = matmul(kx[h, at, :], qx[h, :, cols])
                s = jnp.where(ok, s, masked_score)
                p = jnp.exp(s)
                dp = matmul(vx[h, at, :], dox[h, :, cols])
                ds = (p * dp).astype(BF16)
                dvs = dvs + matmul(p.astype(BF16), dot[h, cols, :])
                dks = dks + matmul(ds, qt[h, cols, :])
                new.append(carry[h] + matmul(kt[h * HDIM : (h + 1) * HDIM, at], ds))
            dv[at, :] = dvs
            dk[at, :] = dks
            return tuple(new)

        init = tuple(jnp.zeros((HDIM, BQ), F32) for _ in range(2))
        res = sweep(tab_ref, i, step, init)
        for h in range(2):
            dq[h * HDIM : (h + 1) * HDIM, cols] = res[h] * (HDIM**-0.5)
        return 0

    lax.fori_loop(0, tokens // BQ, block, 0)

    def finish(part, here, there):
        out_refs[part][here, :PAIR] = dq[:, there].T.astype(BF16)
        out_refs[part][here, PAIR : 2 * PAIR] = dk[there, :].astype(BF16)
        out_refs[part][here, 2 * PAIR :] = dv[there, :].astype(BF16)

    each_block(tab_ref, parts, width, finish)


def lanes_of(first, step):
    return lambda g, t: (0, first + step * g)


def attend_specs(qkv_parts, chunk):
    parts = len(qkv_parts)
    width = qkv_parts[0].shape[0]
    tokens = parts * width
    every = qkv_parts[0].shape[1] // (3 * PAIR)
    pairs = every // chunk[1]
    first = pairs * chunk[0]
    seg_specs = [
        pl.BlockSpec((tokens, 1), lambda g, t: (0, 0)),
        pl.BlockSpec((1, tokens), lambda g, t: (0, 0)),
    ]
    qkv_specs = [pl.BlockSpec((width, 3 * PAIR), lanes_of(first, 1))] * parts
    o_specs = [pl.BlockSpec((width, PAIR), lanes_of(first, 1))] * parts
    ot_spec = pl.BlockSpec((PAIR, tokens), lambda g, t: (first + g, 0))
    lse_spec = pl.BlockSpec((1, 2, tokens), lambda g, t: (first + g, 0, 0))
    return parts, width, tokens, every, pairs, seg_specs, qkv_specs, o_specs, ot_spec, lse_spec


def attend_forward(qkv_parts, seg, keep, tables, chunk, begun=()):
    parts, width, tokens, every, pairs, seg_specs, qkv_specs, o_specs, ot_spec, lse_spec = (
        attend_specs(qkv_parts, chunk)
    )
    kseg = jnp.where(keep == 1, seg, -1)[:, None]
    return pl.pallas_call(
        functools.partial(forward_kernel, parts),
        grid_spec=pltpu.PrefetchScalarGridSpec(
            num_scalar_prefetch=1,
            grid=(pairs,),
            in_specs=seg_specs + qkv_specs + [pl.BlockSpec(memory_space=pl.ANY)] * len(begun),
            out_specs=o_specs + [ot_spec, lse_spec],
            scratch_shapes=[
                pltpu.VMEM((2, tokens, 128), BF16),
                pltpu.VMEM((2, HDIM + 16, tokens), BF16),
                pltpu.VMEM((PAIR, tokens), BF16),
                pltpu.VMEM((2, tokens, BQ), F32),
            ],
        ),
        out_shape=[jax.ShapeDtypeStruct((width, every * PAIR), BF16)] * parts
        + [
            jax.ShapeDtypeStruct((every * PAIR, tokens), BF16),
            jax.ShapeDtypeStruct((every, 2, tokens), F32),
        ],
        compiler_params=pltpu.CompilerParams(vmem_limit_bytes=40 * 2**20),
        cost_estimate=pl.CostEstimate(
            flops=3000 * tokens * tokens * pairs, bytes_accessed=2**23, transcendentals=0
        ),
        input_output_aliases={3 + parts + n: n for n in range(len(begun))},
        name="attend_forward",
    )(tables, kseg, seg[None, :], *qkv_parts, *begun)


def attend_backward(qkv_parts, turned, grad_ctx, lse, seg, keep, tables, chunk):
    parts, width, tokens, every, pairs, seg_specs, qkv_specs, o_specs, ot_spec, lse_spec = (
        attend_specs(qkv_parts, chunk)
    )
    kseg = jnp.where(keep == 1, seg, -1)[:, None]
    return pl.pallas_call(
        functools.partial(backward_kernel, parts),
        grid_spec=pltpu.PrefetchScalarGridSpec(
            num_scalar_prefetch=1,
            grid=(pairs,),
            in_specs=seg_specs + qkv_specs + o_specs + [ot_spec, lse_spec],
            out_specs=[pl.BlockSpec((width, 3 * PAIR), lanes_of(0, 1))] * parts,
            scratch_shapes=[
                pltpu.VMEM((2, tokens, 128), BF16),
                pltpu.VMEM((2, tokens, 128), BF16),
                pltpu.VMEM((PAIR, tokens), BF16),
                pltpu.VMEM((2, 128, tokens), BF16),
                pltpu.VMEM((2, 128, tokens), BF16),
                pltpu.VMEM((2, tokens, 128), BF16),
                pltpu.VMEM((2, tokens, 128), BF16),
                pltpu.VMEM((PAIR, tokens), F32),
                pltpu.VMEM((tokens, 128), F32),
                pltpu.VMEM((tokens, 128), F32),
            ],
        ),
        out_shape=[jax.ShapeDtypeStruct((width, pairs * 3 * PAIR), BF16)] * parts,
        compiler_params=pltpu.CompilerParams(vmem_limit_bytes=48 * 2**20),
        cost_estimate=pl.CostEstimate(
            flops=4000 * tokens * tokens * pairs, bytes_accessed=2**24, transcendentals=0
        ),
        name="attend_backward",
    )(tables, kseg, seg[None, :], *qkv_parts, *grad_ctx, turned, lse)


def gelu_and_slope(u):
    root = 0.7978845608028654
    square = u * u
    t = jnp.tanh(root * u * (1.0 + 0.044715 * square))
    half = 0.5 * (1.0 + t)
    slope = half + 0.5 * u * (1.0 - t * t) * (root * (1.0 + 0.134145 * square))
    return u * half, slope


def after(value, *others):
    return lax.optimization_barrier((value, *others))[0]


class Layout:
    def __init__(self, mesh):
        self.dp, self.n = mesh.shape["dp"], mesh.shape["mp"]
        self.pairs = self.dp // 2
        self.axes = ("dp", "mp")

    def device(self, pair, core, m):
        return (2 * pair + core) * self.n + m

    def at_rank(self, pair, group, rank):
        return self.device(pair, rank % 2, group * (self.n // 2) + rank // 2)

    def each(self):
        for pair in range(self.pairs):
            for group in range(2):
                for rank in range(self.n):
                    yield pair, group, rank

    def stays(self):
        core, m = lax.axis_index("dp") % 2, lax.axis_index("mp")
        return (m // (self.n // 2) == core) & (self.rank() == m)

    def send(self, value, back=False):
        moves = [(self.device(p, g, r), self.at_rank(p, g, r)) for p, g, r in self.each()]
        return lax.ppermute(
            value, self.axes, [(b, a) if back else (a, b) for a, b in moves if a != b]
        )

    def regroup(self, value):
        return jnp.where(self.stays(), value, self.send(value))

    def give_back(self, value):
        return jnp.where(self.stays(), value, self.send(value, True))

    def partner(self, value, bit, only=lambda p, g, r: True):
        def other(p, c):
            return (p, 1 - c) if bit < 0 else (p ^ (1 << bit), c)

        moves = [
            (self.device(*other(p, c), m), self.device(p, c, m))
            for p, c, m in self.each()
            if only(p, c, m)
        ]
        return lax.ppermute(value, self.axes, moves)

    def side(self, bit):
        dp = lax.axis_index("dp")
        return dp % 2 if bit < 0 else (dp // 2 >> bit) % 2

    def joined(self, mine, theirs, bit):
        high = self.side(bit) == 1
        return jnp.concatenate(
            [jnp.where(high, theirs, mine), jnp.where(high, mine, theirs)], 0
        )

    def regroup_spread(self, value):
        bits = (1, 0)
        rows = value.shape[0] // 4
        part = 2 * self.side(0) + self.side(1)
        got = self.send(lax.dynamic_slice_in_dim(value, part * rows, rows, 0))
        for bit in bits:
            got = self.joined(got, self.partner(got, bit, self.moving), bit)
        return jnp.where(self.stays(), value, got)

    def moving(self, pair, core, m):
        return self.at_rank(pair, core, m) != self.device(pair, core, m)

    def to_rank(self, value, ahead):
        moves = [
            (self.at_rank(p, g, r), self.at_rank(p, g, (r + ahead) % self.n))
            for p, g, r in self.each()
        ]
        return lax.ppermute(value, self.axes, moves)

    def rank(self):
        core = lax.axis_index("dp") % 2
        return (lax.axis_index("mp") % (self.n // 2)) * 2 + core

    def gather(self, mine):
        return [mine] + [self.to_rank(mine, self.n - k) for k in range(1, self.n)]

    def scatter_sum(self, shares):
        total = shares[0].astype(jnp.float32)
        for k in range(1, self.n):
            total = total + self.to_rank(shares[k].astype(jnp.bfloat16), k).astype(jnp.float32)
        return total

    def sum_all(self, value):
        devices = self.dp * self.n
        steps = [1 << k for k in range(devices.bit_length() - 1)]
        within = self.n.bit_length() - 1
        for step in steps[within:] + steps[:within]:
            value = value + lax.ppermute(value, self.axes, [(i, i ^ step) for i in range(devices)])
        return value

    def weight_sum(self, grad):
        grad = self.give_back(grad.astype(jnp.bfloat16))
        return lax.psum(grad, "dp").astype(jnp.float32)

    def weight_sum_by_halves(self, grad):
        value = self.give_back(grad.astype(jnp.bfloat16))
        bits = [-1, *range(self.pairs.bit_length() - 1)]
        for bit in bits:
            half, high = value.shape[0] // 2, self.side(bit)
            sent = lax.dynamic_slice_in_dim(value, (1 - high) * half, half, 0)
            kept = lax.dynamic_slice_in_dim(value, high * half, half, 0)
            got = self.partner(sent, bit)
            value = (kept.astype(jnp.float32) + got.astype(jnp.float32)).astype(jnp.bfloat16)
        for bit in bits[::-1]:
            value = self.joined(value, self.partner(value, bit), bit)
        return value.astype(jnp.float32)


def for_kernel(shares, rank):
    width = shares[0].shape[0]
    if width % BQ == 0:
        return shares, rank * (width // BQ)
    return [jnp.roll(jnp.concatenate(shares, 0), rank * width, 0)], 0


def from_kernel(arrays, rank, shares):
    if len(arrays) == shares:
        return arrays
    width = arrays[0].shape[0] // shares
    return jnp.split(jnp.roll(arrays[0], -rank * width, 0), shares, 0)


def by_pairs(weight, pairs):
    return (
        weight.reshape(-1, 3, pairs, PAIR).transpose(0, 2, 1, 3).reshape(-1, 3 * pairs * PAIR)
    )


def total(terms):
    return functools.reduce(jnp.add, terms)


def body(
    layout,
    tokens,
    ln1_gain,
    ln1_bias,
    w_qkv,
    qv_bias,
    w_out,
    out_bias,
    ln2_gain,
    ln2_bias,
    ln3_gain,
    ln3_bias,
    w_up,
    up_bias,
    w_down,
    down_bias,
    ln4_gain,
    ln4_bias,
    row_grid,
    pad_mask,
    cotangent,
):
    f32, bf16 = jnp.float32, jnp.bfloat16
    model_dim = tokens.shape[1]
    group_rows = pad_mask.shape[0]
    width = w_qkv.shape[2]
    units = w_up.shape[1]
    shares = layout.n
    rank = layout.rank()

    small = jnp.concatenate(
        [
            qv_bias.reshape(-1),
            up_bias,
            pad_mask.astype(f32),
            row_grid[0].astype(f32),
        ]
    )
    small = layout.regroup(small)
    qv_bias = small[: 2 * width].reshape(2, width)
    up_bias = small[2 * width : 2 * width + units]
    keep = small[2 * width + units : 2 * width + units + group_rows].astype(jnp.int32)
    grid_row = small[2 * width + units + group_rows :].astype(jnp.int32)
    pairs = width // PAIR
    chunks = 2 if pairs % 2 == 0 else 1
    tokens = layout.regroup(tokens)
    w_qkv = by_pairs(layout.regroup_spread(w_qkv), pairs)
    w_out_far = layout.send(after(w_out, tokens))
    w_up_far = layout.send(after(w_up, tokens))
    w_down = layout.regroup(after(w_down, w_up_far))
    cotangent = layout.regroup(after(cotangent, w_up_far))

    resid_in = tokens.astype(f32)
    norm1_out, normed1, inv1 = norm_parts(resid_in, ln1_gain, ln1_bias)
    a1 = layout.gather(norm1_out.astype(bf16))
    zeros = jnp.zeros((width,), f32)
    qkv_bias = by_pairs(jnp.concatenate([qv_bias[0], zeros, qv_bias[1]]), pairs)
    qkv_scale = by_pairs(
        jnp.concatenate([zeros + HDIM ** (-0.5), zeros + 1.0, zeros + 1.0]), pairs
    )
    qkv = [((matmul(x, w_qkv) + qkv_bias) * qkv_scale).astype(bf16) for x in a1]
    qkv, turn = for_kernel(qkv, rank)
    seg, tables = row_tables(grid_row, group_rows, turn)
    begun = ()
    for chunk in range(chunks):
        if chunk == chunks - 1:
            tables, w_out_far, w_up_far = lax.optimization_barrier((tables, w_out_far, w_up_far))
        begun = attend_forward(qkv, seg, keep, tables, (chunk, chunks), begun)
    *context, context_turned, log_total = begun
    context = from_kernel(context, rank, shares)
    w_out = jnp.where(layout.stays(), w_out, w_out_far)
    w_up = jnp.where(layout.stays(), w_up, w_up_far)
    branch_z = layout.scatter_sum([matmul(x, w_out) for x in context]) + out_bias
    norm2_out, normed2, inv2 = norm_parts(branch_z, ln2_gain, ln2_bias)
    resid_mid = resid_in + norm2_out
    norm3_out, normed3, inv3 = norm_parts(resid_mid, ln3_gain, ln3_bias)
    a3 = layout.gather(norm3_out.astype(bf16))
    hidden, slope = [], []
    for x in a3:
        act, der = gelu_and_slope(matmul(x, w_up) + up_bias)
        hidden.append(act.astype(bf16))
        slope.append(der.astype(bf16))
    branch_f = layout.scatter_sum([matmul(x, w_down) for x in hidden]) + down_bias
    norm4_out, normed4, inv4 = norm_parts(branch_f, ln4_gain, ln4_bias)
    layer_out = layout.give_back((resid_mid + norm4_out).astype(bf16))

    upstream = cotangent.astype(f32)
    grad_f = norm_back(upstream, normed4, inv4, ln4_gain).astype(bf16)
    grad_f_all = layout.gather(grad_f)
    grad_pre = [
        (contract_cols(g, w_down) * s.astype(f32)).astype(bf16)
        for g, s in zip(grad_f_all, slope)
    ]
    grad_a3 = layout.scatter_sum([contract_cols(g, w_up) for g in grad_pre])
    g_w_down = layout.weight_sum(total([contract_rows(x, g) for x, g in zip(hidden, grad_f_all)]))
    g_w_up = layout.weight_sum(total([contract_rows(x, g) for x, g in zip(a3, grad_pre)]))
    g_up_bias = total([jnp.sum(g.astype(f32), 0) for g in grad_pre])
    grad_mid = upstream + norm_back(grad_a3, normed3, inv3, ln3_gain)
    grad_z = norm_back(grad_mid, normed2, inv2, ln2_gain).astype(bf16)
    grad_z_all = layout.gather(grad_z)
    grad_ctx = [contract_cols(g, w_out).astype(bf16) for g in grad_z_all]
    g_w_out = layout.weight_sum(total([contract_rows(x, g) for x, g in zip(context, grad_z_all)]))
    grad_ctx, _ = for_kernel(grad_ctx, rank)
    grad_a1, g_w_qkv, sums = [], [], []
    for chunk in range(chunks):
        grad_qkv = attend_backward(
            qkv, context_turned, grad_ctx, log_total, seg, keep, tables, (chunk, chunks)
        )
        grad_qkv = from_kernel(grad_qkv, rank, shares)
        columns = grad_qkv[0].shape[1]
        w_part = w_qkv[:, chunk * columns : (chunk + 1) * columns]
        grad_a1.append([contract_cols(g, w_part) for g in grad_qkv])
        sums.append(total([jnp.sum(g.astype(f32), 0) for g in grad_qkv]))
        g_w_qkv.append(
            layout.weight_sum_by_halves(total([contract_rows(x, g) for x, g in zip(a1, grad_qkv)]))
        )
    g_w_qkv = (
        jnp.concatenate(g_w_qkv, 1)
        .reshape(model_dim, pairs, 3, PAIR)
        .transpose(0, 2, 1, 3)
        .reshape(model_dim, 3, width)
    )
    sums = jnp.concatenate(sums).reshape(pairs, 3, PAIR).transpose(1, 0, 2).reshape(3, width)
    grad_a1 = layout.scatter_sum([total(terms) for terms in zip(*grad_a1)])
    grad_input = grad_mid + norm_back(grad_a1, normed1, inv1, ln1_gain)
    grad_input = layout.give_back(grad_input.astype(bf16)).astype(f32)

    norm_terms = jnp.stack(
        [
            jnp.sum(grad_a1 * normed1, 0),
            jnp.sum(grad_a1, 0),
            jnp.sum(grad_z.astype(f32), 0),
            jnp.sum(grad_mid * normed2, 0),
            jnp.sum(grad_mid, 0),
            jnp.sum(grad_a3 * normed3, 0),
            jnp.sum(grad_a3, 0),
            jnp.sum(grad_f.astype(f32), 0),
            jnp.sum(upstream * normed4, 0),
            jnp.sum(upstream, 0),
        ],
        0,
    )
    all_units = lax.dynamic_update_slice(jnp.zeros((units * shares,), f32), g_up_bias, (rank * units,))
    all_width = lax.dynamic_update_slice(
        jnp.zeros((2, width * shares), f32), jnp.stack([sums[0], sums[2]], 0), (0, rank * width)
    )
    small = layout.sum_all(
        jnp.concatenate([norm_terms.reshape(-1), all_width.reshape(-1), all_units])
    )
    norm_terms = small[: 10 * model_dim].reshape(10, model_dim)
    all_width = small[10 * model_dim : 12 * model_dim].reshape(2, width * shares)
    all_units = small[12 * model_dim :]
    m = lax.axis_index("mp")
    g_qv_bias = lax.dynamic_slice(all_width, (0, m * width), (2, width))
    g_up_bias = lax.dynamic_slice(all_units, (m * units,), (units,))
    return (
        layer_out,
        grad_input,
        norm_terms[0],
        norm_terms[1],
        g_w_qkv,
        g_qv_bias,
        g_w_out,
        norm_terms[2],
        norm_terms[3],
        norm_terms[4],
        norm_terms[5],
        norm_terms[6],
        g_w_up,
        g_up_bias,
        g_w_down,
        norm_terms[7],
        norm_terms[8],
        norm_terms[9],
    )


def solution(mesh):
    in_specs = (
        P(("dp", "mp"), None),
        P(),
        P(),
        P(None, None, "mp"),
        P(None, "mp"),
        P("mp", None),
        P(),
        P(),
        P(),
        P(),
        P(),
        P(None, "mp"),
        P("mp"),
        P("mp", None),
        P(),
        P(),
        P(),
        P("dp", None),
        P("dp"),
        P(("dp", "mp"), None),
    )
    out_specs = (
        P(("dp", "mp"), None),
        P(("dp", "mp"), None),
        P(),
        P(),
        P(None, None, "mp"),
        P(None, "mp"),
        P("mp", None),
        P(),
        P(),
        P(),
        P(),
        P(),
        P(None, "mp"),
        P("mp"),
        P("mp", None),
        P(),
        P(),
        P(),
    )
    return jax.shard_map(functools.partial(body, Layout(mesh)), mesh=mesh, in_specs=in_specs, out_specs=out_specs, check_vma=False)
```

time: 1050 us -> 909 us (0.87)
  Pallas kernels: 173 us -> 91.5 us
  waiting for transfers between devices: 210 us -> 155 us
  starting transfers between devices: 337 us -> 307 us
  other arithmetic: 62.9 us -> 89 us
    ppermute x13 -> x32, starting transfers between devices: 21.2 us -> 133 us  [the longest x18 104 us: partner(): return lax.ppermute(value, self.axes, moves)]
    ppermute x10 -> x5, waiting for transfers between devices: 105 us -> 29.2 us  [sum_all(): lax.ppermute(value, self.axes, [(i, i ^ step) for i in range(devices)])]
    ppermute x10 -> x5, starting transfers between devices: 75.3 us -> 3.56 us  [sum_all(): lax.ppermute(value, self.axes, [(i, i ^ step) for i in range(devices)])]
    ppermute x8, starting transfers between devices: 240 us -> 171 us  [to_rank(): return lax.ppermute(value, self.axes, moves)]
    ppermute x13 -> x32, waiting for transfers between devices: 0.03 us -> 59.1 us  [the longest x18 59 us: partner(): return lax.ppermute(value, self.axes, moves)]
    pallas_call x1 -> x2, Pallas kernels: 85.5 us -> 37.5 us  [attend_forward(): pl.pallas_call(functools.partial(forward_kernel, parts), grid_spec=pltpu....]
    psum x3 -> x1, waiting for transfers between devices: 101 us -> 64.7 us  [weight_sum(): return lax.psum(grad, 'dp').astype(jnp.float32)]
    pallas_call x1 -> x2, Pallas kernels: 87.8 us -> 54.1 us  [attend_backward(): pl.pallas_call(functools.partial(backward_kernel, parts), grid_spec=pltpu...]
  transfers between devices with their start and end apart: 34 -> 46, of which waited for: 8 -> 15; matrix products, arithmetic and copies ran while one was open for 21% -> 31% of each run, Pallas kernels for 8% -> 8%
where the time goes in v3:
time: 909 us; the launch traced here: 899 us
  starting transfers between devices  307 us (34%)
  matrix products  197 us (22%)
  waiting for transfers between devices  155 us (17%)
  Pallas kernels  91.5 us (10%)
  other arithmetic  89 us (10%)
  local copies, waits for them, and re-layouts  42.6 us (5%)
  between operations  17.3 us (2%)
    ppermute x8, starting transfers between devices, to_rank(): return lax.ppermute(value, self.axes, moves)  171 us
    ppermute x18, starting transfers between devices, partner(): return lax.ppermute(value, self.axes, moves)  104 us
    dot_general x10, matrix products, contract_cols(): lax.dot_general(left, right, (((1,), (1,)), ((), ())), preferred_element_...  72.6 us
    dot_general x10, matrix products, contract_rows(): lax.dot_general(left, right, (((0,), (0,)), ((), ())), preferred_element_...  66.5 us
    psum x1, waiting for transfers between devices, weight_sum(): return lax.psum(grad, 'dp').astype(jnp.float32)  64.7 us
    ppermute x18, waiting for transfers between devices, partner(): return lax.ppermute(value, self.axes, moves)  59 us
    dot_general x8, matrix products, matmul(): return jnp.dot(left, right, preferred_element_type=F32)  58 us
    pallas_call x2, Pallas kernels, attend_backward(): pl.pallas_call(functools.partial(backward_kernel, parts), grid_spec=pltpu...  54.1 us
  transfers between devices with their start and end apart: 46, of which 15 were waited for; matrix products, arithmetic and copies ran while one was open for 31% of the time, Pallas kernels for 8%

profile of v3, /device:TPU:0, one launch (start us, length us, event | category | flops | bytes accessed | tf_op | source)
XLA Modules:
  0.0 899.3 jit_solution(5680790844530673842)
XLA Ops:
  7.2 4.4 copy.80
  30.0 47.1 %collective-permute-start.7 = (bf16[1280,1024]{0,1:T(8,128)(2,1)S(1)}, bf16[1280,1024]{0,1:T(8,128)(2,1)}, u32[]{:S(2)}, u32[]{:S(2)}) collective-permute-start(bf16[1280,1024]{0,1:T(8,128)(2,1)S(1)} %fusion.14), channel_id=1, source_target_pairs={{0,2},{2,0},{1,3},{3,1},{4,6},{6,4},{5,7},{7,5},{8,10},{10,8},{9,1... | collective-permute-start | bytes 7864328 | tf_op jit(solution)/shard_map/ppermute | solution.py:448
  85.7 4.7 fusion.2.refs_0_
  90.4 7.7 fusion.3.refs_1_
  98.1 18.7 %attend_forward.2 = (bf16[1280,512]{1,0:T(8,128)(2,1)S(1)}, bf16[1280,512]{1,0:T(8,128)(2,1)S(1)}, bf16[512,2560]{1,0:T(8,128)(2,1)S(1)}, f32[4,2,2560]{2,1,0:T(2,128)S(1)}) custom-call(s32[3,10]{1,0:T(4,128)S(1)} %add_add_fusion.2.tab_ref, s32[2560,1]{1,0:T(8,128)S(1)} %broadcast_in_dim.17.kseg_ref, s32[1,2560]{1,0:T(1,128)S(1)} %fusion.37.qseg_ref, ...), custom_call_target="tpu_custom_call" | custom-call | flops 39321600000 | bytes 8388608 | tf_op jit(solution)/shard_map/attend_forward/pallas_call | solution.py:301
  118.3 18.7 %attend_forward.3 = (bf16[1280,512]{1,0:T(8,128)(2,1)S(1)}, bf16[1280,512]{1,0:T(8,128)(2,1)S(1)}, bf16[512,2560]{1,0:T(8,128)(2,1)S(1)}, f32[4,2,2560]{2,1,0:T(2,128)S(1)}) custom-call(s32[3,10]{1,0:T(4,128)S(1)} %add_add_fusion.2.tab_ref, ...), custom_call_target="tpu_custom_call", output_to_operand_aliasing={{0}: (5, {}), {1}: (6, {}), {2}: (7, {}), {3}: (8, {})} | custom-call | flops 39321600000 | bytes 8388608 | tf_op jit(solution)/shard_map/attend_forward/pallas_call | solution.py:301
  138.9 25.2 %collective-permute-start.8 = (bf16[1280,1024]{0,1:T(8,128)(2,1)S(1)}, bf16[1280,1024]{0,1:T(8,128)(2,1)S(1)}, u32[]{:S(2)}, u32[]{:S(2)}) collective-permute-start(bf16[1280,1024]{0,1:T(8,128)(2,1)S(1)} %convolution_convert_fusion.2), channel_id=1, source_target_pairs={{0,2},{2,0},{1,3},{3,1},{4,6},{6,4},{5,7},{7,5},{8,10},{10,8},{9,1... | collective-permute-start | bytes 7864328 | tf_op jit(solution)/shard_map/ppermute | solution.py:448
  176.8 4.1 broadcast_select_fusion.1
  181.0 8.8 fusion.50
  189.9 11.6 %convolution_convert_fusion.1 = bf16[1280,1024]{0,1:T(8,128)(2,1)} fusion(bf16[2048,1024]{1,0:T(8,128)(2,1)S(1)} %broadcast_select_fusion.1, f32[1280,2048]{1,0:T(8,128)} %fusion.50, f32[2048]{0:T(1024)S(1)} %slice.133), kind=kOutput, calls=%fused_computation.83 | convolution fusion | flops 5396234240 | bytes 17309696 | tf_op jit(solution)/shard_map/dot_general | solution.py:55
  201.5 35.9 %collective-permute-start.11 = (bf16[1280,1024]{0,1:T(8,128)(2,1)}, bf16[1280,1024]{0,1:T(8,128)(2,1)}, u32[]{:S(2)}, u32[]{:S(2)}) collective-permute-start(bf16[1280,1024]{0,1:T(8,128)(2,1)} %convolution_convert_fusion.1), channel_id=1, source_target_pairs={{0,2},{2,0},{1,3},{3,1},{4,6},{6,4},{5,7},{7,5},{8,10},{10,8},{9,1... | collective-permute-start | bytes 7864328 | tf_op jit(solution)/shard_map/ppermute | solution.py:448
  241.4 11.0 %fusion.49 = f32[1280,2048]{1,0:T(8,128)} fusion(bf16[1280,1024]{0,1:T(8,128)(2,1)} %copy-done.39, bf16[1024,2048]{1,0:T(8,128)(2,1)} %copy-done.25), kind=kOutput, calls=%fused_computation.210 | convolution fusion | flops 5368709120 | bytes 17301504 | tf_op jit(solution)/shard_map/dot_general | solution.py:55
  252.4 10.7 %fusion.48 = (f32[1280]{0:T(1024)S(1)}, f32[1280,1024]{0,1:T(8,128)S(1)}) fusion(f32[1024]{0:T(1024)S(1)} %copy-done.83, bf16[1280,1024]{0,1:T(8,128)(2,1)} %collective-permute-done.11, bf16[2048,1024]{1,0:T(8,128)(2,1)S(1)} %copy-done.28, f32[1280,2048]{1,0:T(8,128)} %fusion.49, f32[2048]{0:T(1024)S(1)} %slice.133), kind=kOutput, calls=%fused_computation.209 | convolution fusion | flops 5400165376 | bytes 22561792 | tf_op jit(solution)/shard_map/dot_general | solution.py:55
  267.4 5.0 convert_reduce_fusion.4
  272.5 9.8 %collective-permute-start.14 = (bf16[1280,1024]{0,1:T(8,128)(2,1)}, bf16[1280,1024]{0,1:T(8,128)(2,1)S(1)}, u32[]{:S(2)}, u32[]{:S(2)}) collective-permute-start(bf16[1280,1024]{0,1:T(8,128)(2,1)} %get-tuple-element.130), channel_id=1, source_target_pairs={{0,2},{2,0},{1,3},{3,1},{4,6},{6,4},{5,7},{7,5},{8,10},{10,8},{9,1... | collective-permute-start | bytes 7864328 | tf_op jit(solution)/shard_map/ppermute | solution.py:448
  284.6 16.5 %convert_reduce_fusion.1 = (f32[2048]{0:T(1024)S(1)}, bf16[1280,2048]{1,0:T(8,128)(2,1)}) fusion(f32[1280,2048]{1,0:T(8,128)} %fusion.49, f32[2048]{0:T(1024)S(1)} %slice.133, bf16[1280,1024]{0,1:T(8,128)(2,1)} %get-tuple-element.130, bf16[2048,1024]{1,0:T(8,128)(2,1)S(1)} %copy-done.29), kind=kOutput, calls=%fused_computation.1 | convolution fusion | flops 5429000192 | bytes 22560768 | tf_op jit(solution)/shard_map/dot_general | solution.py:41
  301.1 10.4 %fusion.54 = f32[1024,2048]{1,0:T(8,128)} fusion(bf16[1280,1024]{0,1:T(8,128)(2,1)S(1)} %copy-done.40, bf16[1280,2048]{1,0:T(8,128)(2,1)} %get-tuple-element.181), kind=kOutput, calls=%fused_computation.215 | convolution fusion | flops 5368709120 | bytes 16252928 | tf_op jit(solution)/shard_map/dot_general | solution.py:35
  311.5 17.1 %convert_reduce_fusion = (f32[2048]{0:T(1024)S(1)}, bf16[1280,2048]{1,0:T(8,128)(2,1)}) fusion(f32[1280,2048]{1,0:T(8,128)} %fusion.50, f32[2048]{0:T(1024)S(1)} %slice.133, bf16[1280,1024]{0,1:T(8,128)(2,1)S(1)} %collective-permute-done.14, bf16[2048,1024]{1,0:T(8,128)(2,1)S(1)} %copy-done.29), kind=kOutput, calls=%fused_computation | convolution fusion | flops 5429000192 | bytes 22560768 | tf_op jit(solution)/shard_map/dot_general | solution.py:41
  328.6 8.5 convolution_convert_fusion
  338.9 12.0 %fusion.42 = f32[2048,1024]{1,0:T(8,128)} fusion(bf16[1280,1024]{0,1:T(8,128)(2,1)S(1)} %copy-done.81, f32[1280,2048]{1,0:T(8,128)} %fusion.50, f32[2048]{0:T(1024)S(1)} %slice.133), kind=kOutput, calls=%fused_computation.204 | convolution fusion | flops 5394923520 | bytes 21504000 | tf_op jit(solution)/shard_map/dot_general | solution.py:35
  350.9 13.8 %add_convert_fusion.2 = bf16[2048,1024]{1,0:T(8,128)(2,1)} fusion(f32[2048,1024]{1,0:T(8,128)} %fusion.42, bf16[1280,1024]{0,1:T(8,128)(2,1)} %get-tuple-element.130, f32[1280,2048]{1,0:T(8,128)} %fusion.49, f32[2048]{0:T(1024)S(1)} %slice.133), kind=kOutput, calls=%fused_computation.20 | convolution fusion | flops 5399117824 | bytes 25698304 | tf_op jit(solution)/shard_map/dot_general | solution.py:35
  367.4 11.2 %add_convert_fusion.3 = bf16[1024,2048]{1,0:T(8,128)(2,1)} fusion(f32[1024,2048]{1,0:T(8,128)} %fusion.54, bf16[1280,1024]{0,1:T(8,128)(2,1)S(1)} %copy-done.77, bf16[1280,2048]{1,0:T(8,128)(2,1)} %get-tuple-element.183), kind=kOutput, calls=%fused_computation.21 | convolution fusion | flops 5372903424 | bytes 20447232 | tf_op jit(solution)/shard_map/dot_general | solution.py:35
  381.5 10.7 %multiply_reduce_fusion = (f32[1024]{0:T(1024)}, f32[1280]{0:T(1024)S(1)}, f32[1280]{0:T(1024)S(1)}, f32[1024]{0:T(1024)}, f32[1280,1024]{0,1:T(8,128)S(1)}) fusion(f32[1280,1024]{0,1:T(8,128)S(1)} %bitcast.86, f32[1280]{0:T(1024)S(1)} %copy-done.56, f32[1280]{0:T(1024)S(1)} %copy-done.50, f32[1024]{0:T(1024)S(1)} %copy-done.64, ...), kind=kOutput, calls=%fused_computation.52 | convolution fusion | flops 5383122944 | bytes 22577152 | tf_op jit(solution)/shard_map/dot_general | solution.py:41
  392.3 5.9 multiply_reduce_fusion.1
  406.9 4.7 broadcast_select_fusion
  411.6 4.6 broadcast_select_fusion.2
  418.5 26.5 %attend_backward.2 = (bf16[1280,768]{1,0:T(8,128)(2,1)S(1)}, bf16[1280,768]{1,0:T(8,128)(2,1)}) custom-call(s32[3,10]{1,0:T(4,128)S(1)} %copy-done.7, s32[2560,1]{1,0:T(8,128)S(1)} %copy-done.3, s32[1,2560]{1,0:T(1,128)S(1)} %copy-done.5, bf16[1280,1536]{1,0:T(8,128)(2,1)} %copy-done.12, bf16[1280,1536]{1,0:T(8,128)(2,1)} %copy-done.13, ...), custom_call_target="tpu_custom_call" | custom-call | flops 52428800000 | bytes 16777216 | tf_op jit(solution)/shard_map/attend_backward/pallas_call | solution.py:334
  445.0 27.6 %attend_backward.3 = (bf16[1280,768]{1,0:T(8,128)(2,1)S(1)}, bf16[1280,768]{1,0:T(8,128)(2,1)}) custom-call(s32[3,10]{1,0:T(4,128)S(1)} %copy-done.7, s32[2560,1]{1,0:T(8,128)S(1)} %copy-done.3, s32[1,2560]{1,0:T(1,128)S(1)} %copy-done.5, bf16[1280,1536]{1,0:T(8,128)(2,1)} %copy-done.12, bf16[1280,1536]{1,0:T(8,128)(2,1)} %copy-done.13, ...), custom_call_target="tpu_custom_call" | custom-call | flops 52428800000 | bytes 16777216 | tf_op jit(solution)/shard_map/attend_backward/pallas_call | solution.py:334
  475.1 4.1 fusion.51
  496.7 50.4 %collective-permute-start.17 = (bf16[1280,1024]{0,1:T(8,128)(2,1)}, bf16[1280,1024]{0,1:T(8,128)(2,1)}, u32[]{:S(2)}, u32[]{:S(2)}) collective-permute-start(bf16[1280,1024]{0,1:T(8,128)(2,1)} %add_convert_fusion.4), channel_id=1, source_target_pairs={{0,2},{2,0},{1,3},{3,1},{4,6},{6,4},{5,7},{7,5},{8,10},{10,8},{9,1... | collective-permute-start | bytes 7864328 | tf_op jit(solution)/shard_map/ppermute | solution.py:448
  556.3 15.2 %collective-permute-start.34 = (bf16[512,768]{1,0:T(8,128)(2,1)S(1)}, bf16[512,768]{1,0:T(8,128)(2,1)S(1)}, u32[]{:S(2)}, u32[]{:S(2)}) collective-permute-start(bf16[512,768]{1,0:T(8,128)(2,1)S(1)} %constant_dynamic-slice_fusion.4), channel_id=1, source_target_pairs={{2,0},{3,1},{0,2},{1,3},{6,4},{7,5},{4,6},{5,7},{10,8},{11,9},{8,1... | collective-permute-start | bytes 2359304 | tf_op jit(solution)/shard_map/ppermute | solution.py:419
  574.9 76.9 %collective-permute-start.26 = (bf16[256,768]{1,0:T(8,128)(2,1)}, bf16[256,768]{1,0:T(8,128)(2,1)}, u32[]{:S(2)}, u32[]{:S(2)}) collective-permute-start(bf16[256,768]{1,0:T(8,128)(2,1)} %constant_dynamic-slice_fusion.7), channel_id=1, source_target_pairs={{4,0},{5,1},{6,2},{7,3},{0,4},{1,5},{2,6},{3,7},{12,8},{13,9},{14,... | collective-permute-start | bytes 1179656 | tf_op jit(solution)/shard_map/ppermute | solution.py:419
  652.1 7.9 fusion.20
  667.7 10.2 %collective-permute-done.20 = f32[16384]{0:T(1024)S(1)} collective-permute-done((f32[16384]{0:T(1024)S(1)}, f32[16384]{0:T(1024)S(1)}, u32[]{:S(2)}, u32[]{:S(2)}) %collective-permute-start.20) | collective-permute-done | bytes 65568 | tf_op jit(solution)/shard_map/ppermute | solution.py:468
  682.5 10.2 %collective-permute-done.27 = bf16[128,768]{1,0:T(8,128)(2,1)S(1)} collective-permute-done((bf16[128,768]{1,0:T(8,128)(2,1)S(1)}, bf16[128,768]{1,0:T(8,128)(2,1)S(1)}, u32[]{:S(2)}, u32[]{:S(2)}) %collective-permute-start.27) | collective-permute-done | bytes 196640 | tf_op jit(solution)/shard_map/ppermute | solution.py:419
  692.8 9.7 %collective-permute-done.36 = bf16[128,768]{1,0:T(8,128)(2,1)S(1)} collective-permute-done((bf16[128,768]{1,0:T(8,128)(2,1)S(1)}, bf16[128,768]{1,0:T(8,128)(2,1)S(1)}, u32[]{:S(2)}, u32[]{:S(2)}) %collective-permute-start.36) | collective-permute-done | bytes 196640 | tf_op jit(solution)/shard_map/ppermute | solution.py:419
  706.7 8.5 collective-permute-done.37
  715.3 5.2 collective-permute-done.29
  725.5 8.6 collective-permute-done.30
  734.1 7.6 collective-permute-done.39
  744.1 5.0 fusion.19
  765.2 18.5 %collective-permute-done.23 = f32[16384]{0:T(1024)S(1)} collective-permute-done((f32[16384]{0:T(1024)S(1)}, f32[16384]{0:T(1024)S(1)}, u32[]{:S(2)}, u32[]{:S(2)}) %collective-permute-start.23) | collective-permute-done | bytes 65568 | tf_op jit(solution)/shard_map/ppermute | solution.py:468
  797.8 6.6 copy.106
  804.4 4.5 select_convert_fusion
  808.9 5.9 copy.105
  814.7 64.7 %all-reduce.3.cloned.1.call-done = (bf16[512,1024]{1,0:T(8,128)(2,1)}, bf16[1024,2048]{1,0:T(8,128)(2,1)}, bf16[2048,1024]{1,0:T(8,128)(2,1)}) async-done(((bf16[512,1024]{1,0:T(8,128)(2,1)}, bf16[1024,2048]{1,0:T(8,128)(2,1)}, bf16[2048,1024]{1,0:T(8,128)(2,1)}), (bf16[512,1024]{1,0:T(8,128)(2,1)}, bf16[1024,2048]{1,0:T(8,128)(2,1)}, bf16[2048,1024]{1,0:T(8,128)(2,1)})) %all-reduce.3.cloned.1.call-update) | async-done | bytes 9437200 | tf_op jit(solution)/shard_map/psum | solution.py:473
  879.4 6.8 convert_element_type.297
  886.2 4.4 convert_element_type.299
  (401 shorter events, 158.2 us)
Async XLA Ops:
  7.2 872.2 %all-reduce.3.cloned.1.call-start = ((), (), s32[]{:S(2)}) async-start(), calls=%async_computation | async-start | bytes 18874368 | tf_op jit(solution)/shard_map/psum | solution.py:473
  11.6 14.0 %collective-permute-start = (bf16[1280,1024]{0,1:T(8,128)(2,1)}, bf16[1280,1024]{0,1:T(8,128)(2,1)}, u32[]{:S(2)}, u32[]{:S(2)}) collective-permute-start(bf16[1280,1024]{0,1:T(8,128)(2,1)} %copy.80), channel_id=1, source_target_pairs={{1,2},{2,1},{5,6},{6,5},{9,10},{10,9},{13,14},{14,13},{17,18},{18,... | collective-permute-start | bytes 7864328 | tf_op jit(solution)/shard_map/ppermute | solution.py:400
  17.2 2.3 collective-permute-start.4
  18.8 2.3 collective-permute-start.1
  19.5 3.7 collective-permute-start.5
  24.9 58.1 %collective-permute-start.6 = (bf16[512,3,512]{0,2,1:T(8,128)(2,1)S(1)}, bf16[512,3,512]{0,2,1:T(8,128)(2,1)S(1)}, u32[]{:S(2)}, u32[]{:S(2)}) collective-permute-start(bf16[512,3,512]{0,2,1:T(8,128)(2,1)S(1)} %pad_maximum_fusion), channel_id=1, source_target_pairs={{5,1},{6,2},{1,5},{2,6},{13,9},{14,10},{9,13},{10,14},{21,17},{22,... | collective-permute-start | bytes 4718600 | tf_op jit(solution)/shard_map/ppermute | solution.py:419
  28.3 142.9 %copy-start.19 = (bf16[1280,1024]{0,1:T(8,128)(2,1)}, bf16[1280,1024]{0,1:T(8,128)(2,1)S(1)}, u32[]{:S(2)}) copy-start(bf16[1280,1024]{0,1:T(8,128)(2,1)S(1)} %get-tuple-element.138) | copy-start | bytes 7864324
  30.0 60.3 %collective-permute-start.7 = (bf16[1280,1024]{0,1:T(8,128)(2,1)S(1)}, bf16[1280,1024]{0,1:T(8,128)(2,1)}, u32[]{:S(2)}, u32[]{:S(2)}) collective-permute-start(bf16[1280,1024]{0,1:T(8,128)(2,1)S(1)} %fusion.14), channel_id=1, source_target_pairs={{0,2},{2,0},{1,3},{3,1},{4,6},{6,4},{5,7},{7,5},{8,10},{10,8},{9,1... | collective-permute-start | bytes 7864328 | tf_op jit(solution)/shard_map/ppermute | solution.py:448
  78.7 38.1 %collective-permute-start.3 = (bf16[1024,2048]{1,0:T(8,128)(2,1)S(1)}, bf16[1024,2048]{1,0:T(8,128)(2,1)}, u32[]{:S(2)}, u32[]{:S(2)}) collective-permute-start(bf16[1024,2048]{1,0:T(8,128)(2,1)S(1)} %copy-done.24), channel_id=1, source_target_pairs={{1,2},{2,1},{5,6},{6,5},{9,10},{10,9},{13,14},{14,13},{17,18},{18,... | collective-permute-start | bytes 12582920 | tf_op jit(solution)/shard_map/ppermute | solution.py:400
  81.4 35.5 %collective-permute-start.2 = (bf16[512,1024]{1,0:T(8,128)(2,1)}, bf16[512,1024]{1,0:T(8,128)(2,1)}, u32[]{:S(2)}, u32[]{:S(2)}) collective-permute-start(bf16[512,1024]{1,0:T(8,128)(2,1)} %param.25), channel_id=1, source_target_pairs={{1,2},{2,1},{5,6},{6,5},{9,10},{10,9},{13,14},{14,13},{17,18},{18,... | collective-permute-start | bytes 3145736 | tf_op jit(solution)/shard_map/ppermute | solution.py:400
  138.9 29.7 %collective-permute-start.8 = (bf16[1280,1024]{0,1:T(8,128)(2,1)S(1)}, bf16[1280,1024]{0,1:T(8,128)(2,1)S(1)}, u32[]{:S(2)}, u32[]{:S(2)}) collective-permute-start(bf16[1280,1024]{0,1:T(8,128)(2,1)S(1)} %convolution_convert_fusion.2), channel_id=1, source_target_pairs={{0,2},{2,0},{1,3},{3,1},{4,6},{6,4},{5,7},{7,5},{8,10},{10,8},{9,1... | collective-permute-start | bytes 7864328 | tf_op jit(solution)/shard_map/ppermute | solution.py:448
  164.1 12.7 %collective-permute-start.9 = (bf16[2048,1024]{1,0:T(8,128)(2,1)}, bf16[2048,1024]{1,0:T(8,128)(2,1)}, u32[]{:S(2)}, u32[]{:S(2)}) collective-permute-start(bf16[2048,1024]{1,0:T(8,128)(2,1)} %param.33), channel_id=1, source_target_pairs={{1,2},{2,1},{5,6},{6,5},{9,10},{10,9},{13,14},{14,13},{17,18},{18,... | collective-permute-start | bytes 12582920 | tf_op jit(solution)/shard_map/ppermute | solution.py:400
  175.3 5.7 collective-permute-start.10
  201.5 50.9 %collective-permute-start.11 = (bf16[1280,1024]{0,1:T(8,128)(2,1)}, bf16[1280,1024]{0,1:T(8,128)(2,1)}, u32[]{:S(2)}, u32[]{:S(2)}) collective-permute-start(bf16[1280,1024]{0,1:T(8,128)(2,1)} %convolution_convert_fusion.1), channel_id=1, source_target_pairs={{0,2},{2,0},{1,3},{3,1},{4,6},{6,4},{5,7},{7,5},{8,10},{10,8},{9,1... | collective-permute-start | bytes 7864328 | tf_op jit(solution)/shard_map/ppermute | solution.py:448
  240.4 23.3 %collective-permute-start.13 = (bf16[1280,1024]{0,1:T(8,128)(2,1)S(1)}, bf16[1280,1024]{0,1:T(8,128)(2,1)S(1)}, u32[]{:S(2)}, u32[]{:S(2)}) collective-permute-start(bf16[1280,1024]{0,1:T(8,128)(2,1)S(1)} %copy.90), channel_id=1, source_target_pairs={{1,2},{2,1},{5,6},{6,5},{9,10},{10,9},{13,14},{14,13},{17,18},{18,... | collective-permute-start | bytes 7864328 | tf_op jit(solution)/shard_map/ppermute | solution.py:400
  272.5 39.0 %collective-permute-start.14 = (bf16[1280,1024]{0,1:T(8,128)(2,1)}, bf16[1280,1024]{0,1:T(8,128)(2,1)S(1)}, u32[]{:S(2)}, u32[]{:S(2)}) collective-permute-start(bf16[1280,1024]{0,1:T(8,128)(2,1)} %get-tuple-element.130), channel_id=1, source_target_pairs={{0,2},{2,0},{1,3},{3,1},{4,6},{6,4},{5,7},{7,5},{8,10},{10,8},{9,1... | collective-permute-start | bytes 7864328 | tf_op jit(solution)/shard_map/ppermute | solution.py:448
  282.3 478.2 %collective-permute-start.12 = (bf16[1280,1024]{0,1:T(8,128)(2,1)}, bf16[1280,1024]{0,1:T(8,128)(2,1)}, u32[]{:S(2)}, u32[]{:S(2)}) collective-permute-start(bf16[1280,1024]{0,1:T(8,128)(2,1)} %get-tuple-element.139), channel_id=1, source_target_pairs={{2,1},{1,2},{6,5},{5,6},{10,9},{9,10},{14,13},{13,14},{18,17},{17,... | collective-permute-start | bytes 7864328 | tf_op jit(solution)/shard_map/ppermute | solution.py:400
  337.1 44.4 %collective-permute-start.15 = (bf16[1280,1024]{0,1:T(8,128)(2,1)S(1)}, bf16[1280,1024]{0,1:T(8,128)(2,1)}, u32[]{:S(2)}, u32[]{:S(2)}) collective-permute-start(bf16[1280,1024]{0,1:T(8,128)(2,1)S(1)} %convolution_convert_fusion), channel_id=1, source_target_pairs={{0,2},{2,0},{1,3},{3,1},{4,6},{6,4},{5,7},{7,5},{8,10},{10,8},{9,1... | collective-permute-start | bytes 7864328 | tf_op jit(solution)/shard_map/ppermute | solution.py:448
  364.6 42.3 %collective-permute-start.44 = (bf16[2048,1024]{1,0:T(8,128)(2,1)}, bf16[2048,1024]{1,0:T(8,128)(2,1)}, u32[]{:S(2)}, u32[]{:S(2)}) collective-permute-start(bf16[2048,1024]{1,0:T(8,128)(2,1)} %add_convert_fusion.2), channel_id=1, source_target_pairs={{2,1},{1,2},{6,5},{5,6},{10,9},{9,10},{14,13},{13,14},{18,17},{17,... | collective-permute-start | bytes 12582920 | tf_op jit(solution)/shard_map/ppermute | solution.py:400
  378.7 32.9 %collective-permute-start.43 = (bf16[1024,2048]{1,0:T(8,128)(2,1)}, bf16[1024,2048]{1,0:T(8,128)(2,1)}, u32[]{:S(2)}, u32[]{:S(2)}) collective-permute-start(bf16[1024,2048]{1,0:T(8,128)(2,1)} %add_convert_fusion.3), channel_id=1, source_target_pairs={{2,1},{1,2},{6,5},{5,6},{10,9},{9,10},{14,13},{13,14},{18,17},{17,... | collective-permute-start | bytes 12582920 | tf_op jit(solution)/shard_map/ppermute | solution.py:400
  400.9 15.3 %collective-permute-start.16 = (bf16[1280,1024]{0,1:T(8,128)(2,1)S(1)}, bf16[1280,1024]{0,1:T(8,128)(2,1)S(1)}, u32[]{:S(2)}, u32[]{:S(2)}) collective-permute-start(bf16[1280,1024]{0,1:T(8,128)(2,1)S(1)} %get-tuple-element.132), channel_id=1, source_target_pairs={{0,2},{2,0},{1,3},{3,1},{4,6},{6,4},{5,7},{7,5},{8,10},{10,8},{9,1... | collective-permute-start | bytes 7864328 | tf_op jit(solution)/shard_map/ppermute | solution.py:448
  445.0 104.6 %copy-start = (bf16[1280,768]{1,0:T(8,128)(2,1)}, bf16[1280,768]{1,0:T(8,128)(2,1)S(1)}, u32[]{:S(2)}) copy-start(bf16[1280,768]{1,0:T(8,128)(2,1)S(1)} %get-tuple-element.52) | copy-start | bytes 5898244
  482.6 70.8 %collective-permute-start.24 = (bf16[1024,768]{1,0:T(8,128)(2,1)}, bf16[1024,768]{1,0:T(8,128)(2,1)}, u32[]{:S(2)}, u32[]{:S(2)}) collective-permute-start(bf16[1024,768]{1,0:T(8,128)(2,1)} %add_convert_fusion.8), channel_id=1, source_target_pairs={{2,1},{1,2},{6,5},{5,6},{10,9},{9,10},{14,13},{13,14},{18,17},{17,... | collective-permute-start | bytes 4718600 | tf_op jit(solution)/shard_map/ppermute | solution.py:400
  490.7 65.4 %collective-permute-start.33 = (bf16[1024,768]{1,0:T(8,128)(2,1)S(1)}, bf16[1024,768]{1,0:T(8,128)(2,1)}, u32[]{:S(2)}, u32[]{:S(2)}) collective-permute-start(bf16[1024,768]{1,0:T(8,128)(2,1)S(1)} %add_convert_fusion.7), channel_id=1, source_target_pairs={{2,1},{1,2},{6,5},{5,6},{10,9},{9,10},{14,13},{13,14},{18,17},{17,... | collective-permute-start | bytes 4718600 | tf_op jit(solution)/shard_map/ppermute | solution.py:400
  496.7 155.4 %collective-permute-start.17 = (bf16[1280,1024]{0,1:T(8,128)(2,1)}, bf16[1280,1024]{0,1:T(8,128)(2,1)}, u32[]{:S(2)}, u32[]{:S(2)}) collective-permute-start(bf16[1280,1024]{0,1:T(8,128)(2,1)} %add_convert_fusion.4), channel_id=1, source_target_pairs={{0,2},{2,0},{1,3},{3,1},{4,6},{6,4},{5,7},{7,5},{8,10},{10,8},{9,1... | collective-permute-start | bytes 7864328 | tf_op jit(solution)/shard_map/ppermute | solution.py:448
  550.8 114.5 %collective-permute-start.42 = (bf16[512,1024]{1,0:T(8,128)(2,1)}, bf16[512,1024]{1,0:T(8,128)(2,1)}, u32[]{:S(2)}, u32[]{:S(2)}) collective-permute-start(bf16[512,1024]{1,0:T(8,128)(2,1)} %add_convert_fusion.9), channel_id=1, source_target_pairs={{2,1},{1,2},{6,5},{5,6},{10,9},{9,10},{14,13},{13,14},{18,17},{17,... | collective-permute-start | bytes 3145736 | tf_op jit(solution)/shard_map/ppermute | solution.py:400
  555.2 18.8 %collective-permute-start.25 = (bf16[512,768]{1,0:T(8,128)(2,1)S(1)}, bf16[512,768]{1,0:T(8,128)(2,1)S(1)}, u32[]{:S(2)}, u32[]{:S(2)}) collective-permute-start(bf16[512,768]{1,0:T(8,128)(2,1)S(1)} %constant_dynamic-slice_fusion.8), channel_id=1, source_target_pairs={{2,0},{3,1},{0,2},{1,3},{6,4},{7,5},{4,6},{5,7},{10,8},{11,9},{8,1... | collective-permute-start | bytes 2359304 | tf_op jit(solution)/shard_map/ppermute | solution.py:419
  556.3 95.6 %collective-permute-start.34 = (bf16[512,768]{1,0:T(8,128)(2,1)S(1)}, bf16[512,768]{1,0:T(8,128)(2,1)S(1)}, u32[]{:S(2)}, u32[]{:S(2)}) collective-permute-start(bf16[512,768]{1,0:T(8,128)(2,1)S(1)} %constant_dynamic-slice_fusion.4), channel_id=1, source_target_pairs={{2,0},{3,1},{0,2},{1,3},{6,4},{7,5},{4,6},{5,7},{10,8},{11,9},{8,1... | collective-permute-start | bytes 2359304 | tf_op jit(solution)/shard_map/ppermute | solution.py:419
  574.9 103.0 %collective-permute-start.26 = (bf16[256,768]{1,0:T(8,128)(2,1)}, bf16[256,768]{1,0:T(8,128)(2,1)}, u32[]{:S(2)}, u32[]{:S(2)}) collective-permute-start(bf16[256,768]{1,0:T(8,128)(2,1)} %constant_dynamic-slice_fusion.7), channel_id=1, source_target_pairs={{4,0},{5,1},{6,2},{7,3},{0,4},{1,5},{2,6},{3,7},{12,8},{13,9},{14,... | collective-permute-start | bytes 1179656 | tf_op jit(solution)/shard_map/ppermute | solution.py:419
  662.3 1.3 collective-permute-start.19
  662.4 18.8 %collective-permute-start.35 = (bf16[256,768]{1,0:T(8,128)(2,1)S(1)}, bf16[256,768]{1,0:T(8,128)(2,1)}, u32[]{:S(2)}, u32[]{:S(2)}) collective-permute-start(bf16[256,768]{1,0:T(8,128)(2,1)S(1)} %constant_dynamic-slice_fusion.3), channel_id=1, source_target_pairs={{4,0},{5,1},{6,2},{7,3},{0,4},{1,5},{2,6},{3,7},{12,8},{13,9},{14,... | collective-permute-start | bytes 1179656 | tf_op jit(solution)/shard_map/ppermute | solution.py:419
  664.3 13.5 %collective-permute-start.20 = (f32[16384]{0:T(1024)S(1)}, f32[16384]{0:T(1024)S(1)}, u32[]{:S(2)}, u32[]{:S(2)}) collective-permute-start(f32[16384]{0:T(1024)S(1)} %fusion.40), channel_id=1, source_target_pairs={{0,4},{1,5},{2,6},{3,7},{4,0},{5,1},{6,2},{7,3},{8,12},{9,13},{10,... | collective-permute-start | bytes 196616 | tf_op jit(solution)/shard_map/ppermute | solution.py:468
  677.8 46.3 %collective-permute-start.21 = (f32[16384]{0:T(1024)S(1)}, f32[16384]{0:T(1024)S(1)}, u32[]{:S(2)}, u32[]{:S(2)}) collective-permute-start(f32[16384]{0:T(1024)S(1)} %add.470), channel_id=1, source_target_pairs={{0,8},{1,9},{2,10},{3,11},{4,12},{5,13},{6,14},{7,15},{8,0},{9,1},... | collective-permute-start | bytes 196616 | tf_op jit(solution)/shard_map/ppermute | solution.py:468
  679.2 13.5 %collective-permute-start.27 = (bf16[128,768]{1,0:T(8,128)(2,1)S(1)}, bf16[128,768]{1,0:T(8,128)(2,1)S(1)}, u32[]{:S(2)}, u32[]{:S(2)}) collective-permute-start(bf16[128,768]{1,0:T(8,128)(2,1)S(1)} %constant_dynamic-slice_fusion.6), channel_id=1, source_target_pairs={{8,0},{9,1},{10,2},{11,3},{12,4},{13,5},{14,6},{15,7},{0,8},{1,9},... | collective-permute-start | bytes 589832 | tf_op jit(solution)/shard_map/ppermute | solution.py:419
  682.3 20.3 %collective-permute-start.36 = (bf16[128,768]{1,0:T(8,128)(2,1)S(1)}, bf16[128,768]{1,0:T(8,128)(2,1)S(1)}, u32[]{:S(2)}, u32[]{:S(2)}) collective-permute-start(bf16[128,768]{1,0:T(8,128)(2,1)S(1)} %constant_dynamic-slice_fusion.2), channel_id=1, source_target_pairs={{8,0},{9,1},{10,2},{11,3},{12,4},{13,5},{14,6},{15,7},{0,8},{1,9},... | collective-permute-start | bytes 589832 | tf_op jit(solution)/shard_map/ppermute | solution.py:419
  692.8 10.4 %collective-permute-start.28 = (bf16[64,768]{1,0:T(8,128)(2,1)S(1)}, bf16[64,768]{1,0:T(8,128)(2,1)S(1)}, u32[]{:S(2)}, u32[]{:S(2)}) collective-permute-start(bf16[64,768]{1,0:T(8,128)(2,1)S(1)} %constant_dynamic-slice_fusion.5), channel_id=1, source_target_pairs={{16,0},{17,1},{18,2},{19,3},{20,4},{21,5},{22,6},{23,7},{24,8},{25... | collective-permute-start | bytes 294920 | tf_op jit(solution)/shard_map/ppermute | solution.py:419
  702.6 12.5 %collective-permute-start.37 = (bf16[64,768]{1,0:T(8,128)(2,1)S(1)}, bf16[64,768]{1,0:T(8,128)(2,1)S(1)}, u32[]{:S(2)}, u32[]{:S(2)}) collective-permute-start(bf16[64,768]{1,0:T(8,128)(2,1)S(1)} %constant_dynamic-slice_fusion.1), channel_id=1, source_target_pairs={{16,0},{17,1},{18,2},{19,3},{20,4},{21,5},{22,6},{23,7},{24,8},{25... | collective-permute-start | bytes 294920 | tf_op jit(solution)/shard_map/ppermute | solution.py:419
  703.2 17.2 %collective-permute-start.29 = (bf16[64,768]{1,0:T(8,128)(2,1)S(1)}, bf16[64,768]{1,0:T(8,128)(2,1)S(1)}, u32[]{:S(2)}, u32[]{:S(2)}) collective-permute-start(bf16[64,768]{1,0:T(8,128)(2,1)S(1)} %add_convert_fusion.17), channel_id=1, source_target_pairs={{16,0},{17,1},{18,2},{19,3},{20,4},{21,5},{22,6},{23,7},{24,8},{25... | collective-permute-start | bytes 294920 | tf_op jit(solution)/shard_map/ppermute | solution.py:419
  715.2 8.8 collective-permute-start.38
  720.5 13.6 %collective-permute-start.30 = (bf16[128,768]{1,0:T(8,128)(2,1)S(1)}, bf16[128,768]{1,0:T(8,128)(2,1)S(1)}, u32[]{:S(2)}, u32[]{:S(2)}) collective-permute-start(bf16[128,768]{1,0:T(8,128)(2,1)S(1)} %pad_maximum_fusion.5), channel_id=1, source_target_pairs={{8,0},{9,1},{10,2},{11,3},{12,4},{13,5},{14,6},{15,7},{0,8},{1,9},... | collective-permute-start | bytes 589832 | tf_op jit(solution)/shard_map/ppermute | solution.py:419
  724.1 17.7 %collective-permute-start.39 = (bf16[128,768]{1,0:T(8,128)(2,1)S(1)}, bf16[128,768]{1,0:T(8,128)(2,1)S(1)}, u32[]{:S(2)}, u32[]{:S(2)}) collective-permute-start(bf16[128,768]{1,0:T(8,128)(2,1)S(1)} %pad_maximum_fusion.6), channel_id=1, source_target_pairs={{8,0},{9,1},{10,2},{11,3},{12,4},{13,5},{14,6},{15,7},{0,8},{1,9},... | collective-permute-start | bytes 589832 | tf_op jit(solution)/shard_map/ppermute | solution.py:419
  724.2 27.3 %collective-permute-start.22 = (f32[16384]{0:T(1024)S(1)}, f32[16384]{0:T(1024)S(1)}, u32[]{:S(2)}, u32[]{:S(2)}) collective-permute-start(f32[16384]{0:T(1024)S(1)} %add.471), channel_id=1, source_target_pairs={{0,16},{1,17},{2,18},{3,19},{4,20},{5,21},{6,22},{7,23},{8,24},{9,... | collective-permute-start | bytes 196616 | tf_op jit(solution)/shard_map/ppermute | solution.py:468
  741.9 12.1 %collective-permute-start.31 = (bf16[256,768]{1,0:T(8,128)(2,1)S(1)}, bf16[256,768]{1,0:T(8,128)(2,1)S(1)}, u32[]{:S(2)}, u32[]{:S(2)}) collective-permute-start(bf16[256,768]{1,0:T(8,128)(2,1)S(1)} %pad_maximum_fusion.3), channel_id=1, source_target_pairs={{4,0},{5,1},{6,2},{7,3},{0,4},{1,5},{2,6},{3,7},{12,8},{13,9},{14,... | collective-permute-start | bytes 1179656 | tf_op jit(solution)/shard_map/ppermute | solution.py:419
  742.8 16.3 %collective-permute-start.40 = (bf16[256,768]{1,0:T(8,128)(2,1)S(1)}, bf16[256,768]{1,0:T(8,128)(2,1)S(1)}, u32[]{:S(2)}, u32[]{:S(2)}) collective-permute-start(bf16[256,768]{1,0:T(8,128)(2,1)S(1)} %pad_maximum_fusion.4), channel_id=1, source_target_pairs={{4,0},{5,1},{6,2},{7,3},{0,4},{1,5},{2,6},{3,7},{12,8},{13,9},{14,... | collective-permute-start | bytes 1179656 | tf_op jit(solution)/shard_map/ppermute | solution.py:419
  749.1 55.3 %collective-permute-start.18 = (bf16[1280,1024]{0,1:T(8,128)(2,1)}, bf16[1280,1024]{0,1:T(8,128)(2,1)}, u32[]{:S(2)}, u32[]{:S(2)}) collective-permute-start(bf16[1280,1024]{0,1:T(8,128)(2,1)} %fusion.19), channel_id=1, source_target_pairs={{2,1},{1,2},{6,5},{5,6},{10,9},{9,10},{14,13},{13,14},{18,17},{17,... | collective-permute-start | bytes 7864328 | tf_op jit(solution)/shard_map/ppermute | solution.py:400
  751.6 32.1 %collective-permute-start.23 = (f32[16384]{0:T(1024)S(1)}, f32[16384]{0:T(1024)S(1)}, u32[]{:S(2)}, u32[]{:S(2)}) collective-permute-start(f32[16384]{0:T(1024)S(1)} %add.472), channel_id=1, source_target_pairs={{0,1},{1,0},{2,3},{3,2},{4,5},{5,4},{6,7},{7,6},{8,9},{9,8},{10,11... | collective-permute-start | bytes 196616 | tf_op jit(solution)/shard_map/ppermute | solution.py:468
  755.1 30.5 %collective-permute-start.32 = (bf16[512,768]{1,0:T(8,128)(2,1)}, bf16[512,768]{1,0:T(8,128)(2,1)}, u32[]{:S(2)}, u32[]{:S(2)}) collective-permute-start(bf16[512,768]{1,0:T(8,128)(2,1)} %pad_maximum_fusion.1), channel_id=1, source_target_pairs={{2,0},{3,1},{0,2},{1,3},{6,4},{7,5},{4,6},{5,7},{10,8},{11,9},{8,1... | collective-permute-start | bytes 2359304 | tf_op jit(solution)/shard_map/ppermute | solution.py:419
  760.3 29.2 %collective-permute-start.41 = (bf16[512,768]{1,0:T(8,128)(2,1)}, bf16[512,768]{1,0:T(8,128)(2,1)}, u32[]{:S(2)}, u32[]{:S(2)}) collective-permute-start(bf16[512,768]{1,0:T(8,128)(2,1)} %pad_maximum_fusion.2), channel_id=1, source_target_pairs={{2,0},{3,1},{0,2},{1,3},{6,4},{7,5},{4,6},{5,7},{10,8},{11,9},{8,1... | collective-permute-start | bytes 2359304 | tf_op jit(solution)/shard_map/ppermute | solution.py:419
  (91 other events, 1925.1 us)
Sparse Core Ops, SparseCore 0:
  667.7 211.6 all-reduce.2

commit v4 on v3

--- a/solution.py
+++ b/solution.py
@@ -46,6 +46,8 @@
 BQ = 256
 BK = 256
 MOST = 4
+FEED = 1024
+FEED_ROWS = 640
 PAIR = 2 * HDIM
 F32 = jnp.float32
 BF16 = jnp.bfloat16
@@ -326,7 +328,7 @@
     )(tables, kseg, seg[None, :], *qkv_parts, *begun)
 
 
-def attend_backward(qkv_parts, turned, grad_ctx, lse, seg, keep, tables, chunk):
+def attend_backward(qkv_parts, turned, grad_ctx, lse, seg, keep, tables, chunk, work):
     parts, width, tokens, every, pairs, seg_specs, qkv_specs, o_specs, ot_spec, lse_spec = (
         attend_specs(qkv_parts, chunk)
     )
@@ -354,19 +356,141 @@
         out_shape=[jax.ShapeDtypeStruct((width, pairs * 3 * PAIR), BF16)] * parts,
         compiler_params=pltpu.CompilerParams(vmem_limit_bytes=48 * 2**20),
         cost_estimate=pl.CostEstimate(
-            flops=4000 * tokens * tokens * pairs, bytes_accessed=2**24, transcendentals=0
+            flops=work * tokens * tokens * pairs, bytes_accessed=2**10, transcendentals=0
         ),
         name="attend_backward",
     )(tables, kseg, seg[None, :], *qkv_parts, *grad_ctx, turned, lse)
 
 
+def row_block(width):
+    return FEED_ROWS if width % FEED_ROWS == 0 else width
+
+
 def gelu_and_slope(u):
     root = 0.7978845608028654
     square = u * u
-    t = jnp.tanh(root * u * (1.0 + 0.044715 * square))
-    half = 0.5 * (1.0 + t)
-    slope = half + 0.5 * u * (1.0 - t * t) * (root * (1.0 + 0.134145 * square))
+    t = jnp.tanh(u * (root + (root * 0.044715) * square))
+    half = 0.5 * t + 0.5
+    slope = half + (0.5 * u) * (1.0 - t * t) * (root + (root * 0.134145) * square)
     return u * half, slope
+
+
+def feed_kernel(step, x_ref, up_ref, bias_ref, down_ref, *refs):
+    x_all, hidden_all, slope_all, out_ref = refs[-4:]
+    x = x_ref[...]
+    x_all[...] = x
+    units = up_ref.shape[1]
+    total = None
+    for first in range(0, units, step):
+        at = slice(first, first + step)
+        act, slope = gelu_and_slope(matmul(x, up_ref[:, at]) + bias_ref[:, at])
+        act = act.astype(BF16)
+        hidden_all[:, at] = act
+        slope_all[:, at] = slope.astype(BF16)
+        term = matmul(act, down_ref[at, :])
+        total = term if total is None else total + term
+    out_ref[...] = total.astype(BF16)
+
+
+def feed_forward(part, parts, x, up, bias, down, begun):
+    width, model = x.shape
+    units = up.shape[1]
+    rows = row_block(width)
+    steps = width // rows
+    own = lambda k: (k, 0)
+    whole = lambda k: (part * steps + k, 0)
+    fixed = lambda k: (0, 0)
+    once = pl.Buffered(1)
+    every = parts * width
+    return pl.pallas_call(
+        functools.partial(feed_kernel, min(units, FEED)),
+        grid=(steps,),
+        in_specs=[
+            pl.BlockSpec((rows, model), own),
+            pl.BlockSpec((model, units), fixed, pipeline_mode=once),
+            pl.BlockSpec((1, units), fixed, pipeline_mode=once),
+            pl.BlockSpec((units, model), fixed, pipeline_mode=once),
+        ]
+        + [pl.BlockSpec(memory_space=pl.ANY)] * len(begun),
+        out_specs=[
+            pl.BlockSpec((rows, model), whole),
+            pl.BlockSpec((rows, units), whole),
+            pl.BlockSpec((rows, units), whole),
+            pl.BlockSpec((rows, model), own),
+        ],
+        out_shape=[
+            jax.ShapeDtypeStruct((every, model), BF16),
+            jax.ShapeDtypeStruct((every, units), BF16),
+            jax.ShapeDtypeStruct((every, units), BF16),
+            jax.ShapeDtypeStruct((width, model), BF16),
+        ],
+        input_output_aliases={4 + n: n for n in range(len(begun))},
+        compiler_params=pltpu.CompilerParams(vmem_limit_bytes=48 * 2**20),
+        cost_estimate=pl.CostEstimate(
+            flops=6 * width * model * units, bytes_accessed=2**24, transcendentals=0
+        ),
+        name="feed_forward",
+    )(x, up, bias[None, :], down, *begun)
+
+
+def feed_back_kernel(step, g_ref, slope_ref, down_ref, up_ref, *refs):
+    pre_all, sums_ref, out_ref = refs[-3:]
+    g = g_ref[...]
+    units = up_ref.shape[1]
+
+    @pl.when(pl.program_id(0) == 0)
+    def _():
+        sums_ref[...] = jnp.zeros_like(sums_ref)
+
+    total = None
+    for first in range(0, units, step):
+        at = slice(first, first + step)
+        pre = contract_cols(g, down_ref[at, :]) * slope_ref[:, at].astype(F32)
+        pre = pre.astype(BF16)
+        pre_all[:, at] = pre
+        sums_ref[:, at] += jnp.sum(pre.astype(F32), axis=0, keepdims=True)
+        term = contract_cols(pre, up_ref[:, at])
+        total = term if total is None else total + term
+    out_ref[...] = total.astype(BF16)
+
+
+def feed_back(part, parts, g, slope_all, up, down, begun):
+    width, model = g.shape
+    units = up.shape[1]
+    rows = row_block(width)
+    steps = width // rows
+    own = lambda k: (k, 0)
+    whole = lambda k: (part * steps + k, 0)
+    fixed = lambda k: (0, 0)
+    once = pl.Buffered(1)
+    every = parts * width
+    return pl.pallas_call(
+        functools.partial(feed_back_kernel, min(units, FEED)),
+        grid=(steps,),
+        in_specs=[
+            pl.BlockSpec((rows, model), own),
+            pl.BlockSpec((rows, units), whole),
+            pl.BlockSpec((units, model), fixed, pipeline_mode=once),
+            pl.BlockSpec((model, units), fixed, pipeline_mode=once),
+        ]
+        + [pl.BlockSpec(memory_space=pl.ANY)] * len(begun),
+        out_specs=[
+            pl.BlockSpec((rows, units), whole),
+            pl.BlockSpec((1, units), fixed),
+            pl.BlockSpec((rows, model), own),
+        ],
+        out_shape=[
+            jax.ShapeDtypeStruct((every, units), BF16),
+            jax.ShapeDtypeStruct((1, units), F32),
+            jax.ShapeDtypeStruct((width, model), BF16),
+        ],
+        input_output_aliases={4 + n: n for n in range(len(begun))},
+        compiler_params=pltpu.CompilerParams(vmem_limit_bytes=48 * 2**20),
+        cost_estimate=pl.CostEstimate(
+            flops=6 * width * model * units, bytes_accessed=2**24, transcendentals=0
+        ),
+        name="feed_back",
+    )(g, slope_all, down, up, *begun)
 
 
 def after(value, *others):
@@ -428,14 +552,15 @@
             [jnp.where(high, theirs, mine), jnp.where(high, mine, theirs)], 0
         )
 
-    def regroup_spread(self, value):
-        bits = (1, 0)
-        rows = value.shape[0] // 4
+    def regroup_first(self, weight, tokens):
+        rows = weight.shape[0] // 4
         part = 2 * self.side(0) + self.side(1)
-        got = self.send(lax.dynamic_slice_in_dim(value, part * rows, rows, 0))
-        for bit in bits:
+        quarter = lax.dynamic_slice_in_dim(weight, part * rows, rows, 0)
+        got = self.send(quarter)
+        tokens = self.regroup(after(tokens, got))
+        for bit in (1, 0):
             got = self.joined(got, self.partner(got, bit, self.moving), bit)
-        return jnp.where(self.stays(), value, got)
+        return jnp.where(self.stays(), weight, got), tokens
 
     def moving(self, pair, core, m):
         return self.at_rank(pair, core, m) != self.device(pair, core, m)
@@ -468,12 +593,12 @@
             value = value + lax.ppermute(value, self.axes, [(i, i ^ step) for i in range(devices)])
         return value
 
-    def weight_sum(self, grad):
-        grad = self.give_back(grad.astype(jnp.bfloat16))
-        return lax.psum(grad, "dp").astype(jnp.float32)
+    def sum_dp(self, value, turn):
+        order = [(i + turn) % self.dp for i in range(self.dp)]
+        return lax.psum(value, "dp", axis_index_groups=[order])
 
     def weight_sum_by_halves(self, grad):
-        value = self.give_back(grad.astype(jnp.bfloat16))
+        value = self.give_back(grad)
         bits = [-1, *range(self.pairs.bit_length() - 1)]
         for bit in bits:
             half, high = value.shape[0] // 2, self.side(bit)
@@ -556,12 +681,16 @@
     grid_row = small[2 * width + units + group_rows :].astype(jnp.int32)
     pairs = width // PAIR
     chunks = 2 if pairs % 2 == 0 else 1
-    tokens = layout.regroup(tokens)
-    w_qkv = by_pairs(layout.regroup_spread(w_qkv), pairs)
+    pairs = width // PAIR
+    chunks = 2 if pairs % 2 == 0 else 1
+    w_qkv, tokens = layout.regroup_first(w_qkv, tokens)
+    w_qkv = by_pairs(w_qkv, pairs)
+    half = units // 2
     w_out_far = layout.send(after(w_out, tokens))
     w_up_far = layout.send(after(w_up, tokens))
-    w_down = layout.regroup(after(w_down, w_up_far))
-    cotangent = layout.regroup(after(cotangent, w_up_far))
+    w_top_far = layout.send(after(w_down[:half], tokens))
+    w_low_far = layout.send(after(w_down[half:], w_up_far))
+    cotangent = layout.regroup(after(cotangent, w_top_far))
 
     resid_in = tokens.astype(f32)
     norm1_out, normed1, inv1 = norm_parts(resid_in, ln1_gain, ln1_bias)
@@ -575,58 +704,83 @@
     qkv, turn = for_kernel(qkv, rank)
     seg, tables = row_tables(grid_row, group_rows, turn)
     begun = ()
-    for chunk in range(chunks):
-        if chunk == chunks - 1:
+    for pair in range(pairs):
+        if pair and pair == pairs // 2:
             tables, w_out_far, w_up_far = lax.optimization_barrier((tables, w_out_far, w_up_far))
-        begun = attend_forward(qkv, seg, keep, tables, (chunk, chunks), begun)
+        if pair and pair == pairs - 1:
+            tables, w_top_far = lax.optimization_barrier((tables, w_top_far))
+        begun = attend_forward(qkv, seg, keep, tables, (pair, pairs), begun)
     *context, context_turned, log_total = begun
     context = from_kernel(context, rank, shares)
-    w_out = jnp.where(layout.stays(), w_out, w_out_far)
-    w_up = jnp.where(layout.stays(), w_up, w_up_far)
+    stays = layout.stays()
+    w_out = jnp.where(stays, w_out, w_out_far)
+    w_up = jnp.where(stays, w_up, w_up_far)
+    w_down = jnp.where(stays, w_down, jnp.concatenate([w_top_far, w_low_far], 0))
     branch_z = layout.scatter_sum([matmul(x, w_out) for x in context]) + out_bias
     norm2_out, normed2, inv2 = norm_parts(branch_z, ln2_gain, ln2_bias)
     resid_mid = resid_in + norm2_out
     norm3_out, normed3, inv3 = norm_parts(resid_mid, ln3_gain, ln3_bias)
     a3 = layout.gather(norm3_out.astype(bf16))
-    hidden, slope = [], []
-    for x in a3:
-        act, der = gelu_and_slope(matmul(x, w_up) + up_bias)
-        hidden.append(act.astype(bf16))
-        slope.append(der.astype(bf16))
-    branch_f = layout.scatter_sum([matmul(x, w_down) for x in hidden]) + down_bias
+    begun, shares_f = (), []
+    for part, x in enumerate(a3):
+        *begun, share = feed_forward(part, shares, x, w_up, up_bias, w_down, begun)
+        shares_f.append(share)
+    a3_all, hidden, slope = begun
+    branch_f = layout.scatter_sum(shares_f) + down_bias
     norm4_out, normed4, inv4 = norm_parts(branch_f, ln4_gain, ln4_bias)
-    layer_out = layout.give_back((resid_mid + norm4_out).astype(bf16))
+    layer_out = (resid_mid + norm4_out).astype(bf16)
 
     upstream = cotangent.astype(f32)
     grad_f = norm_back(upstream, normed4, inv4, ln4_gain).astype(bf16)
     grad_f_all = layout.gather(grad_f)
-    grad_pre = [
-        (contract_cols(g, w_down) * s.astype(f32)).astype(bf16)
-        for g, s in zip(grad_f_all, slope)
-    ]
-    grad_a3 = layout.scatter_sum([contract_cols(g, w_up) for g in grad_pre])
-    g_w_down = layout.weight_sum(total([contract_rows(x, g) for x, g in zip(hidden, grad_f_all)]))
-    g_w_up = layout.weight_sum(total([contract_rows(x, g) for x, g in zip(a3, grad_pre)]))
-    g_up_bias = total([jnp.sum(g.astype(f32), 0) for g in grad_pre])
+    g_w_down = contract_rows(hidden, jnp.concatenate(grad_f_all, 0)).astype(bf16)
+    begun, shares_a3, g_up_bias = (), [], []
+    for part, g in enumerate(grad_f_all):
+        if part:
+            g, g_w_down = lax.optimization_barrier((g, g_w_down))
+        *begun, unit_sums, share = feed_back(part, shares, g, slope, w_up, w_down, begun)
+        shares_a3.append(share)
+        g_up_bias.append(unit_sums[0])
+    [grad_pre] = begun
+    g_w_down_far = layout.send(g_w_down, True)
+    grad_a3 = layout.scatter_sum(shares_a3)
+    g_up_bias = total(g_up_bias)
+    g_w_up = contract_rows(a3_all, grad_pre).astype(bf16)
+    g_w_up_far = layout.send(after(g_w_up, g_w_down_far), True)
     grad_mid = upstream + norm_back(grad_a3, normed3, inv3, ln3_gain)
     grad_z = norm_back(grad_mid, normed2, inv2, ln2_gain).astype(bf16)
     grad_z_all = layout.gather(grad_z)
     grad_ctx = [contract_cols(g, w_out).astype(bf16) for g in grad_z_all]
-    g_w_out = layout.weight_sum(total([contract_rows(x, g) for x, g in zip(context, grad_z_all)]))
+    g_w_out = total([contract_rows(x, g) for x, g in zip(context, grad_z_all)]).astype(bf16)
+    g_w_out_far = layout.send(g_w_out, True)
+    layer_out = layout.give_back(after(layer_out, g_w_out_far))
     grad_ctx, _ = for_kernel(grad_ctx, rank)
+    g_w_down = jnp.where(stays, g_w_down, g_w_down_far)
+    tables, g_w_down = lax.optimization_barrier((tables, g_w_down))
+    g_w_down = layout.sum_dp(g_w_down, 1).astype(f32)
     grad_a1, g_w_qkv, sums = [], [], []
     for chunk in range(chunks):
         grad_qkv = attend_backward(
-            qkv, context_turned, grad_ctx, log_total, seg, keep, tables, (chunk, chunks)
+            qkv, context_turned, grad_ctx, log_total, seg, keep, tables, (chunk, chunks), 4000 * (chunk == 0)
         )
         grad_qkv = from_kernel(grad_qkv, rank, shares)
         columns = grad_qkv[0].shape[1]
         w_part = w_qkv[:, chunk * columns : (chunk + 1) * columns]
         grad_a1.append([contract_cols(g, w_part) for g in grad_qkv])
         sums.append(total([jnp.sum(g.astype(f32), 0) for g in grad_qkv]))
-        g_w_qkv.append(
-            layout.weight_sum_by_halves(total([contract_rows(x, g) for x, g in zip(a1, grad_qkv)]))
-        )
+        g_part = total([contract_rows(x, g) for x, g in zip(a1, grad_qkv)]).astype(bf16)
+        if chunk == 0:
+            g_w_up_far, g_w_out_far, g_part = lax.optimization_barrier(
+                (g_w_up_far, g_w_out_far, g_part)
+            )
+            g_w_up = jnp.where(stays, g_w_up, g_w_up_far)
+            g_w_out = jnp.where(stays, g_w_out, g_w_out_far)
+            tables, g_w_up, g_w_out, g_part = lax.optimization_barrier(
+                (tables, g_w_up, g_w_out, g_part)
+            )
+            g_w_up = layout.sum_dp(g_w_up, 0).astype(f32)
+            g_w_out = layout.sum_dp(g_w_out, 0).astype(f32)
+        g_w_qkv.append(layout.weight_sum_by_halves(g_part))
     g_w_qkv = (
         jnp.concatenate(g_w_qkv, 1)
         .reshape(model_dim, pairs, 3, PAIR)

time: 909 us -> 820 us (0.902)
  Pallas kernels: 91.5 us -> 251 us
  starting transfers between devices: 307 us -> 181 us
  matrix products: 197 us -> 101 us
  waiting for transfers between devices: 155 us -> 111 us
  other arithmetic: 89 us -> 108 us
    ppermute x18, starting transfers between devices: 104 us -> 19 us  [partner(): return lax.ppermute(value, self.axes, moves)]
    pallas_call x0 -> x4, Pallas kernels: none -> 68.2 us  [the longest x2 35.7 us: feed_forward(): pl.pallas_call(functools.partial(feed_kernel, min(units, FEED)), grid=(st...]
    pallas_call x2, Pallas kernels: 54.1 us -> 110 us  [attend_backward(): pl.pallas_call(functools.partial(backward_kernel, parts), grid_spec=pltpu...]
    dot_general x10 -> x6, matrix products: 72.6 us -> 29.8 us  [contract_cols(): lax.dot_general(left, right, (((1,), (1,)), ((), ())), preferred_element_...]
    dot_general x8 -> x4, matrix products: 58 us -> 15.5 us  [matmul(): return jnp.dot(left, right, preferred_element_type=F32)]
    ppermute x8, starting transfers between devices: 171 us -> 131 us  [to_rank(): return lax.ppermute(value, self.axes, moves)]
    pallas_call x2 -> x4, Pallas kernels: 37.5 us -> 72.6 us  [attend_forward(): pl.pallas_call(functools.partial(forward_kernel, parts), grid_spec=pltpu....]
    psum x1 -> x2, waiting for transfers between devices: 64.7 us -> 35.4 us  [sum_dp(): return lax.psum(value, 'dp', axis_index_groups=[order])]
  transfers between devices with their start and end apart: 46 -> 48, of which waited for: 15 -> 17; matrix products, arithmetic and copies ran while one was open for 31% -> 26% of each run, Pallas kernels for 8% -> 22%
where the time goes in v4:
time: 820 us; the launch traced here: 810 us
  Pallas kernels  251 us (31%)
  starting transfers between devices  181 us (22%)
  waiting for transfers between devices  111 us (14%)
  other arithmetic  108 us (13%)
  matrix products  101 us (12%)
  local copies, waits for them, and re-layouts  40.6 us (5%)
  between operations  17.4 us (2%)
    ppermute x8, starting transfers between devices, to_rank(): return lax.ppermute(value, self.axes, moves)  131 us
    pallas_call x2, Pallas kernels, attend_backward(): pl.pallas_call(functools.partial(backward_kernel, parts), grid_spec=pltpu...  110 us
    pallas_call x4, Pallas kernels, attend_forward(): pl.pallas_call(functools.partial(forward_kernel, parts), grid_spec=pltpu....  72.6 us
    ppermute x18, waiting for transfers between devices, partner(): return lax.ppermute(value, self.axes, moves)  63.3 us
    dot_general x8, matrix products, contract_rows(): lax.dot_general(left, right, (((0,), (0,)), ((), ())), preferred_element_...  55.9 us
    pallas_call x2, Pallas kernels, feed_forward(): pl.pallas_call(functools.partial(feed_kernel, min(units, FEED)), grid=(st...  35.7 us
    psum x2, waiting for transfers between devices, sum_dp(): return lax.psum(value, 'dp', axis_index_groups=[order])  35.4 us
    pallas_call x2, Pallas kernels, feed_back(): pl.pallas_call(functools.partial(feed_back_kernel, min(units, FEED)), gri...  32.4 us
  transfers between devices with their start and end apart: 48, of which 17 were waited for; matrix products, arithmetic and copies ran while one was open for 26% of the time, Pallas kernels for 22%

profile of v4, /device:TPU:0, one launch (start us, length us, event | category | flops | bytes accessed | tf_op | source)
XLA Modules:
  0.0 810.2 jit_solution(701235903210839506)
XLA Ops:
  15.1 4.7 fusion.55
  29.2 41.6 %collective-permute-start.8 = (bf16[1280,1024]{1,0:T(8,128)(2,1)S(1)}, bf16[1280,1024]{1,0:T(8,128)(2,1)}, u32[]{:S(2)}, u32[]{:S(2)}) collective-permute-start(bf16[1280,1024]{1,0:T(8,128)(2,1)S(1)} %fusion.14), channel_id=1, source_target_pairs={{0,2},{2,0},{1,3},{3,1},{4,6},{6,4},{5,7},{7,5},{8,10},{10,8},{9,1... | collective-permute-start | bytes 7864328 | tf_op jit(solution)/shard_map/ppermute | solution.py:573
  82.4 4.6 fusion.2.refs_0_
  87.0 7.7 fusion.3.refs_1_
  94.7 18.1 %attend_forward.4 = (bf16[1280,512]{1,0:T(8,128)(2,1)S(1)}, bf16[1280,512]{1,0:T(8,128)(2,1)S(1)}, bf16[512,2560]{1,0:T(8,128)(2,1)S(1)}, f32[4,2,2560]{2,1,0:T(2,128)S(1)}) custom-call(s32[3,10]{1,0:T(4,128)S(1)} %add_add_fusion.2.tab_ref, s32[2560,1]{1,0:T(8,128)S(1)} %broadcast_in_dim.22.kseg_ref, s32[1,2560]{1,0:T(1,128)S(1)} %fusion.48.qseg_ref, ...), custom_call_target="tpu_custom_call" | custom-call | flops 19660800000 | bytes 8388608 | tf_op jit(solution)/shard_map/attend_forward/pallas_call | solution.py:303
  112.8 18.1 %attend_forward.5 = (bf16[1280,512]{1,0:T(8,128)(2,1)S(1)}, bf16[1280,512]{1,0:T(8,128)(2,1)S(1)}, bf16[512,2560]{1,0:T(8,128)(2,1)S(1)}, f32[4,2,2560]{2,1,0:T(2,128)S(1)}) custom-call(s32[3,10]{1,0:T(4,128)S(1)} %add_add_fusion.2.tab_ref, ...), custom_call_target="tpu_custom_call", output_to_operand_aliasing={{0}: (5, {}), {1}: (6, {}), {2}: (7, {}), {3}: (8, {})} | custom-call | flops 19660800000 | bytes 8388608 | tf_op jit(solution)/shard_map/attend_forward/pallas_call | solution.py:303
  131.1 18.1 %attend_forward.6 = (bf16[1280,512]{1,0:T(8,128)(2,1)S(1)}, bf16[1280,512]{1,0:T(8,128)(2,1)S(1)}, bf16[512,2560]{1,0:T(8,128)(2,1)S(1)}, f32[4,2,2560]{2,1,0:T(2,128)S(1)}) custom-call(s32[3,10]{1,0:T(4,128)S(1)} %add_add_fusion.2.tab_ref, ...), custom_call_target="tpu_custom_call", output_to_operand_aliasing={{0}: (5, {}), {1}: (6, {}), {2}: (7, {}), {3}: (8, {})} | custom-call | flops 19660800000 | bytes 8388608 | tf_op jit(solution)/shard_map/attend_forward/pallas_call | solution.py:303
  149.3 18.3 %attend_forward.7 = (bf16[1280,512]{1,0:T(8,128)(2,1)S(1)}, bf16[1280,512]{1,0:T(8,128)(2,1)S(1)}, bf16[512,2560]{1,0:T(8,128)(2,1)S(1)}, f32[4,2,2560]{2,1,0:T(2,128)S(1)}) custom-call(s32[3,10]{1,0:T(4,128)S(1)} %add_add_fusion.2.tab_ref, ...), custom_call_target="tpu_custom_call", output_to_operand_aliasing={{0}: (5, {}), {1}: (6, {}), {2}: (7, {}), {3}: (8, {})} | custom-call | flops 19660800000 | bytes 8388608 | tf_op jit(solution)/shard_map/attend_forward/pallas_call | solution.py:303
  169.4 42.8 %collective-permute-start.9 = (bf16[1280,1024]{1,0:T(8,128)(2,1)S(1)}, bf16[1280,1024]{1,0:T(8,128)(2,1)S(1)}, u32[]{:S(2)}, u32[]{:S(2)}) collective-permute-start(bf16[1280,1024]{1,0:T(8,128)(2,1)S(1)} %convolution_convert_fusion.1), channel_id=1, source_target_pairs={{0,2},{2,0},{1,3},{3,1},{4,6},{6,4},{5,7},{7,5},{8,10},{10,8},{9,1... | collective-permute-start | bytes 7864328 | tf_op jit(solution)/shard_map/ppermute | solution.py:573
  213.0 3.7 collective-permute-done.9
  223.6 4.9 broadcast_select_fusion.2.up_ref
  232.2 17.7 %feed_forward.2 = (bf16[2560,1024]{1,0:T(8,128)(2,1)}, bf16[2560,2048]{1,0:T(8,128)(2,1)}, bf16[2560,2048]{1,0:T(8,128)(2,1)}, bf16[1280,1024]{1,0:T(8,128)(2,1)S(1)}) custom-call(bf16[1280,1024]{1,0:T(8,128)(2,1)S(1)} %add_convert_fusion.2.x_ref, bf16[1024,2048]{1,0:T(8,128)(2,1)} %broadcast_select_fusion.2.up_ref, f32[1,2048]{1,0:T(1,128)S(1)} %bitcast.70, ...), custom_call_target="tpu_custom_call" | custom-call | flops 16106127360 | bytes 16777216 | tf_op jit(solution)/shard_map/feed_forward/pallas_call | solution.py:405
  249.9 18.0 %feed_forward.3 = (bf16[2560,1024]{1,0:T(8,128)(2,1)}, bf16[2560,2048]{1,0:T(8,128)(2,1)}, bf16[2560,2048]{1,0:T(8,128)(2,1)}, bf16[1280,1024]{1,0:T(8,128)(2,1)S(1)}) custom-call(bf16[1280,1024]{1,0:T(8,128)(2,1)S(1)} %collective-permute-done.11.x_ref, ...), custom_call_target="tpu_custom_call", output_to_operand_aliasing={{0}: (4, {}), {1}: (5, {}), {2}: (6, {})} | custom-call | flops 16106127360 | bytes 16777216 | tf_op jit(solution)/shard_map/feed_forward/pallas_call | solution.py:405
  267.9 11.3 %collective-permute-start.12 = (bf16[1280,1024]{1,0:T(8,128)(2,1)S(1)}, bf16[1280,1024]{1,0:T(8,128)(2,1)S(1)}, u32[]{:S(2)}, u32[]{:S(2)}) collective-permute-start(bf16[1280,1024]{1,0:T(8,128)(2,1)S(1)} %get-tuple-element.104), channel_id=1, source_target_pairs={{0,2},{2,0},{1,3},{3,1},{4,6},{6,4},{5,7},{7,5},{8,10},{10,8},{9,1... | collective-permute-start | bytes 7864328 | tf_op jit(solution)/shard_map/ppermute | solution.py:573
  286.0 5.1 fusion.26
  291.2 4.8 convert_reduce_fusion.2
  296.0 26.1 %collective-permute-start.14 = (bf16[1280,1024]{1,0:T(8,128)(2,1)S(1)}, bf16[1280,1024]{1,0:T(8,128)(2,1)S(1)}, u32[]{:S(2)}, u32[]{:S(2)}) collective-permute-start(bf16[1280,1024]{1,0:T(8,128)(2,1)S(1)} %get-tuple-element.171.g_ref), channel_id=1, source_target_pairs={{0,2},{2,0},{1,3},{3,1},{4,6},{6,4},{5,7},{7,5},{8,10},{10,8},{9,1... | collective-permute-start | bytes 7864328 | tf_op jit(solution)/shard_map/ppermute | solution.py:573
  322.1 15.7 %feed_back.2 = (bf16[2560,2048]{1,0:T(8,128)(2,1)}, f32[1,2048]{1,0:T(1,128)S(1)}, bf16[1280,1024]{1,0:T(8,128)(2,1)S(1)}) custom-call(bf16[1280,1024]{1,0:T(8,128)(2,1)S(1)} %get-tuple-element.171.g_ref, bf16[2560,2048]{1,0:T(8,128)(2,1)} %get-tuple-element.106.slope_ref, bf16[2048,1024]{1,0:T(8,128)(2,1)} %maximum_select_fusion.down_ref, ...), custom_call_target="tpu_custom_call" | custom-call | flops 16106127360 | bytes 16777216 | tf_op jit(solution)/shard_map/feed_back/pallas_call | solution.py:467
  337.9 15.6 %fusion.35 = bf16[2048,1024]{1,0:T(8,128)(2,1)} fusion(bf16[2560,2048]{1,0:T(8,128)(2,1)} %get-tuple-element.108, bf16[1280,1024]{1,0:T(8,128)(2,1)S(1)} %collective-permute-done.14.g_ref, bf16[1280,1024]{1,0:T(8,128)(2,1)S(1)} %get-tuple-element.171.g_ref), kind=kOutput, calls=%fused_computation.76 | convolution fusion | flops 10750001152 | bytes 19922944 | tf_op jit(solution)/shard_map/dot_general | solution.py:35
  353.4 16.7 %feed_back.3 = (bf16[2560,2048]{1,0:T(8,128)(2,1)}, f32[1,2048]{1,0:T(1,128)S(1)}, bf16[1280,1024]{1,0:T(8,128)(2,1)}) custom-call(bf16[1280,1024]{1,0:T(8,128)(2,1)S(1)} %collective-permute-done.14.g_ref, bf16[2560,2048]{1,0:T(8,128)(2,1)} %get-tuple-element.106.slope_ref, ...), custom_call_target="tpu_custom_call", output_to_operand_aliasing={{0}: (4, {})} | custom-call | flops 16106127360 | bytes 16777216 | tf_op jit(solution)/shard_map/feed_back/pallas_call | solution.py:467
  375.4 6.6 multiply_reduce_fusion
  382.1 8.2 %multiply_reduce_fusion.1 = (f32[1024]{0:T(1024)}, f32[1280]{0:T(1024)S(1)}, f32[1280]{0:T(1024)S(1)}, f32[1024]{0:T(1024)}, f32[1280,1024]{1,0:T(8,128)S(1)}) fusion(f32[1280,1024]{1,0:T(8,128)} %copy-done.22, f32[1280]{0:T(1024)S(1)} %add_rsqrt_fusion.2, f32[1280]{0:T(1024)S(1)} %broadcast_multiply_fusion.10, f32[1024]{0:T(1024)S(1)} %copy-done.67, ...), kind=kLoop, calls=%fused_computation.43 | loop fusion | flops 27520512 | bytes 23650304 | tf_op jit(solution)/shard_map/reduce_sum | solution.py:800
  390.3 3.7 convert_reduce_fusion.3
  394.2 16.8 %convolution_convert_fusion = bf16[1024,2048]{1,0:T(8,128)(2,1)} fusion(bf16[2560,1024]{1,0:T(8,128)(2,1)} %get-tuple-element.118, bf16[2560,2048]{1,0:T(8,128)(2,1)} %get-tuple-element.119), kind=kOutput, calls=%fused_computation.75 | convolution fusion | flops 10739515392 | bytes 19922944 | tf_op jit(solution)/shard_map/dot_general | solution.py:35
  411.0 4.6 convolution_convert_fusion.3.refs_2_
  424.7 4.4 add_convert_fusion.5
  434.5 55.1 %attend_backward.2 = (bf16[1280,768]{1,0:T(8,128)(2,1)S(1)}, bf16[1280,768]{1,0:T(8,128)(2,1)}) custom-call(s32[3,10]{1,0:T(4,128)S(1)} %copy-done.20, s32[2560,1]{1,0:T(8,128)S(1)} %copy-done.1, s32[1,2560]{1,0:T(1,128)S(1)} %copy-done.18, bf16[1280,1536]{1,0:T(8,128)(2,1)} %copy-done.2, bf16[1280,1536]{1,0:T(8,128)(2,1)} %copy-done.3, ...), custom_call_target="tpu_custom_call" | custom-call | flops 52428800000 | bytes 1024 | tf_op jit(solution)/shard_map/attend_backward/pallas_call | solution.py:336
  492.5 4.8 fusion.60
  497.4 4.6 fusion.40
  515.0 55.3 %attend_backward.3 = (bf16[1280,768]{1,0:T(8,128)(2,1)S(1)}, bf16[1280,768]{1,0:T(8,128)(2,1)}) custom-call(s32[3,10]{1,0:T(4,128)S(1)} %copy-done.20, s32[2560,1]{1,0:T(8,128)S(1)} %copy-done.1, s32[1,2560]{1,0:T(1,128)S(1)} %copy-done.18, bf16[1280,1536]{1,0:T(8,128)(2,1)} %copy-done.2, bf16[1280,1536]{1,0:T(8,128)(2,1)} %copy-done.3, ...), custom_call_target="tpu_custom_call" | custom-call | bytes 1024 | tf_op jit(solution)/shard_map/attend_backward/pallas_call | solution.py:336
  570.3 4.8 fusion.61
  579.6 3.8 add_convert_fusion
  583.4 8.9 %collective-permute-start.21 = (bf16[1280,1024]{1,0:T(8,128)(2,1)}, bf16[1280,1024]{1,0:T(8,128)(2,1)}, u32[]{:S(2)}, u32[]{:S(2)}) collective-permute-start(bf16[1280,1024]{1,0:T(8,128)(2,1)} %add_convert_fusion), channel_id=1, source_target_pairs={{0,2},{2,0},{1,3},{3,1},{4,6},{6,4},{5,7},{7,5},{8,10},{10,8},{9,1... | collective-permute-start | bytes 7864328 | tf_op jit(solution)/shard_map/ppermute | solution.py:573
  592.3 4.6 fusion.42
  599.4 6.8 convert_element_type.259
  621.5 8.7 %fusion.20 = (f32[1024]{0:T(1024)}, f32[1280]{0:T(1024)}, f32[1280]{0:T(1024)}, f32[1024]{0:T(1024)}, f32[1280,1024]{1,0:T(8,128)}) fusion(bf16[1280,1024]{1,0:T(8,128)(2,1)S(1)} %copy-done.24, f32[1280]{0:T(1024)S(1)} %copy-done.64, f32[1280]{0:T(1024)S(1)} %copy-done.61, f32[1024]{0:T(1024)S(1)} %copy-done.71, ...), kind=kOutput, calls=%fused_computation.30 | convolution fusion | flops 2030300672 | bytes 19300352 | tf_op jit(solution)/shard_map/dot_general | solution.py:41
  638.4 13.1 %collective-permute-done.39 = bf16[256,768]{1,0:T(8,128)(2,1)S(1)} collective-permute-done((bf16[256,768]{1,0:T(8,128)(2,1)S(1)}, bf16[256,768]{1,0:T(8,128)(2,1)S(1)}, u32[]{:S(2)}, u32[]{:S(2)}) %collective-permute-start.39) | collective-permute-done | bytes 393248 | tf_op jit(solution)/shard_map/ppermute | solution.py:543
  657.3 8.5 %collective-permute-done.40 = bf16[128,768]{1,0:T(8,128)(2,1)S(1)} collective-permute-done((bf16[128,768]{1,0:T(8,128)(2,1)S(1)}, bf16[128,768]{1,0:T(8,128)(2,1)S(1)}, u32[]{:S(2)}, u32[]{:S(2)}) %collective-permute-start.40) | collective-permute-done | bytes 196640 | tf_op jit(solution)/shard_map/ppermute | solution.py:543
  671.7 3.8 collective-permute-done.41
  675.8 5.4 collective-permute-done.33
  681.3 3.9 collective-permute-done.42
  686.5 9.9 %collective-permute-done.34 = bf16[128,768]{1,0:T(8,128)(2,1)S(1)} collective-permute-done((bf16[128,768]{1,0:T(8,128)(2,1)S(1)}, bf16[128,768]{1,0:T(8,128)(2,1)S(1)}, u32[]{:S(2)}, u32[]{:S(2)}) %collective-permute-start.34) | collective-permute-done | bytes 196640 | tf_op jit(solution)/shard_map/ppermute | solution.py:543
  702.0 3.8 fusion.19
  709.2 7.4 collective-permute-done.35
  717.7 5.4 collective-permute-done.44
  728.5 35.4 %all-reduce.6.cloned.1.call-done = (bf16[512,1024]{1,0:T(8,128)(2,1)}, bf16[1024,2048]{1,0:T(8,128)(2,1)}) async-done(((bf16[512,1024]{1,0:T(8,128)(2,1)}, bf16[1024,2048]{1,0:T(8,128)(2,1)}), (bf16[512,1024]{1,0:T(8,128)(2,1)}, bf16[1024,2048]{1,0:T(8,128)(2,1)})) %all-reduce.6.cloned.1.call-update) | async-done | bytes 5242896 | tf_op jit(solution)/shard_map/psum | solution.py:598
  763.9 6.7 convert_element_type.258
  793.9 6.6 copy.83
  (398 shorter events, 167.6 us)
Async XLA Ops:
  7.2 592.2 %all-reduce.4.cloned.1.call-start = ((), (), s32[]{:S(2)}) async-start(), calls=%async_computation | async-start | bytes 8388608 | tf_op jit(solution)/shard_map/psum | solution.py:598
  10.7 1.6 collective-permute-start
  12.2 13.8 %collective-permute-start.1 = (bf16[1280,1024]{1,0:T(8,128)(2,1)}, bf16[1280,1024]{1,0:T(8,128)(2,1)}, u32[]{:S(2)}, u32[]{:S(2)}) collective-permute-start(bf16[1280,1024]{1,0:T(8,128)(2,1)} %param.20), channel_id=1, source_target_pairs={{1,2},{2,1},{5,6},{6,5},{9,10},{10,9},{13,14},{14,13},{17,18},{18,... | collective-permute-start | bytes 7864328 | tf_op jit(solution)/shard_map/ppermute | solution.py:524
  14.4 7.0 collective-permute-start.2
  19.8 3.7 collective-permute-start.6
  25.3 47.2 %collective-permute-start.7 = (bf16[512,3,512]{0,2,1:T(8,128)(2,1)S(1)}, bf16[512,3,512]{0,2,1:T(8,128)(2,1)S(1)}, u32[]{:S(2)}, u32[]{:S(2)}) collective-permute-start(bf16[512,3,512]{0,2,1:T(8,128)(2,1)S(1)} %pad_maximum_fusion), channel_id=1, source_target_pairs={{5,1},{6,2},{1,5},{2,6},{13,9},{14,10},{9,13},{10,14},{21,17},{22,... | collective-permute-start | bytes 4718600 | tf_op jit(solution)/shard_map/ppermute | solution.py:543
  29.2 57.8 %collective-permute-start.8 = (bf16[1280,1024]{1,0:T(8,128)(2,1)S(1)}, bf16[1280,1024]{1,0:T(8,128)(2,1)}, u32[]{:S(2)}, u32[]{:S(2)}) collective-permute-start(bf16[1280,1024]{1,0:T(8,128)(2,1)S(1)} %fusion.14), channel_id=1, source_target_pairs={{0,2},{2,0},{1,3},{3,1},{4,6},{6,4},{5,7},{7,5},{8,10},{10,8},{9,1... | collective-permute-start | bytes 7864328 | tf_op jit(solution)/shard_map/ppermute | solution.py:573
  76.4 54.5 %collective-permute-start.4 = (bf16[1024,2048]{1,0:T(8,128)(2,1)S(1)}, bf16[1024,2048]{1,0:T(8,128)(2,1)}, u32[]{:S(2)}, u32[]{:S(2)}) collective-permute-start(bf16[1024,2048]{1,0:T(8,128)(2,1)S(1)} %copy-done.32), channel_id=1, source_target_pairs={{1,2},{2,1},{5,6},{6,5},{9,10},{10,9},{13,14},{14,13},{17,18},{18,... | collective-permute-start | bytes 12582920 | tf_op jit(solution)/shard_map/ppermute | solution.py:524
  79.5 51.4 %collective-permute-start.3 = (bf16[512,1024]{1,0:T(8,128)(2,1)S(1)}, bf16[512,1024]{1,0:T(8,128)(2,1)}, u32[]{:S(2)}, u32[]{:S(2)}) collective-permute-start(bf16[512,1024]{1,0:T(8,128)(2,1)S(1)} %copy-done.54), channel_id=1, source_target_pairs={{1,2},{2,1},{5,6},{6,5},{9,10},{10,9},{13,14},{14,13},{17,18},{18,... | collective-permute-start | bytes 3145736 | tf_op jit(solution)/shard_map/ppermute | solution.py:524
  81.1 49.8 %collective-permute-start.5 = (bf16[1024,1024]{1,0:T(8,128)(2,1)}, bf16[1024,1024]{1,0:T(8,128)(2,1)S(1)}, u32[]{:S(2)}, u32[]{:S(2)}) collective-permute-start(bf16[1024,1024]{1,0:T(8,128)(2,1)} %get-tuple-element.80), channel_id=1, source_target_pairs={{1,2},{2,1},{5,6},{6,5},{9,10},{10,9},{13,14},{14,13},{17,18},{18,... | collective-permute-start | bytes 6291464 | tf_op jit(solution)/shard_map/ppermute | solution.py:524
  169.4 47.3 %collective-permute-start.9 = (bf16[1280,1024]{1,0:T(8,128)(2,1)S(1)}, bf16[1280,1024]{1,0:T(8,128)(2,1)S(1)}, u32[]{:S(2)}, u32[]{:S(2)}) collective-permute-start(bf16[1280,1024]{1,0:T(8,128)(2,1)S(1)} %convolution_convert_fusion.1), channel_id=1, source_target_pairs={{0,2},{2,0},{1,3},{3,1},{4,6},{6,4},{5,7},{7,5},{8,10},{10,8},{9,1... | collective-permute-start | bytes 7864328 | tf_op jit(solution)/shard_map/ppermute | solution.py:573
  212.2 16.3 %collective-permute-start.10 = (bf16[1024,1024]{1,0:T(8,128)(2,1)}, bf16[1024,1024]{1,0:T(8,128)(2,1)S(1)}, u32[]{:S(2)}, u32[]{:S(2)}) collective-permute-start(bf16[1024,1024]{1,0:T(8,128)(2,1)} %get-tuple-element.99), channel_id=1, source_target_pairs={{1,2},{2,1},{5,6},{6,5},{9,10},{10,9},{13,14},{14,13},{17,18},{18,... | collective-permute-start | bytes 6291464 | tf_op jit(solution)/shard_map/ppermute | solution.py:524
  223.2 26.7 %collective-permute-start.11 = (bf16[1280,1024]{1,0:T(8,128)(2,1)S(1)}, bf16[1280,1024]{1,0:T(8,128)(2,1)S(1)}, u32[]{:S(2)}, u32[]{:S(2)}) collective-permute-start(bf16[1280,1024]{1,0:T(8,128)(2,1)S(1)} %add_convert_fusion.2.x_ref), channel_id=1, source_target_pairs={{0,2},{2,0},{1,3},{3,1},{4,6},{6,4},{5,7},{7,5},{8,10},{10,8},{9,1... | collective-permute-start | bytes 7864328 | tf_op jit(solution)/shard_map/ppermute | solution.py:573
  267.9 15.8 %collective-permute-start.12 = (bf16[1280,1024]{1,0:T(8,128)(2,1)S(1)}, bf16[1280,1024]{1,0:T(8,128)(2,1)S(1)}, u32[]{:S(2)}, u32[]{:S(2)}) collective-permute-start(bf16[1280,1024]{1,0:T(8,128)(2,1)S(1)} %get-tuple-element.104), channel_id=1, source_target_pairs={{0,2},{2,0},{1,3},{3,1},{4,6},{6,4},{5,7},{7,5},{8,10},{10,8},{9,1... | collective-permute-start | bytes 7864328 | tf_op jit(solution)/shard_map/ppermute | solution.py:573
  279.2 6.8 collective-permute-start.13
  296.0 41.8 %collective-permute-start.14 = (bf16[1280,1024]{1,0:T(8,128)(2,1)S(1)}, bf16[1280,1024]{1,0:T(8,128)(2,1)S(1)}, u32[]{:S(2)}, u32[]{:S(2)}) collective-permute-start(bf16[1280,1024]{1,0:T(8,128)(2,1)S(1)} %get-tuple-element.171.g_ref), channel_id=1, source_target_pairs={{0,2},{2,0},{1,3},{3,1},{4,6},{6,4},{5,7},{7,5},{8,10},{10,8},{9,1... | collective-permute-start | bytes 7864328 | tf_op jit(solution)/shard_map/ppermute | solution.py:573
  370.2 5.3 collective-permute-start.15
  370.2 45.4 %collective-permute-start.19 = (bf16[2048,1024]{1,0:T(8,128)(2,1)}, bf16[2048,1024]{1,0:T(8,128)(2,1)S(1)}, u32[]{:S(2)}, u32[]{:S(2)}) collective-permute-start(bf16[2048,1024]{1,0:T(8,128)(2,1)} %fusion.35), channel_id=1, source_target_pairs={{2,1},{1,2},{6,5},{5,6},{10,9},{9,10},{14,13},{13,14},{18,17},{17,... | collective-permute-start | bytes 12582920 | tf_op jit(solution)/shard_map/ppermute | solution.py:524
  394.0 27.2 %collective-permute-start.16 = (bf16[1280,1024]{1,0:T(8,128)(2,1)}, bf16[1280,1024]{1,0:T(8,128)(2,1)}, u32[]{:S(2)}, u32[]{:S(2)}) collective-permute-start(bf16[1280,1024]{1,0:T(8,128)(2,1)} %get-tuple-element.173), channel_id=1, source_target_pairs={{0,2},{2,0},{1,3},{3,1},{4,6},{6,4},{5,7},{7,5},{8,10},{10,8},{9,1... | collective-permute-start | bytes 7864328 | tf_op jit(solution)/shard_map/ppermute | solution.py:573
  418.2 87.4 %collective-permute-start.20 = (bf16[1024,2048]{1,0:T(8,128)(2,1)}, bf16[1024,2048]{1,0:T(8,128)(2,1)}, u32[]{:S(2)}, u32[]{:S(2)}) collective-permute-start(bf16[1024,2048]{1,0:T(8,128)(2,1)} %convolution_convert_fusion), channel_id=1, source_target_pairs={{2,1},{1,2},{6,5},{5,6},{10,9},{9,10},{14,13},{13,14},{18,17},{17,... | collective-permute-start | bytes 12582920 | tf_op jit(solution)/shard_map/ppermute | solution.py:524
  421.0 342.9 %all-reduce.6.cloned.1.call-start = ((), (), s32[]{:S(2)}) async-start(), calls=%async_computation.1 | async-start | bytes 10485760 | tf_op jit(solution)/shard_map/psum | solution.py:598
  429.1 76.5 %collective-permute-start.17 = (bf16[512,1024]{1,0:T(8,128)(2,1)}, bf16[512,1024]{1,0:T(8,128)(2,1)}, u32[]{:S(2)}, u32[]{:S(2)}) collective-permute-start(bf16[512,1024]{1,0:T(8,128)(2,1)} %add_convert_fusion.5), channel_id=1, source_target_pairs={{2,1},{1,2},{6,5},{5,6},{10,9},{9,10},{14,13},{13,14},{18,17},{17,... | collective-permute-start | bytes 3145736 | tf_op jit(solution)/shard_map/ppermute | solution.py:524
  510.5 96.3 %collective-permute-start.28 = (bf16[1024,768]{1,0:T(8,128)(2,1)}, bf16[1024,768]{1,0:T(8,128)(2,1)}, u32[]{:S(2)}, u32[]{:S(2)}) collective-permute-start(bf16[1024,768]{1,0:T(8,128)(2,1)} %add_convert_fusion.4), channel_id=1, source_target_pairs={{2,1},{1,2},{6,5},{5,6},{10,9},{9,10},{14,13},{13,14},{18,17},{17,... | collective-permute-start | bytes 4718600 | tf_op jit(solution)/shard_map/ppermute | solution.py:524
  577.7 33.4 %collective-permute-start.37 = (bf16[1024,768]{1,0:T(8,128)(2,1)S(1)}, bf16[1024,768]{1,0:T(8,128)(2,1)}, u32[]{:S(2)}, u32[]{:S(2)}) collective-permute-start(bf16[1024,768]{1,0:T(8,128)(2,1)S(1)} %add_convert_fusion.3), channel_id=1, source_target_pairs={{2,1},{1,2},{6,5},{5,6},{10,9},{9,10},{14,13},{13,14},{18,17},{17,... | collective-permute-start | bytes 4718600 | tf_op jit(solution)/shard_map/ppermute | solution.py:524
  583.4 38.1 %collective-permute-start.21 = (bf16[1280,1024]{1,0:T(8,128)(2,1)}, bf16[1280,1024]{1,0:T(8,128)(2,1)}, u32[]{:S(2)}, u32[]{:S(2)}) collective-permute-start(bf16[1280,1024]{1,0:T(8,128)(2,1)} %add_convert_fusion), channel_id=1, source_target_pairs={{0,2},{2,0},{1,3},{3,1},{4,6},{6,4},{5,7},{7,5},{8,10},{10,8},{9,1... | collective-permute-start | bytes 7864328 | tf_op jit(solution)/shard_map/ppermute | solution.py:573
  596.8 128.1 %collective-permute-start.18 = (bf16[1280,1024]{1,0:T(8,128)(2,1)}, bf16[1280,1024]{1,0:T(8,128)(2,1)}, u32[]{:S(2)}, u32[]{:S(2)}) collective-permute-start(bf16[1280,1024]{1,0:T(8,128)(2,1)} %get-tuple-element.112), channel_id=1, source_target_pairs={{2,1},{1,2},{6,5},{5,6},{10,9},{9,10},{14,13},{13,14},{18,17},{17,... | collective-permute-start | bytes 7864328 | tf_op jit(solution)/shard_map/ppermute | solution.py:524
  609.6 4.8 collective-permute-start.29
  612.3 7.0 collective-permute-start.38
  617.0 20.2 %collective-permute-start.30 = (bf16[256,768]{1,0:T(8,128)(2,1)}, bf16[256,768]{1,0:T(8,128)(2,1)}, u32[]{:S(2)}, u32[]{:S(2)}) collective-permute-start(bf16[256,768]{1,0:T(8,128)(2,1)} %constant_dynamic-slice_fusion.7), channel_id=1, source_target_pairs={{4,0},{5,1},{6,2},{7,3},{0,4},{1,5},{2,6},{3,7},{12,8},{13,9},{14,... | collective-permute-start | bytes 1179656 | tf_op jit(solution)/shard_map/ppermute | solution.py:543
  632.6 1.3 collective-permute-start.23
  632.6 18.9 %collective-permute-start.39 = (bf16[256,768]{1,0:T(8,128)(2,1)S(1)}, bf16[256,768]{1,0:T(8,128)(2,1)S(1)}, u32[]{:S(2)}, u32[]{:S(2)}) collective-permute-start(bf16[256,768]{1,0:T(8,128)(2,1)S(1)} %constant_dynamic-slice_fusion.3), channel_id=1, source_target_pairs={{4,0},{5,1},{6,2},{7,3},{0,4},{1,5},{2,6},{3,7},{12,8},{13,9},{14,... | collective-permute-start | bytes 1179656 | tf_op jit(solution)/shard_map/ppermute | solution.py:543
  634.5 18.3 %collective-permute-start.24 = (f32[16384]{0:T(1024)S(1)}, f32[16384]{0:T(1024)S(1)}, u32[]{:S(2)}, u32[]{:S(2)}) collective-permute-start(f32[16384]{0:T(1024)S(1)} %fusion.52), channel_id=1, source_target_pairs={{0,4},{1,5},{2,6},{3,7},{4,0},{5,1},{6,2},{7,3},{8,12},{9,13},{10,... | collective-permute-start | bytes 196616 | tf_op jit(solution)/shard_map/ppermute | solution.py:593
  638.3 15.5 %collective-permute-start.31 = (bf16[128,768]{1,0:T(8,128)(2,1)S(1)}, bf16[128,768]{1,0:T(8,128)(2,1)S(1)}, u32[]{:S(2)}, u32[]{:S(2)}) collective-permute-start(bf16[128,768]{1,0:T(8,128)(2,1)S(1)} %constant_dynamic-slice_fusion.6), channel_id=1, source_target_pairs={{8,0},{9,1},{10,2},{11,3},{12,4},{13,5},{14,6},{15,7},{0,8},{1,9},... | collective-permute-start | bytes 589832 | tf_op jit(solution)/shard_map/ppermute | solution.py:543
  651.7 14.2 %collective-permute-start.40 = (bf16[128,768]{1,0:T(8,128)(2,1)S(1)}, bf16[128,768]{1,0:T(8,128)(2,1)S(1)}, u32[]{:S(2)}, u32[]{:S(2)}) collective-permute-start(bf16[128,768]{1,0:T(8,128)(2,1)S(1)} %constant_dynamic-slice_fusion.2), channel_id=1, source_target_pairs={{8,0},{9,1},{10,2},{11,3},{12,4},{13,5},{14,6},{15,7},{0,8},{1,9},... | collective-permute-start | bytes 589832 | tf_op jit(solution)/shard_map/ppermute | solution.py:543
  652.8 32.6 %collective-permute-start.25 = (f32[16384]{0:T(1024)S(1)}, f32[16384]{0:T(1024)S(1)}, u32[]{:S(2)}, u32[]{:S(2)}) collective-permute-start(f32[16384]{0:T(1024)S(1)} %add.401), channel_id=1, source_target_pairs={{0,8},{1,9},{2,10},{3,11},{4,12},{5,13},{6,14},{7,15},{8,0},{9,1},... | collective-permute-start | bytes 196616 | tf_op jit(solution)/shard_map/ppermute | solution.py:593
  654.0 14.3 %collective-permute-start.32 = (bf16[64,768]{1,0:T(8,128)(2,1)S(1)}, bf16[64,768]{1,0:T(8,128)(2,1)S(1)}, u32[]{:S(2)}, u32[]{:S(2)}) collective-permute-start(bf16[64,768]{1,0:T(8,128)(2,1)S(1)} %constant_dynamic-slice_fusion.5), channel_id=1, source_target_pairs={{16,0},{17,1},{18,2},{19,3},{20,4},{21,5},{22,6},{23,7},{24,8},{25... | collective-permute-start | bytes 294920 | tf_op jit(solution)/shard_map/ppermute | solution.py:543
  665.9 9.7 %collective-permute-start.41 = (bf16[64,768]{1,0:T(8,128)(2,1)S(1)}, bf16[64,768]{1,0:T(8,128)(2,1)S(1)}, u32[]{:S(2)}, u32[]{:S(2)}) collective-permute-start(bf16[64,768]{1,0:T(8,128)(2,1)S(1)} %constant_dynamic-slice_fusion.1), channel_id=1, source_target_pairs={{16,0},{17,1},{18,2},{19,3},{20,4},{21,5},{22,6},{23,7},{24,8},{25... | collective-permute-start | bytes 294920 | tf_op jit(solution)/shard_map/ppermute | solution.py:543
  668.3 12.9 %collective-permute-start.33 = (bf16[64,768]{1,0:T(8,128)(2,1)S(1)}, bf16[64,768]{1,0:T(8,128)(2,1)S(1)}, u32[]{:S(2)}, u32[]{:S(2)}) collective-permute-start(bf16[64,768]{1,0:T(8,128)(2,1)S(1)} %add_convert_fusion.13), channel_id=1, source_target_pairs={{16,0},{17,1},{18,2},{19,3},{20,4},{21,5},{22,6},{23,7},{24,8},{25... | collective-permute-start | bytes 294920 | tf_op jit(solution)/shard_map/ppermute | solution.py:543
  675.6 9.7 %collective-permute-start.42 = (bf16[64,768]{1,0:T(8,128)(2,1)S(1)}, bf16[64,768]{1,0:T(8,128)(2,1)S(1)}, u32[]{:S(2)}, u32[]{:S(2)}) collective-permute-start(bf16[64,768]{1,0:T(8,128)(2,1)S(1)} %add_convert_fusion.12), channel_id=1, source_target_pairs={{16,0},{17,1},{18,2},{19,3},{20,4},{21,5},{22,6},{23,7},{24,8},{25... | collective-permute-start | bytes 294920 | tf_op jit(solution)/shard_map/ppermute | solution.py:543
  681.2 15.2 %collective-permute-start.34 = (bf16[128,768]{1,0:T(8,128)(2,1)S(1)}, bf16[128,768]{1,0:T(8,128)(2,1)S(1)}, u32[]{:S(2)}, u32[]{:S(2)}) collective-permute-start(bf16[128,768]{1,0:T(8,128)(2,1)S(1)} %pad_maximum_fusion.5), channel_id=1, source_target_pairs={{8,0},{9,1},{10,2},{11,3},{12,4},{13,5},{14,6},{15,7},{0,8},{1,9},... | collective-permute-start | bytes 589832 | tf_op jit(solution)/shard_map/ppermute | solution.py:543
  685.3 14.3 %collective-permute-start.43 = (bf16[128,768]{1,0:T(8,128)(2,1)S(1)}, bf16[128,768]{1,0:T(8,128)(2,1)S(1)}, u32[]{:S(2)}, u32[]{:S(2)}) collective-permute-start(bf16[128,768]{1,0:T(8,128)(2,1)S(1)} %pad_maximum_fusion.6), channel_id=1, source_target_pairs={{8,0},{9,1},{10,2},{11,3},{12,4},{13,5},{14,6},{15,7},{0,8},{1,9},... | collective-permute-start | bytes 589832 | tf_op jit(solution)/shard_map/ppermute | solution.py:543
  685.4 22.7 %collective-permute-start.26 = (f32[16384]{0:T(1024)S(1)}, f32[16384]{0:T(1024)S(1)}, u32[]{:S(2)}, u32[]{:S(2)}) collective-permute-start(f32[16384]{0:T(1024)S(1)} %add.402), channel_id=1, source_target_pairs={{0,16},{1,17},{2,18},{3,19},{4,20},{5,21},{6,22},{7,23},{8,24},{9,... | collective-permute-start | bytes 196616 | tf_op jit(solution)/shard_map/ppermute | solution.py:593
  699.8 16.9 %collective-permute-start.35 = (bf16[256,768]{1,0:T(8,128)(2,1)S(1)}, bf16[256,768]{1,0:T(8,128)(2,1)S(1)}, u32[]{:S(2)}, u32[]{:S(2)}) collective-permute-start(bf16[256,768]{1,0:T(8,128)(2,1)S(1)} %pad_maximum_fusion.3), channel_id=1, source_target_pairs={{4,0},{5,1},{6,2},{7,3},{0,4},{1,5},{2,6},{3,7},{12,8},{13,9},{14,... | collective-permute-start | bytes 1179656 | tf_op jit(solution)/shard_map/ppermute | solution.py:543
  700.8 22.3 %collective-permute-start.44 = (bf16[256,768]{1,0:T(8,128)(2,1)S(1)}, bf16[256,768]{1,0:T(8,128)(2,1)S(1)}, u32[]{:S(2)}, u32[]{:S(2)}) collective-permute-start(bf16[256,768]{1,0:T(8,128)(2,1)S(1)} %pad_maximum_fusion.4), channel_id=1, source_target_pairs={{4,0},{5,1},{6,2},{7,3},{0,4},{1,5},{2,6},{3,7},{12,8},{13,9},{14,... | collective-permute-start | bytes 1179656 | tf_op jit(solution)/shard_map/ppermute | solution.py:543
  705.8 94.7 %collective-permute-start.22 = (bf16[1280,1024]{1,0:T(8,128)(2,1)S(1)}, bf16[1280,1024]{1,0:T(8,128)(2,1)}, u32[]{:S(2)}, u32[]{:S(2)}) collective-permute-start(bf16[1280,1024]{1,0:T(8,128)(2,1)S(1)} %fusion.19), channel_id=1, source_target_pairs={{2,1},{1,2},{6,5},{5,6},{10,9},{9,10},{14,13},{13,14},{18,17},{17,... | collective-permute-start | bytes 7864328 | tf_op jit(solution)/shard_map/ppermute | solution.py:524
  708.2 64.0 %collective-permute-start.27 = (f32[16384]{0:T(1024)S(1)}, f32[16384]{0:T(1024)}, u32[]{:S(2)}, u32[]{:S(2)}) collective-permute-start(f32[16384]{0:T(1024)S(1)} %add.403), channel_id=1, source_target_pairs={{0,1},{1,0},{2,3},{3,2},{4,5},{5,4},{6,7},{7,6},{8,9},{9,8},{10,11... | collective-permute-start | bytes 196616 | tf_op jit(solution)/shard_map/ppermute | solution.py:593
  717.7 57.2 %collective-permute-start.36 = (bf16[512,768]{1,0:T(8,128)(2,1)}, bf16[512,768]{1,0:T(8,128)(2,1)}, u32[]{:S(2)}, u32[]{:S(2)}) collective-permute-start(bf16[512,768]{1,0:T(8,128)(2,1)} %pad_maximum_fusion.1), channel_id=1, source_target_pairs={{2,0},{3,1},{0,2},{1,3},{6,4},{7,5},{4,6},{5,7},{10,8},{11,9},{8,1... | collective-permute-start | bytes 2359304 | tf_op jit(solution)/shard_map/ppermute | solution.py:543
  724.9 56.3 %collective-permute-start.45 = (bf16[512,768]{1,0:T(8,128)(2,1)}, bf16[512,768]{1,0:T(8,128)(2,1)}, u32[]{:S(2)}, u32[]{:S(2)}) collective-permute-start(bf16[512,768]{1,0:T(8,128)(2,1)} %pad_maximum_fusion.2), channel_id=1, source_target_pairs={{2,0},{3,1},{0,2},{1,3},{6,4},{7,5},{4,6},{5,7},{10,8},{11,9},{8,1... | collective-permute-start | bytes 2359304 | tf_op jit(solution)/shard_map/ppermute | solution.py:543
  (91 other events, 1727.7 us)
Sparse Core Ops, SparseCore 0:
  421.1 117.2 all-reduce.3
  614.5 149.3 all-reduce.5

commit v5 on v4

--- a/solution.py
+++ b/solution.py
@@ -185,8 +185,7 @@
 def backward_kernel(parts, tab_ref, kseg_ref, qseg_ref, *refs):
     qkv_refs, do_refs = refs[:parts], refs[parts : 2 * parts]
     ot_ref, lse_ref = refs[2 * parts : 2 * parts + 2]
-    out_refs = refs[2 * parts + 2 : 3 * parts + 2]
-    kx, vx, kt, qx, dox, qt, dot, dq, dk, dv = refs[3 * parts + 2 :]
+    *out_refs, kx, vx, kt, qx, dox, qt, dot, dq, dk, dv = refs[-10 - parts :]
     tokens = kt.shape[1]
     width = tokens // parts
     lane = lax.broadcasted_iota(jnp.int32, (BK, 128), 1)
@@ -328,18 +327,23 @@
     )(tables, kseg, seg[None, :], *qkv_parts, *begun)
 
 
-def attend_backward(qkv_parts, turned, grad_ctx, lse, seg, keep, tables, chunk, work):
+def attend_backward(qkv_parts, turned, grad_ctx, lse, seg, keep, tables, chunk, place, begun=()):
     parts, width, tokens, every, pairs, seg_specs, qkv_specs, o_specs, ot_spec, lse_spec = (
         attend_specs(qkv_parts, chunk)
     )
     kseg = jnp.where(keep == 1, seg, -1)[:, None]
+    result = pl.BlockSpec((width, 3 * PAIR), lanes_of(place[0] * pairs, 1))
     return pl.pallas_call(
         functools.partial(backward_kernel, parts),
         grid_spec=pltpu.PrefetchScalarGridSpec(
             num_scalar_prefetch=1,
             grid=(pairs,),
-            in_specs=seg_specs + qkv_specs + o_specs + [ot_spec, lse_spec],
-            out_specs=[pl.BlockSpec((width, 3 * PAIR), lanes_of(0, 1))] * parts,
+            in_specs=seg_specs
+            + qkv_specs
+            + o_specs
+            + [ot_spec, lse_spec]
+            + [pl.BlockSpec(memory_space=pl.ANY)] * len(begun),
+            out_specs=[result] * parts,
             scratch_shapes=[
                 pltpu.VMEM((2, tokens, 128), BF16),
                 pltpu.VMEM((2, tokens, 128), BF16),
@@ -353,13 +357,16 @@
                 pltpu.VMEM((tokens, 128), F32),
             ],
         ),
-        out_shape=[jax.ShapeDtypeStruct((width, pairs * 3 * PAIR), BF16)] * parts,
+        out_shape=[jax.ShapeDtypeStruct((width, place[1] * pairs * 3 * PAIR), BF16)] * parts,
+        input_output_aliases={5 + 2 * parts + n: n for n in range(len(begun))},
         compiler_params=pltpu.CompilerParams(vmem_limit_bytes=48 * 2**20),
         cost_estimate=pl.CostEstimate(
-            flops=work * tokens * tokens * pairs, bytes_accessed=2**10, transcendentals=0
+            flops=(4000 if chunk[0] < chunk[1] - 1 else 0) * tokens * tokens * pairs,
+            bytes_accessed=2**10,
+            transcendentals=0,
         ),
         name="attend_backward",
-    )(tables, kseg, seg[None, :], *qkv_parts, *grad_ctx, turned, lse)
+    )(tables, kseg, seg[None, :], *qkv_parts, *grad_ctx, turned, lse, *begun)
 
 
 def row_block(width):
@@ -552,15 +559,16 @@
             [jnp.where(high, theirs, mine), jnp.where(high, mine, theirs)], 0
         )
 
-    def regroup_first(self, weight, tokens):
+    def regroup_first(self, weight, small, tokens):
         rows = weight.shape[0] // 4
         part = 2 * self.side(0) + self.side(1)
         quarter = lax.dynamic_slice_in_dim(weight, part * rows, rows, 0)
         got = self.send(quarter)
-        tokens = self.regroup(after(tokens, got))
+        small = self.regroup(after(small, got))
+        tokens = self.regroup(after(tokens, got, small))
         for bit in (1, 0):
             got = self.joined(got, self.partner(got, bit, self.moving), bit)
-        return jnp.where(self.stays(), weight, got), tokens
+        return jnp.where(self.stays(), weight, got), small, tokens
 
     def moving(self, pair, core, m):
         return self.at_rank(pair, core, m) != self.device(pair, core, m)
@@ -597,18 +605,22 @@
         order = [(i + turn) % self.dp for i in range(self.dp)]
         return lax.psum(value, "dp", axis_index_groups=[order])
 
-    def weight_sum_by_halves(self, grad):
-        value = self.give_back(grad)
-        bits = [-1, *range(self.pairs.bit_length() - 1)]
+    def halved(self, value, bit):
+        half, high = value.shape[0] // 2, self.side(bit)
+        sent = lax.dynamic_slice_in_dim(value, (1 - high) * half, half, 0)
+        kept = lax.dynamic_slice_in_dim(value, high * half, half, 0)
+        got = self.partner(sent, bit)
+        return (kept.astype(jnp.float32) + got.astype(jnp.float32)).astype(jnp.bfloat16)
+
+    def bits(self):
+        return list(range(self.pairs.bit_length() - 1))
+
+    def sum_rest(self, value, bits):
         for bit in bits:
-            half, high = value.shape[0] // 2, self.side(bit)
-            sent = lax.dynamic_slice_in_dim(value, (1 - high) * half, half, 0)
-            kept = lax.dynamic_slice_in_dim(value, high * half, half, 0)
-            got = self.partner(sent, bit)
-            value = (kept.astype(jnp.float32) + got.astype(jnp.float32)).astype(jnp.bfloat16)
-        for bit in bits[::-1]:
+            value = self.halved(value, bit)
+        for bit in [*self.bits()[::-1], -1]:
             value = self.joined(value, self.partner(value, bit), bit)
-        return value.astype(jnp.float32)
+        return value
 
 
 def for_kernel(shares, rank):
@@ -674,23 +686,20 @@
             row_grid[0].astype(f32),
         ]
     )
-    small = layout.regroup(small)
+    pairs = width // PAIR
+    chunks = 2 if pairs % 2 == 0 else 1
+    w_qkv, small, tokens = layout.regroup_first(w_qkv, small, tokens)
     qv_bias = small[: 2 * width].reshape(2, width)
     up_bias = small[2 * width : 2 * width + units]
     keep = small[2 * width + units : 2 * width + units + group_rows].astype(jnp.int32)
     grid_row = small[2 * width + units + group_rows :].astype(jnp.int32)
-    pairs = width // PAIR
-    chunks = 2 if pairs % 2 == 0 else 1
-    pairs = width // PAIR
-    chunks = 2 if pairs % 2 == 0 else 1
-    w_qkv, tokens = layout.regroup_first(w_qkv, tokens)
     w_qkv = by_pairs(w_qkv, pairs)
     half = units // 2
     w_out_far = layout.send(after(w_out, tokens))
-    w_up_far = layout.send(after(w_up, tokens))
-    w_top_far = layout.send(after(w_down[:half], tokens))
-    w_low_far = layout.send(after(w_down[half:], w_up_far))
-    cotangent = layout.regroup(after(cotangent, w_top_far))
+    w_up_far = layout.send(after(w_up, w_out_far))
+    w_top_far = layout.send(after(w_down[:half], w_up_far))
+    w_low_far = layout.send(after(w_down[half:], w_top_far))
+    cotangent = layout.regroup(after(cotangent, w_low_far))
 
     resid_in = tokens.astype(f32)
     norm1_out, normed1, inv1 = norm_parts(resid_in, ln1_gain, ln1_bias)
@@ -723,6 +732,8 @@
     a3 = layout.gather(norm3_out.astype(bf16))
     begun, shares_f = (), []
     for part, x in enumerate(a3):
+        if part == shares - 1:
+            x, cotangent = lax.optimization_barrier((x, cotangent))
         *begun, share = feed_forward(part, shares, x, w_up, up_bias, w_down, begun)
         shares_f.append(share)
     a3_all, hidden, slope = begun
@@ -756,18 +767,34 @@
     layer_out = layout.give_back(after(layer_out, g_w_out_far))
     grad_ctx, _ = for_kernel(grad_ctx, rank)
     g_w_down = jnp.where(stays, g_w_down, g_w_down_far)
+    g_w_down = layout.halved(g_w_down, -1)
     tables, g_w_down = lax.optimization_barrier((tables, g_w_down))
-    g_w_down = layout.sum_dp(g_w_down, 1).astype(f32)
-    grad_a1, g_w_qkv, sums = [], [], []
+    bits = layout.bits()
+    grad_a1, g_w_qkv, sums, done = [], [], [], []
+    each = pairs // chunks
     for chunk in range(chunks):
-        grad_qkv = attend_backward(
-            qkv, context_turned, grad_ctx, log_total, seg, keep, tables, (chunk, chunks), 4000 * (chunk == 0)
-        )
+        grad_qkv = ()
+        for slot in range(each):
+            pair = chunk * each + slot
+            if pair and bits:
+                g_w_down = layout.halved(g_w_down, bits.pop(0))
+                tables, g_w_down = lax.optimization_barrier((tables, g_w_down))
+            if pair and pair == pairs - 1:
+                tables, g_w_qkv[0] = lax.optimization_barrier((tables, g_w_qkv[0]))
+            grad_qkv = attend_backward(
+                qkv,
+                context_turned,
+                grad_ctx,
+                log_total,
+                seg,
+                keep,
+                tables,
+                (pair, pairs),
+                (slot, each),
+                grad_qkv,
+            )
         grad_qkv = from_kernel(grad_qkv, rank, shares)
-        columns = grad_qkv[0].shape[1]
-        w_part = w_qkv[:, chunk * columns : (chunk + 1) * columns]
-        grad_a1.append([contract_cols(g, w_part) for g in grad_qkv])
-        sums.append(total([jnp.sum(g.astype(f32), 0) for g in grad_qkv]))
+        done.append(grad_qkv)
         g_part = total([contract_rows(x, g) for x, g in zip(a1, grad_qkv)]).astype(bf16)
         if chunk == 0:
             g_w_up_far, g_w_out_far, g_part = lax.optimization_barrier(
@@ -778,12 +805,19 @@
             tables, g_w_up, g_w_out, g_part = lax.optimization_barrier(
                 (tables, g_w_up, g_w_out, g_part)
             )
-            g_w_up = layout.sum_dp(g_w_up, 0).astype(f32)
-            g_w_out = layout.sum_dp(g_w_out, 0).astype(f32)
-        g_w_qkv.append(layout.weight_sum_by_halves(g_part))
+            g_w_up = layout.sum_dp(g_w_up, 0)
+            g_w_out = layout.sum_dp(g_w_out, 0)
+        g_w_qkv.append(layout.halved(layout.give_back(g_part), -1))
+    done = lax.optimization_barrier(done)
+    g_w_down = layout.sum_rest(g_w_down, bits)
+    for chunk, grad_qkv in enumerate(done):
+        columns = grad_qkv[0].shape[1]
+        w_part = w_qkv[:, chunk * columns : (chunk + 1) * columns]
+        grad_a1.append([contract_cols(g, w_part) for g in grad_qkv])
+        sums.append(total([jnp.sum(g.astype(f32), 0) for g in grad_qkv]))
+    g_w_qkv = jnp.concatenate([layout.sum_rest(g, layout.bits()) for g in g_w_qkv], 1).astype(f32)
     g_w_qkv = (
-        jnp.concatenate(g_w_qkv, 1)
-        .reshape(model_dim, pairs, 3, PAIR)
+        g_w_qkv.reshape(model_dim, pairs, 3, PAIR)
         .transpose(0, 2, 1, 3)
         .reshape(model_dim, 3, width)
     )
@@ -820,6 +854,9 @@
     m = lax.axis_index("mp")
     g_qv_bias = lax.dynamic_slice(all_width, (0, m * width), (2, width))
     g_up_bias = lax.dynamic_slice(all_units, (m * units,), (units,))
+    g_w_up, g_w_out, g_w_qkv, grad_input, g_qv_bias = lax.optimization_barrier(
+        (g_w_up, g_w_out, g_w_qkv, grad_input, g_qv_bias)
+    )
     return (
         layer_out,
         grad_input,
@@ -827,15 +864,15 @@
         norm_terms[1],
         g_w_qkv,
         g_qv_bias,
-        g_w_out,
+        g_w_out.astype(f32),
         norm_terms[2],
         norm_terms[3],
         norm_terms[4],
         norm_terms[5],
         norm_terms[6],
-        g_w_up,
+        g_w_up.astype(f32),
         g_up_bias,
-        g_w_down,
+        g_w_down.astype(f32),
         norm_terms[7],
         norm_terms[8],
         norm_terms[9],

time: 820 us -> 819 us (level)
  starting transfers between devices: 181 us -> 192 us
    ppermute x18 -> x26, starting transfers between devices: 19 us -> 73.3 us  [partner(): return lax.ppermute(value, self.axes, moves)]
    ppermute x8, starting transfers between devices: 131 us -> 84.8 us  [to_rank(): return lax.ppermute(value, self.axes, moves)]
    psum x2 -> x1, waiting for transfers between devices: 35.4 us -> 0.01 us  [sum_dp(): return lax.psum(value, 'dp', axis_index_groups=[order])]
    ppermute x5, waiting for transfers between devices: 1.64 us -> 19 us  [sum_all(): lax.ppermute(value, self.axes, [(i, i ^ step) for i in range(devices)])]
    ppermute x18 -> x26, waiting for transfers between devices: 63.3 us -> 77.9 us  [partner(): return lax.ppermute(value, self.axes, moves)]
    dot_general x6, matrix products: 29.8 us -> 21.3 us  [contract_cols(): lax.dot_general(left, right, (((1,), (1,)), ((), ())), preferred_element_...]
    select_n x4 -> x0, local copies, waits for them, and re-layouts: 8.31 us -> none  [the longest x2 4.61 us: joined(): jnp.where(high, mine, theirs)]
    pallas_call x2 -> x4, Pallas kernels: 110 us -> 117 us  [attend_backward(): pl.pallas_call(functools.partial(backward_kernel, parts), grid_spec=pltpu...]
  transfers between devices with their start and end apart: 48 -> 55, of which waited for: 17 -> 17; matrix products, arithmetic and copies ran while one was open for 26% -> 22% of each run, Pallas kernels for 22% -> 25%
where the time goes in v5:
time: 819 us; the launch traced here: 809 us
  Pallas kernels  258 us (32%)
  starting transfers between devices  192 us (23%)
  other arithmetic  106 us (13%)
  waiting for transfers between devices  104 us (13%)
  matrix products  94.2 us (12%)
  local copies, waits for them, and re-layouts  36.7 us (4%)
  between operations  18 us (2%)
    pallas_call x4, Pallas kernels, attend_backward(): pl.pallas_call(functools.partial(backward_kernel, parts), grid_spec=pltpu...  117 us
    ppermute x8, starting transfers between devices, to_rank(): return lax.ppermute(value, self.axes, moves)  84.8 us
    ppermute x26, waiting for transfers between devices, partner(): return lax.ppermute(value, self.axes, moves)  77.9 us
    ppermute x26, starting transfers between devices, partner(): return lax.ppermute(value, self.axes, moves)  73.3 us
    pallas_call x4, Pallas kernels, attend_forward(): pl.pallas_call(functools.partial(forward_kernel, parts), grid_spec=pltpu....  72.4 us
    dot_general x8, matrix products, contract_rows(): lax.dot_general(left, right, (((0,), (0,)), ((), ())), preferred_element_...  54.7 us
    pallas_call x2, Pallas kernels, feed_forward(): pl.pallas_call(functools.partial(feed_kernel, min(units, FEED)), grid=(st...  36.2 us
    pallas_call x2, Pallas kernels, feed_back(): pl.pallas_call(functools.partial(feed_back_kernel, min(units, FEED)), gri...  32.9 us
  transfers between devices with their start and end apart: 55, of which 17 were waited for; matrix products, arithmetic and copies ran while one was open for 22% of the time, Pallas kernels for 25%

profile of v5, /device:TPU:0, one launch (start us, length us, event | category | flops | bytes accessed | tf_op | source)
XLA Modules:
  0.0 809.4 jit_solution(7063333175297576910)
XLA Ops:
  16.9 4.7 fusion.55
  32.8 37.7 %collective-permute-start.8 = (bf16[1280,1024]{1,0:T(8,128)(2,1)}, bf16[1280,1024]{1,0:T(8,128)(2,1)}, u32[]{:S(2)}, u32[]{:S(2)}) collective-permute-start(bf16[1280,1024]{1,0:T(8,128)(2,1)} %fusion.14), channel_id=1, source_target_pairs={{0,2},{2,0},{1,3},{3,1},{4,6},{6,4},{5,7},{7,5},{8,10},{10,8},{9,1... | collective-permute-start | bytes 7864328 | tf_op jit(solution)/shard_map/ppermute | solution.py:581
  77.0 7.1 fusion.2.refs_0_
  87.4 6.3 fusion.3.refs_1_
  93.7 18.1 %attend_forward.4 = (bf16[1280,512]{1,0:T(8,128)(2,1)S(1)}, bf16[1280,512]{1,0:T(8,128)(2,1)S(1)}, bf16[512,2560]{1,0:T(8,128)(2,1)S(1)}, f32[4,2,2560]{2,1,0:T(2,128)S(1)}) custom-call(s32[3,10]{1,0:T(4,128)S(1)} %add_add_fusion.2.tab_ref, s32[2560,1]{1,0:T(8,128)S(1)} %broadcast_in_dim.24.kseg_ref, s32[1,2560]{1,0:T(1,128)S(1)} %fusion.48.qseg_ref, ...), custom_call_target="tpu_custom_call" | custom-call | flops 19660800000 | bytes 8388608 | tf_op jit(solution)/shard_map/attend_forward/pallas_call | solution.py:302
  111.8 18.1 %attend_forward.5 = (bf16[1280,512]{1,0:T(8,128)(2,1)S(1)}, bf16[1280,512]{1,0:T(8,128)(2,1)S(1)}, bf16[512,2560]{1,0:T(8,128)(2,1)S(1)}, f32[4,2,2560]{2,1,0:T(2,128)S(1)}) custom-call(s32[3,10]{1,0:T(4,128)S(1)} %add_add_fusion.2.tab_ref, ...), custom_call_target="tpu_custom_call", output_to_operand_aliasing={{0}: (5, {}), {1}: (6, {}), {2}: (7, {}), {3}: (8, {})} | custom-call | flops 19660800000 | bytes 8388608 | tf_op jit(solution)/shard_map/attend_forward/pallas_call | solution.py:302
  131.8 18.1 %attend_forward.6 = (bf16[1280,512]{1,0:T(8,128)(2,1)S(1)}, bf16[1280,512]{1,0:T(8,128)(2,1)S(1)}, bf16[512,2560]{1,0:T(8,128)(2,1)S(1)}, f32[4,2,2560]{2,1,0:T(2,128)S(1)}) custom-call(s32[3,10]{1,0:T(4,128)S(1)} %add_add_fusion.2.tab_ref, ...), custom_call_target="tpu_custom_call", output_to_operand_aliasing={{0}: (5, {}), {1}: (6, {}), {2}: (7, {}), {3}: (8, {})} | custom-call | flops 19660800000 | bytes 8388608 | tf_op jit(solution)/shard_map/attend_forward/pallas_call | solution.py:302
  150.0 18.1 %attend_forward.7 = (bf16[1280,512]{1,0:T(8,128)(2,1)S(1)}, bf16[1280,512]{1,0:T(8,128)(2,1)S(1)}, bf16[512,2560]{1,0:T(8,128)(2,1)S(1)}, f32[4,2,2560]{2,1,0:T(2,128)S(1)}) custom-call(s32[3,10]{1,0:T(4,128)S(1)} %add_add_fusion.2.tab_ref, ...), custom_call_target="tpu_custom_call", output_to_operand_aliasing={{0}: (5, {}), {1}: (6, {}), {2}: (7, {}), {3}: (8, {})} | custom-call | flops 19660800000 | bytes 8388608 | tf_op jit(solution)/shard_map/attend_forward/pallas_call | solution.py:302
  171.2 18.8 %collective-permute-start.9 = (bf16[1280,1024]{1,0:T(8,128)(2,1)}, bf16[1280,1024]{1,0:T(8,128)(2,1)S(1)}, u32[]{:S(2)}, u32[]{:S(2)}) collective-permute-start(bf16[1280,1024]{1,0:T(8,128)(2,1)} %convolution_convert_fusion.1), channel_id=1, source_target_pairs={{0,2},{2,0},{1,3},{3,1},{4,6},{6,4},{5,7},{7,5},{8,10},{10,8},{9,1... | collective-permute-start | bytes 7864328 | tf_op jit(solution)/shard_map/ppermute | solution.py:581
  205.4 23.5 %collective-permute-start.11 = (bf16[1280,1024]{1,0:T(8,128)(2,1)S(1)}, bf16[1280,1024]{1,0:T(8,128)(2,1)S(1)}, u32[]{:S(2)}, u32[]{:S(2)}) collective-permute-start(bf16[1280,1024]{1,0:T(8,128)(2,1)S(1)} %add_convert_fusion.2.x_ref), channel_id=1, source_target_pairs={{0,2},{2,0},{1,3},{3,1},{4,6},{6,4},{5,7},{7,5},{8,10},{10,8},{9,1... | collective-permute-start | bytes 7864328 | tf_op jit(solution)/shard_map/ppermute | solution.py:581
  228.8 3.7 maximum_select_fusion.down_ref
  232.5 17.7 %feed_forward.2 = (bf16[2560,1024]{1,0:T(8,128)(2,1)}, bf16[2560,2048]{1,0:T(8,128)(2,1)}, bf16[2560,2048]{1,0:T(8,128)(2,1)}, bf16[1280,1024]{1,0:T(8,128)(2,1)S(1)}) custom-call(bf16[1280,1024]{1,0:T(8,128)(2,1)S(1)} %add_convert_fusion.2.x_ref, bf16[1024,2048]{1,0:T(8,128)(2,1)} %broadcast_select_fusion.2.up_ref, f32[1,2048]{1,0:T(1,128)S(1)} %bitcast.68, ...), custom_call_target="tpu_custom_call" | custom-call | flops 16106127360 | bytes 16777216 | tf_op jit(solution)/shard_map/feed_forward/pallas_call | solution.py:412
  252.2 18.6 %feed_forward.3 = (bf16[2560,1024]{1,0:T(8,128)(2,1)}, bf16[2560,2048]{1,0:T(8,128)(2,1)}, bf16[2560,2048]{1,0:T(8,128)(2,1)}, bf16[1280,1024]{1,0:T(8,128)(2,1)S(1)}) custom-call(bf16[1280,1024]{1,0:T(8,128)(2,1)S(1)} %collective-permute-done.11.x_ref, ...), custom_call_target="tpu_custom_call", output_to_operand_aliasing={{0}: (4, {}), {1}: (5, {}), {2}: (6, {})} | custom-call | flops 16106127360 | bytes 16777216 | tf_op jit(solution)/shard_map/feed_forward/pallas_call | solution.py:412
  273.5 4.5 collective-permute-done.13
  280.3 4.2 fusion.26
  284.5 4.8 convert_reduce_fusion.2
  289.7 16.1 %feed_back.2 = (bf16[2560,2048]{1,0:T(8,128)(2,1)}, f32[1,2048]{1,0:T(1,128)S(1)}, bf16[1280,1024]{1,0:T(8,128)(2,1)S(1)}) custom-call(bf16[1280,1024]{1,0:T(8,128)(2,1)S(1)} %get-tuple-element.219.g_ref, bf16[2560,2048]{1,0:T(8,128)(2,1)} %get-tuple-element.133.slope_ref, bf16[2048,1024]{1,0:T(8,128)(2,1)} %maximum_select_fusion.down_ref, ...), custom_call_target="tpu_custom_call" | custom-call | flops 16106127360 | bytes 16777216 | tf_op jit(solution)/shard_map/feed_back/pallas_call | solution.py:474
  305.9 15.2 %fusion.35 = bf16[2048,1024]{1,0:T(8,128)(2,1)} fusion(bf16[2560,2048]{1,0:T(8,128)(2,1)} %get-tuple-element.135, bf16[1280,1024]{1,0:T(8,128)(2,1)S(1)} %collective-permute-done.14.g_ref, bf16[1280,1024]{1,0:T(8,128)(2,1)S(1)} %get-tuple-element.219.g_ref), kind=kOutput, calls=%fused_computation.78 | convolution fusion | flops 10750001152 | bytes 19922944 | tf_op jit(solution)/shard_map/dot_general | solution.py:35
  321.1 16.8 %feed_back.3 = (bf16[2560,2048]{1,0:T(8,128)(2,1)}, f32[1,2048]{1,0:T(1,128)S(1)}, bf16[1280,1024]{1,0:T(8,128)(2,1)}) custom-call(bf16[1280,1024]{1,0:T(8,128)(2,1)S(1)} %collective-permute-done.14.g_ref, bf16[2560,2048]{1,0:T(8,128)(2,1)} %get-tuple-element.133.slope_ref, ...), custom_call_target="tpu_custom_call", output_to_operand_aliasing={{0}: (4, {})} | custom-call | flops 16106127360 | bytes 16777216 | tf_op jit(solution)/shard_map/feed_back/pallas_call | solution.py:474
  343.1 6.7 multiply_reduce_fusion
  349.9 8.2 %multiply_reduce_fusion.1 = (f32[1024]{0:T(1024)}, f32[1280]{0:T(1024)S(1)}, f32[1280]{0:T(1024)S(1)}, f32[1024]{0:T(1024)}, f32[1280,1024]{1,0:T(8,128)S(1)}) fusion(f32[1280,1024]{1,0:T(8,128)} %copy-done.24, f32[1280]{0:T(1024)S(1)} %add_rsqrt_fusion.2, f32[1280]{0:T(1024)S(1)} %broadcast_multiply_fusion.10, f32[1024]{0:T(1024)S(1)} %copy-done.72, ...), kind=kLoop, calls=%fused_computation.43 | loop fusion | flops 27520512 | bytes 23650304 | tf_op jit(solution)/shard_map/reduce_sum | solution.py:834
  363.5 27.9 %collective-permute-start.20 = (bf16[1024,1024]{1,0:T(8,128)(2,1)S(1)}, bf16[1024,1024]{1,0:T(8,128)(2,1)S(1)}, u32[]{:S(2)}, u32[]{:S(2)}) collective-permute-start(bf16[1024,1024]{1,0:T(8,128)(2,1)S(1)} %constant_dynamic-slice_fusion.12), channel_id=1, source_target_pairs={{2,0},{3,1},{0,2},{1,3},{6,4},{7,5},{4,6},{5,7},{10,8},{11,9},{8,1... | collective-permute-start | bytes 6291464 | tf_op jit(solution)/shard_map/ppermute | solution.py:550
  391.4 15.5 %convolution_convert_fusion = bf16[1024,2048]{1,0:T(8,128)(2,1)S(1)} fusion(bf16[2560,1024]{1,0:T(8,128)(2,1)} %get-tuple-element.144, bf16[2560,2048]{1,0:T(8,128)(2,1)} %get-tuple-element.145), kind=kOutput, calls=%fused_computation.77 | convolution fusion | flops 10739515392 | bytes 19922944 | tf_op jit(solution)/shard_map/dot_general | solution.py:35
  419.2 3.3 collective-permute-start.21
  422.5 29.0 %attend_backward.4 = (bf16[1280,768]{1,0:T(8,128)(2,1)S(1)}, bf16[1280,768]{1,0:T(8,128)(2,1)}) custom-call(s32[3,10]{1,0:T(4,128)S(1)} %copy-done.22, s32[2560,1]{1,0:T(8,128)S(1)} %copy-done.1, s32[1,2560]{1,0:T(1,128)S(1)} %copy-done.20, bf16[1280,1536]{1,0:T(8,128)(2,1)} %copy-done.2, bf16[1280,1536]{1,0:T(8,128)(2,1)} %copy-done.3, ...), custom_call_target="tpu_custom_call" | custom-call | flops 26214400000 | bytes 1024 | tf_op jit(solution)/shard_map/attend_backward/pallas_call | solution.py:336
  453.6 29.4 %attend_backward.5 = (bf16[1280,768]{1,0:T(8,128)(2,1)S(1)}, bf16[1280,768]{1,0:T(8,128)(2,1)}) custom-call(s32[3,10]{1,0:T(4,128)S(1)} %copy-done.22, s32[2560,1]{1,0:T(8,128)S(1)} %copy-done.1, s32[1,2560]{1,0:T(1,128)S(1)} %copy-done.20, bf16[1280,1536]{1,0:T(8,128)(2,1)} %copy-done.2, ...), custom_call_target="tpu_custom_call", output_to_operand_aliasing={{0}: (9, {}), {1}: (10, {})} | custom-call | flops 26214400000 | bytes 1024 | tf_op jit(solution)/shard_map/attend_backward/pallas_call | solution.py:336
  483.1 5.4 fusion.60
  488.5 5.3 add_convert_fusion.5
  498.6 14.1 %collective-permute-done.24 = bf16[128,1024]{1,0:T(8,128)(2,1)S(1)} collective-permute-done((bf16[128,1024]{1,0:T(8,128)(2,1)S(1)}, bf16[128,1024]{1,0:T(8,128)(2,1)S(1)}, u32[]{:S(2)}, u32[]{:S(2)}) %collective-permute-start.24) | collective-permute-done | bytes 262176 | tf_op jit(solution)/shard_map/ppermute | solution.py:550
  517.3 4.3 collective-permute-done.50
  525.3 29.2 %attend_backward.6 = (bf16[1280,768]{1,0:T(8,128)(2,1)S(1)}, bf16[1280,768]{1,0:T(8,128)(2,1)}) custom-call(s32[3,10]{1,0:T(4,128)S(1)} %copy-done.22, s32[2560,1]{1,0:T(8,128)S(1)} %copy-done.1, s32[1,2560]{1,0:T(1,128)S(1)} %copy-done.20, bf16[1280,1536]{1,0:T(8,128)(2,1)} %copy-done.2, bf16[1280,1536]{1,0:T(8,128)(2,1)} %copy-done.3, ...), custom_call_target="tpu_custom_call" | custom-call | flops 26214400000 | bytes 1024 | tf_op jit(solution)/shard_map/attend_backward/pallas_call | solution.py:336
  556.5 15.4 %collective-permute-start.26 = (bf16[512,768]{1,0:T(8,128)(2,1)S(1)}, bf16[512,768]{1,0:T(8,128)(2,1)S(1)}, u32[]{:S(2)}, u32[]{:S(2)}) collective-permute-start(bf16[512,768]{1,0:T(8,128)(2,1)S(1)} %constant_dynamic-slice_fusion.8), channel_id=1, source_target_pairs={{2,0},{3,1},{0,2},{1,3},{6,4},{7,5},{4,6},{5,7},{10,8},{11,9},{8,1... | collective-permute-start | bytes 2359304 | tf_op jit(solution)/shard_map/ppermute | solution.py:550
  573.8 19.7 %collective-permute-done.52 = bf16[512,1024]{1,0:T(8,128)(2,1)S(1)} collective-permute-done((bf16[512,1024]{1,0:T(8,128)(2,1)S(1)}, bf16[512,1024]{1,0:T(8,128)(2,1)S(1)}, u32[]{:S(2)}, u32[]{:S(2)}) %collective-permute-start.52) | collective-permute-done | bytes 1048608 | tf_op jit(solution)/shard_map/ppermute | solution.py:550
  599.1 29.3 %attend_backward.7 = (bf16[1280,768]{1,0:T(8,128)(2,1)S(1)}, bf16[1280,768]{1,0:T(8,128)(2,1)}) custom-call(s32[3,10]{1,0:T(4,128)S(1)} %copy-done.22, s32[2560,1]{1,0:T(8,128)S(1)} %copy-done.1, s32[1,2560]{1,0:T(1,128)S(1)} %copy-done.20, bf16[1280,1536]{1,0:T(8,128)(2,1)} %copy-done.2, ...), custom_call_target="tpu_custom_call", output_to_operand_aliasing={{0}: (9, {}), {1}: (10, {})} | custom-call | bytes 1024 | tf_op jit(solution)/shard_map/attend_backward/pallas_call | solution.py:336
  628.4 4.8 fusion.61
  633.1 5.4 add_convert_fusion.4
  642.7 3.7 add_convert_fusion
  647.9 4.6 fusion.42
  653.2 3.5 collective-permute-start.28
  657.4 9.1 %collective-permute-done.28 = bf16[128,768]{1,0:T(8,128)(2,1)S(1)} collective-permute-done((bf16[128,768]{1,0:T(8,128)(2,1)S(1)}, bf16[128,768]{1,0:T(8,128)(2,1)S(1)}, u32[]{:S(2)}, u32[]{:S(2)}) %collective-permute-start.28) | collective-permute-done | bytes 196640 | tf_op jit(solution)/shard_map/ppermute | solution.py:550
  669.6 7.5 collective-permute-done.29
  677.2 9.4 %collective-permute-done.30 = bf16[64,768]{1,0:T(8,128)(2,1)S(1)} collective-permute-done((bf16[64,768]{1,0:T(8,128)(2,1)S(1)}, bf16[64,768]{1,0:T(8,128)(2,1)S(1)}, u32[]{:S(2)}, u32[]{:S(2)}) %collective-permute-start.30) | collective-permute-done | bytes 98336 | tf_op jit(solution)/shard_map/ppermute | solution.py:550
  691.4 7.7 fusion.20
  703.5 4.0 collective-permute-done.37
  743.3 4.5 maximum_convert_fusion
  747.8 18.6 %collective-permute-done.49 = f32[16384]{0:T(1024)S(1)} collective-permute-done((f32[16384]{0:T(1024)S(1)}, f32[16384]{0:T(1024)S(1)}, u32[]{:S(2)}, u32[]{:S(2)}) %collective-permute-start.49) | collective-permute-done | bytes 65568 | tf_op jit(solution)/shard_map/ppermute | solution.py:601
  787.3 6.6 copy.87
  795.5 6.7 convert_element_type.304
  (449 shorter events, 180.7 us)
Async XLA Ops:
  7.2 780.1 %all-reduce.3.cloned.1.call-start = ((), (), s32[]{:S(2)}) async-start(), calls=%async_computation | async-start | bytes 10485760 | tf_op jit(solution)/shard_map/psum | solution.py:606
  13.2 15.5 %collective-permute-start.2 = (bf16[1280,1024]{1,0:T(8,128)(2,1)}, bf16[1280,1024]{1,0:T(8,128)(2,1)}, u32[]{:S(2)}, u32[]{:S(2)}) collective-permute-start(bf16[1280,1024]{1,0:T(8,128)(2,1)} %param.20), channel_id=1, source_target_pairs={{1,2},{2,1},{5,6},{6,5},{9,10},{10,9},{13,14},{14,13},{17,18},{18,... | collective-permute-start | bytes 7864328 | tf_op jit(solution)/shard_map/ppermute | solution.py:531
  15.4 8.4 %collective-permute-start.6 = (bf16[256,3,512]{0,2,1:T(8,128)(2,1)}, bf16[256,3,512]{0,2,1:T(8,128)(2,1)}, u32[]{:S(2)}, u32[]{:S(2)}) collective-permute-start(bf16[256,3,512]{0,2,1:T(8,128)(2,1)} %copy-done.66), channel_id=1, source_target_pairs={{9,1},{10,2},{13,5},{14,6},{1,9},{2,10},{5,13},{6,14},{25,17},{26,... | collective-permute-start | bytes 2359304 | tf_op jit(solution)/shard_map/ppermute | solution.py:550
  26.7 45.4 %collective-permute-start.7 = (bf16[512,3,512]{0,2,1:T(8,128)(2,1)}, bf16[512,3,512]{0,2,1:T(8,128)(2,1)}, u32[]{:S(2)}, u32[]{:S(2)}) collective-permute-start(bf16[512,3,512]{0,2,1:T(8,128)(2,1)} %pad_maximum_fusion.1), channel_id=1, source_target_pairs={{5,1},{6,2},{1,5},{2,6},{13,9},{14,10},{9,13},{10,14},{21,17},{22,... | collective-permute-start | bytes 4718600 | tf_op jit(solution)/shard_map/ppermute | solution.py:550
  32.8 54.5 %collective-permute-start.8 = (bf16[1280,1024]{1,0:T(8,128)(2,1)}, bf16[1280,1024]{1,0:T(8,128)(2,1)}, u32[]{:S(2)}, u32[]{:S(2)}) collective-permute-start(bf16[1280,1024]{1,0:T(8,128)(2,1)} %fusion.14), channel_id=1, source_target_pairs={{0,2},{2,0},{1,3},{3,1},{4,6},{6,4},{5,7},{7,5},{8,10},{10,8},{9,1... | collective-permute-start | bytes 7864328 | tf_op jit(solution)/shard_map/ppermute | solution.py:581
  74.2 9.8 %collective-permute-start.3 = (bf16[512,1024]{1,0:T(8,128)(2,1)S(1)}, bf16[512,1024]{1,0:T(8,128)(2,1)S(1)}, u32[]{:S(2)}, u32[]{:S(2)}) collective-permute-start(bf16[512,1024]{1,0:T(8,128)(2,1)S(1)} %copy-done.59), channel_id=1, source_target_pairs={{1,2},{2,1},{5,6},{6,5},{9,10},{10,9},{13,14},{14,13},{17,18},{18,... | collective-permute-start | bytes 3145736 | tf_op jit(solution)/shard_map/ppermute | solution.py:531
  84.1 45.9 %collective-permute-start.4 = (bf16[1024,2048]{1,0:T(8,128)(2,1)S(1)}, bf16[1024,2048]{1,0:T(8,128)(2,1)}, u32[]{:S(2)}, u32[]{:S(2)}) collective-permute-start(bf16[1024,2048]{1,0:T(8,128)(2,1)S(1)} %copy-done.42), channel_id=1, source_target_pairs={{1,2},{2,1},{5,6},{6,5},{9,10},{10,9},{13,14},{14,13},{17,18},{18,... | collective-permute-start | bytes 12582920 | tf_op jit(solution)/shard_map/ppermute | solution.py:531
  129.9 20.0 %collective-permute-start.5 = (bf16[1024,1024]{1,0:T(8,128)(2,1)S(1)}, bf16[1024,1024]{1,0:T(8,128)(2,1)S(1)}, u32[]{:S(2)}, u32[]{:S(2)}) collective-permute-start(bf16[1024,1024]{1,0:T(8,128)(2,1)S(1)} %copy-done.55), channel_id=1, source_target_pairs={{1,2},{2,1},{5,6},{6,5},{9,10},{10,9},{13,14},{14,13},{17,18},{18,... | collective-permute-start | bytes 6291464 | tf_op jit(solution)/shard_map/ppermute | solution.py:531
  171.2 24.7 %collective-permute-start.9 = (bf16[1280,1024]{1,0:T(8,128)(2,1)}, bf16[1280,1024]{1,0:T(8,128)(2,1)S(1)}, u32[]{:S(2)}, u32[]{:S(2)}) collective-permute-start(bf16[1280,1024]{1,0:T(8,128)(2,1)} %convolution_convert_fusion.1), channel_id=1, source_target_pairs={{0,2},{2,0},{1,3},{3,1},{4,6},{6,4},{5,7},{7,5},{8,10},{10,8},{9,1... | collective-permute-start | bytes 7864328 | tf_op jit(solution)/shard_map/ppermute | solution.py:581
  193.8 56.3 %collective-permute-start.12 = (bf16[1280,1024]{1,0:T(8,128)(2,1)}, bf16[1280,1024]{1,0:T(8,128)(2,1)}, u32[]{:S(2)}, u32[]{:S(2)}) collective-permute-start(bf16[1280,1024]{1,0:T(8,128)(2,1)} %param.39), channel_id=1, source_target_pairs={{1,2},{2,1},{5,6},{6,5},{9,10},{10,9},{13,14},{14,13},{17,18},{18,... | collective-permute-start | bytes 7864328 | tf_op jit(solution)/shard_map/ppermute | solution.py:531
  205.4 46.8 %collective-permute-start.11 = (bf16[1280,1024]{1,0:T(8,128)(2,1)S(1)}, bf16[1280,1024]{1,0:T(8,128)(2,1)S(1)}, u32[]{:S(2)}, u32[]{:S(2)}) collective-permute-start(bf16[1280,1024]{1,0:T(8,128)(2,1)S(1)} %add_convert_fusion.2.x_ref), channel_id=1, source_target_pairs={{0,2},{2,0},{1,3},{3,1},{4,6},{6,4},{5,7},{7,5},{8,10},{10,8},{9,1... | collective-permute-start | bytes 7864328 | tf_op jit(solution)/shard_map/ppermute | solution.py:581
  270.8 7.2 collective-permute-start.13
  289.4 16.5 %collective-permute-start.14 = (bf16[1280,1024]{1,0:T(8,128)(2,1)S(1)}, bf16[1280,1024]{1,0:T(8,128)(2,1)S(1)}, u32[]{:S(2)}, u32[]{:S(2)}) collective-permute-start(bf16[1280,1024]{1,0:T(8,128)(2,1)S(1)} %get-tuple-element.219.g_ref), channel_id=1, source_target_pairs={{0,2},{2,0},{1,3},{3,1},{4,6},{6,4},{5,7},{7,5},{8,10},{10,8},{9,1... | collective-permute-start | bytes 7864328 | tf_op jit(solution)/shard_map/ppermute | solution.py:581
  338.0 22.7 %collective-permute-start.19 = (bf16[2048,1024]{1,0:T(8,128)(2,1)}, bf16[2048,1024]{1,0:T(8,128)(2,1)}, u32[]{:S(2)}, u32[]{:S(2)}) collective-permute-start(bf16[2048,1024]{1,0:T(8,128)(2,1)} %fusion.35), channel_id=1, source_target_pairs={{2,1},{1,2},{6,5},{5,6},{10,9},{9,10},{14,13},{13,14},{18,17},{17,... | collective-permute-start | bytes 12582920 | tf_op jit(solution)/shard_map/ppermute | solution.py:531
  360.5 51.1 %collective-permute-start.16 = (bf16[1280,1024]{1,0:T(8,128)(2,1)S(1)}, bf16[1280,1024]{1,0:T(8,128)(2,1)S(1)}, u32[]{:S(2)}, u32[]{:S(2)}) collective-permute-start(bf16[1280,1024]{1,0:T(8,128)(2,1)S(1)} %get-tuple-element.221), channel_id=1, source_target_pairs={{0,2},{2,0},{1,3},{3,1},{4,6},{6,4},{5,7},{7,5},{8,10},{10,8},{9,1... | collective-permute-start | bytes 7864328 | tf_op jit(solution)/shard_map/ppermute | solution.py:581
  363.5 54.6 %collective-permute-start.20 = (bf16[1024,1024]{1,0:T(8,128)(2,1)S(1)}, bf16[1024,1024]{1,0:T(8,128)(2,1)S(1)}, u32[]{:S(2)}, u32[]{:S(2)}) collective-permute-start(bf16[1024,1024]{1,0:T(8,128)(2,1)S(1)} %constant_dynamic-slice_fusion.12), channel_id=1, source_target_pairs={{2,0},{3,1},{0,2},{1,3},{6,4},{7,5},{4,6},{5,7},{10,8},{11,9},{8,1... | collective-permute-start | bytes 6291464 | tf_op jit(solution)/shard_map/ppermute | solution.py:550
  408.6 85.4 %collective-permute-start.22 = (bf16[1024,2048]{1,0:T(8,128)(2,1)S(1)}, bf16[1024,2048]{1,0:T(8,128)(2,1)}, u32[]{:S(2)}, u32[]{:S(2)}) collective-permute-start(bf16[1024,2048]{1,0:T(8,128)(2,1)S(1)} %convolution_convert_fusion), channel_id=1, source_target_pairs={{2,1},{1,2},{6,5},{5,6},{10,9},{9,10},{14,13},{13,14},{18,17},{17,... | collective-permute-start | bytes 12582920 | tf_op jit(solution)/shard_map/ppermute | solution.py:531
  414.8 79.2 %collective-permute-start.17 = (bf16[512,1024]{1,0:T(8,128)(2,1)S(1)}, bf16[512,1024]{1,0:T(8,128)(2,1)}, u32[]{:S(2)}, u32[]{:S(2)}) collective-permute-start(bf16[512,1024]{1,0:T(8,128)(2,1)S(1)} %add_convert_fusion.7), channel_id=1, source_target_pairs={{2,1},{1,2},{6,5},{5,6},{10,9},{9,10},{14,13},{13,14},{18,17},{17,... | collective-permute-start | bytes 3145736 | tf_op jit(solution)/shard_map/ppermute | solution.py:531
  419.2 32.4 %collective-permute-start.21 = (bf16[512,1024]{1,0:T(8,128)(2,1)S(1)}, bf16[512,1024]{1,0:T(8,128)(2,1)S(1)}, u32[]{:S(2)}, u32[]{:S(2)}) collective-permute-start(bf16[512,1024]{1,0:T(8,128)(2,1)S(1)} %constant_dynamic-slice_fusion.11), channel_id=1, source_target_pairs={{4,0},{5,1},{6,2},{7,3},{0,4},{1,5},{2,6},{3,7},{12,8},{13,9},{14,... | collective-permute-start | bytes 3145736 | tf_op jit(solution)/shard_map/ppermute | solution.py:550
  452.0 41.7 %collective-permute-start.23 = (bf16[256,1024]{1,0:T(8,128)(2,1)S(1)}, bf16[256,1024]{1,0:T(8,128)(2,1)S(1)}, u32[]{:S(2)}, u32[]{:S(2)}) collective-permute-start(bf16[256,1024]{1,0:T(8,128)(2,1)S(1)} %constant_dynamic-slice_fusion.10), channel_id=1, source_target_pairs={{8,0},{9,1},{10,2},{11,3},{12,4},{13,5},{14,6},{15,7},{0,8},{1,9},... | collective-permute-start | bytes 1572872 | tf_op jit(solution)/shard_map/ppermute | solution.py:550
  497.5 15.2 %collective-permute-start.24 = (bf16[128,1024]{1,0:T(8,128)(2,1)S(1)}, bf16[128,1024]{1,0:T(8,128)(2,1)S(1)}, u32[]{:S(2)}, u32[]{:S(2)}) collective-permute-start(bf16[128,1024]{1,0:T(8,128)(2,1)S(1)} %constant_dynamic-slice_fusion.9), channel_id=1, source_target_pairs={{16,0},{17,1},{18,2},{19,3},{20,4},{21,5},{22,6},{23,7},{24,8},{25... | collective-permute-start | bytes 786440 | tf_op jit(solution)/shard_map/ppermute | solution.py:550
  512.8 8.8 %collective-permute-start.50 = (bf16[128,1024]{1,0:T(8,128)(2,1)S(1)}, bf16[128,1024]{1,0:T(8,128)(2,1)S(1)}, u32[]{:S(2)}, u32[]{:S(2)}) collective-permute-start(bf16[128,1024]{1,0:T(8,128)(2,1)S(1)} %add_convert_fusion.13), channel_id=1, source_target_pairs={{16,0},{17,1},{18,2},{19,3},{20,4},{21,5},{22,6},{23,7},{24,8},{25... | collective-permute-start | bytes 786440 | tf_op jit(solution)/shard_map/ppermute | solution.py:550
  513.3 58.7 %collective-permute-start.18 = (bf16[1280,1024]{1,0:T(8,128)(2,1)}, bf16[1280,1024]{1,0:T(8,128)(2,1)}, u32[]{:S(2)}, u32[]{:S(2)}) collective-permute-start(bf16[1280,1024]{1,0:T(8,128)(2,1)} %get-tuple-element.139), channel_id=1, source_target_pairs={{2,1},{1,2},{6,5},{5,6},{10,9},{9,10},{14,13},{13,14},{18,17},{17,... | collective-permute-start | bytes 7864328 | tf_op jit(solution)/shard_map/ppermute | solution.py:531
  515.4 40.8 %collective-permute-start.25 = (bf16[1024,768]{1,0:T(8,128)(2,1)}, bf16[1024,768]{1,0:T(8,128)(2,1)}, u32[]{:S(2)}, u32[]{:S(2)}) collective-permute-start(bf16[1024,768]{1,0:T(8,128)(2,1)} %add_convert_fusion.5), channel_id=1, source_target_pairs={{2,1},{1,2},{6,5},{5,6},{10,9},{9,10},{14,13},{13,14},{18,17},{17,... | collective-permute-start | bytes 4718600 | tf_op jit(solution)/shard_map/ppermute | solution.py:531
  522.7 31.9 %collective-permute-start.51 = (bf16[256,1024]{1,0:T(8,128)(2,1)}, bf16[256,1024]{1,0:T(8,128)(2,1)}, u32[]{:S(2)}, u32[]{:S(2)}) collective-permute-start(bf16[256,1024]{1,0:T(8,128)(2,1)} %pad_maximum_fusion.7), channel_id=1, source_target_pairs={{8,0},{9,1},{10,2},{11,3},{12,4},{13,5},{14,6},{15,7},{0,8},{1,9},... | collective-permute-start | bytes 1572872 | tf_op jit(solution)/shard_map/ppermute | solution.py:550
  556.2 37.3 %collective-permute-start.52 = (bf16[512,1024]{1,0:T(8,128)(2,1)S(1)}, bf16[512,1024]{1,0:T(8,128)(2,1)S(1)}, u32[]{:S(2)}, u32[]{:S(2)}) collective-permute-start(bf16[512,1024]{1,0:T(8,128)(2,1)S(1)} %pad_maximum_fusion.4), channel_id=1, source_target_pairs={{4,0},{5,1},{6,2},{7,3},{0,4},{1,5},{2,6},{3,7},{12,8},{13,9},{14,... | collective-permute-start | bytes 3145736 | tf_op jit(solution)/shard_map/ppermute | solution.py:550
  556.5 42.3 %collective-permute-start.26 = (bf16[512,768]{1,0:T(8,128)(2,1)S(1)}, bf16[512,768]{1,0:T(8,128)(2,1)S(1)}, u32[]{:S(2)}, u32[]{:S(2)}) collective-permute-start(bf16[512,768]{1,0:T(8,128)(2,1)S(1)} %constant_dynamic-slice_fusion.8), channel_id=1, source_target_pairs={{2,0},{3,1},{0,2},{1,3},{6,4},{7,5},{4,6},{5,7},{10,8},{11,9},{8,1... | collective-permute-start | bytes 2359304 | tf_op jit(solution)/shard_map/ppermute | solution.py:550
  595.6 119.3 %collective-permute-start.53 = (bf16[1024,1024]{1,0:T(8,128)(2,1)}, bf16[1024,1024]{1,0:T(8,128)(2,1)}, u32[]{:S(2)}, u32[]{:S(2)}) collective-permute-start(bf16[1024,1024]{1,0:T(8,128)(2,1)} %pad_maximum_fusion), channel_id=1, source_target_pairs={{2,0},{3,1},{0,2},{1,3},{6,4},{7,5},{4,6},{5,7},{10,8},{11,9},{8,1... | collective-permute-start | bytes 6291464 | tf_op jit(solution)/shard_map/ppermute | solution.py:550
  638.5 28.8 %collective-permute-start.34 = (bf16[1024,768]{1,0:T(8,128)(2,1)}, bf16[1024,768]{1,0:T(8,128)(2,1)}, u32[]{:S(2)}, u32[]{:S(2)}) collective-permute-start(bf16[1024,768]{1,0:T(8,128)(2,1)} %add_convert_fusion.4), channel_id=1, source_target_pairs={{2,1},{1,2},{6,5},{5,6},{10,9},{9,10},{14,13},{13,14},{18,17},{17,... | collective-permute-start | bytes 4718600 | tf_op jit(solution)/shard_map/ppermute | solution.py:531
  640.4 12.7 %collective-permute-start.27 = (bf16[256,768]{1,0:T(8,128)(2,1)S(1)}, bf16[256,768]{1,0:T(8,128)(2,1)S(1)}, u32[]{:S(2)}, u32[]{:S(2)}) collective-permute-start(bf16[256,768]{1,0:T(8,128)(2,1)S(1)} %constant_dynamic-slice_fusion.7), channel_id=1, source_target_pairs={{4,0},{5,1},{6,2},{7,3},{0,4},{1,5},{2,6},{3,7},{12,8},{13,9},{14,... | collective-permute-start | bytes 1179656 | tf_op jit(solution)/shard_map/ppermute | solution.py:550
  646.4 44.9 %collective-permute-start.43 = (bf16[1280,1024]{1,0:T(8,128)(2,1)}, bf16[1280,1024]{1,0:T(8,128)(2,1)}, u32[]{:S(2)}, u32[]{:S(2)}) collective-permute-start(bf16[1280,1024]{1,0:T(8,128)(2,1)} %add_convert_fusion), channel_id=1, source_target_pairs={{0,2},{2,0},{1,3},{3,1},{4,6},{6,4},{5,7},{7,5},{8,10},{10,8},{9,1... | collective-permute-start | bytes 7864328 | tf_op jit(solution)/shard_map/ppermute | solution.py:581
  653.2 13.2 %collective-permute-start.28 = (bf16[128,768]{1,0:T(8,128)(2,1)S(1)}, bf16[128,768]{1,0:T(8,128)(2,1)S(1)}, u32[]{:S(2)}, u32[]{:S(2)}) collective-permute-start(bf16[128,768]{1,0:T(8,128)(2,1)S(1)} %constant_dynamic-slice_fusion.6), channel_id=1, source_target_pairs={{8,0},{9,1},{10,2},{11,3},{12,4},{13,5},{14,6},{15,7},{0,8},{1,9},... | collective-permute-start | bytes 589832 | tf_op jit(solution)/shard_map/ppermute | solution.py:550
  666.5 10.5 %collective-permute-start.29 = (bf16[64,768]{1,0:T(8,128)(2,1)S(1)}, bf16[64,768]{1,0:T(8,128)(2,1)S(1)}, u32[]{:S(2)}, u32[]{:S(2)}) collective-permute-start(bf16[64,768]{1,0:T(8,128)(2,1)S(1)} %constant_dynamic-slice_fusion.5), channel_id=1, source_target_pairs={{16,0},{17,1},{18,2},{19,3},{20,4},{21,5},{22,6},{23,7},{24,8},{25... | collective-permute-start | bytes 294920 | tf_op jit(solution)/shard_map/ppermute | solution.py:550
  669.5 17.9 %collective-permute-start.35 = (bf16[512,768]{1,0:T(8,128)(2,1)S(1)}, bf16[512,768]{1,0:T(8,128)(2,1)S(1)}, u32[]{:S(2)}, u32[]{:S(2)}) collective-permute-start(bf16[512,768]{1,0:T(8,128)(2,1)S(1)} %constant_dynamic-slice_fusion.4), channel_id=1, source_target_pairs={{2,0},{3,1},{0,2},{1,3},{6,4},{7,5},{4,6},{5,7},{10,8},{11,9},{8,1... | collective-permute-start | bytes 2359304 | tf_op jit(solution)/shard_map/ppermute | solution.py:550
  677.1 9.5 %collective-permute-start.30 = (bf16[64,768]{1,0:T(8,128)(2,1)S(1)}, bf16[64,768]{1,0:T(8,128)(2,1)S(1)}, u32[]{:S(2)}, u32[]{:S(2)}) collective-permute-start(bf16[64,768]{1,0:T(8,128)(2,1)S(1)} %add_convert_fusion.17), channel_id=1, source_target_pairs={{16,0},{17,1},{18,2},{19,3},{20,4},{21,5},{22,6},{23,7},{24,8},{25... | collective-permute-start | bytes 294920 | tf_op jit(solution)/shard_map/ppermute | solution.py:550
  687.4 37.2 %collective-permute-start.31 = (bf16[128,768]{1,0:T(8,128)(2,1)}, bf16[128,768]{1,0:T(8,128)(2,1)}, u32[]{:S(2)}, u32[]{:S(2)}) collective-permute-start(bf16[128,768]{1,0:T(8,128)(2,1)} %pad_maximum_fusion.10), channel_id=1, source_target_pairs={{8,0},{9,1},{10,2},{11,3},{12,4},{13,5},{14,6},{15,7},{0,8},{1,9},... | collective-permute-start | bytes 589832 | tf_op jit(solution)/shard_map/ppermute | solution.py:550
  689.3 11.2 %collective-permute-start.36 = (bf16[256,768]{1,0:T(8,128)(2,1)}, bf16[256,768]{1,0:T(8,128)(2,1)}, u32[]{:S(2)}, u32[]{:S(2)}) collective-permute-start(bf16[256,768]{1,0:T(8,128)(2,1)} %constant_dynamic-slice_fusion.3), channel_id=1, source_target_pairs={{4,0},{5,1},{6,2},{7,3},{0,4},{1,5},{2,6},{3,7},{12,8},{13,9},{14,... | collective-permute-start | bytes 1179656 | tf_op jit(solution)/shard_map/ppermute | solution.py:550
  701.7 5.8 collective-permute-start.37
  703.5 5.7 collective-permute-start.45
  709.2 8.5 %collective-permute-start.46 = (f32[16384]{0:T(1024)S(1)}, f32[16384]{0:T(1024)S(1)}, u32[]{:S(2)}, u32[]{:S(2)}) collective-permute-start(f32[16384]{0:T(1024)S(1)} %fusion.52), channel_id=1, source_target_pairs={{0,4},{1,5},{2,6},{3,7},{4,0},{5,1},{6,2},{7,3},{8,12},{9,13},{10,... | collective-permute-start | bytes 196616 | tf_op jit(solution)/shard_map/ppermute | solution.py:601
  719.0 6.5 collective-permute-start.40
  722.2 11.3 %collective-permute-start.48 = (f32[16384]{0:T(1024)S(1)}, f32[16384]{0:T(1024)S(1)}, u32[]{:S(2)}, u32[]{:S(2)}) collective-permute-start(f32[16384]{0:T(1024)S(1)} %add.473), channel_id=1, source_target_pairs={{0,16},{1,17},{2,18},{3,19},{4,20},{5,21},{6,22},{7,23},{8,24},{9,... | collective-permute-start | bytes 196616 | tf_op jit(solution)/shard_map/ppermute | solution.py:601
  726.6 11.4 %collective-permute-start.41 = (bf16[256,768]{1,0:T(8,128)(2,1)S(1)}, bf16[256,768]{1,0:T(8,128)(2,1)S(1)}, u32[]{:S(2)}, u32[]{:S(2)}) collective-permute-start(bf16[256,768]{1,0:T(8,128)(2,1)S(1)} %pad_maximum_fusion.9), channel_id=1, source_target_pairs={{4,0},{5,1},{6,2},{7,3},{0,4},{1,5},{2,6},{3,7},{12,8},{13,9},{14,... | collective-permute-start | bytes 1179656 | tf_op jit(solution)/shard_map/ppermute | solution.py:550
  729.2 13.1 %collective-permute-start.32 = (bf16[256,768]{1,0:T(8,128)(2,1)S(1)}, bf16[256,768]{1,0:T(8,128)(2,1)S(1)}, u32[]{:S(2)}, u32[]{:S(2)}) collective-permute-start(bf16[256,768]{1,0:T(8,128)(2,1)S(1)} %pad_maximum_fusion.8), channel_id=1, source_target_pairs={{4,0},{5,1},{6,2},{7,3},{0,4},{1,5},{2,6},{3,7},{12,8},{13,9},{14,... | collective-permute-start | bytes 1179656 | tf_op jit(solution)/shard_map/ppermute | solution.py:550
  731.3 53.3 %collective-permute-start.44 = (bf16[1280,1024]{1,0:T(8,128)(2,1)S(1)}, bf16[1280,1024]{1,0:T(8,128)(2,1)}, u32[]{:S(2)}, u32[]{:S(2)}) collective-permute-start(bf16[1280,1024]{1,0:T(8,128)(2,1)S(1)} %fusion.19), channel_id=1, source_target_pairs={{2,1},{1,2},{6,5},{5,6},{10,9},{9,10},{14,13},{13,14},{18,17},{17,... | collective-permute-start | bytes 7864328 | tf_op jit(solution)/shard_map/ppermute | solution.py:531
  733.5 32.9 %collective-permute-start.49 = (f32[16384]{0:T(1024)S(1)}, f32[16384]{0:T(1024)S(1)}, u32[]{:S(2)}, u32[]{:S(2)}) collective-permute-start(f32[16384]{0:T(1024)S(1)} %add.474), channel_id=1, source_target_pairs={{0,1},{1,0},{2,3},{3,2},{4,5},{5,4},{6,7},{7,6},{8,9},{9,8},{10,11... | collective-permute-start | bytes 196616 | tf_op jit(solution)/shard_map/ppermute | solution.py:601
  739.2 29.1 %collective-permute-start.42 = (bf16[512,768]{1,0:T(8,128)(2,1)}, bf16[512,768]{1,0:T(8,128)(2,1)}, u32[]{:S(2)}, u32[]{:S(2)}) collective-permute-start(bf16[512,768]{1,0:T(8,128)(2,1)} %pad_maximum_fusion.6), channel_id=1, source_target_pairs={{2,0},{3,1},{0,2},{1,3},{6,4},{7,5},{4,6},{5,7},{10,8},{11,9},{8,1... | collective-permute-start | bytes 2359304 | tf_op jit(solution)/shard_map/ppermute | solution.py:550
  743.3 30.4 %collective-permute-start.33 = (bf16[512,768]{1,0:T(8,128)(2,1)}, bf16[512,768]{1,0:T(8,128)(2,1)}, u32[]{:S(2)}, u32[]{:S(2)}) collective-permute-start(bf16[512,768]{1,0:T(8,128)(2,1)} %pad_maximum_fusion.5), channel_id=1, source_target_pairs={{2,0},{3,1},{0,2},{1,3},{6,4},{7,5},{4,6},{5,7},{10,8},{11,9},{8,1... | collective-permute-start | bytes 2359304 | tf_op jit(solution)/shard_map/ppermute | solution.py:550
  (108 other events, 1424.5 us)
Sparse Core Ops, SparseCore 0:
  554.6 145.7 all-reduce.2

commit v6 on v5

--- a/solution.py
+++ b/solution.py
@@ -361,7 +361,7 @@
         input_output_aliases={5 + 2 * parts + n: n for n in range(len(begun))},
         compiler_params=pltpu.CompilerParams(vmem_limit_bytes=48 * 2**20),
         cost_estimate=pl.CostEstimate(
-            flops=(4000 if chunk[0] < chunk[1] - 1 else 0) * tokens * tokens * pairs,
+            flops=2**10,
             bytes_accessed=2**10,
             transcendentals=0,
         ),
@@ -494,7 +494,7 @@
         input_output_aliases={4 + n: n for n in range(len(begun))},
         compiler_params=pltpu.CompilerParams(vmem_limit_bytes=48 * 2**20),
         cost_estimate=pl.CostEstimate(
-            flops=6 * width * model * units, bytes_accessed=2**24, transcendentals=0
+            flops=2**10, bytes_accessed=2**10, transcendentals=0
         ),
         name="feed_back",
     )(g, slope_all, down, up, *begun)
@@ -615,10 +615,10 @@
     def bits(self):
         return list(range(self.pairs.bit_length() - 1))
 
-    def sum_rest(self, value, bits):
-        for bit in bits:
+    def sum_rest(self, value):
+        for bit in self.bits():
             value = self.halved(value, bit)
-        for bit in [*self.bits()[::-1], -1]:
+        for bit in self.bits()[::-1]:
             value = self.joined(value, self.partner(value, bit), bit)
         return value
 
@@ -720,6 +720,7 @@
             tables, w_top_far = lax.optimization_barrier((tables, w_top_far))
         begun = attend_forward(qkv, seg, keep, tables, (pair, pairs), begun)
     *context, context_turned, log_total = begun
+    *context, w_low_far = lax.optimization_barrier((*context, w_low_far))
     context = from_kernel(context, rank, shares)
     stays = layout.stays()
     w_out = jnp.where(stays, w_out, w_out_far)
@@ -763,24 +764,18 @@
     grad_z_all = layout.gather(grad_z)
     grad_ctx = [contract_cols(g, w_out).astype(bf16) for g in grad_z_all]
     g_w_out = total([contract_rows(x, g) for x, g in zip(context, grad_z_all)]).astype(bf16)
-    g_w_out_far = layout.send(g_w_out, True)
-    layer_out = layout.give_back(after(layer_out, g_w_out_far))
+    g_w_out_far = layout.send(after(g_w_out, g_w_up_far), True)
+    g_w_down_far, g_w_up, *grad_ctx = lax.optimization_barrier((g_w_down_far, g_w_up, *grad_ctx))
     grad_ctx, _ = for_kernel(grad_ctx, rank)
     g_w_down = jnp.where(stays, g_w_down, g_w_down_far)
-    g_w_down = layout.halved(g_w_down, -1)
     tables, g_w_down = lax.optimization_barrier((tables, g_w_down))
-    bits = layout.bits()
+    g_w_down = layout.sum_dp(g_w_down, 1)
     grad_a1, g_w_qkv, sums, done = [], [], [], []
     each = pairs // chunks
     for chunk in range(chunks):
+        calls = 1 if chunk == 0 else each
         grad_qkv = ()
-        for slot in range(each):
-            pair = chunk * each + slot
-            if pair and bits:
-                g_w_down = layout.halved(g_w_down, bits.pop(0))
-                tables, g_w_down = lax.optimization_barrier((tables, g_w_down))
-            if pair and pair == pairs - 1:
-                tables, g_w_qkv[0] = lax.optimization_barrier((tables, g_w_qkv[0]))
+        for call in range(calls):
             grad_qkv = attend_backward(
                 qkv,
                 context_turned,
@@ -789,10 +784,14 @@
                 seg,
                 keep,
                 tables,
-                (pair, pairs),
-                (slot, each),
+                (chunk * calls + call, chunks * calls),
+                (call, calls),
                 grad_qkv,
             )
+            if chunk and call < calls - 1:
+                tables, g_w_qkv[0], *grad_qkv = lax.optimization_barrier(
+                    (tables, g_w_qkv[0], *grad_qkv)
+                )
         grad_qkv = from_kernel(grad_qkv, rank, shares)
         done.append(grad_qkv)
         g_part = total([contract_rows(x, g) for x, g in zip(a1, grad_qkv)]).astype(bf16)
@@ -802,20 +801,23 @@
             )
             g_w_up = jnp.where(stays, g_w_up, g_w_up_far)
             g_w_out = jnp.where(stays, g_w_out, g_w_out_far)
-            tables, g_w_up, g_w_out, g_part = lax.optimization_barrier(
-                (tables, g_w_up, g_w_out, g_part)
+            tables, g_w_down, g_w_up, g_w_out, g_part = lax.optimization_barrier(
+                (tables, g_w_down, g_w_up, g_w_out, g_part)
             )
             g_w_up = layout.sum_dp(g_w_up, 0)
             g_w_out = layout.sum_dp(g_w_out, 0)
         g_w_qkv.append(layout.halved(layout.give_back(g_part), -1))
+    layer_out = layout.give_back(after(layer_out, g_w_qkv[0]))
     done = lax.optimization_barrier(done)
-    g_w_down = layout.sum_rest(g_w_down, bits)
     for chunk, grad_qkv in enumerate(done):
         columns = grad_qkv[0].shape[1]
         w_part = w_qkv[:, chunk * columns : (chunk + 1) * columns]
         grad_a1.append([contract_cols(g, w_part) for g in grad_qkv])
         sums.append(total([jnp.sum(g.astype(f32), 0) for g in grad_qkv]))
-    g_w_qkv = jnp.concatenate([layout.sum_rest(g, layout.bits()) for g in g_w_qkv], 1).astype(f32)
+    g_w_qkv = [layout.sum_rest(g) for g in g_w_qkv]
+    g_w_up, g_w_out, *g_w_qkv = lax.optimization_barrier((g_w_up, g_w_out, *g_w_qkv))
+    g_w_qkv = [layout.joined(g, layout.partner(g, -1), -1) for g in g_w_qkv]
+    g_w_qkv = jnp.concatenate(g_w_qkv, 1).astype(f32)
     g_w_qkv = (
         g_w_qkv.reshape(model_dim, pairs, 3, PAIR)
         .transpose(0, 2, 1, 3)
@@ -854,9 +856,6 @@
     m = lax.axis_index("mp")
     g_qv_bias = lax.dynamic_slice(all_width, (0, m * width), (2, width))
     g_up_bias = lax.dynamic_slice(all_units, (m * units,), (units,))
-    g_w_up, g_w_out, g_w_qkv, grad_input, g_qv_bias = lax.optimization_barrier(
-        (g_w_up, g_w_out, g_w_qkv, grad_input, g_qv_bias)
-    )
     return (
         layer_out,
         grad_input,

time: 819 us -> 821 us (level)
  Pallas kernels: 258 us -> 162 us
  waiting for transfers between devices: 104 us -> 193 us
  starting transfers between devices: 192 us -> 204 us
  local copies, waits for them, and re-layouts: 36.7 us -> 46.3 us
    psum x1 -> x2, waiting for transfers between devices: 0.01 us -> 98.4 us  [sum_dp(): return lax.psum(value, 'dp', axis_index_groups=[order])]
    pallas_call x4 -> x3, Pallas kernels: 117 us -> 56.2 us  [attend_backward(): pl.pallas_call(functools.partial(backward_kernel, parts), grid_spec=pltpu...]
    pallas_call x4, Pallas kernels: 72.4 us -> 38.4 us  [attend_forward(): pl.pallas_call(functools.partial(forward_kernel, parts), grid_spec=pltpu....]
    ppermute x8, starting transfers between devices: 84.8 us -> 99.6 us  [to_rank(): return lax.ppermute(value, self.axes, moves)]
    ppermute x26 -> x18, waiting for transfers between devices: 77.9 us -> 64.9 us  [partner(): return lax.ppermute(value, self.axes, moves)]
    ppermute x26 -> x18, starting transfers between devices: 73.3 us -> 62.4 us  [partner(): return lax.ppermute(value, self.axes, moves)]
    ppermute x15, starting transfers between devices: 26.9 us -> 36.9 us  [send(): lax.ppermute(value, self.axes, [(b, a) if back else (a, b) for a, b in mo...]
    unnamed x206 -> x172, local copies, waits for them, and re-layouts: 18.2 us -> 25.8 us
  transfers between devices with their start and end apart: 55 -> 48, of which waited for: 17 -> 17; matrix products, arithmetic and copies ran while one was open for 22% -> 23% of each run, Pallas kernels for 25% -> 16%
where the time goes in v6:
time: 821 us; the launch traced here: 816 us
  starting transfers between devices  204 us (25%)
  waiting for transfers between devices  193 us (24%)
  Pallas kernels  162 us (20%)
  other arithmetic  98.9 us (12%)
  matrix products  94.5 us (12%)
  local copies, waits for them, and re-layouts  46.3 us (6%)
  between operations  17.3 us (2%)
    ppermute x8, starting transfers between devices, to_rank(): return lax.ppermute(value, self.axes, moves)  99.6 us
    psum x2, waiting for transfers between devices, sum_dp(): return lax.psum(value, 'dp', axis_index_groups=[order])  98.4 us
    ppermute x18, waiting for transfers between devices, partner(): return lax.ppermute(value, self.axes, moves)  64.9 us
    ppermute x18, starting transfers between devices, partner(): return lax.ppermute(value, self.axes, moves)  62.4 us
    pallas_call x3, Pallas kernels, attend_backward(): pl.pallas_call(functools.partial(backward_kernel, parts), grid_spec=pltpu...  56.2 us
    dot_general x8, matrix products, contract_rows(): lax.dot_general(left, right, (((0,), (0,)), ((), ())), preferred_element_...  53.3 us
    pallas_call x4, Pallas kernels, attend_forward(): pl.pallas_call(functools.partial(forward_kernel, parts), grid_spec=pltpu....  38.4 us
    ppermute x15, starting transfers between devices, send(): lax.ppermute(value, self.axes, [(b, a) if back else (a, b) for a, b in mo...  36.9 us
  transfers between devices with their start and end apart: 48, of which 17 were waited for; matrix products, arithmetic and copies ran while one was open for 23% of the time, Pallas kernels for 16%

profile of v6, /device:TPU:0, one launch (start us, length us, event | category | flops | bytes accessed | tf_op | source)
XLA Modules:
  0.0 816.3 jit_solution(12212441937017501193)
XLA Ops:
  16.8 4.7 fusion.55
  32.8 37.7 %collective-permute-start.8 = (bf16[1280,1024]{1,0:T(8,128)(2,1)}, bf16[1280,1024]{1,0:T(8,128)(2,1)}, u32[]{:S(2)}, u32[]{:S(2)}) collective-permute-start(bf16[1280,1024]{1,0:T(8,128)(2,1)} %fusion.14), channel_id=1, source_target_pairs={{0,2},{2,0},{1,3},{3,1},{4,6},{6,4},{5,7},{7,5},{8,10},{10,8},{9,1... | collective-permute-start | bytes 7864328 | tf_op jit(solution)/shard_map/ppermute | solution.py:581
  83.2 7.1 fusion.2.refs_0_
  90.4 7.8 fusion.3.refs_1_
  98.2 9.6 %attend_forward.4 = (bf16[1280,512]{1,0:T(8,128)(2,1)S(1)}, bf16[1280,512]{1,0:T(8,128)(2,1)S(1)}, bf16[512,2560]{1,0:T(8,128)(2,1)S(1)}, f32[4,2,2560]{2,1,0:T(2,128)S(1)}) custom-call(s32[3,10]{1,0:T(4,128)S(1)} %add_add_fusion.2.tab_ref, s32[2560,1]{1,0:T(8,128)S(1)} %copy-done.3, s32[1,2560]{1,0:T(1,128)S(1)} %fusion.48.qseg_ref, ...), custom_call_target="tpu_custom_call" | custom-call | flops 19660800000 | bytes 8388608 | tf_op jit(solution)/shard_map/attend_forward/pallas_call | solution.py:302
  108.6 9.6 %attend_forward.5 = (bf16[1280,512]{1,0:T(8,128)(2,1)S(1)}, bf16[1280,512]{1,0:T(8,128)(2,1)S(1)}, bf16[512,2560]{1,0:T(8,128)(2,1)S(1)}, f32[4,2,2560]{2,1,0:T(2,128)S(1)}) custom-call(s32[3,10]{1,0:T(4,128)S(1)} %add_add_fusion.2.tab_ref, s32[2560,1]{1,0:T(8,128)S(1)} %copy-done.3, ...), custom_call_target="tpu_custom_call", output_to_operand_aliasing={{0}: (5, {}), {1}: (6, {}), {2}: (7, {}), {3}: (8, {})} | custom-call | flops 19660800000 | bytes 8388608 | tf_op jit(solution)/shard_map/attend_forward/pallas_call | solution.py:302
  118.2 9.6 %attend_forward.6 = (bf16[1280,512]{1,0:T(8,128)(2,1)S(1)}, bf16[1280,512]{1,0:T(8,128)(2,1)S(1)}, bf16[512,2560]{1,0:T(8,128)(2,1)S(1)}, f32[4,2,2560]{2,1,0:T(2,128)S(1)}) custom-call(s32[3,10]{1,0:T(4,128)S(1)} %add_add_fusion.2.tab_ref, s32[2560,1]{1,0:T(8,128)S(1)} %copy-done.3, ...), custom_call_target="tpu_custom_call", output_to_operand_aliasing={{0}: (5, {}), {1}: (6, {}), {2}: (7, {}), {3}: (8, {})} | custom-call | flops 19660800000 | bytes 8388608 | tf_op jit(solution)/shard_map/attend_forward/pallas_call | solution.py:302
  127.8 12.8 %collective-permute-start.9 = (bf16[1024,1024]{1,0:T(8,128)(2,1)}, bf16[1024,1024]{1,0:T(8,128)(2,1)}, u32[]{:S(2)}, u32[]{:S(2)}) collective-permute-start(bf16[1024,1024]{1,0:T(8,128)(2,1)} %get-tuple-element.123), channel_id=1, source_target_pairs={{1,2},{2,1},{5,6},{6,5},{9,10},{10,9},{13,14},{14,13},{17,18},{18,... | collective-permute-start | bytes 6291464 | tf_op jit(solution)/shard_map/ppermute | solution.py:531
  142.0 9.6 %attend_forward.7 = (bf16[1280,512]{1,0:T(8,128)(2,1)S(1)}, bf16[1280,512]{1,0:T(8,128)(2,1)S(1)}, bf16[512,2560]{1,0:T(8,128)(2,1)S(1)}, f32[4,2,2560]{2,1,0:T(2,128)S(1)}) custom-call(s32[3,10]{1,0:T(4,128)S(1)} %add_add_fusion.2.tab_ref, s32[2560,1]{1,0:T(8,128)S(1)} %copy-done.3, ...), custom_call_target="tpu_custom_call", output_to_operand_aliasing={{0}: (5, {}), {1}: (6, {}), {2}: (7, {}), {3}: (8, {})} | custom-call | flops 19660800000 | bytes 8388608 | tf_op jit(solution)/shard_map/attend_forward/pallas_call | solution.py:302
  153.5 40.2 %collective-permute-start.10 = (bf16[1280,1024]{1,0:T(8,128)(2,1)S(1)}, bf16[1280,1024]{1,0:T(8,128)(2,1)S(1)}, u32[]{:S(2)}, u32[]{:S(2)}) collective-permute-start(bf16[1280,1024]{1,0:T(8,128)(2,1)S(1)} %convolution_convert_fusion.1), channel_id=1, source_target_pairs={{0,2},{2,0},{1,3},{3,1},{4,6},{6,4},{5,7},{7,5},{8,10},{10,8},{9,1... | collective-permute-start | bytes 7864328 | tf_op jit(solution)/shard_map/ppermute | solution.py:581
  211.8 4.5 maximum_select_fusion.down_ref
  216.7 17.8 %feed_forward.2 = (bf16[2560,1024]{1,0:T(8,128)(2,1)}, bf16[2560,2048]{1,0:T(8,128)(2,1)}, bf16[2560,2048]{1,0:T(8,128)(2,1)}, bf16[1280,1024]{1,0:T(8,128)(2,1)S(1)}) custom-call(bf16[1280,1024]{1,0:T(8,128)(2,1)S(1)} %add_convert_fusion.2.x_ref, bf16[1024,2048]{1,0:T(8,128)(2,1)} %broadcast_select_fusion.2.up_ref, f32[1,2048]{1,0:T(1,128)S(1)} %bitcast.68, ...), custom_call_target="tpu_custom_call" | custom-call | flops 16106127360 | bytes 16777216 | tf_op jit(solution)/shard_map/feed_forward/pallas_call | solution.py:412
  234.5 18.0 %feed_forward.3 = (bf16[2560,1024]{1,0:T(8,128)(2,1)}, bf16[2560,2048]{1,0:T(8,128)(2,1)}, bf16[2560,2048]{1,0:T(8,128)(2,1)}, bf16[1280,1024]{1,0:T(8,128)(2,1)S(1)}) custom-call(bf16[1280,1024]{1,0:T(8,128)(2,1)S(1)} %collective-permute-done.11.x_ref, ...), custom_call_target="tpu_custom_call", output_to_operand_aliasing={{0}: (4, {}), {1}: (5, {}), {2}: (6, {})} | custom-call | flops 16106127360 | bytes 16777216 | tf_op jit(solution)/shard_map/feed_forward/pallas_call | solution.py:412
  252.5 15.3 %collective-permute-start.13 = (bf16[1280,1024]{1,0:T(8,128)(2,1)S(1)}, bf16[1280,1024]{1,0:T(8,128)(2,1)S(1)}, u32[]{:S(2)}, u32[]{:S(2)}) collective-permute-start(bf16[1280,1024]{1,0:T(8,128)(2,1)S(1)} %get-tuple-element.136), channel_id=1, source_target_pairs={{0,2},{2,0},{1,3},{3,1},{4,6},{6,4},{5,7},{7,5},{8,10},{10,8},{9,1... | collective-permute-start | bytes 7864328 | tf_op jit(solution)/shard_map/ppermute | solution.py:581
  267.8 4.5 collective-permute-done.13
  274.6 4.2 fusion.26
  278.7 4.8 convert_reduce_fusion.2
  283.9 15.9 %feed_back.2 = (bf16[2560,2048]{1,0:T(8,128)(2,1)}, f32[1,2048]{1,0:T(1,128)S(1)}, bf16[1280,1024]{1,0:T(8,128)(2,1)S(1)}) custom-call(bf16[1280,1024]{1,0:T(8,128)(2,1)S(1)} %get-tuple-element.223.g_ref, bf16[2560,2048]{1,0:T(8,128)(2,1)} %get-tuple-element.142.slope_ref, bf16[2048,1024]{1,0:T(8,128)(2,1)} %maximum_select_fusion.down_ref, ...), custom_call_target="tpu_custom_call" | custom-call | flops 1024 | bytes 1024 | tf_op jit(solution)/shard_map/feed_back/pallas_call | solution.py:474
  299.8 15.3 %fusion.35 = bf16[2048,1024]{1,0:T(8,128)(2,1)} fusion(bf16[2560,2048]{1,0:T(8,128)(2,1)} %get-tuple-element.138, bf16[1280,1024]{1,0:T(8,128)(2,1)S(1)} %collective-permute-done.14.g_ref, bf16[1280,1024]{1,0:T(8,128)(2,1)S(1)} %get-tuple-element.223.g_ref), kind=kOutput, calls=%fused_computation.76 | convolution fusion | flops 10750001152 | bytes 19922944 | tf_op jit(solution)/shard_map/dot_general | solution.py:35
  315.1 15.9 %feed_back.3 = (bf16[2560,2048]{1,0:T(8,128)(2,1)}, f32[1,2048]{1,0:T(1,128)S(1)}, bf16[1280,1024]{1,0:T(8,128)(2,1)S(1)}) custom-call(bf16[1280,1024]{1,0:T(8,128)(2,1)S(1)} %collective-permute-done.14.g_ref, bf16[2560,2048]{1,0:T(8,128)(2,1)} %get-tuple-element.142.slope_ref, ...), custom_call_target="tpu_custom_call", output_to_operand_aliasing={{0}: (4, {})} | custom-call | flops 1024 | bytes 1024 | tf_op jit(solution)/shard_map/feed_back/pallas_call | solution.py:474
  339.7 6.2 multiply_reduce_fusion.1
  348.3 17.6 %convolution_convert_fusion = bf16[1024,2048]{1,0:T(8,128)(2,1)} fusion(bf16[2560,1024]{1,0:T(8,128)(2,1)} %get-tuple-element.140, bf16[2560,2048]{1,0:T(8,128)(2,1)} %get-tuple-element.144), kind=kOutput, calls=%fused_computation.75 | convolution fusion | flops 10739515392 | bytes 19922944 | tf_op jit(solution)/shard_map/dot_general | solution.py:35
  379.3 26.5 %attend_backward.3 = (bf16[1280,768]{1,0:T(8,128)(2,1)S(1)}, bf16[1280,768]{1,0:T(8,128)(2,1)}) custom-call(s32[3,10]{1,0:T(4,128)S(1)} %add_add_fusion.2.tab_ref, s32[2560,1]{1,0:T(8,128)S(1)} %copy-done.4, s32[1,2560]{1,0:T(1,128)S(1)} %fusion.48.qseg_ref, bf16[1280,1536]{1,0:T(8,128)(2,1)} %copy-done, bf16[1280,1536]{1,0:T(8,128)(2,1)} %copy-done.1, ...), custom_call_target="tpu_custom_call" | custom-call | flops 1024 | bytes 1024 | tf_op jit(solution)/shard_map/attend_backward/pallas_call | solution.py:336
  415.1 5.2 add_convert_fusion.4
  421.4 4.7 broadcast_select_fusion.1
  426.1 98.4 %all-reduce.4.cloned.1.call-done = bf16[2048,1024]{1,0:T(8,128)(2,1)} async-done(((bf16[2048,1024]{1,0:T(8,128)(2,1)}), bf16[2048,1024]{1,0:T(8,128)(2,1)}) %all-reduce.4.cloned.1.call-update) | async-done | bytes 4194320 | tf_op jit(solution)/shard_map/psum | solution.py:606
  530.0 20.1 %collective-permute-start.21 = (bf16[512,768]{1,0:T(8,128)(2,1)}, bf16[512,768]{1,0:T(8,128)(2,1)S(1)}, u32[]{:S(2)}, u32[]{:S(2)}) collective-permute-start(bf16[512,768]{1,0:T(8,128)(2,1)} %constant_dynamic-slice_fusion.8), channel_id=1, source_target_pairs={{2,0},{3,1},{0,2},{1,3},{6,4},{7,5},{4,6},{5,7},{10,8},{11,9},{8,1... | collective-permute-start | bytes 2359304 | tf_op jit(solution)/shard_map/ppermute | solution.py:550
  551.7 14.9 %attend_backward.4 = (bf16[1280,768]{1,0:T(8,128)(2,1)S(1)}, bf16[1280,768]{1,0:T(8,128)(2,1)}) custom-call(s32[3,10]{1,0:T(4,128)S(1)} %add_add_fusion.2.tab_ref, s32[2560,1]{1,0:T(8,128)S(1)} %copy-done.4, s32[1,2560]{1,0:T(1,128)S(1)} %fusion.48.qseg_ref, bf16[1280,1536]{1,0:T(8,128)(2,1)} %copy-done, bf16[1280,1536]{1,0:T(8,128)(2,1)} %copy-done.1, ...), custom_call_target="tpu_custom_call" | custom-call | flops 1024 | bytes 1024 | tf_op jit(solution)/shard_map/attend_backward/pallas_call | solution.py:336
  567.9 4.4 convert_element_type.257
  577.7 14.8 %attend_backward.5 = (bf16[1280,768]{1,0:T(8,128)(2,1)S(1)}, bf16[1280,768]{1,0:T(8,128)(2,1)}) custom-call(s32[3,10]{1,0:T(4,128)S(1)} %add_add_fusion.2.tab_ref, s32[2560,1]{1,0:T(8,128)S(1)} %copy-done.4, s32[1,2560]{1,0:T(1,128)S(1)} %fusion.48.qseg_ref, bf16[1280,1536]{1,0:T(8,128)(2,1)} %copy-done, ...), custom_call_target="tpu_custom_call", output_to_operand_aliasing={{0}: (9, {}), {1}: (10, {})} | custom-call | flops 1024 | bytes 1024 | tf_op jit(solution)/shard_map/attend_backward/pallas_call | solution.py:336
  604.2 4.2 add_convert_fusion.3
  609.6 20.8 %collective-permute-start.30 = (bf16[256,768]{1,0:T(8,128)(2,1)S(1)}, bf16[256,768]{1,0:T(8,128)(2,1)S(1)}, u32[]{:S(2)}, u32[]{:S(2)}) collective-permute-start(bf16[256,768]{1,0:T(8,128)(2,1)S(1)} %constant_dynamic-slice_fusion.7), channel_id=1, source_target_pairs={{4,0},{5,1},{6,2},{7,3},{0,4},{1,5},{2,6},{3,7},{12,8},{13,9},{14,... | collective-permute-start | bytes 1179656 | tf_op jit(solution)/shard_map/ppermute | solution.py:550
  630.4 4.6 fusion.42
  635.6 4.8 collective-permute-done.30
  641.3 8.7 %collective-permute-start.31 = (bf16[128,768]{1,0:T(8,128)(2,1)}, bf16[128,768]{1,0:T(8,128)(2,1)}, u32[]{:S(2)}, u32[]{:S(2)}) collective-permute-start(bf16[128,768]{1,0:T(8,128)(2,1)} %constant_dynamic-slice_fusion.6), channel_id=1, source_target_pairs={{8,0},{9,1},{10,2},{11,3},{12,4},{13,5},{14,6},{15,7},{0,8},{1,9},... | collective-permute-start | bytes 589832 | tf_op jit(solution)/shard_map/ppermute | solution.py:550
  650.6 5.5 collective-permute-done.31
  659.2 9.8 %collective-permute-done.32 = bf16[64,768]{1,0:T(8,128)(2,1)S(1)} collective-permute-done((bf16[64,768]{1,0:T(8,128)(2,1)S(1)}, bf16[64,768]{1,0:T(8,128)(2,1)S(1)}, u32[]{:S(2)}, u32[]{:S(2)}) %collective-permute-start.32) | collective-permute-done | bytes 98336 | tf_op jit(solution)/shard_map/ppermute | solution.py:550
  669.8 6.8 collective-permute-done.33
  680.5 8.2 %fusion.20 = (f32[1024]{0:T(1024)}, f32[1280]{0:T(1024)}, f32[1280]{0:T(1024)}, f32[1024]{0:T(1024)}, f32[1280,1024]{1,0:T(8,128)}) fusion(bf16[1280,1024]{1,0:T(8,128)(2,1)S(1)} %copy-done.21, f32[1280]{0:T(1024)S(1)} %copy-done.54, f32[1280]{0:T(1024)S(1)} %copy-done.52, f32[1024]{0:T(1024)S(1)} %copy-done.60, ...), kind=kOutput, calls=%fused_computation.30 | convolution fusion | flops 2030300672 | bytes 19306496 | tf_op jit(solution)/shard_map/dot_general | solution.py:41
  691.7 7.2 collective-permute-done.38
  701.1 10.5 %collective-permute-done.39 = bf16[128,768]{1,0:T(8,128)(2,1)S(1)} collective-permute-done((bf16[128,768]{1,0:T(8,128)(2,1)S(1)}, bf16[128,768]{1,0:T(8,128)(2,1)S(1)}, u32[]{:S(2)}, u32[]{:S(2)}) %collective-permute-start.39) | collective-permute-done | bytes 196640 | tf_op jit(solution)/shard_map/ppermute | solution.py:550
  715.1 5.8 collective-permute-done.40
  738.7 4.7 fusion.19
  749.7 5.7 collective-permute-done.43
  757.5 19.0 %collective-permute-done.29 = f32[16384]{0:T(1024)S(1)} collective-permute-done((f32[16384]{0:T(1024)S(1)}, f32[16384]{0:T(1024)S(1)}, u32[]{:S(2)}, u32[]{:S(2)}) %collective-permute-start.29) | collective-permute-done | bytes 65568 | tf_op jit(solution)/shard_map/ppermute | solution.py:601
  781.2 6.7 convert_element_type.256
  798.3 6.6 copy.83
  804.8 4.4 select_convert_fusion
  (384 shorter events, 177.5 us)
Async XLA Ops:
  7.2 517.2 %all-reduce.4.cloned.1.call-start = ((), (), s32[]{:S(2)}) async-start(), calls=%async_computation | async-start | bytes 8388608 | tf_op jit(solution)/shard_map/psum | solution.py:606
  10.7 0.8 collective-permute-start
  12.4 0.7 collective-permute-start.1
  13.1 15.6 %collective-permute-start.2 = (bf16[1280,1024]{1,0:T(8,128)(2,1)}, bf16[1280,1024]{1,0:T(8,128)(2,1)}, u32[]{:S(2)}, u32[]{:S(2)}) collective-permute-start(bf16[1280,1024]{1,0:T(8,128)(2,1)} %param.20), channel_id=1, source_target_pairs={{1,2},{2,1},{5,6},{6,5},{9,10},{10,9},{13,14},{14,13},{17,18},{18,... | collective-permute-start | bytes 7864328 | tf_op jit(solution)/shard_map/ppermute | solution.py:531
  15.3 8.3 %collective-permute-start.6 = (bf16[256,3,512]{0,2,1:T(8,128)(2,1)}, bf16[256,3,512]{0,2,1:T(8,128)(2,1)}, u32[]{:S(2)}, u32[]{:S(2)}) collective-permute-start(bf16[256,3,512]{0,2,1:T(8,128)(2,1)} %copy-done.49), channel_id=1, source_target_pairs={{9,1},{10,2},{13,5},{14,6},{1,9},{2,10},{5,13},{6,14},{25,17},{26,... | collective-permute-start | bytes 2359304 | tf_op jit(solution)/shard_map/ppermute | solution.py:550
  26.7 48.4 %collective-permute-start.7 = (bf16[512,3,512]{0,2,1:T(8,128)(2,1)}, bf16[512,3,512]{0,2,1:T(8,128)(2,1)}, u32[]{:S(2)}, u32[]{:S(2)}) collective-permute-start(bf16[512,3,512]{0,2,1:T(8,128)(2,1)} %pad_maximum_fusion), channel_id=1, source_target_pairs={{5,1},{6,2},{1,5},{2,6},{13,9},{14,10},{9,13},{10,14},{21,17},{22,... | collective-permute-start | bytes 4718600 | tf_op jit(solution)/shard_map/ppermute | solution.py:550
  32.8 57.6 %collective-permute-start.8 = (bf16[1280,1024]{1,0:T(8,128)(2,1)}, bf16[1280,1024]{1,0:T(8,128)(2,1)}, u32[]{:S(2)}, u32[]{:S(2)}) collective-permute-start(bf16[1280,1024]{1,0:T(8,128)(2,1)} %fusion.14), channel_id=1, source_target_pairs={{0,2},{2,0},{1,3},{3,1},{4,6},{6,4},{5,7},{7,5},{8,10},{10,8},{9,1... | collective-permute-start | bytes 7864328 | tf_op jit(solution)/shard_map/ppermute | solution.py:581
  70.5 7.2 collective-permute-start.3
  78.3 29.5 %collective-permute-start.4 = (bf16[1024,2048]{1,0:T(8,128)(2,1)S(1)}, bf16[1024,2048]{1,0:T(8,128)(2,1)}, u32[]{:S(2)}, u32[]{:S(2)}) collective-permute-start(bf16[1024,2048]{1,0:T(8,128)(2,1)S(1)} %copy-done.33), channel_id=1, source_target_pairs={{1,2},{2,1},{5,6},{6,5},{9,10},{10,9},{13,14},{14,13},{17,18},{18,... | collective-permute-start | bytes 12582920 | tf_op jit(solution)/shard_map/ppermute | solution.py:531
  107.8 20.0 %collective-permute-start.5 = (bf16[1024,1024]{1,0:T(8,128)(2,1)}, bf16[1024,1024]{1,0:T(8,128)(2,1)S(1)}, u32[]{:S(2)}, u32[]{:S(2)}) collective-permute-start(bf16[1024,1024]{1,0:T(8,128)(2,1)} %get-tuple-element.107), channel_id=1, source_target_pairs={{1,2},{2,1},{5,6},{6,5},{9,10},{10,9},{13,14},{14,13},{17,18},{18,... | collective-permute-start | bytes 6291464 | tf_op jit(solution)/shard_map/ppermute | solution.py:531
  127.8 23.8 %collective-permute-start.9 = (bf16[1024,1024]{1,0:T(8,128)(2,1)}, bf16[1024,1024]{1,0:T(8,128)(2,1)}, u32[]{:S(2)}, u32[]{:S(2)}) collective-permute-start(bf16[1024,1024]{1,0:T(8,128)(2,1)} %get-tuple-element.123), channel_id=1, source_target_pairs={{1,2},{2,1},{5,6},{6,5},{9,10},{10,9},{13,14},{14,13},{17,18},{18,... | collective-permute-start | bytes 6291464 | tf_op jit(solution)/shard_map/ppermute | solution.py:531
  153.5 44.7 %collective-permute-start.10 = (bf16[1280,1024]{1,0:T(8,128)(2,1)S(1)}, bf16[1280,1024]{1,0:T(8,128)(2,1)S(1)}, u32[]{:S(2)}, u32[]{:S(2)}) collective-permute-start(bf16[1280,1024]{1,0:T(8,128)(2,1)S(1)} %convolution_convert_fusion.1), channel_id=1, source_target_pairs={{0,2},{2,0},{1,3},{3,1},{4,6},{6,4},{5,7},{7,5},{8,10},{10,8},{9,1... | collective-permute-start | bytes 7864328 | tf_op jit(solution)/shard_map/ppermute | solution.py:581
  196.3 20.1 %collective-permute-start.12 = (bf16[1280,1024]{1,0:T(8,128)(2,1)S(1)}, bf16[1280,1024]{1,0:T(8,128)(2,1)S(1)}, u32[]{:S(2)}, u32[]{:S(2)}) collective-permute-start(bf16[1280,1024]{1,0:T(8,128)(2,1)S(1)} %copy-done.39), channel_id=1, source_target_pairs={{1,2},{2,1},{5,6},{6,5},{9,10},{10,9},{13,14},{14,13},{17,18},{18,... | collective-permute-start | bytes 7864328 | tf_op jit(solution)/shard_map/ppermute | solution.py:531
  207.7 26.8 %collective-permute-start.11 = (bf16[1280,1024]{1,0:T(8,128)(2,1)S(1)}, bf16[1280,1024]{1,0:T(8,128)(2,1)S(1)}, u32[]{:S(2)}, u32[]{:S(2)}) collective-permute-start(bf16[1280,1024]{1,0:T(8,128)(2,1)S(1)} %add_convert_fusion.2.x_ref), channel_id=1, source_target_pairs={{0,2},{2,0},{1,3},{3,1},{4,6},{6,4},{5,7},{7,5},{8,10},{10,8},{9,1... | collective-permute-start | bytes 7864328 | tf_op jit(solution)/shard_map/ppermute | solution.py:581
  252.5 19.8 %collective-permute-start.13 = (bf16[1280,1024]{1,0:T(8,128)(2,1)S(1)}, bf16[1280,1024]{1,0:T(8,128)(2,1)S(1)}, u32[]{:S(2)}, u32[]{:S(2)}) collective-permute-start(bf16[1280,1024]{1,0:T(8,128)(2,1)S(1)} %get-tuple-element.136), channel_id=1, source_target_pairs={{0,2},{2,0},{1,3},{3,1},{4,6},{6,4},{5,7},{7,5},{8,10},{10,8},{9,1... | collective-permute-start | bytes 7864328 | tf_op jit(solution)/shard_map/ppermute | solution.py:581
  283.6 16.2 %collective-permute-start.14 = (bf16[1280,1024]{1,0:T(8,128)(2,1)S(1)}, bf16[1280,1024]{1,0:T(8,128)(2,1)S(1)}, u32[]{:S(2)}, u32[]{:S(2)}) collective-permute-start(bf16[1280,1024]{1,0:T(8,128)(2,1)S(1)} %get-tuple-element.223.g_ref), channel_id=1, source_target_pairs={{0,2},{2,0},{1,3},{3,1},{4,6},{6,4},{5,7},{7,5},{8,10},{10,8},{9,1... | collective-permute-start | bytes 7864328 | tf_op jit(solution)/shard_map/ppermute | solution.py:581
  331.0 5.0 collective-permute-start.16
  331.2 34.7 %collective-permute-start.15 = (bf16[2048,1024]{1,0:T(8,128)(2,1)}, bf16[2048,1024]{1,0:T(8,128)(2,1)}, u32[]{:S(2)}, u32[]{:S(2)}) collective-permute-start(bf16[2048,1024]{1,0:T(8,128)(2,1)} %fusion.35), channel_id=1, source_target_pairs={{2,1},{1,2},{6,5},{5,6},{10,9},{9,10},{14,13},{13,14},{18,17},{17,... | collective-permute-start | bytes 12582920 | tf_op jit(solution)/shard_map/ppermute | solution.py:531
  348.2 22.4 %collective-permute-start.17 = (bf16[1280,1024]{1,0:T(8,128)(2,1)S(1)}, bf16[1280,1024]{1,0:T(8,128)(2,1)S(1)}, u32[]{:S(2)}, u32[]{:S(2)}) collective-permute-start(bf16[1280,1024]{1,0:T(8,128)(2,1)S(1)} %get-tuple-element.225), channel_id=1, source_target_pairs={{0,2},{2,0},{1,3},{3,1},{4,6},{6,4},{5,7},{7,5},{8,10},{10,8},{9,1... | collective-permute-start | bytes 7864328 | tf_op jit(solution)/shard_map/ppermute | solution.py:581
  365.9 44.2 %collective-permute-start.18 = (bf16[1024,2048]{1,0:T(8,128)(2,1)}, bf16[1024,2048]{1,0:T(8,128)(2,1)}, u32[]{:S(2)}, u32[]{:S(2)}) collective-permute-start(bf16[1024,2048]{1,0:T(8,128)(2,1)} %convolution_convert_fusion), channel_id=1, source_target_pairs={{2,1},{1,2},{6,5},{5,6},{10,9},{9,10},{14,13},{13,14},{18,17},{17,... | collective-permute-start | bytes 12582920 | tf_op jit(solution)/shard_map/ppermute | solution.py:531
  376.7 378.9 %all-reduce.6.cloned.1.call-start = ((), (), s32[]{:S(2)}) async-start(), calls=%async_computation.1 | async-start | bytes 10485760 | tf_op jit(solution)/shard_map/psum | solution.py:606
  410.2 10.1 %collective-permute-start.19 = (bf16[512,1024]{1,0:T(8,128)(2,1)S(1)}, bf16[512,1024]{1,0:T(8,128)(2,1)S(1)}, u32[]{:S(2)}, u32[]{:S(2)}) collective-permute-start(bf16[512,1024]{1,0:T(8,128)(2,1)S(1)} %add_convert_fusion.5), channel_id=1, source_target_pairs={{2,1},{1,2},{6,5},{5,6},{10,9},{9,10},{14,13},{13,14},{18,17},{17,... | collective-permute-start | bytes 3145736 | tf_op jit(solution)/shard_map/ppermute | solution.py:531
  524.4 1.8 collective-permute-start.20
  530.0 42.4 %collective-permute-start.21 = (bf16[512,768]{1,0:T(8,128)(2,1)}, bf16[512,768]{1,0:T(8,128)(2,1)S(1)}, u32[]{:S(2)}, u32[]{:S(2)}) collective-permute-start(bf16[512,768]{1,0:T(8,128)(2,1)} %constant_dynamic-slice_fusion.8), channel_id=1, source_target_pairs={{2,0},{3,1},{0,2},{1,3},{6,4},{7,5},{4,6},{5,7},{10,8},{11,9},{8,1... | collective-permute-start | bytes 2359304 | tf_op jit(solution)/shard_map/ppermute | solution.py:550
  573.8 181.9 %collective-permute-start.22 = (bf16[1280,1024]{1,0:T(8,128)(2,1)}, bf16[1280,1024]{1,0:T(8,128)(2,1)}, u32[]{:S(2)}, u32[]{:S(2)}) collective-permute-start(bf16[1280,1024]{1,0:T(8,128)(2,1)} %get-tuple-element.167), channel_id=1, source_target_pairs={{2,1},{1,2},{6,5},{5,6},{10,9},{9,10},{14,13},{13,14},{18,17},{17,... | collective-permute-start | bytes 7864328 | tf_op jit(solution)/shard_map/ppermute | solution.py:531
  598.6 81.9 %collective-permute-start.23 = (bf16[1280,1024]{1,0:T(8,128)(2,1)}, bf16[1280,1024]{1,0:T(8,128)(2,1)}, u32[]{:S(2)}, u32[]{:S(2)}) collective-permute-start(bf16[1280,1024]{1,0:T(8,128)(2,1)} %add_convert_fusion), channel_id=1, source_target_pairs={{0,2},{2,0},{1,3},{3,1},{4,6},{6,4},{5,7},{7,5},{8,10},{10,8},{9,1... | collective-permute-start | bytes 7864328 | tf_op jit(solution)/shard_map/ppermute | solution.py:581
  608.4 50.4 %collective-permute-start.36 = (bf16[1024,768]{1,0:T(8,128)(2,1)S(1)}, bf16[1024,768]{1,0:T(8,128)(2,1)S(1)}, u32[]{:S(2)}, u32[]{:S(2)}) collective-permute-start(bf16[1024,768]{1,0:T(8,128)(2,1)S(1)} %add_convert_fusion.3), channel_id=1, source_target_pairs={{2,1},{1,2},{6,5},{5,6},{10,9},{9,10},{14,13},{13,14},{18,17},{17,... | collective-permute-start | bytes 4718600 | tf_op jit(solution)/shard_map/ppermute | solution.py:531
  609.6 30.8 %collective-permute-start.30 = (bf16[256,768]{1,0:T(8,128)(2,1)S(1)}, bf16[256,768]{1,0:T(8,128)(2,1)S(1)}, u32[]{:S(2)}, u32[]{:S(2)}) collective-permute-start(bf16[256,768]{1,0:T(8,128)(2,1)S(1)} %constant_dynamic-slice_fusion.7), channel_id=1, source_target_pairs={{4,0},{5,1},{6,2},{7,3},{0,4},{1,5},{2,6},{3,7},{12,8},{13,9},{14,... | collective-permute-start | bytes 1179656 | tf_op jit(solution)/shard_map/ppermute | solution.py:550
  641.3 14.8 %collective-permute-start.31 = (bf16[128,768]{1,0:T(8,128)(2,1)}, bf16[128,768]{1,0:T(8,128)(2,1)}, u32[]{:S(2)}, u32[]{:S(2)}) collective-permute-start(bf16[128,768]{1,0:T(8,128)(2,1)} %constant_dynamic-slice_fusion.6), channel_id=1, source_target_pairs={{8,0},{9,1},{10,2},{11,3},{12,4},{13,5},{14,6},{15,7},{0,8},{1,9},... | collective-permute-start | bytes 589832 | tf_op jit(solution)/shard_map/ppermute | solution.py:550
  657.1 12.0 %collective-permute-start.32 = (bf16[64,768]{1,0:T(8,128)(2,1)S(1)}, bf16[64,768]{1,0:T(8,128)(2,1)S(1)}, u32[]{:S(2)}, u32[]{:S(2)}) collective-permute-start(bf16[64,768]{1,0:T(8,128)(2,1)S(1)} %constant_dynamic-slice_fusion.5), channel_id=1, source_target_pairs={{16,0},{17,1},{18,2},{19,3},{20,4},{21,5},{22,6},{23,7},{24,8},{25... | collective-permute-start | bytes 294920 | tf_op jit(solution)/shard_map/ppermute | solution.py:550
  659.1 18.2 %collective-permute-start.37 = (bf16[512,768]{1,0:T(8,128)(2,1)S(1)}, bf16[512,768]{1,0:T(8,128)(2,1)S(1)}, u32[]{:S(2)}, u32[]{:S(2)}) collective-permute-start(bf16[512,768]{1,0:T(8,128)(2,1)S(1)} %constant_dynamic-slice_fusion.4), channel_id=1, source_target_pairs={{2,0},{3,1},{0,2},{1,3},{6,4},{7,5},{4,6},{5,7},{10,8},{11,9},{8,1... | collective-permute-start | bytes 2359304 | tf_op jit(solution)/shard_map/ppermute | solution.py:550
  669.1 7.6 collective-permute-start.33
  678.4 20.6 %collective-permute-start.38 = (bf16[256,768]{1,0:T(8,128)(2,1)}, bf16[256,768]{1,0:T(8,128)(2,1)}, u32[]{:S(2)}, u32[]{:S(2)}) collective-permute-start(bf16[256,768]{1,0:T(8,128)(2,1)} %constant_dynamic-slice_fusion.3), channel_id=1, source_target_pairs={{4,0},{5,1},{6,2},{7,3},{0,4},{1,5},{2,6},{3,7},{12,8},{13,9},{14,... | collective-permute-start | bytes 1179656 | tf_op jit(solution)/shard_map/ppermute | solution.py:550
  700.1 11.5 %collective-permute-start.39 = (bf16[128,768]{1,0:T(8,128)(2,1)S(1)}, bf16[128,768]{1,0:T(8,128)(2,1)S(1)}, u32[]{:S(2)}, u32[]{:S(2)}) collective-permute-start(bf16[128,768]{1,0:T(8,128)(2,1)S(1)} %constant_dynamic-slice_fusion.2), channel_id=1, source_target_pairs={{8,0},{9,1},{10,2},{11,3},{12,4},{13,5},{14,6},{15,7},{0,8},{1,9},... | collective-permute-start | bytes 589832 | tf_op jit(solution)/shard_map/ppermute | solution.py:550
  701.1 10.9 %collective-permute-start.25 = (f32[16384]{0:T(1024)S(1)}, f32[16384]{0:T(1024)S(1)}, u32[]{:S(2)}, u32[]{:S(2)}) collective-permute-start(f32[16384]{0:T(1024)S(1)} %pad_maximum_fusion.9), channel_id=1, source_target_pairs={{0,2},{1,3},{2,0},{3,1},{4,6},{5,7},{6,4},{7,5},{8,10},{9,11},{10,... | collective-permute-start | bytes 196616 | tf_op jit(solution)/shard_map/ppermute | solution.py:601
  711.7 9.2 %collective-permute-start.40 = (bf16[64,768]{1,0:T(8,128)(2,1)S(1)}, bf16[64,768]{1,0:T(8,128)(2,1)S(1)}, u32[]{:S(2)}, u32[]{:S(2)}) collective-permute-start(bf16[64,768]{1,0:T(8,128)(2,1)S(1)} %constant_dynamic-slice_fusion.1), channel_id=1, source_target_pairs={{16,0},{17,1},{18,2},{19,3},{20,4},{21,5},{22,6},{23,7},{24,8},{25... | collective-permute-start | bytes 294920 | tf_op jit(solution)/shard_map/ppermute | solution.py:550
  712.7 11.9 %collective-permute-start.26 = (f32[16384]{0:T(1024)S(1)}, f32[16384]{0:T(1024)S(1)}, u32[]{:S(2)}, u32[]{:S(2)}) collective-permute-start(f32[16384]{0:T(1024)S(1)} %fusion.52), channel_id=1, source_target_pairs={{0,4},{1,5},{2,6},{3,7},{4,0},{5,1},{6,2},{7,3},{8,12},{9,13},{10,... | collective-permute-start | bytes 196616 | tf_op jit(solution)/shard_map/ppermute | solution.py:601
  720.9 7.6 collective-permute-start.41
  721.9 12.2 %collective-permute-start.34 = (bf16[128,768]{1,0:T(8,128)(2,1)S(1)}, bf16[128,768]{1,0:T(8,128)(2,1)S(1)}, u32[]{:S(2)}, u32[]{:S(2)}) collective-permute-start(bf16[128,768]{1,0:T(8,128)(2,1)S(1)} %pad_maximum_fusion.7), channel_id=1, source_target_pairs={{8,0},{9,1},{10,2},{11,3},{12,4},{13,5},{14,6},{15,7},{0,8},{1,9},... | collective-permute-start | bytes 589832 | tf_op jit(solution)/shard_map/ppermute | solution.py:550
  724.6 7.3 collective-permute-start.27
  728.5 7.8 collective-permute-start.42
  732.0 13.9 %collective-permute-start.28 = (f32[16384]{0:T(1024)S(1)}, f32[16384]{0:T(1024)S(1)}, u32[]{:S(2)}, u32[]{:S(2)}) collective-permute-start(f32[16384]{0:T(1024)S(1)} %add.404), channel_id=1, source_target_pairs={{0,16},{1,17},{2,18},{3,19},{4,20},{5,21},{6,22},{7,23},{8,24},{9,... | collective-permute-start | bytes 196616 | tf_op jit(solution)/shard_map/ppermute | solution.py:601
  736.5 12.1 %collective-permute-start.35 = (bf16[256,768]{1,0:T(8,128)(2,1)S(1)}, bf16[256,768]{1,0:T(8,128)(2,1)S(1)}, u32[]{:S(2)}, u32[]{:S(2)}) collective-permute-start(bf16[256,768]{1,0:T(8,128)(2,1)S(1)} %pad_maximum_fusion.5), channel_id=1, source_target_pairs={{4,0},{5,1},{6,2},{7,3},{0,4},{1,5},{2,6},{3,7},{12,8},{13,9},{14,... | collective-permute-start | bytes 1179656 | tf_op jit(solution)/shard_map/ppermute | solution.py:550
  736.9 18.5 %collective-permute-start.43 = (bf16[256,768]{1,0:T(8,128)(2,1)S(1)}, bf16[256,768]{1,0:T(8,128)(2,1)S(1)}, u32[]{:S(2)}, u32[]{:S(2)}) collective-permute-start(bf16[256,768]{1,0:T(8,128)(2,1)S(1)} %pad_maximum_fusion.6), channel_id=1, source_target_pairs={{4,0},{5,1},{6,2},{7,3},{0,4},{1,5},{2,6},{3,7},{12,8},{13,9},{14,... | collective-permute-start | bytes 1179656 | tf_op jit(solution)/shard_map/ppermute | solution.py:550
  743.5 61.3 %collective-permute-start.24 = (bf16[1280,1024]{1,0:T(8,128)(2,1)}, bf16[1280,1024]{1,0:T(8,128)(2,1)}, u32[]{:S(2)}, u32[]{:S(2)}) collective-permute-start(bf16[1280,1024]{1,0:T(8,128)(2,1)} %fusion.19), channel_id=1, source_target_pairs={{2,1},{1,2},{6,5},{5,6},{10,9},{9,10},{14,13},{13,14},{18,17},{17,... | collective-permute-start | bytes 7864328 | tf_op jit(solution)/shard_map/ppermute | solution.py:531
  745.9 30.7 %collective-permute-start.29 = (f32[16384]{0:T(1024)S(1)}, f32[16384]{0:T(1024)S(1)}, u32[]{:S(2)}, u32[]{:S(2)}) collective-permute-start(f32[16384]{0:T(1024)S(1)} %add.405), channel_id=1, source_target_pairs={{0,1},{1,0},{2,3},{3,2},{4,5},{5,4},{6,7},{7,6},{8,9},{9,8},{10,11... | collective-permute-start | bytes 196616 | tf_op jit(solution)/shard_map/ppermute | solution.py:601
  755.6 32.2 %collective-permute-start.45 = (bf16[512,768]{1,0:T(8,128)(2,1)S(1)}, bf16[512,768]{1,0:T(8,128)(2,1)}, u32[]{:S(2)}, u32[]{:S(2)}) collective-permute-start(bf16[512,768]{1,0:T(8,128)(2,1)S(1)} %pad_maximum_fusion.4), channel_id=1, source_target_pairs={{2,0},{3,1},{0,2},{1,3},{6,4},{7,5},{4,6},{5,7},{10,8},{11,9},{8,1... | collective-permute-start | bytes 2359304 | tf_op jit(solution)/shard_map/ppermute | solution.py:550
  777.2 12.8 %collective-permute-start.44 = (bf16[512,768]{1,0:T(8,128)(2,1)}, bf16[512,768]{1,0:T(8,128)(2,1)}, u32[]{:S(2)}, u32[]{:S(2)}) collective-permute-start(bf16[512,768]{1,0:T(8,128)(2,1)} %pad_maximum_fusion.3), channel_id=1, source_target_pairs={{2,0},{3,1},{0,2},{1,3},{6,4},{7,5},{4,6},{5,7},{10,8},{11,9},{8,1... | collective-permute-start | bytes 2359304 | tf_op jit(solution)/shard_map/ppermute | solution.py:550
  (84 other events, 1142.5 us)
Sparse Core Ops, SparseCore 0:
  376.8 147.5 all-reduce.3
  572.5 151.6 all-reduce.5

commit v7 on v6

--- a/solution.py
+++ b/solution.py
@@ -281,8 +281,7 @@
     width = qkv_parts[0].shape[0]
     tokens = parts * width
     every = qkv_parts[0].shape[1] // (3 * PAIR)
-    pairs = every // chunk[1]
-    first = pairs * chunk[0]
+    first, pairs = chunk
     seg_specs = [
         pl.BlockSpec((tokens, 1), lambda g, t: (0, 0)),
         pl.BlockSpec((1, tokens), lambda g, t: (0, 0)),
@@ -320,19 +319,19 @@
         ],
         compiler_params=pltpu.CompilerParams(vmem_limit_bytes=40 * 2**20),
         cost_estimate=pl.CostEstimate(
-            flops=3000 * tokens * tokens * pairs, bytes_accessed=2**23, transcendentals=0
+            flops=2**10, bytes_accessed=2**10, transcendentals=0
         ),
         input_output_aliases={3 + parts + n: n for n in range(len(begun))},
         name="attend_forward",
     )(tables, kseg, seg[None, :], *qkv_parts, *begun)
 
 
-def attend_backward(qkv_parts, turned, grad_ctx, lse, seg, keep, tables, chunk, place, begun=()):
+def attend_backward(qkv_parts, turned, grad_ctx, lse, seg, keep, tables, chunk, begun=()):
     parts, width, tokens, every, pairs, seg_specs, qkv_specs, o_specs, ot_spec, lse_spec = (
         attend_specs(qkv_parts, chunk)
     )
     kseg = jnp.where(keep == 1, seg, -1)[:, None]
-    result = pl.BlockSpec((width, 3 * PAIR), lanes_of(place[0] * pairs, 1))
+    result = pl.BlockSpec((width, 3 * PAIR), lanes_of(chunk[0], 1))
     return pl.pallas_call(
         functools.partial(backward_kernel, parts),
         grid_spec=pltpu.PrefetchScalarGridSpec(
@@ -357,11 +356,11 @@
                 pltpu.VMEM((tokens, 128), F32),
             ],
         ),
-        out_shape=[jax.ShapeDtypeStruct((width, place[1] * pairs * 3 * PAIR), BF16)] * parts,
+        out_shape=[jax.ShapeDtypeStruct((width, every * 3 * PAIR), BF16)] * parts,
         input_output_aliases={5 + 2 * parts + n: n for n in range(len(begun))},
         compiler_params=pltpu.CompilerParams(vmem_limit_bytes=48 * 2**20),
         cost_estimate=pl.CostEstimate(
-            flops=2**10,
+            flops=4000 * tokens * tokens * (pairs - 1),
             bytes_accessed=2**10,
             transcendentals=0,
         ),
@@ -500,6 +499,59 @@
     )(g, slope_all, down, up, *begun)
 
 
+def weight_grad_kernel(parts, *refs):
+    a_refs, d_refs = refs[:parts], refs[parts : 2 * parts]
+    out_ref, sums_ref = refs[2 * parts :]
+    out_ref[...] = total([contract_rows(a[...], d[...]) for a, d in zip(a_refs, d_refs)]).astype(BF16)
+    sums_ref[...] = total([jnp.sum(d[...].astype(F32), axis=0, keepdims=True) for d in d_refs])
+
+
+def weight_grad(a_parts, d_parts, first, count):
+    parts = len(a_parts)
+    width, model = a_parts[0].shape
+    columns = 3 * PAIR
+    return pl.pallas_call(
+        functools.partial(weight_grad_kernel, parts),
+        grid=(count,),
+        in_specs=[pl.BlockSpec((width, model), lambda k: (0, 0), pipeline_mode=pl.Buffered(1))] * parts
+        + [pl.BlockSpec((width, columns), lambda k: (0, first + k))] * parts,
+        out_specs=[
+            pl.BlockSpec((model, columns), lambda k: (0, k)),
+            pl.BlockSpec((1, columns), lambda k: (0, k)),
+        ],
+        out_shape=[
+            jax.ShapeDtypeStruct((model, count * columns), BF16),
+            jax.ShapeDtypeStruct((1, count * columns), F32),
+        ],
+        compiler_params=pltpu.CompilerParams(vmem_limit_bytes=40 * 2**20),
+        cost_estimate=pl.CostEstimate(flops=2**10, bytes_accessed=2**10, transcendentals=0),
+        name="weight_grad",
+    )(*a_parts, *d_parts)
+
+
+def input_grad_kernel(d_ref, w_ref, out_ref):
+    out_ref[...] = contract_cols(d_ref[...], w_ref[...]).astype(BF16)
+
+
+def input_grad(d, weight):
+    width, columns = d.shape
+    model = weight.shape[0]
+    rows = row_block(width)
+    return pl.pallas_call(
+        input_grad_kernel,
+        grid=(width // rows,),
+        in_specs=[
+            pl.BlockSpec((rows, columns), lambda k: (k, 0)),
+            pl.BlockSpec((model, columns), lambda k: (0, 0), pipeline_mode=pl.Buffered(1)),
+        ],
+        out_specs=pl.BlockSpec((rows, model), lambda k: (k, 0)),
+        out_shape=jax.ShapeDtypeStruct((width, model), BF16),
+        compiler_params=pltpu.CompilerParams(vmem_limit_bytes=40 * 2**20),
+        cost_estimate=pl.CostEstimate(flops=2**10, bytes_accessed=2**10, transcendentals=0),
+        name="input_grad",
+    )(d, weight)
+
+
 def after(value, *others):
     return lax.optimization_barrier((value, *others))[0]
 
@@ -596,14 +648,9 @@
     def sum_all(self, value):
         devices = self.dp * self.n
         steps = [1 << k for k in range(devices.bit_length() - 1)]
-        within = self.n.bit_length() - 1
-        for step in steps[within:] + steps[:within]:
+        for step in steps:
             value = value + lax.ppermute(value, self.axes, [(i, i ^ step) for i in range(devices)])
         return value
-
-    def sum_dp(self, value, turn):
-        order = [(i + turn) % self.dp for i in range(self.dp)]
-        return lax.psum(value, "dp", axis_index_groups=[order])
 
     def halved(self, value, bit):
         half, high = value.shape[0] // 2, self.side(bit)
@@ -612,13 +659,17 @@
         got = self.partner(sent, bit)
         return (kept.astype(jnp.float32) + got.astype(jnp.float32)).astype(jnp.bfloat16)
 
-    def bits(self):
-        return list(range(self.pairs.bit_length() - 1))
-
-    def sum_rest(self, value):
-        for bit in self.bits():
+    def order(self, first):
+        bits = list(range(self.pairs.bit_length() - 1))
+        return bits[first:] + bits[:first]
+
+    def halved_by(self, value, bits):
+        for bit in bits:
             value = self.halved(value, bit)
-        for bit in self.bits()[::-1]:
+        return value
+
+    def joined_by(self, value, bits):
+        for bit in bits[::-1]:
             value = self.joined(value, self.partner(value, bit), bit)
         return value
 
@@ -696,10 +747,10 @@
     w_qkv = by_pairs(w_qkv, pairs)
     half = units // 2
     w_out_far = layout.send(after(w_out, tokens))
-    w_up_far = layout.send(after(w_up, w_out_far))
-    w_top_far = layout.send(after(w_down[:half], w_up_far))
-    w_low_far = layout.send(after(w_down[half:], w_top_far))
-    cotangent = layout.regroup(after(cotangent, w_low_far))
+    w_up_far = layout.send(after(w_up, tokens))
+    w_top_far = layout.send(after(w_down[:half], tokens))
+    w_low_far = layout.send(after(w_down[half:], w_up_far))
+    cotangent = layout.regroup(after(cotangent, w_top_far))
 
     resid_in = tokens.astype(f32)
     norm1_out, normed1, inv1 = norm_parts(resid_in, ln1_gain, ln1_bias)
@@ -716,11 +767,9 @@
     for pair in range(pairs):
         if pair and pair == pairs // 2:
             tables, w_out_far, w_up_far = lax.optimization_barrier((tables, w_out_far, w_up_far))
-        if pair and pair == pairs - 1:
-            tables, w_top_far = lax.optimization_barrier((tables, w_top_far))
-        begun = attend_forward(qkv, seg, keep, tables, (pair, pairs), begun)
+        begun = attend_forward(qkv, seg, keep, tables, (pair, 1), begun)
     *context, context_turned, log_total = begun
-    *context, w_low_far = lax.optimization_barrier((*context, w_low_far))
+    *context, w_top_far = lax.optimization_barrier((*context, w_top_far))
     context = from_kernel(context, rank, shares)
     stays = layout.stays()
     w_out = jnp.where(stays, w_out, w_out_far)
@@ -758,75 +807,71 @@
     grad_a3 = layout.scatter_sum(shares_a3)
     g_up_bias = total(g_up_bias)
     g_w_up = contract_rows(a3_all, grad_pre).astype(bf16)
-    g_w_up_far = layout.send(after(g_w_up, g_w_down_far), True)
+    g_w_up_far = layout.send(g_w_up, True)
     grad_mid = upstream + norm_back(grad_a3, normed3, inv3, ln3_gain)
     grad_z = norm_back(grad_mid, normed2, inv2, ln2_gain).astype(bf16)
+    grad_z, g_w_down_far = lax.optimization_barrier((grad_z, g_w_down_far))
     grad_z_all = layout.gather(grad_z)
     grad_ctx = [contract_cols(g, w_out).astype(bf16) for g in grad_z_all]
     g_w_out = total([contract_rows(x, g) for x, g in zip(context, grad_z_all)]).astype(bf16)
-    g_w_out_far = layout.send(after(g_w_out, g_w_up_far), True)
-    g_w_down_far, g_w_up, *grad_ctx = lax.optimization_barrier((g_w_down_far, g_w_up, *grad_ctx))
+    g_w_out_far = layout.send(g_w_out, True)
     grad_ctx, _ = for_kernel(grad_ctx, rank)
+    grad_qkv = ()
+    if pairs > 1:
+        grad_qkv = attend_backward(
+            qkv, context_turned, grad_ctx, log_total, seg, keep, tables, (0, 1), grad_qkv
+        )
+        g_w_up_far, g_w_out_far, *grad_qkv = lax.optimization_barrier(
+            (g_w_up_far, g_w_out_far, *grad_qkv)
+        )
     g_w_down = jnp.where(stays, g_w_down, g_w_down_far)
-    tables, g_w_down = lax.optimization_barrier((tables, g_w_down))
-    g_w_down = layout.sum_dp(g_w_down, 1)
-    grad_a1, g_w_qkv, sums, done = [], [], [], []
+    g_w_up = jnp.where(stays, g_w_up, g_w_up_far)
+    g_w_out = jnp.where(stays, g_w_out, g_w_out_far)
+    tables, g_w_down, g_w_up, g_w_out = lax.optimization_barrier(
+        (tables, g_w_down, g_w_up, g_w_out)
+    )
+    g_w_down = lax.psum(g_w_down, "dp")
+    g_w_up = lax.psum(g_w_up, "dp")
+    g_w_out = lax.psum(g_w_out, "dp")
+    first = len(grad_qkv) and 1
+    grad_qkv = attend_backward(
+        qkv,
+        context_turned,
+        grad_ctx,
+        log_total,
+        seg,
+        keep,
+        tables,
+        (first, pairs - first),
+        grad_qkv,
+    )
+    layer_out = layout.give_back(after(layer_out, g_w_out_far))
+    grad_qkv = from_kernel(grad_qkv, rank, shares)
+    grad_a1 = [input_grad(g, w_qkv) for g in grad_qkv]
+    grad_a1 = layout.scatter_sum(grad_a1)
+    grad_input = grad_mid + norm_back(grad_a1, normed1, inv1, ln1_gain)
+    grad_input = grad_input.astype(bf16)
+    g_w_qkv, sums = [], []
     each = pairs // chunks
     for chunk in range(chunks):
-        calls = 1 if chunk == 0 else each
-        grad_qkv = ()
-        for call in range(calls):
-            grad_qkv = attend_backward(
-                qkv,
-                context_turned,
-                grad_ctx,
-                log_total,
-                seg,
-                keep,
-                tables,
-                (chunk * calls + call, chunks * calls),
-                (call, calls),
-                grad_qkv,
+        if chunk == chunks - 1:
+            g_w_down, g_w_up, g_w_out, grad_input, *grad_qkv = lax.optimization_barrier(
+                (g_w_down, g_w_up, g_w_out, grad_input, *grad_qkv)
             )
-            if chunk and call < calls - 1:
-                tables, g_w_qkv[0], *grad_qkv = lax.optimization_barrier(
-                    (tables, g_w_qkv[0], *grad_qkv)
-                )
-        grad_qkv = from_kernel(grad_qkv, rank, shares)
-        done.append(grad_qkv)
-        g_part = total([contract_rows(x, g) for x, g in zip(a1, grad_qkv)]).astype(bf16)
-        if chunk == 0:
-            g_w_up_far, g_w_out_far, g_part = lax.optimization_barrier(
-                (g_w_up_far, g_w_out_far, g_part)
-            )
-            g_w_up = jnp.where(stays, g_w_up, g_w_up_far)
-            g_w_out = jnp.where(stays, g_w_out, g_w_out_far)
-            tables, g_w_down, g_w_up, g_w_out, g_part = lax.optimization_barrier(
-                (tables, g_w_down, g_w_up, g_w_out, g_part)
-            )
-            g_w_up = layout.sum_dp(g_w_up, 0)
-            g_w_out = layout.sum_dp(g_w_out, 0)
+        g_part, part_sums = weight_grad(a1, grad_qkv, chunk * each, each)
         g_w_qkv.append(layout.halved(layout.give_back(g_part), -1))
-    layer_out = layout.give_back(after(layer_out, g_w_qkv[0]))
-    done = lax.optimization_barrier(done)
-    for chunk, grad_qkv in enumerate(done):
-        columns = grad_qkv[0].shape[1]
-        w_part = w_qkv[:, chunk * columns : (chunk + 1) * columns]
-        grad_a1.append([contract_cols(g, w_part) for g in grad_qkv])
-        sums.append(total([jnp.sum(g.astype(f32), 0) for g in grad_qkv]))
-    g_w_qkv = [layout.sum_rest(g) for g in g_w_qkv]
-    g_w_up, g_w_out, *g_w_qkv = lax.optimization_barrier((g_w_up, g_w_out, *g_w_qkv))
-    g_w_qkv = [layout.joined(g, layout.partner(g, -1), -1) for g in g_w_qkv]
+        sums.append(part_sums)
+    sums = jnp.concatenate(sums, 1)
+    g_w_qkv = [layout.halved_by(g, layout.order(k)) for k, g in enumerate(g_w_qkv)]
+    g_w_qkv = [layout.joined_by(g, [-1, *layout.order(k)]) for k, g in enumerate(g_w_qkv)]
     g_w_qkv = jnp.concatenate(g_w_qkv, 1).astype(f32)
     g_w_qkv = (
         g_w_qkv.reshape(model_dim, pairs, 3, PAIR)
         .transpose(0, 2, 1, 3)
         .reshape(model_dim, 3, width)
     )
-    sums = jnp.concatenate(sums).reshape(pairs, 3, PAIR).transpose(1, 0, 2).reshape(3, width)
-    grad_a1 = layout.scatter_sum([total(terms) for terms in zip(*grad_a1)])
-    grad_input = grad_mid + norm_back(grad_a1, normed1, inv1, ln1_gain)
-    grad_input = layout.give_back(grad_input.astype(bf16)).astype(f32)
+    sums = sums.reshape(pairs, 3, PAIR).transpose(1, 0, 2).reshape(3, width)
+    grad_input = layout.give_back(grad_input).astype(f32)
 
     norm_terms = jnp.stack(
         [

time: 821 us -> 943 us (1.15)
  Pallas kernels: 162 us -> 279 us
  matrix products: 94.5 us -> 55.8 us
  waiting for transfers between devices: 193 us -> 226 us
    psum x2 -> x1, waiting for transfers between devices: 98.4 us -> 156 us  [body(): g_w_down = lax.psum(g_w_down, 'dp')]
    pallas_call x3 -> x2, Pallas kernels: 56.2 us -> 111 us  [attend_backward(): pl.pallas_call(functools.partial(backward_kernel, parts), grid_spec=pltpu...]
    ppermute x8, starting transfers between devices: 99.6 us -> 143 us  [to_rank(): return lax.ppermute(value, self.axes, moves)]
    ppermute x18, starting transfers between devices: 62.4 us -> 23.8 us  [partner(): return lax.ppermute(value, self.axes, moves)]
    pallas_call x4, Pallas kernels: 38.4 us -> 72.8 us  [attend_forward(): pl.pallas_call(functools.partial(forward_kernel, parts), grid_spec=pltpu....]
    pallas_call x0 -> x4, Pallas kernels: none -> 28.6 us  [the longest x2 18.6 us: weight_grad(): pl.pallas_call(functools.partial(weight_grad_kernel, parts), grid=(count,...]
    dot_general x6 -> x2, matrix products: 23 us -> 3.12 us  [contract_cols(): lax.dot_general(left, right, (((1,), (1,)), ((), ())), preferred_element_...]
    ppermute x18, waiting for transfers between devices: 64.9 us -> 45.9 us  [partner(): return lax.ppermute(value, self.axes, moves)]
  transfers between devices with their start and end apart: 48 -> 47, of which waited for: 17 -> 14; matrix products, arithmetic and copies ran while one was open for 23% -> 15% of each run, Pallas kernels for 16% -> 17%
where the time goes in v7:
time: 943 us; the launch traced here: 933 us
  Pallas kernels  279 us (30%)
  waiting for transfers between devices  226 us (24%)
  starting transfers between devices  195 us (21%)
  other arithmetic  108 us (11%)
  matrix products  55.8 us (6%)
  local copies, waits for them, and re-layouts  50.7 us (5%)
  between operations  17.4 us (2%)
    psum x1, waiting for transfers between devices, body(): g_w_down = lax.psum(g_w_down, 'dp')  156 us
    ppermute x8, starting transfers between devices, to_rank(): return lax.ppermute(value, self.axes, moves)  143 us
    pallas_call x2, Pallas kernels, attend_backward(): pl.pallas_call(functools.partial(backward_kernel, parts), grid_spec=pltpu...  111 us
    pallas_call x4, Pallas kernels, attend_forward(): pl.pallas_call(functools.partial(forward_kernel, parts), grid_spec=pltpu....  72.8 us
    ppermute x18, waiting for transfers between devices, partner(): return lax.ppermute(value, self.axes, moves)  45.9 us
    pallas_call x2, Pallas kernels, feed_forward(): pl.pallas_call(functools.partial(feed_kernel, min(units, FEED)), grid=(st...  35.5 us
    dot_general x4, matrix products, contract_rows(): lax.dot_general(left, right, (((0,), (0,)), ((), ())), preferred_element_...  35.3 us
    pallas_call x2, Pallas kernels, feed_back(): pl.pallas_call(functools.partial(feed_back_kernel, min(units, FEED)), gri...  31.8 us
  transfers between devices with their start and end apart: 47, of which 14 were waited for; matrix products, arithmetic and copies ran while one was open for 15% of the time, Pallas kernels for 17%

profile of v7, /device:TPU:0, one launch (start us, length us, event | category | flops | bytes accessed | tf_op | source)
XLA Modules:
  0.0 933.2 jit_solution(4217518425448466222)
XLA Ops:
  16.9 4.7 fusion.52
  37.0 37.1 %collective-permute-start.7 = (bf16[1280,1024]{1,0:T(8,128)(2,1)}, bf16[1280,1024]{1,0:T(8,128)(2,1)}, u32[]{:S(2)}, u32[]{:S(2)}) collective-permute-start(bf16[1280,1024]{1,0:T(8,128)(2,1)} %fusion.14.refs_0_), channel_id=1, source_target_pairs={{0,2},{2,0},{1,3},{3,1},{4,6},{6,4},{5,7},{7,5},{8,10},{10,8},{9,1... | collective-permute-start | bytes 7864328 | tf_op jit(solution)/shard_map/ppermute | solution.py:633
  81.8 6.4 fusion.2.refs_0_
  88.3 7.7 fusion.3.refs_1_
  95.9 18.1 %attend_forward.4 = (bf16[1280,512]{1,0:T(8,128)(2,1)S(1)}, bf16[1280,512]{1,0:T(8,128)(2,1)S(1)}, bf16[512,2560]{1,0:T(8,128)(2,1)S(1)}, f32[4,2,2560]{2,1,0:T(2,128)S(1)}) custom-call(s32[3,10]{1,0:T(4,128)S(1)} %add_add_fusion.2.tab_ref, s32[2560,1]{1,0:T(8,128)S(1)} %broadcast_in_dim.22.kseg_ref, s32[1,2560]{1,0:T(1,128)S(1)} %fusion.45.qseg_ref, ...), custom_call_target="tpu_custom_call" | custom-call | flops 1024 | bytes 1024 | tf_op jit(solution)/shard_map/attend_forward/pallas_call | solution.py:301
  114.1 18.1 %attend_forward.5 = (bf16[1280,512]{1,0:T(8,128)(2,1)S(1)}, bf16[1280,512]{1,0:T(8,128)(2,1)S(1)}, bf16[512,2560]{1,0:T(8,128)(2,1)S(1)}, f32[4,2,2560]{2,1,0:T(2,128)S(1)}) custom-call(s32[3,10]{1,0:T(4,128)S(1)} %add_add_fusion.2.tab_ref, ...), custom_call_target="tpu_custom_call", output_to_operand_aliasing={{0}: (5, {}), {1}: (6, {}), {2}: (7, {}), {3}: (8, {})} | custom-call | flops 1024 | bytes 1024 | tf_op jit(solution)/shard_map/attend_forward/pallas_call | solution.py:301
  132.2 18.1 %attend_forward.6 = (bf16[1280,512]{1,0:T(8,128)(2,1)S(1)}, bf16[1280,512]{1,0:T(8,128)(2,1)S(1)}, bf16[512,2560]{1,0:T(8,128)(2,1)S(1)}, f32[4,2,2560]{2,1,0:T(2,128)S(1)}) custom-call(s32[3,10]{1,0:T(4,128)S(1)} %add_add_fusion.2.tab_ref, ...), custom_call_target="tpu_custom_call", output_to_operand_aliasing={{0}: (5, {}), {1}: (6, {}), {2}: (7, {}), {3}: (8, {})} | custom-call | flops 1024 | bytes 1024 | tf_op jit(solution)/shard_map/attend_forward/pallas_call | solution.py:301
  150.3 18.5 %attend_forward.7 = (bf16[1280,512]{1,0:T(8,128)(2,1)S(1)}, bf16[1280,512]{1,0:T(8,128)(2,1)S(1)}, bf16[512,2560]{1,0:T(8,128)(2,1)S(1)}, f32[4,2,2560]{2,1,0:T(2,128)S(1)}) custom-call(s32[3,10]{1,0:T(4,128)S(1)} %add_add_fusion.2.tab_ref, ...), custom_call_target="tpu_custom_call", output_to_operand_aliasing={{0}: (5, {}), {1}: (6, {}), {2}: (7, {}), {3}: (8, {})} | custom-call | flops 1024 | bytes 1024 | tf_op jit(solution)/shard_map/attend_forward/pallas_call | solution.py:301
  170.8 18.7 %collective-permute-start.9 = (bf16[1280,1024]{1,0:T(8,128)(2,1)S(1)}, bf16[1280,1024]{1,0:T(8,128)(2,1)S(1)}, u32[]{:S(2)}, u32[]{:S(2)}) collective-permute-start(bf16[1280,1024]{1,0:T(8,128)(2,1)S(1)} %convolution_convert_fusion.1), channel_id=1, source_target_pairs={{0,2},{2,0},{1,3},{3,1},{4,6},{6,4},{5,7},{7,5},{8,10},{10,8},{9,1... | collective-permute-start | bytes 7864328 | tf_op jit(solution)/shard_map/ppermute | solution.py:633
  193.8 4.6 broadcast_select_fusion.2.up_ref
  212.7 5.5 maximum_select_fusion.down_ref
  218.2 17.7 %feed_forward.2 = (bf16[2560,1024]{1,0:T(8,128)(2,1)}, bf16[2560,2048]{1,0:T(8,128)(2,1)}, bf16[2560,2048]{1,0:T(8,128)(2,1)}, bf16[1280,1024]{1,0:T(8,128)(2,1)S(1)}) custom-call(bf16[1280,1024]{1,0:T(8,128)(2,1)S(1)} %add_convert_fusion.1.x_ref, bf16[1024,2048]{1,0:T(8,128)(2,1)} %broadcast_select_fusion.2.up_ref, f32[1,2048]{1,0:T(1,128)S(1)} %bitcast.55, ...), custom_call_target="tpu_custom_call" | custom-call | flops 16106127360 | bytes 16777216 | tf_op jit(solution)/shard_map/feed_forward/pallas_call | solution.py:411
  235.9 17.8 %feed_forward.3 = (bf16[2560,1024]{1,0:T(8,128)(2,1)}, bf16[2560,2048]{1,0:T(8,128)(2,1)}, bf16[2560,2048]{1,0:T(8,128)(2,1)}, bf16[1280,1024]{1,0:T(8,128)(2,1)S(1)}) custom-call(bf16[1280,1024]{1,0:T(8,128)(2,1)S(1)} %collective-permute-done.11.x_ref, ...), custom_call_target="tpu_custom_call", output_to_operand_aliasing={{0}: (4, {}), {1}: (5, {}), {2}: (6, {})} | custom-call | flops 16106127360 | bytes 16777216 | tf_op jit(solution)/shard_map/feed_forward/pallas_call | solution.py:411
  253.8 33.1 %collective-permute-start.13 = (bf16[1280,1024]{1,0:T(8,128)(2,1)S(1)}, bf16[1280,1024]{1,0:T(8,128)(2,1)S(1)}, u32[]{:S(2)}, u32[]{:S(2)}) collective-permute-start(bf16[1280,1024]{1,0:T(8,128)(2,1)S(1)} %get-tuple-element.122), channel_id=1, source_target_pairs={{0,2},{2,0},{1,3},{3,1},{4,6},{6,4},{5,7},{7,5},{8,10},{10,8},{9,1... | collective-permute-start | bytes 7864328 | tf_op jit(solution)/shard_map/ppermute | solution.py:633
  286.9 4.5 collective-permute-done.13
  293.7 4.2 fusion.26
  298.0 6.4 convert_reduce_fusion.2
  304.7 16.1 %feed_back.2 = (bf16[2560,2048]{1,0:T(8,128)(2,1)}, f32[1,2048]{1,0:T(1,128)S(1)}, bf16[1280,1024]{1,0:T(8,128)(2,1)S(1)}) custom-call(bf16[1280,1024]{1,0:T(8,128)(2,1)S(1)} %get-tuple-element.200.g_ref, bf16[2560,2048]{1,0:T(8,128)(2,1)} %get-tuple-element.127.slope_ref, bf16[2048,1024]{1,0:T(8,128)(2,1)} %maximum_select_fusion.down_ref, ...), custom_call_target="tpu_custom_call" | custom-call | flops 1024 | bytes 1024 | tf_op jit(solution)/shard_map/feed_back/pallas_call | solution.py:473
  320.8 15.4 %fusion.38 = bf16[2048,1024]{1,0:T(8,128)(2,1)} fusion(bf16[2560,2048]{1,0:T(8,128)(2,1)} %get-tuple-element.125, bf16[1280,1024]{1,0:T(8,128)(2,1)S(1)} %collective-permute-done.14.g_ref, bf16[1280,1024]{1,0:T(8,128)(2,1)S(1)} %get-tuple-element.200.g_ref), kind=kOutput, calls=%fused_computation.73 | convolution fusion | flops 10750001152 | bytes 19922944 | tf_op jit(solution)/shard_map/dot_general | solution.py:35
  336.3 15.7 %feed_back.3 = (bf16[2560,2048]{1,0:T(8,128)(2,1)}, f32[1,2048]{1,0:T(1,128)S(1)}, bf16[1280,1024]{1,0:T(8,128)(2,1)S(1)}) custom-call(bf16[1280,1024]{1,0:T(8,128)(2,1)S(1)} %collective-permute-done.14.g_ref, bf16[2560,2048]{1,0:T(8,128)(2,1)} %get-tuple-element.127.slope_ref, ...), custom_call_target="tpu_custom_call", output_to_operand_aliasing={{0}: (4, {})} | custom-call | flops 1024 | bytes 1024 | tf_op jit(solution)/shard_map/feed_back/pallas_call | solution.py:473
  353.1 3.8 collective-permute-done.16
  357.0 5.2 multiply_reduce_fusion
  362.2 8.1 multiply_reduce_fusion.1
  372.7 29.9 %collective-permute-start.18 = (bf16[1280,1024]{1,0:T(8,128)(2,1)S(1)}, bf16[1280,1024]{1,0:T(8,128)(2,1)S(1)}, u32[]{:S(2)}, u32[]{:S(2)}) collective-permute-start(bf16[1280,1024]{1,0:T(8,128)(2,1)S(1)} %multiply_convert_fusion), channel_id=1, source_target_pairs={{0,2},{2,0},{1,3},{3,1},{4,6},{6,4},{5,7},{7,5},{8,10},{10,8},{9,1... | collective-permute-start | bytes 7864328 | tf_op jit(solution)/shard_map/ppermute | solution.py:633
  402.6 16.8 %convolution_convert_fusion = bf16[1024,2048]{1,0:T(8,128)(2,1)} fusion(bf16[2560,1024]{1,0:T(8,128)(2,1)} %get-tuple-element.123, bf16[2560,2048]{1,0:T(8,128)(2,1)} %get-tuple-element.129), kind=kOutput, calls=%fused_computation.72 | convolution fusion | flops 10739515392 | bytes 19922944 | tf_op jit(solution)/shard_map/dot_general | solution.py:35
  432.2 29.4 %attend_backward.2 = (bf16[1280,1536]{1,0:T(8,128)(2,1)}, bf16[1280,1536]{1,0:T(8,128)(2,1)}) custom-call(s32[3,10]{1,0:T(4,128)S(1)} %add_add_fusion.2.tab_ref, s32[2560,1]{1,0:T(8,128)S(1)} %broadcast_in_dim.22.kseg_ref, s32[1,2560]{1,0:T(1,128)S(1)} %fusion.45.qseg_ref, bf16[1280,1536]{1,0:T(8,128)(2,1)} %copy-done, bf16[1280,1536]{1,0:T(8,128)(2,1)} %copy-done.1, ...), custom_call_target="tpu_custom_call" | custom-call | bytes 1024 | tf_op jit(solution)/shard_map/attend_backward/pallas_call | solution.py:335
  461.7 4.7 broadcast_select_fusion.1
  468.8 81.2 %attend_backward.3 = (bf16[1280,1536]{1,0:T(8,128)(2,1)}, bf16[1280,1536]{1,0:T(8,128)(2,1)}) custom-call(s32[3,10]{1,0:T(4,128)S(1)} %add_add_fusion.2.tab_ref, s32[2560,1]{1,0:T(8,128)S(1)} %broadcast_in_dim.22.kseg_ref, s32[1,2560]{1,0:T(1,128)S(1)} %fusion.45.qseg_ref, ...), custom_call_target="tpu_custom_call", output_to_operand_aliasing={{0}: (9, {}), {1}: (10, {})} | custom-call | flops 52428800000 | bytes 1024 | tf_op jit(solution)/shard_map/attend_backward/pallas_call | solution.py:335
  552.2 9.7 %weight_grad.2 = (bf16[1024,768]{1,0:T(8,128)(2,1)}, f32[1,768]{1,0:T(1,128)S(1)}) custom-call(bf16[1280,1024]{1,0:T(8,128)(2,1)} %fusion.14.refs_0_, bf16[1280,1024]{1,0:T(8,128)(2,1)} %collective-permute-done.7.refs_1_, bf16[1280,1536]{1,0:T(8,128)(2,1)S(1)} %copy-done.3, bf16[1280,1536]{1,0:T(8,128)(2,1)} %get-tuple-element.153.d_ref.refs_3_), custom_call_target="tpu_custom_call" | custom-call | flops 1024 | bytes 1024 | tf_op jit(solution)/shard_map/weight_grad/pallas_call | solution.py:513
  569.1 5.5 input_grad.3
  574.7 20.7 %collective-permute-start.21 = (bf16[1280,1024]{1,0:T(8,128)(2,1)}, bf16[1280,1024]{1,0:T(8,128)(2,1)}, u32[]{:S(2)}, u32[]{:S(2)}) collective-permute-start(bf16[1280,1024]{1,0:T(8,128)(2,1)} %input_grad.3), channel_id=1, source_target_pairs={{0,2},{2,0},{1,3},{3,1},{4,6},{6,4},{5,7},{7,5},{8,10},{10,8},{9,1... | collective-permute-start | bytes 7864328 | tf_op jit(solution)/shard_map/ppermute | solution.py:633
  599.1 9.1 collective-permute-start.29
  610.4 4.5 input_grad.2
  616.6 4.7 fusion.20
  621.4 4.8 fusion.19
  626.2 156.4 %all-reduce.3.cloned.1.call-done = (bf16[2048,1024]{1,0:T(8,128)(2,1)}, bf16[1024,2048]{1,0:T(8,128)(2,1)}, bf16[512,1024]{1,0:T(8,128)(2,1)}) async-done(((bf16[2048,1024]{1,0:T(8,128)(2,1)}, bf16[1024,2048]{1,0:T(8,128)(2,1)}, bf16[512,1024]{1,0:T(8,128)(2,1)}), (bf16[2048,1024]{1,0:T(8,128)(2,1)}, bf16[1024,2048]{1,0:T(8,128)(2,1)}, bf16[512,1024]{1,0:T(8,128)(2,1)})) %all-reduce.3.cloned.1.call-update) | async-done | bytes 9437200 | tf_op jit(solution)/shard_map/psum | solution.py:833
  784.7 8.9 weight_grad.3
  797.2 5.6 collective-permute-done.31
  805.3 5.9 collective-permute-done.32
  811.6 6.9 collective-permute-done.33
  833.0 3.7 collective-permute-done.35
  840.6 8.5 collective-permute-done.39
  850.1 14.0 %collective-permute-done.23 = f32[16384]{0:T(1024)S(1)} collective-permute-done((f32[16384]{0:T(1024)S(1)}, f32[16384]{0:T(1024)S(1)}, u32[]{:S(2)}, u32[]{:S(2)}) %collective-permute-start.23) | collective-permute-done | bytes 65568 | tf_op jit(solution)/shard_map/ppermute | solution.py:652
  877.6 10.0 %collective-permute-done.43 = bf16[128,768]{1,0:T(8,128)(2,1)S(1)} collective-permute-done((bf16[128,768]{1,0:T(8,128)(2,1)S(1)}, bf16[128,768]{1,0:T(8,128)(2,1)S(1)}, u32[]{:S(2)}, u32[]{:S(2)}) %collective-permute-start.43) | collective-permute-done | bytes 196640 | tf_op jit(solution)/shard_map/ppermute | solution.py:602
  894.5 6.8 convert_element_type.232
  901.3 4.4 convert_element_type.233
  916.4 3.2 copy.85
  919.6 6.6 copy.86
  (359 shorter events, 148.1 us)
Async XLA Ops:
  7.2 775.4 %all-reduce.3.cloned.1.call-start = ((), (), s32[]{:S(2)}) async-start(), calls=%async_computation | async-start | bytes 18874368 | tf_op jit(solution)/shard_map/psum | solution.py:833
  10.7 0.8 collective-permute-start
  12.4 0.7 collective-permute-start.1
  13.1 15.3 %collective-permute-start.2 = (bf16[1280,1024]{1,0:T(8,128)(2,1)}, bf16[1280,1024]{1,0:T(8,128)(2,1)}, u32[]{:S(2)}, u32[]{:S(2)}) collective-permute-start(bf16[1280,1024]{1,0:T(8,128)(2,1)} %param.20), channel_id=1, source_target_pairs={{1,2},{2,1},{5,6},{6,5},{9,10},{10,9},{13,14},{14,13},{17,18},{18,... | collective-permute-start | bytes 7864328 | tf_op jit(solution)/shard_map/ppermute | solution.py:583
  15.3 8.3 collective-permute-start.5
  26.5 49.2 %collective-permute-start.6 = (bf16[512,3,512]{0,2,1:T(8,128)(2,1)}, bf16[512,3,512]{0,2,1:T(8,128)(2,1)}, u32[]{:S(2)}, u32[]{:S(2)}) collective-permute-start(bf16[512,3,512]{0,2,1:T(8,128)(2,1)} %pad_maximum_fusion), channel_id=1, source_target_pairs={{5,1},{6,2},{1,5},{2,6},{13,9},{14,10},{9,13},{10,14},{21,17},{22,... | collective-permute-start | bytes 4718600 | tf_op jit(solution)/shard_map/ppermute | solution.py:602
  31.0 101.2 %collective-permute-start.4 = (bf16[1024,2048]{1,0:T(8,128)(2,1)}, bf16[1024,2048]{1,0:T(8,128)(2,1)}, u32[]{:S(2)}, u32[]{:S(2)}) collective-permute-start(bf16[1024,2048]{1,0:T(8,128)(2,1)} %param.31), channel_id=1, source_target_pairs={{1,2},{2,1},{5,6},{6,5},{9,10},{10,9},{13,14},{14,13},{17,18},{18,... | collective-permute-start | bytes 12582920 | tf_op jit(solution)/shard_map/ppermute | solution.py:583
  37.0 51.2 %collective-permute-start.7 = (bf16[1280,1024]{1,0:T(8,128)(2,1)}, bf16[1280,1024]{1,0:T(8,128)(2,1)}, u32[]{:S(2)}, u32[]{:S(2)}) collective-permute-start(bf16[1280,1024]{1,0:T(8,128)(2,1)} %fusion.14.refs_0_), channel_id=1, source_target_pairs={{0,2},{2,0},{1,3},{3,1},{4,6},{6,4},{5,7},{7,5},{8,10},{10,8},{9,1... | collective-permute-start | bytes 7864328 | tf_op jit(solution)/shard_map/ppermute | solution.py:633
  77.6 91.3 %collective-permute-start.8 = (bf16[1024,1024]{1,0:T(8,128)(2,1)}, bf16[1024,1024]{1,0:T(8,128)(2,1)S(1)}, u32[]{:S(2)}, u32[]{:S(2)}) collective-permute-start(bf16[1024,1024]{1,0:T(8,128)(2,1)} %get-tuple-element.109), channel_id=1, source_target_pairs={{1,2},{2,1},{5,6},{6,5},{9,10},{10,9},{13,14},{14,13},{17,18},{18,... | collective-permute-start | bytes 6291464 | tf_op jit(solution)/shard_map/ppermute | solution.py:583
  80.9 51.3 %collective-permute-start.3 = (bf16[512,1024]{1,0:T(8,128)(2,1)S(1)}, bf16[512,1024]{1,0:T(8,128)(2,1)S(1)}, u32[]{:S(2)}, u32[]{:S(2)}) collective-permute-start(bf16[512,1024]{1,0:T(8,128)(2,1)S(1)} %copy-done.42), channel_id=1, source_target_pairs={{1,2},{2,1},{5,6},{6,5},{9,10},{10,9},{13,14},{14,13},{17,18},{18,... | collective-permute-start | bytes 3145736 | tf_op jit(solution)/shard_map/ppermute | solution.py:583
  170.8 27.7 %collective-permute-start.9 = (bf16[1280,1024]{1,0:T(8,128)(2,1)S(1)}, bf16[1280,1024]{1,0:T(8,128)(2,1)S(1)}, u32[]{:S(2)}, u32[]{:S(2)}) collective-permute-start(bf16[1280,1024]{1,0:T(8,128)(2,1)S(1)} %convolution_convert_fusion.1), channel_id=1, source_target_pairs={{0,2},{2,0},{1,3},{3,1},{4,6},{6,4},{5,7},{7,5},{8,10},{10,8},{9,1... | collective-permute-start | bytes 7864328 | tf_op jit(solution)/shard_map/ppermute | solution.py:633
  189.5 22.9 %collective-permute-start.12 = (bf16[1280,1024]{1,0:T(8,128)(2,1)S(1)}, bf16[1280,1024]{1,0:T(8,128)(2,1)}, u32[]{:S(2)}, u32[]{:S(2)}) collective-permute-start(bf16[1280,1024]{1,0:T(8,128)(2,1)S(1)} %copy-done.39), channel_id=1, source_target_pairs={{1,2},{2,1},{5,6},{6,5},{9,10},{10,9},{13,14},{14,13},{17,18},{18,... | collective-permute-start | bytes 7864328 | tf_op jit(solution)/shard_map/ppermute | solution.py:583
  191.7 21.0 %collective-permute-start.10 = (bf16[1024,1024]{1,0:T(8,128)(2,1)}, bf16[1024,1024]{1,0:T(8,128)(2,1)}, u32[]{:S(2)}, u32[]{:S(2)}) collective-permute-start(bf16[1024,1024]{1,0:T(8,128)(2,1)} %get-tuple-element.115), channel_id=1, source_target_pairs={{1,2},{2,1},{5,6},{6,5},{9,10},{10,9},{13,14},{14,13},{17,18},{18,... | collective-permute-start | bytes 6291464 | tf_op jit(solution)/shard_map/ppermute | solution.py:583
  209.5 26.4 %collective-permute-start.11 = (bf16[1280,1024]{1,0:T(8,128)(2,1)S(1)}, bf16[1280,1024]{1,0:T(8,128)(2,1)S(1)}, u32[]{:S(2)}, u32[]{:S(2)}) collective-permute-start(bf16[1280,1024]{1,0:T(8,128)(2,1)S(1)} %add_convert_fusion.1.x_ref), channel_id=1, source_target_pairs={{0,2},{2,0},{1,3},{3,1},{4,6},{6,4},{5,7},{7,5},{8,10},{10,8},{9,1... | collective-permute-start | bytes 7864328 | tf_op jit(solution)/shard_map/ppermute | solution.py:633
  212.7 81.0 %copy-start.23 = (bf16[1280,1024]{1,0:T(8,128)(2,1)}, bf16[1280,1024]{1,0:T(8,128)(2,1)S(1)}, u32[]{:S(2)}) copy-start(bf16[1280,1024]{1,0:T(8,128)(2,1)S(1)} %broadcast_select_fusion.4) | copy-start | bytes 7864324
  253.8 37.7 %collective-permute-start.13 = (bf16[1280,1024]{1,0:T(8,128)(2,1)S(1)}, bf16[1280,1024]{1,0:T(8,128)(2,1)S(1)}, u32[]{:S(2)}, u32[]{:S(2)}) collective-permute-start(bf16[1280,1024]{1,0:T(8,128)(2,1)S(1)} %get-tuple-element.122), channel_id=1, source_target_pairs={{0,2},{2,0},{1,3},{3,1},{4,6},{6,4},{5,7},{7,5},{8,10},{10,8},{9,1... | collective-permute-start | bytes 7864328 | tf_op jit(solution)/shard_map/ppermute | solution.py:633
  304.4 16.5 %collective-permute-start.14 = (bf16[1280,1024]{1,0:T(8,128)(2,1)S(1)}, bf16[1280,1024]{1,0:T(8,128)(2,1)S(1)}, u32[]{:S(2)}, u32[]{:S(2)}) collective-permute-start(bf16[1280,1024]{1,0:T(8,128)(2,1)S(1)} %get-tuple-element.200.g_ref), channel_id=1, source_target_pairs={{0,2},{2,0},{1,3},{3,1},{4,6},{6,4},{5,7},{7,5},{8,10},{10,8},{9,1... | collective-permute-start | bytes 7864328 | tf_op jit(solution)/shard_map/ppermute | solution.py:633
  352.0 5.0 collective-permute-start.16
  352.2 20.5 %collective-permute-start.17 = (bf16[2048,1024]{1,0:T(8,128)(2,1)}, bf16[2048,1024]{1,0:T(8,128)(2,1)S(1)}, u32[]{:S(2)}, u32[]{:S(2)}) collective-permute-start(bf16[2048,1024]{1,0:T(8,128)(2,1)} %fusion.38), channel_id=1, source_target_pairs={{2,1},{1,2},{6,5},{5,6},{10,9},{9,10},{14,13},{13,14},{18,17},{17,... | collective-permute-start | bytes 12582920 | tf_op jit(solution)/shard_map/ppermute | solution.py:583
  372.7 51.1 %collective-permute-start.18 = (bf16[1280,1024]{1,0:T(8,128)(2,1)S(1)}, bf16[1280,1024]{1,0:T(8,128)(2,1)S(1)}, u32[]{:S(2)}, u32[]{:S(2)}) collective-permute-start(bf16[1280,1024]{1,0:T(8,128)(2,1)S(1)} %multiply_convert_fusion), channel_id=1, source_target_pairs={{0,2},{2,0},{1,3},{3,1},{4,6},{6,4},{5,7},{7,5},{8,10},{10,8},{9,1... | collective-permute-start | bytes 7864328 | tf_op jit(solution)/shard_map/ppermute | solution.py:633
  419.4 42.2 %collective-permute-start.15 = (bf16[1024,2048]{1,0:T(8,128)(2,1)}, bf16[1024,2048]{1,0:T(8,128)(2,1)}, u32[]{:S(2)}, u32[]{:S(2)}) collective-permute-start(bf16[1024,2048]{1,0:T(8,128)(2,1)} %convolution_convert_fusion), channel_id=1, source_target_pairs={{2,1},{1,2},{6,5},{5,6},{10,9},{9,10},{14,13},{13,14},{18,17},{17,... | collective-permute-start | bytes 12582920 | tf_op jit(solution)/shard_map/ppermute | solution.py:583
  426.9 34.7 %collective-permute-start.19 = (bf16[512,1024]{1,0:T(8,128)(2,1)S(1)}, bf16[512,1024]{1,0:T(8,128)(2,1)S(1)}, u32[]{:S(2)}, u32[]{:S(2)}) collective-permute-start(bf16[512,1024]{1,0:T(8,128)(2,1)S(1)} %add_convert_fusion.2), channel_id=1, source_target_pairs={{2,1},{1,2},{6,5},{5,6},{10,9},{9,10},{14,13},{13,14},{18,17},{17,... | collective-permute-start | bytes 3145736 | tf_op jit(solution)/shard_map/ppermute | solution.py:583
  561.8 33.6 %collective-permute-start.28 = (bf16[1024,768]{1,0:T(8,128)(2,1)}, bf16[1024,768]{1,0:T(8,128)(2,1)}, u32[]{:S(2)}, u32[]{:S(2)}) collective-permute-start(bf16[1024,768]{1,0:T(8,128)(2,1)} %get-tuple-element.157), channel_id=1, source_target_pairs={{2,1},{1,2},{6,5},{5,6},{10,9},{9,10},{14,13},{13,14},{18,17},{17,... | collective-permute-start | bytes 4718600 | tf_op jit(solution)/shard_map/ppermute | solution.py:583
  574.7 41.9 %collective-permute-start.21 = (bf16[1280,1024]{1,0:T(8,128)(2,1)}, bf16[1280,1024]{1,0:T(8,128)(2,1)}, u32[]{:S(2)}, u32[]{:S(2)}) collective-permute-start(bf16[1280,1024]{1,0:T(8,128)(2,1)} %input_grad.3), channel_id=1, source_target_pairs={{0,2},{2,0},{1,3},{3,1},{4,6},{6,4},{5,7},{7,5},{8,10},{10,8},{9,1... | collective-permute-start | bytes 7864328 | tf_op jit(solution)/shard_map/ppermute | solution.py:633
  599.1 15.8 %collective-permute-start.29 = (bf16[512,768]{1,0:T(8,128)(2,1)}, bf16[512,768]{1,0:T(8,128)(2,1)}, u32[]{:S(2)}, u32[]{:S(2)}) collective-permute-start(bf16[512,768]{1,0:T(8,128)(2,1)} %constant_dynamic-slice_fusion.8), channel_id=1, source_target_pairs={{2,0},{3,1},{0,2},{1,3},{6,4},{7,5},{4,6},{5,7},{10,8},{11,9},{8,1... | collective-permute-start | bytes 2359304 | tf_op jit(solution)/shard_map/ppermute | solution.py:602
  616.5 179.0 %collective-permute-start.30 = (bf16[256,768]{1,0:T(8,128)(2,1)S(1)}, bf16[256,768]{1,0:T(8,128)(2,1)S(1)}, u32[]{:S(2)}, u32[]{:S(2)}) collective-permute-start(bf16[256,768]{1,0:T(8,128)(2,1)S(1)} %constant_dynamic-slice_fusion.7), channel_id=1, source_target_pairs={{4,0},{5,1},{6,2},{7,3},{0,4},{1,5},{2,6},{3,7},{12,8},{13,9},{14,... | collective-permute-start | bytes 1179656 | tf_op jit(solution)/shard_map/ppermute | solution.py:602
  793.7 25.0 %collective-permute-start.37 = (bf16[1024,768]{1,0:T(8,128)(2,1)S(1)}, bf16[1024,768]{1,0:T(8,128)(2,1)}, u32[]{:S(2)}, u32[]{:S(2)}) collective-permute-start(bf16[1024,768]{1,0:T(8,128)(2,1)S(1)} %get-tuple-element.158), channel_id=1, source_target_pairs={{2,1},{1,2},{6,5},{5,6},{10,9},{9,10},{14,13},{13,14},{18,17},{17,... | collective-permute-start | bytes 4718600 | tf_op jit(solution)/shard_map/ppermute | solution.py:583
  795.6 7.1 collective-permute-start.31
  802.9 8.3 collective-permute-start.32
  811.2 7.4 collective-permute-start.33
  818.6 6.9 collective-permute-start.34
  821.0 17.0 %collective-permute-start.38 = (bf16[512,768]{1,0:T(8,128)(2,1)}, bf16[512,768]{1,0:T(8,128)(2,1)}, u32[]{:S(2)}, u32[]{:S(2)}) collective-permute-start(bf16[512,768]{1,0:T(8,128)(2,1)} %constant_dynamic-slice_fusion.4), channel_id=1, source_target_pairs={{2,0},{3,1},{0,2},{1,3},{6,4},{7,5},{4,6},{5,7},{10,8},{11,9},{8,1... | collective-permute-start | bytes 2359304 | tf_op jit(solution)/shard_map/ppermute | solution.py:602
  826.3 10.3 %collective-permute-start.35 = (bf16[256,768]{1,0:T(8,128)(2,1)S(1)}, bf16[256,768]{1,0:T(8,128)(2,1)}, u32[]{:S(2)}, u32[]{:S(2)}) collective-permute-start(bf16[256,768]{1,0:T(8,128)(2,1)S(1)} %pad_maximum_fusion.5), channel_id=1, source_target_pairs={{4,0},{5,1},{6,2},{7,3},{0,4},{1,5},{2,6},{3,7},{12,8},{13,9},{14,... | collective-permute-start | bytes 1179656 | tf_op jit(solution)/shard_map/ppermute | solution.py:602
  830.4 39.7 %collective-permute-start.20 = (bf16[1280,1024]{1,0:T(8,128)(2,1)}, bf16[1280,1024]{1,0:T(8,128)(2,1)}, u32[]{:S(2)}, u32[]{:S(2)}) collective-permute-start(bf16[1280,1024]{1,0:T(8,128)(2,1)} %get-tuple-element.139), channel_id=1, source_target_pairs={{2,1},{1,2},{6,5},{5,6},{10,9},{9,10},{14,13},{13,14},{18,17},{17,... | collective-permute-start | bytes 7864328 | tf_op jit(solution)/shard_map/ppermute | solution.py:583
  839.8 9.3 %collective-permute-start.39 = (bf16[256,768]{1,0:T(8,128)(2,1)S(1)}, bf16[256,768]{1,0:T(8,128)(2,1)S(1)}, u32[]{:S(2)}, u32[]{:S(2)}) collective-permute-start(bf16[256,768]{1,0:T(8,128)(2,1)S(1)} %constant_dynamic-slice_fusion.3), channel_id=1, source_target_pairs={{8,0},{9,1},{10,2},{11,3},{12,4},{13,5},{14,6},{15,7},{0,8},{1,9},... | collective-permute-start | bytes 1179656 | tf_op jit(solution)/shard_map/ppermute | solution.py:602
  840.5 23.5 %collective-permute-start.23 = (f32[16384]{0:T(1024)S(1)}, f32[16384]{0:T(1024)S(1)}, u32[]{:S(2)}, u32[]{:S(2)}) collective-permute-start(f32[16384]{0:T(1024)S(1)} %pad_maximum_fusion.9), channel_id=1, source_target_pairs={{0,1},{1,0},{2,3},{3,2},{4,5},{5,4},{6,7},{7,6},{8,9},{9,8},{10,11... | collective-permute-start | bytes 196616 | tf_op jit(solution)/shard_map/ppermute | solution.py:652
  849.2 14.9 %collective-permute-start.40 = (bf16[128,768]{1,0:T(8,128)(2,1)S(1)}, bf16[128,768]{1,0:T(8,128)(2,1)S(1)}, u32[]{:S(2)}, u32[]{:S(2)}) collective-permute-start(bf16[128,768]{1,0:T(8,128)(2,1)S(1)} %constant_dynamic-slice_fusion.2), channel_id=1, source_target_pairs={{16,0},{17,1},{18,2},{19,3},{20,4},{21,5},{22,6},{23,7},{24,8},{25... | collective-permute-start | bytes 589832 | tf_op jit(solution)/shard_map/ppermute | solution.py:602
  864.0 3.2 collective-permute-start.24
  864.2 5.2 collective-permute-start.41
  864.9 9.9 %collective-permute-start.36 = (bf16[512,768]{1,0:T(8,128)(2,1)S(1)}, bf16[512,768]{1,0:T(8,128)(2,1)S(1)}, u32[]{:S(2)}, u32[]{:S(2)}) collective-permute-start(bf16[512,768]{1,0:T(8,128)(2,1)S(1)} %pad_maximum_fusion.3), channel_id=1, source_target_pairs={{2,0},{3,1},{0,2},{1,3},{6,4},{7,5},{4,6},{5,7},{10,8},{11,9},{8,1... | collective-permute-start | bytes 2359304 | tf_op jit(solution)/shard_map/ppermute | solution.py:602
  865.2 44.6 %collective-permute-start.22 = (bf16[1280,1024]{1,0:T(8,128)(2,1)S(1)}, bf16[1280,1024]{1,0:T(8,128)(2,1)}, u32[]{:S(2)}, u32[]{:S(2)}) collective-permute-start(bf16[1280,1024]{1,0:T(8,128)(2,1)S(1)} %copy-done.30), channel_id=1, source_target_pairs={{2,1},{1,2},{6,5},{5,6},{10,9},{9,10},{14,13},{13,14},{18,17},{17,... | collective-permute-start | bytes 7864328 | tf_op jit(solution)/shard_map/ppermute | solution.py:583
  867.3 4.7 collective-permute-start.25
  869.5 4.7 collective-permute-start.42
  872.0 4.8 collective-permute-start.26
  874.2 13.4 %collective-permute-start.43 = (bf16[128,768]{1,0:T(8,128)(2,1)S(1)}, bf16[128,768]{1,0:T(8,128)(2,1)S(1)}, u32[]{:S(2)}, u32[]{:S(2)}) collective-permute-start(bf16[128,768]{1,0:T(8,128)(2,1)S(1)} %pad_maximum_fusion.8), channel_id=1, source_target_pairs={{16,0},{17,1},{18,2},{19,3},{20,4},{21,5},{22,6},{23,7},{24,8},{25... | collective-permute-start | bytes 589832 | tf_op jit(solution)/shard_map/ppermute | solution.py:602
  876.8 28.9 %collective-permute-start.27 = (f32[16384]{0:T(1024)S(1)}, f32[16384]{0:T(1024)}, u32[]{:S(2)}, u32[]{:S(2)}) collective-permute-start(f32[16384]{0:T(1024)S(1)} %add.382), channel_id=1, source_target_pairs={{0,16},{1,17},{2,18},{3,19},{4,20},{5,21},{6,22},{7,23},{8,24},{9,... | collective-permute-start | bytes 196616 | tf_op jit(solution)/shard_map/ppermute | solution.py:652
  887.8 20.7 %collective-permute-start.44 = (bf16[256,768]{1,0:T(8,128)(2,1)S(1)}, bf16[256,768]{1,0:T(8,128)(2,1)}, u32[]{:S(2)}, u32[]{:S(2)}) collective-permute-start(bf16[256,768]{1,0:T(8,128)(2,1)S(1)} %pad_maximum_fusion.6), channel_id=1, source_target_pairs={{8,0},{9,1},{10,2},{11,3},{12,4},{13,5},{14,6},{15,7},{0,8},{1,9},... | collective-permute-start | bytes 1179656 | tf_op jit(solution)/shard_map/ppermute | solution.py:602
  909.7 2.8 collective-permute-start.45
  (74 other events, 795.0 us)
Sparse Core Ops, SparseCore 0:
  595.6 187.0 all-reduce.2

commit v8 on v7

--- a/solution.py
+++ b/solution.py
@@ -360,7 +360,7 @@
         input_output_aliases={5 + 2 * parts + n: n for n in range(len(begun))},
         compiler_params=pltpu.CompilerParams(vmem_limit_bytes=48 * 2**20),
         cost_estimate=pl.CostEstimate(
-            flops=4000 * tokens * tokens * (pairs - 1),
+            flops=2**10,
             bytes_accessed=2**10,
             transcendentals=0,
         ),
@@ -552,6 +552,42 @@
     )(d, weight)
 
 
+def spread_kernel(tab_ref, mine_ref, theirs_ref, out_ref):
+    mine = pl.program_id(1) == tab_ref[0]
+
+    def put(ref):
+        for c in range(3):
+            out_ref[c] = ref[:, c * PAIR : (c + 1) * PAIR].astype(F32)
+
+    @pl.when(mine)
+    def _():
+        put(mine_ref)
+
+    @pl.when(jnp.logical_not(mine))
+    def _():
+        put(theirs_ref)
+
+
+def spread(mine, theirs, side, out_pairs, first, begun):
+    half, columns = mine.shape
+    count = columns // (3 * PAIR)
+    block = pl.BlockSpec((half, 3 * PAIR), lambda k, s, t: (0, k))
+    return pl.pallas_call(
+        lambda tab, a, b, *refs: spread_kernel(tab, a, b, refs[-1]),
+        grid_spec=pltpu.PrefetchScalarGridSpec(
+            num_scalar_prefetch=1,
+            grid=(count, 2),
+            in_specs=[block, block] + [pl.BlockSpec(memory_space=pl.ANY)] * len(begun),
+            out_specs=pl.BlockSpec((3, half, PAIR), lambda k, s, t: (0, s, first + k)),
+        ),
+        out_shape=jax.ShapeDtypeStruct((3, 2 * half, out_pairs * PAIR), F32),
+        input_output_aliases={3 + n: n for n in range(len(begun))},
+        compiler_params=pltpu.CompilerParams(vmem_limit_bytes=32 * 2**20),
+        cost_estimate=pl.CostEstimate(flops=2**10, bytes_accessed=2**10, transcendentals=0),
+        name="spread",
+    )(jnp.reshape(side, (1,)).astype(jnp.int32), mine, theirs, *begun)
+
+
 def after(value, *others):
     return lax.optimization_barrier((value, *others))[0]
 
@@ -651,6 +687,10 @@
         for step in steps:
             value = value + lax.ppermute(value, self.axes, [(i, i ^ step) for i in range(devices)])
         return value
+
+    def sum_dp(self, value, turn):
+        order = [(i + turn) % self.dp for i in range(self.dp)]
+        return lax.psum(value, "dp", axis_index_groups=[order])
 
     def halved(self, value, bit):
         half, high = value.shape[0] // 2, self.side(bit)
@@ -749,8 +789,8 @@
     w_out_far = layout.send(after(w_out, tokens))
     w_up_far = layout.send(after(w_up, tokens))
     w_top_far = layout.send(after(w_down[:half], tokens))
-    w_low_far = layout.send(after(w_down[half:], w_up_far))
-    cotangent = layout.regroup(after(cotangent, w_top_far))
+    w_low_far = layout.send(after(w_down[half:], tokens))
+    cotangent = layout.regroup(after(cotangent, w_low_far))
 
     resid_in = tokens.astype(f32)
     norm1_out, normed1, inv1 = norm_parts(resid_in, ln1_gain, ln1_bias)
@@ -766,10 +806,12 @@
     begun = ()
     for pair in range(pairs):
         if pair and pair == pairs // 2:
-            tables, w_out_far, w_up_far = lax.optimization_barrier((tables, w_out_far, w_up_far))
+            tables, w_up_far = lax.optimization_barrier((tables, w_up_far))
         begun = attend_forward(qkv, seg, keep, tables, (pair, 1), begun)
     *context, context_turned, log_total = begun
-    *context, w_top_far = lax.optimization_barrier((*context, w_top_far))
+    *context, w_out_far, w_top_far, w_low_far = lax.optimization_barrier(
+        (*context, w_out_far, w_top_far, w_low_far)
+    )
     context = from_kernel(context, rank, shares)
     stays = layout.stays()
     w_out = jnp.where(stays, w_out, w_out_far)
@@ -810,41 +852,33 @@
     g_w_up_far = layout.send(g_w_up, True)
     grad_mid = upstream + norm_back(grad_a3, normed3, inv3, ln3_gain)
     grad_z = norm_back(grad_mid, normed2, inv2, ln2_gain).astype(bf16)
-    grad_z, g_w_down_far = lax.optimization_barrier((grad_z, g_w_down_far))
     grad_z_all = layout.gather(grad_z)
     grad_ctx = [contract_cols(g, w_out).astype(bf16) for g in grad_z_all]
     g_w_out = total([contract_rows(x, g) for x, g in zip(context, grad_z_all)]).astype(bf16)
     g_w_out_far = layout.send(g_w_out, True)
+    g_w_down_far, g_w_up, *grad_ctx = lax.optimization_barrier((g_w_down_far, g_w_up, *grad_ctx))
     grad_ctx, _ = for_kernel(grad_ctx, rank)
+    g_w_down = jnp.where(stays, g_w_down, g_w_down_far)
+    tables, g_w_down = lax.optimization_barrier((tables, g_w_down))
+    g_w_down = layout.sum_dp(g_w_down, 1)
+    calls = [(0, pairs // 2)] if pairs > 1 else []
+    calls += [(k, 1) for k in range(pairs // 2, pairs)]
     grad_qkv = ()
-    if pairs > 1:
+    for call in calls:
+        if call == calls[-1]:
+            g_w_up_far, g_w_out_far, *grad_qkv = lax.optimization_barrier(
+                (g_w_up_far, g_w_out_far, *grad_qkv)
+            )
+            g_w_up = jnp.where(stays, g_w_up, g_w_up_far)
+            g_w_out = jnp.where(stays, g_w_out, g_w_out_far)
+            tables, g_w_down, g_w_up, g_w_out = lax.optimization_barrier(
+                (tables, g_w_down, g_w_up, g_w_out)
+            )
+            g_w_up = layout.sum_dp(g_w_up, 0)
+            g_w_out = layout.sum_dp(g_w_out, 0)
         grad_qkv = attend_backward(
-            qkv, context_turned, grad_ctx, log_total, seg, keep, tables, (0, 1), grad_qkv
+            qkv, context_turned, grad_ctx, log_total, seg, keep, tables, call, grad_qkv
         )
-        g_w_up_far, g_w_out_far, *grad_qkv = lax.optimization_barrier(
-            (g_w_up_far, g_w_out_far, *grad_qkv)
-        )
-    g_w_down = jnp.where(stays, g_w_down, g_w_down_far)
-    g_w_up = jnp.where(stays, g_w_up, g_w_up_far)
-    g_w_out = jnp.where(stays, g_w_out, g_w_out_far)
-    tables, g_w_down, g_w_up, g_w_out = lax.optimization_barrier(
-        (tables, g_w_down, g_w_up, g_w_out)
-    )
-    g_w_down = lax.psum(g_w_down, "dp")
-    g_w_up = lax.psum(g_w_up, "dp")
-    g_w_out = lax.psum(g_w_out, "dp")
-    first = len(grad_qkv) and 1
-    grad_qkv = attend_backward(
-        qkv,
-        context_turned,
-        grad_ctx,
-        log_total,
-        seg,
-        keep,
-        tables,
-        (first, pairs - first),
-        grad_qkv,
-    )
     layer_out = layout.give_back(after(layer_out, g_w_out_far))
     grad_qkv = from_kernel(grad_qkv, rank, shares)
     grad_a1 = [input_grad(g, w_qkv) for g in grad_qkv]
@@ -854,22 +888,17 @@
     g_w_qkv, sums = [], []
     each = pairs // chunks
     for chunk in range(chunks):
-        if chunk == chunks - 1:
-            g_w_down, g_w_up, g_w_out, grad_input, *grad_qkv = lax.optimization_barrier(
-                (g_w_down, g_w_up, g_w_out, grad_input, *grad_qkv)
-            )
         g_part, part_sums = weight_grad(a1, grad_qkv, chunk * each, each)
         g_w_qkv.append(layout.halved(layout.give_back(g_part), -1))
         sums.append(part_sums)
     sums = jnp.concatenate(sums, 1)
     g_w_qkv = [layout.halved_by(g, layout.order(k)) for k, g in enumerate(g_w_qkv)]
-    g_w_qkv = [layout.joined_by(g, [-1, *layout.order(k)]) for k, g in enumerate(g_w_qkv)]
-    g_w_qkv = jnp.concatenate(g_w_qkv, 1).astype(f32)
-    g_w_qkv = (
-        g_w_qkv.reshape(model_dim, pairs, 3, PAIR)
-        .transpose(0, 2, 1, 3)
-        .reshape(model_dim, 3, width)
-    )
+    g_w_qkv = [layout.joined_by(g, layout.order(k)) for k, g in enumerate(g_w_qkv)]
+    begun = ()
+    for chunk, mine in enumerate(g_w_qkv):
+        theirs = layout.partner(mine, -1)
+        begun = (spread(mine, theirs, layout.side(-1), pairs, chunk * each, begun),)
+    g_w_qkv = begun[0].transpose(1, 0, 2)
     sums = sums.reshape(pairs, 3, PAIR).transpose(1, 0, 2).reshape(3, width)
     grad_input = layout.give_back(grad_input).astype(f32)
 

time: 943 us -> 761 us (0.81)
  waiting for transfers between devices: 226 us -> 152 us
  Pallas kernels: 279 us -> 228 us
  starting transfers between devices: 195 us -> 151 us
    psum x1 -> x2, waiting for transfers between devices: 156 us -> 95.1 us  [sum_dp(): return lax.psum(value, 'dp', axis_index_groups=[order])]
    ppermute x8, starting transfers between devices: 143 us -> 89.7 us  [to_rank(): return lax.ppermute(value, self.axes, moves)]
    pallas_call x2 -> x3, Pallas kernels: 111 us -> 76.7 us  [attend_backward(): pl.pallas_call(functools.partial(backward_kernel, parts), grid_spec=pltpu...]
    pallas_call x4, Pallas kernels: 72.8 us -> 50.6 us  [attend_forward(): pl.pallas_call(functools.partial(forward_kernel, parts), grid_spec=pltpu....]
    unnamed x154 -> x137, local copies, waits for them, and re-layouts: 30.1 us -> 24.3 us
  transfers between devices with their start and end apart: 47 -> 48, of which waited for: 14 -> 12; matrix products, arithmetic and copies ran while one was open for 15% -> 19% of each run, Pallas kernels for 17% -> 22%
where the time goes in v8:
time: 761 us; the launch traced here: 752 us
  Pallas kernels  228 us (30%)
  waiting for transfers between devices  152 us (20%)
  starting transfers between devices  151 us (20%)
  other arithmetic  107 us (14%)
  matrix products  54.9 us (7%)
  local copies, waits for them, and re-layouts  41.4 us (5%)
  between operations  17.7 us (2%)
    psum x2, waiting for transfers between devices, sum_dp(): return lax.psum(value, 'dp', axis_index_groups=[order])  95.1 us
    ppermute x8, starting transfers between devices, to_rank(): return lax.ppermute(value, self.axes, moves)  89.7 us
    pallas_call x3, Pallas kernels, attend_backward(): pl.pallas_call(functools.partial(backward_kernel, parts), grid_spec=pltpu...  76.7 us
    pallas_call x4, Pallas kernels, attend_forward(): pl.pallas_call(functools.partial(forward_kernel, parts), grid_spec=pltpu....  50.6 us
    ppermute x18, waiting for transfers between devices, partner(): return lax.ppermute(value, self.axes, moves)  37 us
    pallas_call x2, Pallas kernels, feed_forward(): pl.pallas_call(functools.partial(feed_kernel, min(units, FEED)), grid=(st...  35.6 us
    dot_general x4, matrix products, contract_rows(): lax.dot_general(left, right, (((0,), (0,)), ((), ())), preferred_element_...  35.1 us
    pallas_call x2, Pallas kernels, feed_back(): pl.pallas_call(functools.partial(feed_back_kernel, min(units, FEED)), gri...  32 us
  transfers between devices with their start and end apart: 48, of which 12 were waited for; matrix products, arithmetic and copies ran while one was open for 19% of the time, Pallas kernels for 22%

profile of v8, /device:TPU:0, one launch (start us, length us, event | category | flops | bytes accessed | tf_op | source)
XLA Modules:
  0.0 752.0 jit_solution(16339950794976433434)
XLA Ops:
  16.9 4.7 fusion.52
  34.6 38.5 %collective-permute-start.6 = (bf16[1280,1024]{1,0:T(8,128)(2,1)S(1)}, bf16[1280,1024]{1,0:T(8,128)(2,1)}, u32[]{:S(2)}, u32[]{:S(2)}) collective-permute-start(bf16[1280,1024]{1,0:T(8,128)(2,1)S(1)} %fusion.14.refs_0_), channel_id=1, source_target_pairs={{0,2},{2,0},{1,3},{3,1},{4,6},{6,4},{5,7},{7,5},{8,10},{10,8},{9,1... | collective-permute-start | bytes 7864328 | tf_op jit(solution)/shard_map/ppermute | solution.py:669
  84.4 4.5 fusion.2.refs_0_
  89.0 7.8 %fusion.3.refs_1_ = bf16[1280,1536]{1,0:T(8,128)(2,1)S(1)} fusion(bf16[1280,1024]{1,0:T(8,128)(2,1)} %collective-permute-done.6.refs_1_, bf16[1024,1536]{0,1:T(8,128)(2,1)S(1)} %bitcast.60, f32[1536]{0:T(1024)S(1)} %copy-done.60, f32[1536]{0:T(1024)S(1)} %add.349), kind=kOutput, calls=%fused_computation.12 | convolution fusion | flops 4032430080 | bytes 9711616 | tf_op jit(solution)/shard_map/dot_general | solution.py:57
  96.7 12.5 %attend_forward.4 = (bf16[1280,512]{1,0:T(8,128)(2,1)S(1)}, bf16[1280,512]{1,0:T(8,128)(2,1)S(1)}, bf16[512,2560]{1,0:T(8,128)(2,1)S(1)}, f32[4,2,2560]{2,1,0:T(2,128)S(1)}) custom-call(s32[3,10]{1,0:T(4,128)S(1)} %add_add_fusion.2.tab_ref, s32[2560,1]{1,0:T(8,128)S(1)} %copy-done.6, s32[1,2560]{1,0:T(1,128)S(1)} %fusion.45.qseg_ref, ...), custom_call_target="tpu_custom_call" | custom-call | flops 1024 | bytes 1024 | tf_op jit(solution)/shard_map/attend_forward/pallas_call | solution.py:301
  109.3 12.5 %attend_forward.5 = (bf16[1280,512]{1,0:T(8,128)(2,1)S(1)}, bf16[1280,512]{1,0:T(8,128)(2,1)S(1)}, bf16[512,2560]{1,0:T(8,128)(2,1)S(1)}, f32[4,2,2560]{2,1,0:T(2,128)S(1)}) custom-call(s32[3,10]{1,0:T(4,128)S(1)} %add_add_fusion.2.tab_ref, s32[2560,1]{1,0:T(8,128)S(1)} %copy-done.6, ...), custom_call_target="tpu_custom_call", output_to_operand_aliasing={{0}: (5, {}), {1}: (6, {}), {2}: (7, {}), {3}: (8, {})} | custom-call | flops 1024 | bytes 1024 | tf_op jit(solution)/shard_map/attend_forward/pallas_call | solution.py:301
  121.8 12.5 %attend_forward.6 = (bf16[1280,512]{1,0:T(8,128)(2,1)S(1)}, bf16[1280,512]{1,0:T(8,128)(2,1)S(1)}, bf16[512,2560]{1,0:T(8,128)(2,1)S(1)}, f32[4,2,2560]{2,1,0:T(2,128)S(1)}) custom-call(s32[3,10]{1,0:T(4,128)S(1)} %add_add_fusion.2.tab_ref, s32[2560,1]{1,0:T(8,128)S(1)} %copy-done.6, ...), custom_call_target="tpu_custom_call", output_to_operand_aliasing={{0}: (5, {}), {1}: (6, {}), {2}: (7, {}), {3}: (8, {})} | custom-call | flops 1024 | bytes 1024 | tf_op jit(solution)/shard_map/attend_forward/pallas_call | solution.py:301
  134.4 13.0 %attend_forward.7 = (bf16[1280,512]{1,0:T(8,128)(2,1)S(1)}, bf16[1280,512]{1,0:T(8,128)(2,1)S(1)}, bf16[512,2560]{1,0:T(8,128)(2,1)S(1)}, f32[4,2,2560]{2,1,0:T(2,128)S(1)}) custom-call(s32[3,10]{1,0:T(4,128)S(1)} %add_add_fusion.2.tab_ref, s32[2560,1]{1,0:T(8,128)S(1)} %copy-done.6, ...), custom_call_target="tpu_custom_call", output_to_operand_aliasing={{0}: (5, {}), {1}: (6, {}), {2}: (7, {}), {3}: (8, {})} | custom-call | flops 1024 | bytes 1024 | tf_op jit(solution)/shard_map/attend_forward/pallas_call | solution.py:301
  152.5 25.4 %collective-permute-start.10 = (bf16[1280,1024]{1,0:T(8,128)(2,1)S(1)}, bf16[1280,1024]{1,0:T(8,128)(2,1)S(1)}, u32[]{:S(2)}, u32[]{:S(2)}) collective-permute-start(bf16[1280,1024]{1,0:T(8,128)(2,1)S(1)} %convolution_convert_fusion.1), channel_id=1, source_target_pairs={{0,2},{2,0},{1,3},{3,1},{4,6},{6,4},{5,7},{7,5},{8,10},{10,8},{9,1... | collective-permute-start | bytes 7864328 | tf_op jit(solution)/shard_map/ppermute | solution.py:669
  178.9 4.6 broadcast_select_fusion.2.up_ref
  194.8 4.4 collective-permute-start.11
  199.2 3.7 maximum_select_fusion.down_ref
  203.3 17.7 %feed_forward.2 = (bf16[2560,1024]{1,0:T(8,128)(2,1)}, bf16[2560,2048]{1,0:T(8,128)(2,1)}, bf16[2560,2048]{1,0:T(8,128)(2,1)}, bf16[1280,1024]{1,0:T(8,128)(2,1)S(1)}) custom-call(bf16[1280,1024]{1,0:T(8,128)(2,1)S(1)} %add_convert_fusion.1.x_ref, bf16[1024,2048]{1,0:T(8,128)(2,1)} %broadcast_select_fusion.2.up_ref, f32[1,2048]{1,0:T(1,128)S(1)} %bitcast.52, ...), custom_call_target="tpu_custom_call" | custom-call | flops 16106127360 | bytes 16777216 | tf_op jit(solution)/shard_map/feed_forward/pallas_call | solution.py:411
  221.1 17.8 %feed_forward.3 = (bf16[2560,1024]{1,0:T(8,128)(2,1)}, bf16[2560,2048]{1,0:T(8,128)(2,1)}, bf16[2560,2048]{1,0:T(8,128)(2,1)}, bf16[1280,1024]{1,0:T(8,128)(2,1)S(1)}) custom-call(bf16[1280,1024]{1,0:T(8,128)(2,1)S(1)} %collective-permute-done.11.x_ref, ...), custom_call_target="tpu_custom_call", output_to_operand_aliasing={{0}: (4, {}), {1}: (5, {}), {2}: (6, {})} | custom-call | flops 16106127360 | bytes 16777216 | tf_op jit(solution)/shard_map/feed_forward/pallas_call | solution.py:411
  238.9 9.5 %collective-permute-start.13 = (bf16[1280,1024]{1,0:T(8,128)(2,1)S(1)}, bf16[1280,1024]{1,0:T(8,128)(2,1)S(1)}, u32[]{:S(2)}, u32[]{:S(2)}) collective-permute-start(bf16[1280,1024]{1,0:T(8,128)(2,1)S(1)} %get-tuple-element.124), channel_id=1, source_target_pairs={{0,2},{2,0},{1,3},{3,1},{4,6},{6,4},{5,7},{7,5},{8,10},{10,8},{9,1... | collective-permute-start | bytes 7864328 | tf_op jit(solution)/shard_map/ppermute | solution.py:669
  248.4 4.5 collective-permute-done.13
  255.2 3.6 fusion.26
  258.9 4.9 convert_reduce_fusion.2
  264.1 15.9 %feed_back.2 = (bf16[2560,2048]{1,0:T(8,128)(2,1)}, f32[1,2048]{1,0:T(1,128)S(1)}, bf16[1280,1024]{1,0:T(8,128)(2,1)S(1)}) custom-call(bf16[1280,1024]{1,0:T(8,128)(2,1)S(1)} %get-tuple-element.183.g_ref, bf16[2560,2048]{1,0:T(8,128)(2,1)} %get-tuple-element.129.slope_ref, bf16[2048,1024]{1,0:T(8,128)(2,1)} %maximum_select_fusion.down_ref, ...), custom_call_target="tpu_custom_call" | custom-call | flops 1024 | bytes 1024 | tf_op jit(solution)/shard_map/feed_back/pallas_call | solution.py:473
  280.1 15.3 %fusion.38 = bf16[2048,1024]{1,0:T(8,128)(2,1)} fusion(bf16[2560,2048]{1,0:T(8,128)(2,1)} %get-tuple-element.127, bf16[1280,1024]{1,0:T(8,128)(2,1)S(1)} %collective-permute-done.14.g_ref, bf16[1280,1024]{1,0:T(8,128)(2,1)S(1)} %get-tuple-element.183.g_ref), kind=kOutput, calls=%fused_computation.72 | convolution fusion | flops 10750001152 | bytes 19922944 | tf_op jit(solution)/shard_map/dot_general | solution.py:35
  295.3 16.1 %feed_back.3 = (bf16[2560,2048]{1,0:T(8,128)(2,1)}, f32[1,2048]{1,0:T(1,128)S(1)}, bf16[1280,1024]{1,0:T(8,128)(2,1)S(1)}) custom-call(bf16[1280,1024]{1,0:T(8,128)(2,1)S(1)} %collective-permute-done.14.g_ref, bf16[2560,2048]{1,0:T(8,128)(2,1)} %get-tuple-element.129.slope_ref, ...), custom_call_target="tpu_custom_call", output_to_operand_aliasing={{0}: (4, {})} | custom-call | flops 1024 | bytes 1024 | tf_op jit(solution)/shard_map/feed_back/pallas_call | solution.py:473
  316.4 4.9 multiply_reduce_fusion
  321.4 8.1 %multiply_reduce_fusion.1 = (f32[1024]{0:T(1024)S(1)}, f32[1280]{0:T(1024)S(1)}, f32[1280]{0:T(1024)S(1)}, f32[1024]{0:T(1024)S(1)}, f32[1280,1024]{1,0:T(8,128)S(1)}) fusion(f32[1280,1024]{1,0:T(8,128)} %copy-done.18, f32[1280]{0:T(1024)S(1)} %add_rsqrt_fusion.2, f32[1280]{0:T(1024)S(1)} %broadcast_multiply_fusion.10, f32[1024]{0:T(1024)S(1)} %copy-done.46, ...), kind=kLoop, calls=%fused_computation.42 | loop fusion | flops 27520512 | bytes 23650304 | tf_op jit(solution)/shard_map/reduce_sum | solution.py:910
  332.0 15.7 %convolution_convert_fusion = bf16[1024,2048]{1,0:T(8,128)(2,1)} fusion(bf16[2560,1024]{1,0:T(8,128)(2,1)S(1)} %bitcast.82, bf16[2560,2048]{1,0:T(8,128)(2,1)} %get-tuple-element.131), kind=kOutput, calls=%fused_computation.71 | convolution fusion | flops 10739515392 | bytes 19922944 | tf_op jit(solution)/shard_map/dot_general | solution.py:35
  365.8 36.6 %attend_backward.3 = (bf16[1280,1536]{1,0:T(8,128)(2,1)}, bf16[1280,1536]{1,0:T(8,128)(2,1)}) custom-call(s32[3,10]{1,0:T(4,128)S(1)} %add_add_fusion.2.tab_ref, s32[2560,1]{1,0:T(8,128)S(1)} %copy-done.7, s32[1,2560]{1,0:T(1,128)S(1)} %fusion.45.qseg_ref, bf16[1280,1536]{1,0:T(8,128)(2,1)} %copy-done, bf16[1280,1536]{1,0:T(8,128)(2,1)} %copy-done.1, ...), custom_call_target="tpu_custom_call" | custom-call | flops 1024 | bytes 1024 | tf_op jit(solution)/shard_map/attend_backward/pallas_call | solution.py:335
  402.5 20.0 %attend_backward.4 = (bf16[1280,1536]{1,0:T(8,128)(2,1)}, bf16[1280,1536]{1,0:T(8,128)(2,1)}) custom-call(s32[3,10]{1,0:T(4,128)S(1)} %add_add_fusion.2.tab_ref, s32[2560,1]{1,0:T(8,128)S(1)} %copy-done.7, s32[1,2560]{1,0:T(1,128)S(1)} %fusion.45.qseg_ref, bf16[1280,1536]{1,0:T(8,128)(2,1)} %copy-done, ...), custom_call_target="tpu_custom_call", output_to_operand_aliasing={{0}: (9, {}), {1}: (10, {})} | custom-call | flops 1024 | bytes 1024 | tf_op jit(solution)/shard_map/attend_backward/pallas_call | solution.py:335
  424.8 4.6 broadcast_select_fusion.1
  429.4 50.7 %all-reduce.4.cloned.1.call-done = bf16[2048,1024]{1,0:T(8,128)(2,1)} async-done(((bf16[2048,1024]{1,0:T(8,128)(2,1)}), bf16[2048,1024]{1,0:T(8,128)(2,1)}) %all-reduce.4.cloned.1.call-update) | async-done | bytes 4194320 | tf_op jit(solution)/shard_map/psum | solution.py:693
  481.4 20.1 %attend_backward.5 = (bf16[1280,1536]{1,0:T(8,128)(2,1)}, bf16[1280,1536]{1,0:T(8,128)(2,1)}) custom-call(s32[3,10]{1,0:T(4,128)S(1)} %add_add_fusion.2.tab_ref, s32[2560,1]{1,0:T(8,128)S(1)} %copy-done.7, s32[1,2560]{1,0:T(1,128)S(1)} %fusion.45.qseg_ref, bf16[1280,1536]{1,0:T(8,128)(2,1)} %copy-done, ...), custom_call_target="tpu_custom_call", output_to_operand_aliasing={{0}: (9, {}), {1}: (10, {})} | custom-call | flops 1024 | bytes 1024 | tf_op jit(solution)/shard_map/attend_backward/pallas_call | solution.py:335
  503.6 9.1 %weight_grad.3 = (bf16[1024,768]{1,0:T(8,128)(2,1)}, f32[1,768]{1,0:T(1,128)S(1)}) custom-call(bf16[1280,1024]{1,0:T(8,128)(2,1)S(1)} %copy-done.9, bf16[1280,1024]{1,0:T(8,128)(2,1)} %collective-permute-done.6.refs_1_, bf16[1280,1536]{1,0:T(8,128)(2,1)S(1)} %copy-done.2, bf16[1280,1536]{1,0:T(8,128)(2,1)} %get-tuple-element.154.d_ref.refs_3_), custom_call_target="tpu_custom_call" | custom-call | flops 1024 | bytes 1024 | tf_op jit(solution)/shard_map/weight_grad/pallas_call | solution.py:513
  514.6 9.0 %weight_grad.2 = (bf16[1024,768]{1,0:T(8,128)(2,1)}, f32[1,768]{1,0:T(1,128)S(1)}) custom-call(bf16[1280,1024]{1,0:T(8,128)(2,1)S(1)} %copy-done.9, bf16[1280,1024]{1,0:T(8,128)(2,1)} %collective-permute-done.6.refs_1_, bf16[1280,1536]{1,0:T(8,128)(2,1)S(1)} %copy-done.2, bf16[1280,1536]{1,0:T(8,128)(2,1)} %get-tuple-element.154.d_ref.refs_3_), custom_call_target="tpu_custom_call" | custom-call | flops 1024 | bytes 1024 | tf_op jit(solution)/shard_map/weight_grad/pallas_call | solution.py:513
  530.7 5.5 input_grad.3
  536.2 11.1 %collective-permute-start.21 = (bf16[1280,1024]{1,0:T(8,128)(2,1)}, bf16[1280,1024]{1,0:T(8,128)(2,1)}, u32[]{:S(2)}, u32[]{:S(2)}) collective-permute-start(bf16[1280,1024]{1,0:T(8,128)(2,1)} %input_grad.3), channel_id=1, source_target_pairs={{0,2},{2,0},{1,3},{3,1},{4,6},{6,4},{5,7},{7,5},{8,10},{10,8},{9,1... | collective-permute-start | bytes 7864328 | tf_op jit(solution)/shard_map/ppermute | solution.py:669
  554.0 10.5 %collective-permute-start.38 = (bf16[512,768]{1,0:T(8,128)(2,1)}, bf16[512,768]{1,0:T(8,128)(2,1)}, u32[]{:S(2)}, u32[]{:S(2)}) collective-permute-start(bf16[512,768]{1,0:T(8,128)(2,1)} %constant_dynamic-slice_fusion.4), channel_id=1, source_target_pairs={{2,0},{3,1},{0,2},{1,3},{6,4},{7,5},{4,6},{5,7},{10,8},{11,9},{8,1... | collective-permute-start | bytes 2359304 | tf_op jit(solution)/shard_map/ppermute | solution.py:638
  569.2 4.7 input_grad.2
  582.4 5.3 fusion.20
  591.2 8.5 %collective-permute-done.23 = f32[16384]{0:T(1024)S(1)} collective-permute-done((f32[16384]{0:T(1024)S(1)}, f32[16384]{0:T(1024)S(1)}, u32[]{:S(2)}, u32[]{:S(2)}) %collective-permute-start.23) | collective-permute-done | bytes 65568 | tf_op jit(solution)/shard_map/ppermute | solution.py:688
  599.8 6.6 fusion.19
  614.3 12.3 %collective-permute-done.31 = bf16[128,768]{1,0:T(8,128)(2,1)S(1)} collective-permute-done((bf16[128,768]{1,0:T(8,128)(2,1)S(1)}, bf16[128,768]{1,0:T(8,128)(2,1)S(1)}, u32[]{:S(2)}, u32[]{:S(2)}) %collective-permute-start.31) | collective-permute-done | bytes 196640 | tf_op jit(solution)/shard_map/ppermute | solution.py:638
  628.6 3.4 collective-permute-start.41
  633.4 3.5 collective-permute-done.41
  640.1 10.6 %collective-permute-done.42 = bf16[64,768]{1,0:T(8,128)(2,1)S(1)} collective-permute-done((bf16[64,768]{1,0:T(8,128)(2,1)S(1)}, bf16[64,768]{1,0:T(8,128)(2,1)S(1)}, u32[]{:S(2)}, u32[]{:S(2)}) %collective-permute-start.42) | collective-permute-done | bytes 98336 | tf_op jit(solution)/shard_map/ppermute | solution.py:638
  650.9 7.6 %collective-permute-done.34 = bf16[128,768]{1,0:T(8,128)(2,1)S(1)} collective-permute-done((bf16[128,768]{1,0:T(8,128)(2,1)S(1)}, bf16[128,768]{1,0:T(8,128)(2,1)S(1)}, u32[]{:S(2)}, u32[]{:S(2)}) %collective-permute-start.34) | collective-permute-done | bytes 196640 | tf_op jit(solution)/shard_map/ppermute | solution.py:638
  664.2 6.8 convert_element_type.231
  671.0 5.0 collective-permute-done.26
  679.9 44.4 %all-reduce.6.cloned.1.call-done = (bf16[512,1024]{1,0:T(8,128)(2,1)}, bf16[1024,2048]{1,0:T(8,128)(2,1)}) async-done(((bf16[512,1024]{1,0:T(8,128)(2,1)}, bf16[1024,2048]{1,0:T(8,128)(2,1)}), (bf16[512,1024]{1,0:T(8,128)(2,1)}, bf16[1024,2048]{1,0:T(8,128)(2,1)})) %all-reduce.6.cloned.1.call-update) | async-done | bytes 5242896 | tf_op jit(solution)/shard_map/psum | solution.py:693
  727.1 6.7 convert_element_type.230
  740.2 4.4 select_convert_fusion
  (339 shorter events, 148.8 us)
Async XLA Ops:
  7.2 472.8 %all-reduce.4.cloned.1.call-start = ((), (), s32[]{:S(2)}) async-start(), calls=%async_computation | async-start | bytes 8388608 | tf_op jit(solution)/shard_map/psum | solution.py:693
  10.7 0.8 collective-permute-start
  12.4 0.7 collective-permute-start.1
  13.1 15.6 %collective-permute-start.2 = (bf16[1280,1024]{1,0:T(8,128)(2,1)}, bf16[1280,1024]{1,0:T(8,128)(2,1)}, u32[]{:S(2)}, u32[]{:S(2)}) collective-permute-start(bf16[1280,1024]{1,0:T(8,128)(2,1)} %param.20), channel_id=1, source_target_pairs={{1,2},{2,1},{5,6},{6,5},{9,10},{10,9},{13,14},{14,13},{17,18},{18,... | collective-permute-start | bytes 7864328 | tf_op jit(solution)/shard_map/ppermute | solution.py:619
  15.3 8.5 %collective-permute-start.4 = (bf16[256,3,512]{0,2,1:T(8,128)(2,1)}, bf16[256,3,512]{0,2,1:T(8,128)(2,1)}, u32[]{:S(2)}, u32[]{:S(2)}) collective-permute-start(bf16[256,3,512]{0,2,1:T(8,128)(2,1)} %copy-done.40), channel_id=1, source_target_pairs={{9,1},{10,2},{13,5},{14,6},{1,9},{2,10},{5,13},{6,14},{25,17},{26,... | collective-permute-start | bytes 2359304 | tf_op jit(solution)/shard_map/ppermute | solution.py:638
  26.7 49.5 %collective-permute-start.5 = (bf16[512,3,512]{0,2,1:T(8,128)(2,1)}, bf16[512,3,512]{0,2,1:T(8,128)(2,1)}, u32[]{:S(2)}, u32[]{:S(2)}) collective-permute-start(bf16[512,3,512]{0,2,1:T(8,128)(2,1)} %pad_maximum_fusion), channel_id=1, source_target_pairs={{5,1},{6,2},{1,5},{2,6},{13,9},{14,10},{9,13},{10,14},{21,17},{22,... | collective-permute-start | bytes 4718600 | tf_op jit(solution)/shard_map/ppermute | solution.py:638
  29.6 92.2 %collective-permute-start.3 = (bf16[1024,2048]{1,0:T(8,128)(2,1)}, bf16[1024,2048]{1,0:T(8,128)(2,1)}, u32[]{:S(2)}, u32[]{:S(2)}) collective-permute-start(bf16[1024,2048]{1,0:T(8,128)(2,1)} %param.31), channel_id=1, source_target_pairs={{1,2},{2,1},{5,6},{6,5},{9,10},{10,9},{13,14},{14,13},{17,18},{18,... | collective-permute-start | bytes 12582920 | tf_op jit(solution)/shard_map/ppermute | solution.py:619
  34.6 54.3 %collective-permute-start.6 = (bf16[1280,1024]{1,0:T(8,128)(2,1)S(1)}, bf16[1280,1024]{1,0:T(8,128)(2,1)}, u32[]{:S(2)}, u32[]{:S(2)}) collective-permute-start(bf16[1280,1024]{1,0:T(8,128)(2,1)S(1)} %fusion.14.refs_0_), channel_id=1, source_target_pairs={{0,2},{2,0},{1,3},{3,1},{4,6},{6,4},{5,7},{7,5},{8,10},{10,8},{9,1... | collective-permute-start | bytes 7864328 | tf_op jit(solution)/shard_map/ppermute | solution.py:669
  78.9 68.5 %collective-permute-start.8 = (bf16[1024,1024]{1,0:T(8,128)(2,1)}, bf16[1024,1024]{1,0:T(8,128)(2,1)S(1)}, u32[]{:S(2)}, u32[]{:S(2)}) collective-permute-start(bf16[1024,1024]{1,0:T(8,128)(2,1)} %get-tuple-element.110), channel_id=1, source_target_pairs={{1,2},{2,1},{5,6},{6,5},{9,10},{10,9},{13,14},{14,13},{17,18},{18,... | collective-permute-start | bytes 6291464 | tf_op jit(solution)/shard_map/ppermute | solution.py:619
  79.7 67.7 %collective-permute-start.9 = (bf16[1024,1024]{1,0:T(8,128)(2,1)S(1)}, bf16[1024,1024]{1,0:T(8,128)(2,1)S(1)}, u32[]{:S(2)}, u32[]{:S(2)}) collective-permute-start(bf16[1024,1024]{1,0:T(8,128)(2,1)S(1)} %copy-done.37), channel_id=1, source_target_pairs={{1,2},{2,1},{5,6},{6,5},{9,10},{10,9},{13,14},{14,13},{17,18},{18,... | collective-permute-start | bytes 6291464 | tf_op jit(solution)/shard_map/ppermute | solution.py:619
  82.2 65.2 %collective-permute-start.7 = (bf16[512,1024]{1,0:T(8,128)(2,1)}, bf16[512,1024]{1,0:T(8,128)(2,1)}, u32[]{:S(2)}, u32[]{:S(2)}) collective-permute-start(bf16[512,1024]{1,0:T(8,128)(2,1)} %param.25), channel_id=1, source_target_pairs={{1,2},{2,1},{5,6},{6,5},{9,10},{10,9},{13,14},{14,13},{17,18},{18,... | collective-permute-start | bytes 3145736 | tf_op jit(solution)/shard_map/ppermute | solution.py:619
  152.5 31.0 %collective-permute-start.10 = (bf16[1280,1024]{1,0:T(8,128)(2,1)S(1)}, bf16[1280,1024]{1,0:T(8,128)(2,1)S(1)}, u32[]{:S(2)}, u32[]{:S(2)}) collective-permute-start(bf16[1280,1024]{1,0:T(8,128)(2,1)S(1)} %convolution_convert_fusion.1), channel_id=1, source_target_pairs={{0,2},{2,0},{1,3},{3,1},{4,6},{6,4},{5,7},{7,5},{8,10},{10,8},{9,1... | collective-permute-start | bytes 7864328 | tf_op jit(solution)/shard_map/ppermute | solution.py:669
  177.9 25.0 %collective-permute-start.12 = (bf16[1280,1024]{1,0:T(8,128)(2,1)S(1)}, bf16[1280,1024]{1,0:T(8,128)(2,1)S(1)}, u32[]{:S(2)}, u32[]{:S(2)}) collective-permute-start(bf16[1280,1024]{1,0:T(8,128)(2,1)S(1)} %copy-done.32), channel_id=1, source_target_pairs={{1,2},{2,1},{5,6},{6,5},{9,10},{10,9},{13,14},{14,13},{17,18},{18,... | collective-permute-start | bytes 7864328 | tf_op jit(solution)/shard_map/ppermute | solution.py:619
  194.8 26.2 %collective-permute-start.11 = (bf16[1280,1024]{1,0:T(8,128)(2,1)S(1)}, bf16[1280,1024]{1,0:T(8,128)(2,1)S(1)}, u32[]{:S(2)}, u32[]{:S(2)}) collective-permute-start(bf16[1280,1024]{1,0:T(8,128)(2,1)S(1)} %add_convert_fusion.1.x_ref), channel_id=1, source_target_pairs={{0,2},{2,0},{1,3},{3,1},{4,6},{6,4},{5,7},{7,5},{8,10},{10,8},{9,1... | collective-permute-start | bytes 7864328 | tf_op jit(solution)/shard_map/ppermute | solution.py:669
  238.9 14.1 %collective-permute-start.13 = (bf16[1280,1024]{1,0:T(8,128)(2,1)S(1)}, bf16[1280,1024]{1,0:T(8,128)(2,1)S(1)}, u32[]{:S(2)}, u32[]{:S(2)}) collective-permute-start(bf16[1280,1024]{1,0:T(8,128)(2,1)S(1)} %get-tuple-element.124), channel_id=1, source_target_pairs={{0,2},{2,0},{1,3},{3,1},{4,6},{6,4},{5,7},{7,5},{8,10},{10,8},{9,1... | collective-permute-start | bytes 7864328 | tf_op jit(solution)/shard_map/ppermute | solution.py:669
  263.8 16.3 %collective-permute-start.14 = (bf16[1280,1024]{1,0:T(8,128)(2,1)S(1)}, bf16[1280,1024]{1,0:T(8,128)(2,1)S(1)}, u32[]{:S(2)}, u32[]{:S(2)}) collective-permute-start(bf16[1280,1024]{1,0:T(8,128)(2,1)S(1)} %get-tuple-element.183.g_ref), channel_id=1, source_target_pairs={{0,2},{2,0},{1,3},{3,1},{4,6},{6,4},{5,7},{7,5},{8,10},{10,8},{9,1... | collective-permute-start | bytes 7864328 | tf_op jit(solution)/shard_map/ppermute | solution.py:669
  311.4 5.0 collective-permute-start.16
  311.7 49.0 %collective-permute-start.19 = (bf16[2048,1024]{1,0:T(8,128)(2,1)}, bf16[2048,1024]{1,0:T(8,128)(2,1)}, u32[]{:S(2)}, u32[]{:S(2)}) collective-permute-start(bf16[2048,1024]{1,0:T(8,128)(2,1)} %fusion.38), channel_id=1, source_target_pairs={{2,1},{1,2},{6,5},{5,6},{10,9},{9,10},{14,13},{13,14},{18,17},{17,... | collective-permute-start | bytes 12582920 | tf_op jit(solution)/shard_map/ppermute | solution.py:619
  331.8 20.3 %collective-permute-start.17 = (bf16[1280,1024]{1,0:T(8,128)(2,1)S(1)}, bf16[1280,1024]{1,0:T(8,128)(2,1)S(1)}, u32[]{:S(2)}, u32[]{:S(2)}) collective-permute-start(bf16[1280,1024]{1,0:T(8,128)(2,1)S(1)} %get-tuple-element.185), channel_id=1, source_target_pairs={{0,2},{2,0},{1,3},{3,1},{4,6},{6,4},{5,7},{7,5},{8,10},{10,8},{9,1... | collective-permute-start | bytes 7864328 | tf_op jit(solution)/shard_map/ppermute | solution.py:669
  347.7 74.7 %collective-permute-start.15 = (bf16[1024,2048]{1,0:T(8,128)(2,1)}, bf16[1024,2048]{1,0:T(8,128)(2,1)}, u32[]{:S(2)}, u32[]{:S(2)}) collective-permute-start(bf16[1024,2048]{1,0:T(8,128)(2,1)} %convolution_convert_fusion), channel_id=1, source_target_pairs={{2,1},{1,2},{6,5},{5,6},{10,9},{9,10},{14,13},{13,14},{18,17},{17,... | collective-permute-start | bytes 12582920 | tf_op jit(solution)/shard_map/ppermute | solution.py:619
  356.2 66.2 %collective-permute-start.18 = (bf16[512,1024]{1,0:T(8,128)(2,1)}, bf16[512,1024]{1,0:T(8,128)(2,1)}, u32[]{:S(2)}, u32[]{:S(2)}) collective-permute-start(bf16[512,1024]{1,0:T(8,128)(2,1)} %add_convert_fusion.2), channel_id=1, source_target_pairs={{2,1},{1,2},{6,5},{5,6},{10,9},{9,10},{14,13},{13,14},{18,17},{17,... | collective-permute-start | bytes 3145736 | tf_op jit(solution)/shard_map/ppermute | solution.py:619
  363.2 361.1 %all-reduce.6.cloned.1.call-start = ((), (), s32[]{:S(2)}) async-start(), calls=%async_computation.1 | async-start | bytes 10485760 | tf_op jit(solution)/shard_map/psum | solution.py:693
  512.8 34.6 %collective-permute-start.28 = (bf16[1024,768]{1,0:T(8,128)(2,1)}, bf16[1024,768]{1,0:T(8,128)(2,1)}, u32[]{:S(2)}, u32[]{:S(2)}) collective-permute-start(bf16[1024,768]{1,0:T(8,128)(2,1)} %get-tuple-element.159), channel_id=1, source_target_pairs={{2,1},{1,2},{6,5},{5,6},{10,9},{9,10},{14,13},{13,14},{18,17},{17,... | collective-permute-start | bytes 4718600 | tf_op jit(solution)/shard_map/ppermute | solution.py:619
  523.5 26.8 %collective-permute-start.37 = (bf16[1024,768]{1,0:T(8,128)(2,1)}, bf16[1024,768]{1,0:T(8,128)(2,1)}, u32[]{:S(2)}, u32[]{:S(2)}) collective-permute-start(bf16[1024,768]{1,0:T(8,128)(2,1)} %get-tuple-element.160), channel_id=1, source_target_pairs={{2,1},{1,2},{6,5},{5,6},{10,9},{9,10},{14,13},{13,14},{18,17},{17,... | collective-permute-start | bytes 4718600 | tf_op jit(solution)/shard_map/ppermute | solution.py:619
  536.2 46.1 %collective-permute-start.21 = (bf16[1280,1024]{1,0:T(8,128)(2,1)}, bf16[1280,1024]{1,0:T(8,128)(2,1)}, u32[]{:S(2)}, u32[]{:S(2)}) collective-permute-start(bf16[1280,1024]{1,0:T(8,128)(2,1)} %input_grad.3), channel_id=1, source_target_pairs={{0,2},{2,0},{1,3},{3,1},{4,6},{6,4},{5,7},{7,5},{8,10},{10,8},{9,1... | collective-permute-start | bytes 7864328 | tf_op jit(solution)/shard_map/ppermute | solution.py:669
  549.9 25.7 %collective-permute-start.29 = (bf16[512,768]{1,0:T(8,128)(2,1)}, bf16[512,768]{1,0:T(8,128)(2,1)}, u32[]{:S(2)}, u32[]{:S(2)}) collective-permute-start(bf16[512,768]{1,0:T(8,128)(2,1)} %constant_dynamic-slice_fusion.8), channel_id=1, source_target_pairs={{2,0},{3,1},{0,2},{1,3},{6,4},{7,5},{4,6},{5,7},{10,8},{11,9},{8,1... | collective-permute-start | bytes 2359304 | tf_op jit(solution)/shard_map/ppermute | solution.py:638
  554.0 24.3 %collective-permute-start.38 = (bf16[512,768]{1,0:T(8,128)(2,1)}, bf16[512,768]{1,0:T(8,128)(2,1)}, u32[]{:S(2)}, u32[]{:S(2)}) collective-permute-start(bf16[512,768]{1,0:T(8,128)(2,1)} %constant_dynamic-slice_fusion.4), channel_id=1, source_target_pairs={{2,0},{3,1},{0,2},{1,3},{6,4},{7,5},{4,6},{5,7},{10,8},{11,9},{8,1... | collective-permute-start | bytes 2359304 | tf_op jit(solution)/shard_map/ppermute | solution.py:638
  564.9 113.1 %collective-permute-start.20 = (bf16[1280,1024]{1,0:T(8,128)(2,1)}, bf16[1280,1024]{1,0:T(8,128)(2,1)}, u32[]{:S(2)}, u32[]{:S(2)}) collective-permute-start(bf16[1280,1024]{1,0:T(8,128)(2,1)} %get-tuple-element.146), channel_id=1, source_target_pairs={{2,1},{1,2},{6,5},{5,6},{10,9},{9,10},{14,13},{13,14},{18,17},{17,... | collective-permute-start | bytes 7864328 | tf_op jit(solution)/shard_map/ppermute | solution.py:619
  578.1 30.6 %collective-permute-start.30 = (bf16[256,768]{1,0:T(8,128)(2,1)}, bf16[256,768]{1,0:T(8,128)(2,1)}, u32[]{:S(2)}, u32[]{:S(2)}) collective-permute-start(bf16[256,768]{1,0:T(8,128)(2,1)} %constant_dynamic-slice_fusion.7), channel_id=1, source_target_pairs={{8,0},{9,1},{10,2},{11,3},{12,4},{13,5},{14,6},{15,7},{0,8},{1,9},... | collective-permute-start | bytes 1179656 | tf_op jit(solution)/shard_map/ppermute | solution.py:638
  580.7 30.2 %collective-permute-start.39 = (bf16[256,768]{1,0:T(8,128)(2,1)}, bf16[256,768]{1,0:T(8,128)(2,1)}, u32[]{:S(2)}, u32[]{:S(2)}) collective-permute-start(bf16[256,768]{1,0:T(8,128)(2,1)} %constant_dynamic-slice_fusion.3), channel_id=1, source_target_pairs={{4,0},{5,1},{6,2},{7,3},{0,4},{1,5},{2,6},{3,7},{12,8},{13,9},{14,... | collective-permute-start | bytes 1179656 | tf_op jit(solution)/shard_map/ppermute | solution.py:638
  589.1 10.6 %collective-permute-start.23 = (f32[16384]{0:T(1024)S(1)}, f32[16384]{0:T(1024)S(1)}, u32[]{:S(2)}, u32[]{:S(2)}) collective-permute-start(f32[16384]{0:T(1024)S(1)} %pad_maximum_fusion.7), channel_id=1, source_target_pairs={{0,1},{1,0},{2,3},{3,2},{4,5},{5,4},{6,7},{7,6},{8,9},{9,8},{10,11... | collective-permute-start | bytes 196616 | tf_op jit(solution)/shard_map/ppermute | solution.py:688
  599.7 8.8 %collective-permute-start.24 = (f32[16384]{0:T(1024)S(1)}, f32[16384]{0:T(1024)S(1)}, u32[]{:S(2)}, u32[]{:S(2)}) collective-permute-start(f32[16384]{0:T(1024)S(1)} %fusion.49), channel_id=1, source_target_pairs={{0,2},{1,3},{2,0},{3,1},{4,6},{5,7},{6,4},{7,5},{8,10},{9,11},{10,... | collective-permute-start | bytes 196616 | tf_op jit(solution)/shard_map/ppermute | solution.py:688
  606.4 133.8 %collective-permute-start.22 = (bf16[1280,1024]{1,0:T(8,128)(2,1)}, bf16[1280,1024]{1,0:T(8,128)(2,1)}, u32[]{:S(2)}, u32[]{:S(2)}) collective-permute-start(bf16[1280,1024]{1,0:T(8,128)(2,1)} %fusion.19), channel_id=1, source_target_pairs={{2,1},{1,2},{6,5},{5,6},{10,9},{9,10},{14,13},{13,14},{18,17},{17,... | collective-permute-start | bytes 7864328 | tf_op jit(solution)/shard_map/ppermute | solution.py:619
  608.5 50.2 %collective-permute-start.25 = (f32[16384]{0:T(1024)S(1)}, f32[16384]{0:T(1024)S(1)}, u32[]{:S(2)}, u32[]{:S(2)}) collective-permute-start(f32[16384]{0:T(1024)S(1)} %add.380), channel_id=1, source_target_pairs={{0,4},{1,5},{2,6},{3,7},{4,0},{5,1},{6,2},{7,3},{8,12},{9,13},{10,... | collective-permute-start | bytes 196616 | tf_op jit(solution)/shard_map/ppermute | solution.py:688
  609.9 16.8 %collective-permute-start.31 = (bf16[128,768]{1,0:T(8,128)(2,1)S(1)}, bf16[128,768]{1,0:T(8,128)(2,1)S(1)}, u32[]{:S(2)}, u32[]{:S(2)}) collective-permute-start(bf16[128,768]{1,0:T(8,128)(2,1)S(1)} %constant_dynamic-slice_fusion.6), channel_id=1, source_target_pairs={{16,0},{17,1},{18,2},{19,3},{20,4},{21,5},{22,6},{23,7},{24,8},{25... | collective-permute-start | bytes 589832 | tf_op jit(solution)/shard_map/ppermute | solution.py:638
  612.0 16.5 %collective-permute-start.40 = (bf16[128,768]{1,0:T(8,128)(2,1)S(1)}, bf16[128,768]{1,0:T(8,128)(2,1)S(1)}, u32[]{:S(2)}, u32[]{:S(2)}) collective-permute-start(bf16[128,768]{1,0:T(8,128)(2,1)S(1)} %constant_dynamic-slice_fusion.2), channel_id=1, source_target_pairs={{8,0},{9,1},{10,2},{11,3},{12,4},{13,5},{14,6},{15,7},{0,8},{1,9},... | collective-permute-start | bytes 589832 | tf_op jit(solution)/shard_map/ppermute | solution.py:638
  626.7 5.3 collective-permute-start.32
  628.6 8.4 %collective-permute-start.41 = (bf16[64,768]{1,0:T(8,128)(2,1)S(1)}, bf16[64,768]{1,0:T(8,128)(2,1)S(1)}, u32[]{:S(2)}, u32[]{:S(2)}) collective-permute-start(bf16[64,768]{1,0:T(8,128)(2,1)S(1)} %constant_dynamic-slice_fusion.1), channel_id=1, source_target_pairs={{16,0},{17,1},{18,2},{19,3},{20,4},{21,5},{22,6},{23,7},{24,8},{25... | collective-permute-start | bytes 294920 | tf_op jit(solution)/shard_map/ppermute | solution.py:638
  632.1 5.7 collective-permute-start.33
  637.0 13.7 %collective-permute-start.42 = (bf16[64,768]{1,0:T(8,128)(2,1)S(1)}, bf16[64,768]{1,0:T(8,128)(2,1)S(1)}, u32[]{:S(2)}, u32[]{:S(2)}) collective-permute-start(bf16[64,768]{1,0:T(8,128)(2,1)S(1)} %add_convert_fusion.9), channel_id=1, source_target_pairs={{16,0},{17,1},{18,2},{19,3},{20,4},{21,5},{22,6},{23,7},{24,8},{25... | collective-permute-start | bytes 294920 | tf_op jit(solution)/shard_map/ppermute | solution.py:638
  637.8 20.7 %collective-permute-start.34 = (bf16[128,768]{1,0:T(8,128)(2,1)S(1)}, bf16[128,768]{1,0:T(8,128)(2,1)S(1)}, u32[]{:S(2)}, u32[]{:S(2)}) collective-permute-start(bf16[128,768]{1,0:T(8,128)(2,1)S(1)} %pad_maximum_fusion.5), channel_id=1, source_target_pairs={{16,0},{17,1},{18,2},{19,3},{20,4},{21,5},{22,6},{23,7},{24,8},{25... | collective-permute-start | bytes 589832 | tf_op jit(solution)/shard_map/ppermute | solution.py:638
  650.8 11.6 %collective-permute-start.43 = (bf16[128,768]{1,0:T(8,128)(2,1)S(1)}, bf16[128,768]{1,0:T(8,128)(2,1)S(1)}, u32[]{:S(2)}, u32[]{:S(2)}) collective-permute-start(bf16[128,768]{1,0:T(8,128)(2,1)S(1)} %pad_maximum_fusion.6), channel_id=1, source_target_pairs={{8,0},{9,1},{10,2},{11,3},{12,4},{13,5},{14,6},{15,7},{0,8},{1,9},... | collective-permute-start | bytes 589832 | tf_op jit(solution)/shard_map/ppermute | solution.py:638
  658.6 17.5 %collective-permute-start.35 = (bf16[256,768]{1,0:T(8,128)(2,1)S(1)}, bf16[256,768]{1,0:T(8,128)(2,1)S(1)}, u32[]{:S(2)}, u32[]{:S(2)}) collective-permute-start(bf16[256,768]{1,0:T(8,128)(2,1)S(1)} %pad_maximum_fusion.3), channel_id=1, source_target_pairs={{8,0},{9,1},{10,2},{11,3},{12,4},{13,5},{14,6},{15,7},{0,8},{1,9},... | collective-permute-start | bytes 1179656 | tf_op jit(solution)/shard_map/ppermute | solution.py:638
  658.7 17.3 %collective-permute-start.26 = (f32[16384]{0:T(1024)S(1)}, f32[16384]{0:T(1024)S(1)}, u32[]{:S(2)}, u32[]{:S(2)}) collective-permute-start(f32[16384]{0:T(1024)S(1)} %add.381), channel_id=1, source_target_pairs={{0,8},{1,9},{2,10},{3,11},{4,12},{5,13},{6,14},{7,15},{8,0},{9,1},... | collective-permute-start | bytes 196616 | tf_op jit(solution)/shard_map/ppermute | solution.py:688
  662.4 15.3 %collective-permute-start.44 = (bf16[256,768]{1,0:T(8,128)(2,1)S(1)}, bf16[256,768]{1,0:T(8,128)(2,1)S(1)}, u32[]{:S(2)}, u32[]{:S(2)}) collective-permute-start(bf16[256,768]{1,0:T(8,128)(2,1)S(1)} %pad_maximum_fusion.4), channel_id=1, source_target_pairs={{4,0},{5,1},{6,2},{7,3},{0,4},{1,5},{2,6},{3,7},{12,8},{13,9},{14,... | collective-permute-start | bytes 1179656 | tf_op jit(solution)/shard_map/ppermute | solution.py:638
  676.0 57.8 %collective-permute-start.27 = (f32[16384]{0:T(1024)S(1)}, f32[16384]{0:T(1024)S(1)}, u32[]{:S(2)}, u32[]{:S(2)}) collective-permute-start(f32[16384]{0:T(1024)S(1)} %add.382), channel_id=1, source_target_pairs={{0,16},{1,17},{2,18},{3,19},{4,20},{5,21},{6,22},{7,23},{8,24},{9,... | collective-permute-start | bytes 196616 | tf_op jit(solution)/shard_map/ppermute | solution.py:688
  676.3 61.6 %collective-permute-start.36 = (bf16[512,768]{1,0:T(8,128)(2,1)S(1)}, bf16[512,768]{1,0:T(8,128)(2,1)S(1)}, u32[]{:S(2)}, u32[]{:S(2)}) collective-permute-start(bf16[512,768]{1,0:T(8,128)(2,1)S(1)} %pad_maximum_fusion.1.a), channel_id=1, source_target_pairs={{2,0},{3,1},{0,2},{1,3},{6,4},{7,5},{4,6},{5,7},{10,8},{11,9},{8,1... | collective-permute-start | bytes 2359304 | tf_op jit(solution)/shard_map/ppermute | solution.py:638
  677.9 57.7 %collective-permute-start.45 = (bf16[512,768]{1,0:T(8,128)(2,1)S(1)}, bf16[512,768]{1,0:T(8,128)(2,1)S(1)}, u32[]{:S(2)}, u32[]{:S(2)}) collective-permute-start(bf16[512,768]{1,0:T(8,128)(2,1)S(1)} %pad_maximum_fusion.2.a), channel_id=1, source_target_pairs={{2,0},{3,1},{0,2},{1,3},{6,4},{7,5},{4,6},{5,7},{10,8},{11,9},{8,1... | collective-permute-start | bytes 2359304 | tf_op jit(solution)/shard_map/ppermute | solution.py:638
  (67 other events, 586.3 us)
Sparse Core Ops, SparseCore 0:
  363.3 116.6 all-reduce.3
  575.7 148.6 all-reduce.5

commit v9 on v8

--- a/solution.py
+++ b/solution.py
@@ -568,16 +568,18 @@
         put(theirs_ref)
 
 
-def spread(mine, theirs, side, out_pairs, first, begun):
-    half, columns = mine.shape
+def spread(mine, theirs, side, half, out_pairs, first, begun):
+    columns = mine.shape[1]
+    low = mine.shape[0] // half - 1
     count = columns // (3 * PAIR)
-    block = pl.BlockSpec((half, 3 * PAIR), lambda k, s, t: (0, k))
+    upper = pl.BlockSpec((half, 3 * PAIR), lambda k, s, t: (0, k))
+    lower = pl.BlockSpec((half, 3 * PAIR), lambda k, s, t: (low, k))
     return pl.pallas_call(
         lambda tab, a, b, *refs: spread_kernel(tab, a, b, refs[-1]),
         grid_spec=pltpu.PrefetchScalarGridSpec(
             num_scalar_prefetch=1,
             grid=(count, 2),
-            in_specs=[block, block] + [pl.BlockSpec(memory_space=pl.ANY)] * len(begun),
+            in_specs=[upper, lower] + [pl.BlockSpec(memory_space=pl.ANY)] * len(begun),
             out_specs=pl.BlockSpec((3, half, PAIR), lambda k, s, t: (0, s, first + k)),
         ),
         out_shape=jax.ShapeDtypeStruct((3, 2 * half, out_pairs * PAIR), F32),
@@ -848,34 +850,26 @@
     g_w_down_far = layout.send(g_w_down, True)
     grad_a3 = layout.scatter_sum(shares_a3)
     g_up_bias = total(g_up_bias)
-    g_w_up = contract_rows(a3_all, grad_pre).astype(bf16)
-    g_w_up_far = layout.send(g_w_up, True)
     grad_mid = upstream + norm_back(grad_a3, normed3, inv3, ln3_gain)
     grad_z = norm_back(grad_mid, normed2, inv2, ln2_gain).astype(bf16)
     grad_z_all = layout.gather(grad_z)
     grad_ctx = [contract_cols(g, w_out).astype(bf16) for g in grad_z_all]
     g_w_out = total([contract_rows(x, g) for x, g in zip(context, grad_z_all)]).astype(bf16)
     g_w_out_far = layout.send(g_w_out, True)
-    g_w_down_far, g_w_up, *grad_ctx = lax.optimization_barrier((g_w_down_far, g_w_up, *grad_ctx))
+    g_w_down_far, *grad_ctx = lax.optimization_barrier((g_w_down_far, *grad_ctx))
     grad_ctx, _ = for_kernel(grad_ctx, rank)
     g_w_down = jnp.where(stays, g_w_down, g_w_down_far)
-    tables, g_w_down = lax.optimization_barrier((tables, g_w_down))
+    grad_pre, g_w_down = lax.optimization_barrier((grad_pre, g_w_down))
     g_w_down = layout.sum_dp(g_w_down, 1)
+    g_w_up = contract_rows(a3_all, grad_pre).astype(bf16)
+    g_w_up_far = layout.send(g_w_up, True)
+    tables, g_w_up = lax.optimization_barrier((tables, g_w_up))
     calls = [(0, pairs // 2)] if pairs > 1 else []
     calls += [(k, 1) for k in range(pairs // 2, pairs)]
     grad_qkv = ()
     for call in calls:
         if call == calls[-1]:
-            g_w_up_far, g_w_out_far, *grad_qkv = lax.optimization_barrier(
-                (g_w_up_far, g_w_out_far, *grad_qkv)
-            )
-            g_w_up = jnp.where(stays, g_w_up, g_w_up_far)
-            g_w_out = jnp.where(stays, g_w_out, g_w_out_far)
-            tables, g_w_down, g_w_up, g_w_out = lax.optimization_barrier(
-                (tables, g_w_down, g_w_up, g_w_out)
-            )
-            g_w_up = layout.sum_dp(g_w_up, 0)
-            g_w_out = layout.sum_dp(g_w_out, 0)
+            tables, g_w_down = lax.optimization_barrier((tables, g_w_down))
         grad_qkv = attend_backward(
             qkv, context_turned, grad_ctx, log_total, seg, keep, tables, call, grad_qkv
         )
@@ -889,15 +883,21 @@
     each = pairs // chunks
     for chunk in range(chunks):
         g_part, part_sums = weight_grad(a1, grad_qkv, chunk * each, each)
-        g_w_qkv.append(layout.halved(layout.give_back(g_part), -1))
+        g_w_qkv.append(layout.give_back(g_part))
         sums.append(part_sums)
     sums = jnp.concatenate(sums, 1)
-    g_w_qkv = [layout.halved_by(g, layout.order(k)) for k, g in enumerate(g_w_qkv)]
-    g_w_qkv = [layout.joined_by(g, layout.order(k)) for k, g in enumerate(g_w_qkv)]
+    g_w_up = layout.sum_dp(jnp.where(stays, g_w_up, g_w_up_far), 0)
+    g_w_out = layout.sum_dp(jnp.where(stays, g_w_out, g_w_out_far), 0)
     begun = ()
-    for chunk, mine in enumerate(g_w_qkv):
-        theirs = layout.partner(mine, -1)
-        begun = (spread(mine, theirs, layout.side(-1), pairs, chunk * each, begun),)
+    for chunk, part in enumerate(g_w_qkv):
+        if chunk == 0:
+            mine = theirs = layout.sum_dp(part, 0)
+            side = jnp.zeros((), jnp.int32)
+        else:
+            part = layout.halved_by(part, [-1, *layout.order(0)])
+            mine, side = layout.joined_by(part, layout.order(0)), layout.side(-1)
+            theirs = layout.partner(mine, -1)
+        begun = (spread(mine, theirs, side, model_dim // 2, pairs, chunk * each, begun),)
     g_w_qkv = begun[0].transpose(1, 0, 2)
     sums = sums.reshape(pairs, 3, PAIR).transpose(1, 0, 2).reshape(3, width)
     grad_input = layout.give_back(grad_input).astype(f32)

time: 761 us -> 759 us (level)
  waiting for transfers between devices: 152 us -> 196 us
  Pallas kernels: 228 us -> 196 us
    psum x2, waiting for transfers between devices: 95.1 us -> 141 us  [sum_dp(): return lax.psum(value, 'dp', axis_index_groups=[order])]
    pallas_call x3, Pallas kernels: 76.7 us -> 56.9 us  [attend_backward(): pl.pallas_call(functools.partial(backward_kernel, parts), grid_spec=pltpu...]
    ppermute x18 -> x10, starting transfers between devices: 30.8 us -> 12 us  [partner(): return lax.ppermute(value, self.axes, moves)]
    ppermute x18 -> x10, waiting for transfers between devices: 37 us -> 18.9 us  [partner(): return lax.ppermute(value, self.axes, moves)]
    ppermute x8, starting transfers between devices: 89.7 us -> 106 us  [to_rank(): return lax.ppermute(value, self.axes, moves)]
    ppermute x5, waiting for transfers between devices: 13.5 us -> 25.6 us  [sum_all(): lax.ppermute(value, self.axes, [(i, i ^ step) for i in range(devices)])]
    pallas_call x4, Pallas kernels: 50.6 us -> 38.8 us  [attend_forward(): pl.pallas_call(functools.partial(forward_kernel, parts), grid_spec=pltpu....]
    unnamed x137 -> x141, local copies, waits for them, and re-layouts: 24.3 us -> 20.2 us
  transfers between devices with their start and end apart: 48 -> 40, of which waited for: 12 -> 13; matrix products, arithmetic and copies ran while one was open for 19% -> 18% of each run, Pallas kernels for 22% -> 21%
where the time goes in v9:
time: 759 us; the launch traced here: 750 us
  waiting for transfers between devices  196 us (26%)
  Pallas kernels  196 us (26%)
  starting transfers between devices  150 us (20%)
  other arithmetic  99.6 us (13%)
  matrix products  56.4 us (7%)
  local copies, waits for them, and re-layouts  34.6 us (5%)
  between operations  17.4 us (2%)
    psum x2, waiting for transfers between devices, sum_dp(): return lax.psum(value, 'dp', axis_index_groups=[order])  141 us
    ppermute x8, starting transfers between devices, to_rank(): return lax.ppermute(value, self.axes, moves)  106 us
    pallas_call x3, Pallas kernels, attend_backward(): pl.pallas_call(functools.partial(backward_kernel, parts), grid_spec=pltpu...  56.9 us
    pallas_call x4, Pallas kernels, attend_forward(): pl.pallas_call(functools.partial(forward_kernel, parts), grid_spec=pltpu....  38.8 us
    dot_general x4, matrix products, contract_rows(): lax.dot_general(left, right, (((0,), (0,)), ((), ())), preferred_element_...  36.5 us
    pallas_call x2, Pallas kernels, feed_forward(): pl.pallas_call(functools.partial(feed_kernel, min(units, FEED)), grid=(st...  35.6 us
    pallas_call x2, Pallas kernels, feed_back(): pl.pallas_call(functools.partial(feed_back_kernel, min(units, FEED)), gri...  32 us
    ppermute x15, starting transfers between devices, send(): lax.ppermute(value, self.axes, [(b, a) if back else (a, b) for a, b in mo...  26.1 us
  transfers between devices with their start and end apart: 40, of which 13 were waited for; matrix products, arithmetic and copies ran while one was open for 18% of the time, Pallas kernels for 21%

profile of v9, /device:TPU:0, one launch (start us, length us, event | category | flops | bytes accessed | tf_op | source)
XLA Modules:
  0.0 749.6 jit_solution(10344228141440469540)
XLA Ops:
  7.3 3.2 copy.71
  16.9 4.7 fusion.52
  34.7 38.5 %collective-permute-start.6 = (bf16[1280,1024]{1,0:T(8,128)(2,1)S(1)}, bf16[1280,1024]{1,0:T(8,128)(2,1)}, u32[]{:S(2)}, u32[]{:S(2)}) collective-permute-start(bf16[1280,1024]{1,0:T(8,128)(2,1)S(1)} %fusion.14.refs_0_), channel_id=1, source_target_pairs={{0,2},{2,0},{1,3},{3,1},{4,6},{6,4},{5,7},{7,5},{8,10},{10,8},{9,1... | collective-permute-start | bytes 7864328 | tf_op jit(solution)/shard_map/ppermute | solution.py:671
  83.9 4.6 fusion.2.refs_0_
  88.6 7.8 %fusion.3.refs_1_ = bf16[1280,1536]{1,0:T(8,128)(2,1)S(1)} fusion(bf16[1280,1024]{1,0:T(8,128)(2,1)} %collective-permute-done.6.refs_1_, bf16[1024,1536]{0,1:T(8,128)(2,1)S(1)} %bitcast.60, f32[1536]{0:T(1024)S(1)} %copy-done.64, f32[1536]{0:T(1024)S(1)} %add.311), kind=kOutput, calls=%fused_computation.12 | convolution fusion | flops 4032430080 | bytes 9711616 | tf_op jit(solution)/shard_map/dot_general | solution.py:57
  96.4 9.6 %attend_forward.4 = (bf16[1280,512]{1,0:T(8,128)(2,1)S(1)}, bf16[1280,512]{1,0:T(8,128)(2,1)S(1)}, bf16[512,2560]{1,0:T(8,128)(2,1)S(1)}, f32[4,2,2560]{2,1,0:T(2,128)S(1)}) custom-call(s32[3,10]{1,0:T(4,128)S(1)} %add_add_fusion.2.tab_ref, s32[2560,1]{1,0:T(8,128)S(1)} %copy-done.6, s32[1,2560]{1,0:T(1,128)S(1)} %fusion.45.qseg_ref, ...), custom_call_target="tpu_custom_call" | custom-call | flops 1024 | bytes 1024 | tf_op jit(solution)/shard_map/attend_forward/pallas_call | solution.py:301
  106.0 9.6 %attend_forward.5 = (bf16[1280,512]{1,0:T(8,128)(2,1)S(1)}, bf16[1280,512]{1,0:T(8,128)(2,1)S(1)}, bf16[512,2560]{1,0:T(8,128)(2,1)S(1)}, f32[4,2,2560]{2,1,0:T(2,128)S(1)}) custom-call(s32[3,10]{1,0:T(4,128)S(1)} %add_add_fusion.2.tab_ref, s32[2560,1]{1,0:T(8,128)S(1)} %copy-done.6, ...), custom_call_target="tpu_custom_call", output_to_operand_aliasing={{0}: (5, {}), {1}: (6, {}), {2}: (7, {}), {3}: (8, {})} | custom-call | flops 1024 | bytes 1024 | tf_op jit(solution)/shard_map/attend_forward/pallas_call | solution.py:301
  115.6 9.6 %attend_forward.6 = (bf16[1280,512]{1,0:T(8,128)(2,1)S(1)}, bf16[1280,512]{1,0:T(8,128)(2,1)S(1)}, bf16[512,2560]{1,0:T(8,128)(2,1)S(1)}, f32[4,2,2560]{2,1,0:T(2,128)S(1)}) custom-call(s32[3,10]{1,0:T(4,128)S(1)} %add_add_fusion.2.tab_ref, s32[2560,1]{1,0:T(8,128)S(1)} %copy-done.6, ...), custom_call_target="tpu_custom_call", output_to_operand_aliasing={{0}: (5, {}), {1}: (6, {}), {2}: (7, {}), {3}: (8, {})} | custom-call | flops 1024 | bytes 1024 | tf_op jit(solution)/shard_map/attend_forward/pallas_call | solution.py:301
  125.3 10.0 %attend_forward.7 = (bf16[1280,512]{1,0:T(8,128)(2,1)S(1)}, bf16[1280,512]{1,0:T(8,128)(2,1)S(1)}, bf16[512,2560]{1,0:T(8,128)(2,1)S(1)}, f32[4,2,2560]{2,1,0:T(2,128)S(1)}) custom-call(s32[3,10]{1,0:T(4,128)S(1)} %add_add_fusion.2.tab_ref, s32[2560,1]{1,0:T(8,128)S(1)} %copy-done.6, ...), custom_call_target="tpu_custom_call", output_to_operand_aliasing={{0}: (5, {}), {1}: (6, {}), {2}: (7, {}), {3}: (8, {})} | custom-call | flops 1024 | bytes 1024 | tf_op jit(solution)/shard_map/attend_forward/pallas_call | solution.py:301
  139.1 36.2 %collective-permute-start.10 = (bf16[1280,1024]{1,0:T(8,128)(2,1)S(1)}, bf16[1280,1024]{1,0:T(8,128)(2,1)S(1)}, u32[]{:S(2)}, u32[]{:S(2)}) collective-permute-start(bf16[1280,1024]{1,0:T(8,128)(2,1)S(1)} %convolution_convert_fusion.1), channel_id=1, source_target_pairs={{0,2},{2,0},{1,3},{3,1},{4,6},{6,4},{5,7},{7,5},{8,10},{10,8},{9,1... | collective-permute-start | bytes 7864328 | tf_op jit(solution)/shard_map/ppermute | solution.py:671
  176.3 4.6 broadcast_select_fusion.2.up_ref
  183.5 2.9 copy-done.20
  190.4 3.6 collective-permute-start.11
  194.0 4.6 maximum_select_fusion.down_ref
  200.5 17.8 %feed_forward.2 = (bf16[2560,1024]{1,0:T(8,128)(2,1)}, bf16[2560,2048]{1,0:T(8,128)(2,1)}, bf16[2560,2048]{1,0:T(8,128)(2,1)}, bf16[1280,1024]{1,0:T(8,128)(2,1)S(1)}) custom-call(bf16[1280,1024]{1,0:T(8,128)(2,1)S(1)} %add_convert_fusion.1.x_ref, bf16[1024,2048]{1,0:T(8,128)(2,1)} %broadcast_select_fusion.2.up_ref, f32[1,2048]{1,0:T(1,128)S(1)} %bitcast.52, ...), custom_call_target="tpu_custom_call" | custom-call | flops 16106127360 | bytes 16777216 | tf_op jit(solution)/shard_map/feed_forward/pallas_call | solution.py:411
  218.3 17.9 %feed_forward.3 = (bf16[2560,1024]{1,0:T(8,128)(2,1)}, bf16[2560,2048]{1,0:T(8,128)(2,1)}, bf16[2560,2048]{1,0:T(8,128)(2,1)}, bf16[1280,1024]{1,0:T(8,128)(2,1)S(1)}) custom-call(bf16[1280,1024]{1,0:T(8,128)(2,1)S(1)} %collective-permute-done.11.x_ref, ...), custom_call_target="tpu_custom_call", output_to_operand_aliasing={{0}: (4, {}), {1}: (5, {}), {2}: (6, {})} | custom-call | flops 16106127360 | bytes 16777216 | tf_op jit(solution)/shard_map/feed_forward/pallas_call | solution.py:411
  236.2 9.1 %collective-permute-start.13 = (bf16[1280,1024]{1,0:T(8,128)(2,1)S(1)}, bf16[1280,1024]{1,0:T(8,128)(2,1)S(1)}, u32[]{:S(2)}, u32[]{:S(2)}) collective-permute-start(bf16[1280,1024]{1,0:T(8,128)(2,1)S(1)} %get-tuple-element.119), channel_id=1, source_target_pairs={{0,2},{2,0},{1,3},{3,1},{4,6},{6,4},{5,7},{7,5},{8,10},{10,8},{9,1... | collective-permute-start | bytes 7864328 | tf_op jit(solution)/shard_map/ppermute | solution.py:671
  245.2 4.5 collective-permute-done.13
  252.0 3.6 fusion.26
  255.7 4.9 convert_reduce_fusion.2
  260.9 15.9 %feed_back.2 = (bf16[2560,2048]{1,0:T(8,128)(2,1)}, f32[1,2048]{1,0:T(1,128)S(1)}, bf16[1280,1024]{1,0:T(8,128)(2,1)S(1)}) custom-call(bf16[1280,1024]{1,0:T(8,128)(2,1)S(1)} %get-tuple-element.174.g_ref, bf16[2560,2048]{1,0:T(8,128)(2,1)} %get-tuple-element.121.slope_ref, bf16[2048,1024]{1,0:T(8,128)(2,1)} %maximum_select_fusion.down_ref, ...), custom_call_target="tpu_custom_call" | custom-call | flops 1024 | bytes 1024 | tf_op jit(solution)/shard_map/feed_back/pallas_call | solution.py:473
  276.9 15.3 %fusion.38 = bf16[2048,1024]{1,0:T(8,128)(2,1)} fusion(bf16[2560,2048]{1,0:T(8,128)(2,1)} %get-tuple-element.123, bf16[1280,1024]{1,0:T(8,128)(2,1)S(1)} %collective-permute-done.14.g_ref, bf16[1280,1024]{1,0:T(8,128)(2,1)S(1)} %get-tuple-element.174.g_ref), kind=kOutput, calls=%fused_computation.72 | convolution fusion | flops 10750001152 | bytes 19922944 | tf_op jit(solution)/shard_map/dot_general | solution.py:35
  292.2 16.1 %feed_back.3 = (bf16[2560,2048]{1,0:T(8,128)(2,1)}, f32[1,2048]{1,0:T(1,128)S(1)}, bf16[1280,1024]{1,0:T(8,128)(2,1)S(1)}) custom-call(bf16[1280,1024]{1,0:T(8,128)(2,1)S(1)} %collective-permute-done.14.g_ref, bf16[2560,2048]{1,0:T(8,128)(2,1)} %get-tuple-element.121.slope_ref, ...), custom_call_target="tpu_custom_call", output_to_operand_aliasing={{0}: (4, {})} | custom-call | flops 1024 | bytes 1024 | tf_op jit(solution)/shard_map/feed_back/pallas_call | solution.py:473
  313.2 3.2 multiply_reduce_fusion
  316.5 7.8 %multiply_reduce_fusion.1 = (f32[1024]{0:T(1024)}, f32[1280]{0:T(1024)S(1)}, f32[1280]{0:T(1024)S(1)}, f32[1024]{0:T(1024)}, f32[1280,1024]{1,0:T(8,128)S(1)}) fusion(f32[1280,1024]{1,0:T(8,128)} %copy-done.22, f32[1280]{0:T(1024)S(1)} %add_rsqrt_fusion.2, f32[1280]{0:T(1024)S(1)} %broadcast_multiply_fusion.10, f32[1024]{0:T(1024)S(1)} %copy-done.49, ...), kind=kLoop, calls=%fused_computation.42 | loop fusion | flops 27520512 | bytes 23650304 | tf_op jit(solution)/shard_map/reduce_sum | solution.py:910
  328.4 3.2 collective-permute-done.16
  337.2 17.1 %convolution_convert_fusion = bf16[1024,2048]{1,0:T(8,128)(2,1)} fusion(bf16[2560,1024]{1,0:T(8,128)(2,1)} %get-tuple-element.128, bf16[2560,2048]{1,0:T(8,128)(2,1)} %get-tuple-element.132), kind=kOutput, calls=%fused_computation.71 | convolution fusion | flops 10739515392 | bytes 19922944 | tf_op jit(solution)/shard_map/dot_general | solution.py:35
  362.8 26.8 %attend_backward.3 = (bf16[1280,1536]{1,0:T(8,128)(2,1)}, bf16[1280,1536]{1,0:T(8,128)(2,1)}) custom-call(s32[3,10]{1,0:T(4,128)S(1)} %add_add_fusion.2.tab_ref, s32[2560,1]{1,0:T(8,128)S(1)} %copy-done.7, s32[1,2560]{1,0:T(1,128)S(1)} %fusion.45.qseg_ref, bf16[1280,1536]{1,0:T(8,128)(2,1)} %copy-done, bf16[1280,1536]{1,0:T(8,128)(2,1)} %copy-done.1, ...), custom_call_target="tpu_custom_call" | custom-call | flops 1024 | bytes 1024 | tf_op jit(solution)/shard_map/attend_backward/pallas_call | solution.py:335
  389.5 15.0 %attend_backward.4 = (bf16[1280,1536]{1,0:T(8,128)(2,1)}, bf16[1280,1536]{1,0:T(8,128)(2,1)}) custom-call(s32[3,10]{1,0:T(4,128)S(1)} %add_add_fusion.2.tab_ref, s32[2560,1]{1,0:T(8,128)S(1)} %copy-done.7, s32[1,2560]{1,0:T(1,128)S(1)} %fusion.45.qseg_ref, bf16[1280,1536]{1,0:T(8,128)(2,1)} %copy-done, ...), custom_call_target="tpu_custom_call", output_to_operand_aliasing={{0}: (9, {}), {1}: (10, {})} | custom-call | flops 1024 | bytes 1024 | tf_op jit(solution)/shard_map/attend_backward/pallas_call | solution.py:335
  404.5 71.8 %all-reduce.4.cloned.1.call-done = bf16[2048,1024]{1,0:T(8,128)(2,1)} async-done(((bf16[2048,1024]{1,0:T(8,128)(2,1)}), bf16[2048,1024]{1,0:T(8,128)(2,1)}) %all-reduce.4.cloned.1.call-update) | async-done | bytes 4194320 | tf_op jit(solution)/shard_map/psum | solution.py:695
  477.6 15.1 %attend_backward.5 = (bf16[1280,1536]{1,0:T(8,128)(2,1)}, bf16[1280,1536]{1,0:T(8,128)(2,1)}) custom-call(s32[3,10]{1,0:T(4,128)S(1)} %add_add_fusion.2.tab_ref, s32[2560,1]{1,0:T(8,128)S(1)} %copy-done.7, s32[1,2560]{1,0:T(1,128)S(1)} %fusion.45.qseg_ref, bf16[1280,1536]{1,0:T(8,128)(2,1)} %copy-done, ...), custom_call_target="tpu_custom_call", output_to_operand_aliasing={{0}: (9, {}), {1}: (10, {})} | custom-call | flops 1024 | bytes 1024 | tf_op jit(solution)/shard_map/attend_backward/pallas_call | solution.py:335
  494.9 9.1 %weight_grad.3 = (bf16[1024,768]{1,0:T(8,128)(2,1)}, f32[1,768]{1,0:T(1,128)S(1)}) custom-call(bf16[1280,1024]{1,0:T(8,128)(2,1)S(1)} %copy-done.9, bf16[1280,1024]{1,0:T(8,128)(2,1)} %collective-permute-done.6.refs_1_, bf16[1280,1536]{1,0:T(8,128)(2,1)S(1)} %copy-done.2, bf16[1280,1536]{1,0:T(8,128)(2,1)} %get-tuple-element.145.d_ref.refs_3_), custom_call_target="tpu_custom_call" | custom-call | flops 1024 | bytes 1024 | tf_op jit(solution)/shard_map/weight_grad/pallas_call | solution.py:513
  505.8 8.9 %weight_grad.2 = (bf16[1024,768]{1,0:T(8,128)(2,1)}, f32[1,768]{1,0:T(1,128)S(1)}) custom-call(bf16[1280,1024]{1,0:T(8,128)(2,1)S(1)} %copy-done.9, bf16[1280,1024]{1,0:T(8,128)(2,1)} %collective-permute-done.6.refs_1_, bf16[1280,1536]{1,0:T(8,128)(2,1)S(1)} %copy-done.2, bf16[1280,1536]{1,0:T(8,128)(2,1)} %get-tuple-element.145.d_ref.refs_3_), custom_call_target="tpu_custom_call" | custom-call | flops 1024 | bytes 1024 | tf_op jit(solution)/shard_map/weight_grad/pallas_call | solution.py:513
  516.6 3.2 copy.83.w_ref
  521.9 5.5 input_grad.3
  527.4 17.5 %collective-permute-start.20 = (bf16[1280,1024]{1,0:T(8,128)(2,1)}, bf16[1280,1024]{1,0:T(8,128)(2,1)}, u32[]{:S(2)}, u32[]{:S(2)}) collective-permute-start(bf16[1280,1024]{1,0:T(8,128)(2,1)} %input_grad.3), channel_id=1, source_target_pairs={{0,2},{2,0},{1,3},{3,1},{4,6},{6,4},{5,7},{7,5},{8,10},{10,8},{9,1... | collective-permute-start | bytes 7864328 | tf_op jit(solution)/shard_map/ppermute | solution.py:671
  551.9 4.7 input_grad.2
  566.1 4.6 broadcast_select_fusion.1
  573.6 5.8 fusion.20
  579.4 10.7 %collective-permute-done.29 = bf16[256,768]{1,0:T(8,128)(2,1)S(1)} collective-permute-done((bf16[256,768]{1,0:T(8,128)(2,1)S(1)}, bf16[256,768]{1,0:T(8,128)(2,1)S(1)}, u32[]{:S(2)}, u32[]{:S(2)}) %collective-permute-start.29) | collective-permute-done | bytes 393248 | tf_op jit(solution)/shard_map/ppermute | solution.py:640
  592.2 4.9 fusion.19
  603.9 6.6 collective-permute-done.31
  611.6 18.2 %collective-permute-done.22 = f32[16384]{0:T(1024)S(1)} collective-permute-done((f32[16384]{0:T(1024)S(1)}, f32[16384]{0:T(1024)S(1)}, u32[]{:S(2)}, u32[]{:S(2)}) %collective-permute-start.22) | collective-permute-done | bytes 65568 | tf_op jit(solution)/shard_map/ppermute | solution.py:690
  637.1 7.1 convert_element_type.183
  649.0 4.1 collective-permute-done.26
  656.3 4.5 select_convert_fusion
  660.7 69.3 %all-reduce.6.cloned.1.call-done = (bf16[1024,768]{1,0:T(8,128)(2,1)}, bf16[512,1024]{1,0:T(8,128)(2,1)}, bf16[1024,2048]{1,0:T(8,128)(2,1)}) async-done(((bf16[1024,768]{1,0:T(8,128)(2,1)}, bf16[512,1024]{1,0:T(8,128)(2,1)}, bf16[1024,2048]{1,0:T(8,128)(2,1)}), (bf16[1024,768]{1,0:T(8,128)(2,1)}, bf16[512,1024]{1,0:T(8,128)(2,1)}, bf16[1024,2048]{1,0:T(8,128)(2,1)})) %all-reduce.6.cloned.1.call-update) | async-done | bytes 6815760 | tf_op jit(solution)/shard_map/psum | solution.py:695
  735.5 4.5 convert_element_type.182
  (312 shorter events, 128.3 us)
Async XLA Ops:
  7.2 469.1 %all-reduce.4.cloned.1.call-start = ((), (), s32[]{:S(2)}) async-start(), calls=%async_computation | async-start | bytes 8388608 | tf_op jit(solution)/shard_map/psum | solution.py:695
  10.7 0.8 collective-permute-start
  12.4 0.7 collective-permute-start.1
  13.1 15.6 %collective-permute-start.2 = (bf16[1280,1024]{1,0:T(8,128)(2,1)}, bf16[1280,1024]{1,0:T(8,128)(2,1)}, u32[]{:S(2)}, u32[]{:S(2)}) collective-permute-start(bf16[1280,1024]{1,0:T(8,128)(2,1)} %param.20), channel_id=1, source_target_pairs={{1,2},{2,1},{5,6},{6,5},{9,10},{10,9},{13,14},{14,13},{17,18},{18,... | collective-permute-start | bytes 7864328 | tf_op jit(solution)/shard_map/ppermute | solution.py:621
  15.3 8.5 %collective-permute-start.4 = (bf16[256,3,512]{0,2,1:T(8,128)(2,1)}, bf16[256,3,512]{0,2,1:T(8,128)(2,1)}, u32[]{:S(2)}, u32[]{:S(2)}) collective-permute-start(bf16[256,3,512]{0,2,1:T(8,128)(2,1)} %copy-done.43), channel_id=1, source_target_pairs={{9,1},{10,2},{13,5},{14,6},{1,9},{2,10},{5,13},{6,14},{25,17},{26,... | collective-permute-start | bytes 2359304 | tf_op jit(solution)/shard_map/ppermute | solution.py:640
  26.8 49.6 %collective-permute-start.5 = (bf16[512,3,512]{0,2,1:T(8,128)(2,1)}, bf16[512,3,512]{0,2,1:T(8,128)(2,1)}, u32[]{:S(2)}, u32[]{:S(2)}) collective-permute-start(bf16[512,3,512]{0,2,1:T(8,128)(2,1)} %pad_maximum_fusion), channel_id=1, source_target_pairs={{5,1},{6,2},{1,5},{2,6},{13,9},{14,10},{9,13},{10,14},{21,17},{22,... | collective-permute-start | bytes 4718600 | tf_op jit(solution)/shard_map/ppermute | solution.py:640
  29.7 85.9 %collective-permute-start.3 = (bf16[1024,2048]{1,0:T(8,128)(2,1)}, bf16[1024,2048]{1,0:T(8,128)(2,1)}, u32[]{:S(2)}, u32[]{:S(2)}) collective-permute-start(bf16[1024,2048]{1,0:T(8,128)(2,1)} %param.31), channel_id=1, source_target_pairs={{1,2},{2,1},{5,6},{6,5},{9,10},{10,9},{13,14},{14,13},{17,18},{18,... | collective-permute-start | bytes 12582920 | tf_op jit(solution)/shard_map/ppermute | solution.py:621
  32.5 42.7 %copy-start.44 = (f32[1280]{0:T(1024)}, f32[1280]{0:T(1024)S(1)}, u32[]{:S(2)}) copy-start(f32[1280]{0:T(1024)S(1)} %broadcast_multiply_fusion.11) | copy-start | bytes 15364
  33.4 42.1 %copy-start.46 = (f32[1280]{0:T(1024)}, f32[1280]{0:T(1024)S(1)}, u32[]{:S(2)}) copy-start(f32[1280]{0:T(1024)S(1)} %add_rsqrt_fusion.3) | copy-start | bytes 15364
  34.7 49.2 %copy-start.8 = (bf16[1280,1024]{1,0:T(8,128)(2,1)}, bf16[1280,1024]{1,0:T(8,128)(2,1)S(1)}, u32[]{:S(2)}) copy-start(bf16[1280,1024]{1,0:T(8,128)(2,1)S(1)} %fusion.14.refs_0_) | copy-start | bytes 7864324
  34.7 53.9 %collective-permute-start.6 = (bf16[1280,1024]{1,0:T(8,128)(2,1)S(1)}, bf16[1280,1024]{1,0:T(8,128)(2,1)}, u32[]{:S(2)}, u32[]{:S(2)}) collective-permute-start(bf16[1280,1024]{1,0:T(8,128)(2,1)S(1)} %fusion.14.refs_0_), channel_id=1, source_target_pairs={{0,2},{2,0},{1,3},{3,1},{4,6},{6,4},{5,7},{7,5},{8,10},{10,8},{9,1... | collective-permute-start | bytes 7864328 | tf_op jit(solution)/shard_map/ppermute | solution.py:671
  78.6 56.8 %collective-permute-start.8 = (bf16[1024,1024]{1,0:T(8,128)(2,1)}, bf16[1024,1024]{1,0:T(8,128)(2,1)S(1)}, u32[]{:S(2)}, u32[]{:S(2)}) collective-permute-start(bf16[1024,1024]{1,0:T(8,128)(2,1)} %get-tuple-element.105), channel_id=1, source_target_pairs={{1,2},{2,1},{5,6},{6,5},{9,10},{10,9},{13,14},{14,13},{17,18},{18,... | collective-permute-start | bytes 6291464 | tf_op jit(solution)/shard_map/ppermute | solution.py:621
  79.4 56.0 %collective-permute-start.9 = (bf16[1024,1024]{1,0:T(8,128)(2,1)}, bf16[1024,1024]{1,0:T(8,128)(2,1)}, u32[]{:S(2)}, u32[]{:S(2)}) collective-permute-start(bf16[1024,1024]{1,0:T(8,128)(2,1)} %get-tuple-element.106), channel_id=1, source_target_pairs={{1,2},{2,1},{5,6},{6,5},{9,10},{10,9},{13,14},{14,13},{17,18},{18,... | collective-permute-start | bytes 6291464 | tf_op jit(solution)/shard_map/ppermute | solution.py:621
  83.0 52.4 %collective-permute-start.7 = (bf16[512,1024]{1,0:T(8,128)(2,1)}, bf16[512,1024]{1,0:T(8,128)(2,1)S(1)}, u32[]{:S(2)}, u32[]{:S(2)}) collective-permute-start(bf16[512,1024]{1,0:T(8,128)(2,1)} %param.25), channel_id=1, source_target_pairs={{1,2},{2,1},{5,6},{6,5},{9,10},{10,9},{13,14},{14,13},{17,18},{18,... | collective-permute-start | bytes 3145736 | tf_op jit(solution)/shard_map/ppermute | solution.py:621
  88.6 36.7 %copy-start = (bf16[1280,1536]{1,0:T(8,128)(2,1)}, bf16[1280,1536]{1,0:T(8,128)(2,1)S(1)}, u32[]{:S(2)}) copy-start(bf16[1280,1536]{1,0:T(8,128)(2,1)S(1)} %fusion.2.refs_0_) | copy-start | bytes 11796484
  96.4 28.9 %copy-start.1 = (bf16[1280,1536]{1,0:T(8,128)(2,1)}, bf16[1280,1536]{1,0:T(8,128)(2,1)S(1)}, u32[]{:S(2)}) copy-start(bf16[1280,1536]{1,0:T(8,128)(2,1)S(1)} %fusion.3.refs_1_) | copy-start | bytes 11796484
  135.3 45.6 %copy-start.12 = (bf16[1280,512]{1,0:T(8,128)(2,1)}, bf16[1280,512]{1,0:T(8,128)(2,1)S(1)}, u32[]{:S(2)}) copy-start(bf16[1280,512]{1,0:T(8,128)(2,1)S(1)} %get-tuple-element.107) | copy-start | bytes 3932164
  137.5 43.4 %copy-start.41 = (bf16[512,1024]{1,0:T(8,128)(2,1)}, bf16[512,1024]{1,0:T(8,128)(2,1)S(1)}, u32[]{:S(2)}) copy-start(bf16[512,1024]{1,0:T(8,128)(2,1)S(1)} %broadcast_select_fusion.11) | copy-start | bytes 3145732
  139.1 41.8 %collective-permute-start.10 = (bf16[1280,1024]{1,0:T(8,128)(2,1)S(1)}, bf16[1280,1024]{1,0:T(8,128)(2,1)S(1)}, u32[]{:S(2)}, u32[]{:S(2)}) collective-permute-start(bf16[1280,1024]{1,0:T(8,128)(2,1)S(1)} %convolution_convert_fusion.1), channel_id=1, source_target_pairs={{0,2},{2,0},{1,3},{3,1},{4,6},{6,4},{5,7},{7,5},{8,10},{10,8},{9,1... | collective-permute-start | bytes 7864328 | tf_op jit(solution)/shard_map/ppermute | solution.py:671
  175.3 23.2 %collective-permute-start.12 = (bf16[1280,1024]{1,0:T(8,128)(2,1)}, bf16[1280,1024]{1,0:T(8,128)(2,1)S(1)}, u32[]{:S(2)}, u32[]{:S(2)}) collective-permute-start(bf16[1280,1024]{1,0:T(8,128)(2,1)} %param.39), channel_id=1, source_target_pairs={{1,2},{2,1},{5,6},{6,5},{9,10},{10,9},{13,14},{14,13},{17,18},{18,... | collective-permute-start | bytes 7864328 | tf_op jit(solution)/shard_map/ppermute | solution.py:621
  190.4 27.9 %collective-permute-start.11 = (bf16[1280,1024]{1,0:T(8,128)(2,1)S(1)}, bf16[1280,1024]{1,0:T(8,128)(2,1)S(1)}, u32[]{:S(2)}, u32[]{:S(2)}) collective-permute-start(bf16[1280,1024]{1,0:T(8,128)(2,1)S(1)} %add_convert_fusion.1.x_ref), channel_id=1, source_target_pairs={{0,2},{2,0},{1,3},{3,1},{4,6},{6,4},{5,7},{7,5},{8,10},{10,8},{9,1... | collective-permute-start | bytes 7864328 | tf_op jit(solution)/shard_map/ppermute | solution.py:671
  218.3 31.5 %copy-start.48 = (f32[1024]{0:T(1024)S(1)}, f32[1024]{0:T(1024)}, u32[]{:S(2)}) copy-start(f32[1024]{0:T(1024)} %param.34) | copy-start | bytes 12292
  236.2 13.6 %collective-permute-start.13 = (bf16[1280,1024]{1,0:T(8,128)(2,1)S(1)}, bf16[1280,1024]{1,0:T(8,128)(2,1)S(1)}, u32[]{:S(2)}, u32[]{:S(2)}) collective-permute-start(bf16[1280,1024]{1,0:T(8,128)(2,1)S(1)} %get-tuple-element.119), channel_id=1, source_target_pairs={{0,2},{2,0},{1,3},{3,1},{4,6},{6,4},{5,7},{7,5},{8,10},{10,8},{9,1... | collective-permute-start | bytes 7864328 | tf_op jit(solution)/shard_map/ppermute | solution.py:671
  260.6 16.3 %collective-permute-start.14 = (bf16[1280,1024]{1,0:T(8,128)(2,1)S(1)}, bf16[1280,1024]{1,0:T(8,128)(2,1)S(1)}, u32[]{:S(2)}, u32[]{:S(2)}) collective-permute-start(bf16[1280,1024]{1,0:T(8,128)(2,1)S(1)} %get-tuple-element.174.g_ref), channel_id=1, source_target_pairs={{0,2},{2,0},{1,3},{3,1},{4,6},{6,4},{5,7},{7,5},{8,10},{10,8},{9,1... | collective-permute-start | bytes 7864328 | tf_op jit(solution)/shard_map/ppermute | solution.py:671
  308.3 5.0 collective-permute-start.15
  308.5 25.7 %collective-permute-start.19 = (bf16[2048,1024]{1,0:T(8,128)(2,1)}, bf16[2048,1024]{1,0:T(8,128)(2,1)}, u32[]{:S(2)}, u32[]{:S(2)}) collective-permute-start(bf16[2048,1024]{1,0:T(8,128)(2,1)} %fusion.38), channel_id=1, source_target_pairs={{2,1},{1,2},{6,5},{5,6},{10,9},{9,10},{14,13},{13,14},{18,17},{17,... | collective-permute-start | bytes 12582920 | tf_op jit(solution)/shard_map/ppermute | solution.py:621
  326.7 4.9 collective-permute-start.16
  337.1 393.0 %all-reduce.6.cloned.1.call-start = ((), (), s32[]{:S(2)}) async-start(), calls=%async_computation.1 | async-start | bytes 13631488 | tf_op jit(solution)/shard_map/psum | solution.py:695
  354.3 211.9 %collective-permute-start.37 = (bf16[1024,2048]{1,0:T(8,128)(2,1)}, bf16[1024,2048]{1,0:T(8,128)(2,1)}, u32[]{:S(2)}, u32[]{:S(2)}) collective-permute-start(bf16[1024,2048]{1,0:T(8,128)(2,1)} %convolution_convert_fusion), channel_id=1, source_target_pairs={{2,1},{1,2},{6,5},{5,6},{10,9},{9,10},{14,13},{13,14},{18,17},{17,... | collective-permute-start | bytes 12582920 | tf_op jit(solution)/shard_map/ppermute | solution.py:621
  361.1 184.1 %collective-permute-start.17 = (bf16[512,1024]{1,0:T(8,128)(2,1)}, bf16[512,1024]{1,0:T(8,128)(2,1)}, u32[]{:S(2)}, u32[]{:S(2)}) collective-permute-start(bf16[512,1024]{1,0:T(8,128)(2,1)} %add_convert_fusion.2), channel_id=1, source_target_pairs={{2,1},{1,2},{6,5},{5,6},{10,9},{9,10},{14,13},{13,14},{18,17},{17,... | collective-permute-start | bytes 3145736 | tf_op jit(solution)/shard_map/ppermute | solution.py:621
  504.0 54.2 %collective-permute-start.27 = (bf16[1024,768]{1,0:T(8,128)(2,1)}, bf16[1024,768]{1,0:T(8,128)(2,1)}, u32[]{:S(2)}, u32[]{:S(2)}) collective-permute-start(bf16[1024,768]{1,0:T(8,128)(2,1)} %get-tuple-element.150), channel_id=1, source_target_pairs={{2,1},{1,2},{6,5},{5,6},{10,9},{9,10},{14,13},{13,14},{18,17},{17,... | collective-permute-start | bytes 4718600 | tf_op jit(solution)/shard_map/ppermute | solution.py:621
  514.8 48.6 %collective-permute-start.36 = (bf16[1024,768]{1,0:T(8,128)(2,1)}, bf16[1024,768]{1,0:T(8,128)(2,1)}, u32[]{:S(2)}, u32[]{:S(2)}) collective-permute-start(bf16[1024,768]{1,0:T(8,128)(2,1)} %get-tuple-element.151), channel_id=1, source_target_pairs={{2,1},{1,2},{6,5},{5,6},{10,9},{9,10},{14,13},{13,14},{18,17},{17,... | collective-permute-start | bytes 4718600 | tf_op jit(solution)/shard_map/ppermute | solution.py:621
  527.4 45.2 %collective-permute-start.20 = (bf16[1280,1024]{1,0:T(8,128)(2,1)}, bf16[1280,1024]{1,0:T(8,128)(2,1)}, u32[]{:S(2)}, u32[]{:S(2)}) collective-permute-start(bf16[1280,1024]{1,0:T(8,128)(2,1)} %input_grad.3), channel_id=1, source_target_pairs={{0,2},{2,0},{1,3},{3,1},{4,6},{6,4},{5,7},{7,5},{8,10},{10,8},{9,1... | collective-permute-start | bytes 7864328 | tf_op jit(solution)/shard_map/ppermute | solution.py:671
  545.3 102.0 %collective-permute-start.18 = (bf16[1280,1024]{1,0:T(8,128)(2,1)}, bf16[1280,1024]{1,0:T(8,128)(2,1)}, u32[]{:S(2)}, u32[]{:S(2)}) collective-permute-start(bf16[1280,1024]{1,0:T(8,128)(2,1)} %get-tuple-element.127), channel_id=1, source_target_pairs={{2,1},{1,2},{6,5},{5,6},{10,9},{9,10},{14,13},{13,14},{18,17},{17,... | collective-permute-start | bytes 7864328 | tf_op jit(solution)/shard_map/ppermute | solution.py:621
  561.9 8.9 %collective-permute-start.28 = (bf16[512,768]{1,0:T(8,128)(2,1)}, bf16[512,768]{1,0:T(8,128)(2,1)S(1)}, u32[]{:S(2)}, u32[]{:S(2)}) collective-permute-start(bf16[512,768]{1,0:T(8,128)(2,1)} %constant_dynamic-slice_fusion.4), channel_id=1, source_target_pairs={{2,0},{3,1},{0,2},{1,3},{6,4},{7,5},{4,6},{5,7},{10,8},{11,9},{8,1... | collective-permute-start | bytes 2359304 | tf_op jit(solution)/shard_map/ppermute | solution.py:640
  572.4 17.6 %collective-permute-start.29 = (bf16[256,768]{1,0:T(8,128)(2,1)S(1)}, bf16[256,768]{1,0:T(8,128)(2,1)S(1)}, u32[]{:S(2)}, u32[]{:S(2)}) collective-permute-start(bf16[256,768]{1,0:T(8,128)(2,1)S(1)} %constant_dynamic-slice_fusion.3), channel_id=1, source_target_pairs={{4,0},{5,1},{6,2},{7,3},{0,4},{1,5},{2,6},{3,7},{12,8},{13,9},{14,... | collective-permute-start | bytes 1179656 | tf_op jit(solution)/shard_map/ppermute | solution.py:640
  590.2 10.5 %collective-permute-start.30 = (bf16[128,768]{1,0:T(8,128)(2,1)S(1)}, bf16[128,768]{1,0:T(8,128)(2,1)S(1)}, u32[]{:S(2)}, u32[]{:S(2)}) collective-permute-start(bf16[128,768]{1,0:T(8,128)(2,1)S(1)} %constant_dynamic-slice_fusion.2), channel_id=1, source_target_pairs={{8,0},{9,1},{10,2},{11,3},{12,4},{13,5},{14,6},{15,7},{0,8},{1,9},... | collective-permute-start | bytes 589832 | tf_op jit(solution)/shard_map/ppermute | solution.py:640
  597.0 59.2 %collective-permute-start.21 = (bf16[1280,1024]{1,0:T(8,128)(2,1)}, bf16[1280,1024]{1,0:T(8,128)(2,1)}, u32[]{:S(2)}, u32[]{:S(2)}) collective-permute-start(bf16[1280,1024]{1,0:T(8,128)(2,1)} %fusion.19), channel_id=1, source_target_pairs={{2,1},{1,2},{6,5},{5,6},{10,9},{9,10},{14,13},{13,14},{18,17},{17,... | collective-permute-start | bytes 7864328 | tf_op jit(solution)/shard_map/ppermute | solution.py:621
  600.8 9.7 %collective-permute-start.31 = (bf16[64,768]{1,0:T(8,128)(2,1)S(1)}, bf16[64,768]{1,0:T(8,128)(2,1)S(1)}, u32[]{:S(2)}, u32[]{:S(2)}) collective-permute-start(bf16[64,768]{1,0:T(8,128)(2,1)S(1)} %constant_dynamic-slice_fusion.1), channel_id=1, source_target_pairs={{16,0},{17,1},{18,2},{19,3},{20,4},{21,5},{22,6},{23,7},{24,8},{25... | collective-permute-start | bytes 294920 | tf_op jit(solution)/shard_map/ppermute | solution.py:640
  603.2 26.6 %collective-permute-start.22 = (f32[16384]{0:T(1024)S(1)}, f32[16384]{0:T(1024)S(1)}, u32[]{:S(2)}, u32[]{:S(2)}) collective-permute-start(f32[16384]{0:T(1024)S(1)} %pad_maximum_fusion.4), channel_id=1, source_target_pairs={{0,1},{1,0},{2,3},{3,2},{4,5},{5,4},{6,7},{7,6},{8,9},{9,8},{10,11... | collective-permute-start | bytes 196616 | tf_op jit(solution)/shard_map/ppermute | solution.py:690
  610.6 19.3 %collective-permute-start.32 = (bf16[64,768]{1,0:T(8,128)(2,1)S(1)}, bf16[64,768]{1,0:T(8,128)(2,1)S(1)}, u32[]{:S(2)}, u32[]{:S(2)}) collective-permute-start(bf16[64,768]{1,0:T(8,128)(2,1)S(1)} %add_convert_fusion.6), channel_id=1, source_target_pairs={{16,0},{17,1},{18,2},{19,3},{20,4},{21,5},{22,6},{23,7},{24,8},{25... | collective-permute-start | bytes 294920 | tf_op jit(solution)/shard_map/ppermute | solution.py:640
  629.8 1.3 collective-permute-start.23
  630.0 16.1 %collective-permute-start.33 = (bf16[128,768]{1,0:T(8,128)(2,1)S(1)}, bf16[128,768]{1,0:T(8,128)(2,1)S(1)}, u32[]{:S(2)}, u32[]{:S(2)}) collective-permute-start(bf16[128,768]{1,0:T(8,128)(2,1)S(1)} %pad_maximum_fusion.3), channel_id=1, source_target_pairs={{8,0},{9,1},{10,2},{11,3},{12,4},{13,5},{14,6},{15,7},{0,8},{1,9},... | collective-permute-start | bytes 589832 | tf_op jit(solution)/shard_map/ppermute | solution.py:640
  631.2 4.9 collective-permute-start.24
  636.1 8.1 %collective-permute-start.25 = (f32[16384]{0:T(1024)S(1)}, f32[16384]{0:T(1024)S(1)}, u32[]{:S(2)}, u32[]{:S(2)}) collective-permute-start(f32[16384]{0:T(1024)S(1)} %add.343), channel_id=1, source_target_pairs={{0,8},{1,9},{2,10},{3,11},{4,12},{5,13},{6,14},{7,15},{8,0},{9,1},... | collective-permute-start | bytes 196616 | tf_op jit(solution)/shard_map/ppermute | solution.py:690
  644.2 8.9 %collective-permute-start.26 = (f32[16384]{0:T(1024)S(1)}, f32[16384]{0:T(1024)S(1)}, u32[]{:S(2)}, u32[]{:S(2)}) collective-permute-start(f32[16384]{0:T(1024)S(1)} %add.344), channel_id=1, source_target_pairs={{0,16},{1,17},{2,18},{3,19},{4,20},{5,21},{6,22},{7,23},{8,24},{9,... | collective-permute-start | bytes 196616 | tf_op jit(solution)/shard_map/ppermute | solution.py:690
  646.2 9.8 %collective-permute-start.34 = (bf16[256,768]{1,0:T(8,128)(2,1)S(1)}, bf16[256,768]{1,0:T(8,128)(2,1)S(1)}, u32[]{:S(2)}, u32[]{:S(2)}) collective-permute-start(bf16[256,768]{1,0:T(8,128)(2,1)S(1)} %pad_maximum_fusion.2), channel_id=1, source_target_pairs={{4,0},{5,1},{6,2},{7,3},{0,4},{1,5},{2,6},{3,7},{12,8},{13,9},{14,... | collective-permute-start | bytes 1179656 | tf_op jit(solution)/shard_map/ppermute | solution.py:640
  656.2 83.8 %collective-permute-start.35 = (bf16[512,768]{1,0:T(8,128)(2,1)S(1)}, bf16[512,768]{1,0:T(8,128)(2,1)S(1)}, u32[]{:S(2)}, u32[]{:S(2)}) collective-permute-start(bf16[512,768]{1,0:T(8,128)(2,1)S(1)} %pad_maximum_fusion.1.a), channel_id=1, source_target_pairs={{2,0},{3,1},{0,2},{1,3},{6,4},{7,5},{4,6},{5,7},{10,8},{11,9},{8,1... | collective-permute-start | bytes 2359304 | tf_op jit(solution)/shard_map/ppermute | solution.py:640
  (61 other events, 320.3 us)
Sparse Core Ops, SparseCore 0:
  337.2 139.0 all-reduce.3
  570.9 159.0 all-reduce.5

commit v10 on v8

--- a/solution.py
+++ b/solution.py
@@ -326,12 +326,12 @@
     )(tables, kseg, seg[None, :], *qkv_parts, *begun)
 
 
-def attend_backward(qkv_parts, turned, grad_ctx, lse, seg, keep, tables, chunk, begun=()):
+def attend_backward(qkv_parts, turned, grad_ctx, lse, seg, keep, tables, chunk, place, begun=()):
     parts, width, tokens, every, pairs, seg_specs, qkv_specs, o_specs, ot_spec, lse_spec = (
         attend_specs(qkv_parts, chunk)
     )
     kseg = jnp.where(keep == 1, seg, -1)[:, None]
-    result = pl.BlockSpec((width, 3 * PAIR), lanes_of(chunk[0], 1))
+    result = pl.BlockSpec((width, 3 * PAIR), lanes_of(place[0], 1))
     return pl.pallas_call(
         functools.partial(backward_kernel, parts),
         grid_spec=pltpu.PrefetchScalarGridSpec(
@@ -356,7 +356,7 @@
                 pltpu.VMEM((tokens, 128), F32),
             ],
         ),
-        out_shape=[jax.ShapeDtypeStruct((width, every * 3 * PAIR), BF16)] * parts,
+        out_shape=[jax.ShapeDtypeStruct((width, place[1] * 3 * PAIR), BF16)] * parts,
         input_output_aliases={5 + 2 * parts + n: n for n in range(len(begun))},
         compiler_params=pltpu.CompilerParams(vmem_limit_bytes=48 * 2**20),
         cost_estimate=pl.CostEstimate(
@@ -529,27 +529,33 @@
     )(*a_parts, *d_parts)
 
 
-def input_grad_kernel(d_ref, w_ref, out_ref):
-    out_ref[...] = contract_cols(d_ref[...], w_ref[...]).astype(BF16)
-
-
-def input_grad(d, weight):
-    width, columns = d.shape
+def input_grad_kernel(w_ref, *refs):
+    *d_refs, out_ref = refs
+    columns = d_refs[0].shape[1]
+    terms = [
+        contract_cols(d[...], w_ref[:, k * columns : (k + 1) * columns])
+        for k, d in enumerate(d_refs)
+    ]
+    out_ref[...] = total(terms).astype(BF16)
+
+
+def input_grad(chunks, weight):
+    width, columns = chunks[0].shape
     model = weight.shape[0]
     rows = row_block(width)
     return pl.pallas_call(
         input_grad_kernel,
         grid=(width // rows,),
         in_specs=[
-            pl.BlockSpec((rows, columns), lambda k: (k, 0)),
-            pl.BlockSpec((model, columns), lambda k: (0, 0), pipeline_mode=pl.Buffered(1)),
-        ],
+            pl.BlockSpec(weight.shape, lambda k: (0, 0), pipeline_mode=pl.Buffered(1)),
+        ]
+        + [pl.BlockSpec((rows, columns), lambda k: (k, 0))] * len(chunks),
         out_specs=pl.BlockSpec((rows, model), lambda k: (k, 0)),
         out_shape=jax.ShapeDtypeStruct((width, model), BF16),
         compiler_params=pltpu.CompilerParams(vmem_limit_bytes=40 * 2**20),
         cost_estimate=pl.CostEstimate(flops=2**10, bytes_accessed=2**10, transcendentals=0),
         name="input_grad",
-    )(d, weight)
+    )(weight, *chunks)
 
 
 def spread_kernel(tab_ref, mine_ref, theirs_ref, out_ref):
@@ -861,11 +867,11 @@
     g_w_down = jnp.where(stays, g_w_down, g_w_down_far)
     tables, g_w_down = lax.optimization_barrier((tables, g_w_down))
     g_w_down = layout.sum_dp(g_w_down, 1)
-    calls = [(0, pairs // 2)] if pairs > 1 else []
-    calls += [(k, 1) for k in range(pairs // 2, pairs)]
-    grad_qkv = ()
+    each = pairs // chunks
+    calls = [(0, each)] + [(k, 1) for k in range(each, pairs)]
+    done, g_w_qkv, sums, grad_qkv = [], [], [], ()
     for call in calls:
-        if call == calls[-1]:
+        if len(calls) > 1 and call == calls[-1]:
             g_w_up_far, g_w_out_far, *grad_qkv = lax.optimization_barrier(
                 (g_w_up_far, g_w_out_far, *grad_qkv)
             )
@@ -874,25 +880,41 @@
             tables, g_w_down, g_w_up, g_w_out = lax.optimization_barrier(
                 (tables, g_w_down, g_w_up, g_w_out)
             )
-            g_w_up = layout.sum_dp(g_w_up, 0)
-            g_w_out = layout.sum_dp(g_w_out, 0)
         grad_qkv = attend_backward(
-            qkv, context_turned, grad_ctx, log_total, seg, keep, tables, call, grad_qkv
+            qkv,
+            context_turned,
+            grad_ctx,
+            log_total,
+            seg,
+            keep,
+            tables,
+            call,
+            (call[0] % each, each),
+            grad_qkv,
         )
-    layer_out = layout.give_back(after(layer_out, g_w_out_far))
-    grad_qkv = from_kernel(grad_qkv, rank, shares)
-    grad_a1 = [input_grad(g, w_qkv) for g in grad_qkv]
+        if sum(call) % each == 0:
+            shared = from_kernel(grad_qkv, rank, shares)
+            g_part, part_sums = weight_grad(a1, shared, 0, each)
+            tables, g_part = lax.optimization_barrier((tables, g_part))
+            g_w_qkv.append(layout.halved(layout.give_back(g_part), -1))
+            sums.append(part_sums)
+            done.append(shared)
+            grad_qkv = ()
+    if len(calls) == 1:
+        g_w_up = jnp.where(stays, g_w_up, g_w_up_far)
+        g_w_out = jnp.where(stays, g_w_out, g_w_out_far)
+    g_w_up = layout.sum_dp(g_w_up, 0)
+    g_w_out = layout.sum_dp(g_w_out, 0)
+    layer_out = layout.give_back(after(layer_out, g_w_qkv[0]))
+    sums = jnp.concatenate(sums, 1)
+    grad_a1 = [input_grad(d, w_qkv) for d in zip(*done)]
     grad_a1 = layout.scatter_sum(grad_a1)
     grad_input = grad_mid + norm_back(grad_a1, normed1, inv1, ln1_gain)
     grad_input = grad_input.astype(bf16)
-    g_w_qkv, sums = [], []
-    each = pairs // chunks
-    for chunk in range(chunks):
-        g_part, part_sums = weight_grad(a1, grad_qkv, chunk * each, each)
-        g_w_qkv.append(layout.halved(layout.give_back(g_part), -1))
-        sums.append(part_sums)
-    sums = jnp.concatenate(sums, 1)
-    g_w_qkv = [layout.halved_by(g, layout.order(k)) for k, g in enumerate(g_w_qkv)]
+    steps = [layout.order(k) for k in range(chunks)]
+    g_w_qkv[0] = layout.halved(g_w_qkv[0], steps[0].pop(0))
+    g_w_qkv = list(lax.optimization_barrier(tuple(g_w_qkv)))
+    g_w_qkv = [layout.halved_by(g, s) for g, s in zip(g_w_qkv, steps)]
     g_w_qkv = [layout.joined_by(g, layout.order(k)) for k, g in enumerate(g_w_qkv)]
     begun = ()
     for chunk, mine in enumerate(g_w_qkv):

time: 761 us -> 763 us (level)
  starting transfers between devices: 151 us -> 138 us
  local copies, waits for them, and re-layouts: 41.4 us -> 49.5 us
    ppermute x8, starting transfers between devices: 89.7 us -> 78.1 us  [to_rank(): return lax.ppermute(value, self.axes, moves)]
    psum x2, waiting for transfers between devices: 95.1 us -> 105 us  [sum_dp(): return lax.psum(value, 'dp', axis_index_groups=[order])]
    unnamed x137 -> x157, local copies, waits for them, and re-layouts: 24.3 us -> 31.1 us
  transfers between devices with their start and end apart: 48 -> 48, of which waited for: 12 -> 14; matrix products, arithmetic and copies ran while one was open for 19% -> 20% of each run, Pallas kernels for 22% -> 26%
where the time goes in v10:
time: 763 us; the launch traced here: 754 us
  Pallas kernels  227 us (30%)
  waiting for transfers between devices  156 us (20%)
  starting transfers between devices  138 us (18%)
  other arithmetic  110 us (14%)
  matrix products  56 us (7%)
  local copies, waits for them, and re-layouts  49.5 us (6%)
  between operations  17.4 us (2%)
    psum x2, waiting for transfers between devices, sum_dp(): return lax.psum(value, 'dp', axis_index_groups=[order])  105 us
    ppermute x8, starting transfers between devices, to_rank(): return lax.ppermute(value, self.axes, moves)  78.1 us
    pallas_call x3, Pallas kernels, attend_backward(): pl.pallas_call(functools.partial(backward_kernel, parts), grid_spec=pltpu...  76.6 us
    pallas_call x4, Pallas kernels, attend_forward(): pl.pallas_call(functools.partial(forward_kernel, parts), grid_spec=pltpu....  50.3 us
    dot_general x4, matrix products, contract_rows(): lax.dot_general(left, right, (((0,), (0,)), ((), ())), preferred_element_...  36.2 us
    pallas_call x2, Pallas kernels, feed_forward(): pl.pallas_call(functools.partial(feed_kernel, min(units, FEED)), grid=(st...  35.6 us
    ppermute x18, waiting for transfers between devices, partner(): return lax.ppermute(value, self.axes, moves)  34.5 us
    pallas_call x2, Pallas kernels, feed_back(): pl.pallas_call(functools.partial(feed_back_kernel, min(units, FEED)), gri...  32 us
  transfers between devices with their start and end apart: 48, of which 14 were waited for; matrix products, arithmetic and copies ran while one was open for 20% of the time, Pallas kernels for 26%

profile of v10, /device:TPU:0, one launch (start us, length us, event | category | flops | bytes accessed | tf_op | source)
XLA Modules:
  0.0 753.9 jit_solution(6098632510835913247)
XLA Ops:
  7.3 3.2 copy.69
  16.9 4.7 fusion.52
  34.6 38.5 %collective-permute-start.6 = (bf16[1280,1024]{1,0:T(8,128)(2,1)S(1)}, bf16[1280,1024]{1,0:T(8,128)(2,1)}, u32[]{:S(2)}, u32[]{:S(2)}) collective-permute-start(bf16[1280,1024]{1,0:T(8,128)(2,1)S(1)} %fusion.14.refs_0_), channel_id=1, source_target_pairs={{0,2},{2,0},{1,3},{3,1},{4,6},{6,4},{5,7},{7,5},{8,10},{10,8},{9,1... | collective-permute-start | bytes 7864328 | tf_op jit(solution)/shard_map/ppermute | solution.py:675
  84.7 4.5 fusion.2.refs_0_
  89.3 7.8 %fusion.3.refs_1_ = bf16[1280,1536]{1,0:T(8,128)(2,1)S(1)} fusion(bf16[1280,1024]{1,0:T(8,128)(2,1)} %collective-permute-done.6.refs_1_, bf16[1024,1536]{0,1:T(8,128)(2,1)S(1)} %bitcast.60, f32[1536]{0:T(1024)S(1)} %copy-done.72, f32[1536]{0:T(1024)S(1)} %add.349), kind=kOutput, calls=%fused_computation.12 | convolution fusion | flops 4032430080 | bytes 9711616 | tf_op jit(solution)/shard_map/dot_general | solution.py:57
  97.0 12.5 %attend_forward.4 = (bf16[1280,512]{1,0:T(8,128)(2,1)S(1)}, bf16[1280,512]{1,0:T(8,128)(2,1)S(1)}, bf16[512,2560]{1,0:T(8,128)(2,1)S(1)}, f32[4,2,2560]{2,1,0:T(2,128)S(1)}) custom-call(s32[3,10]{1,0:T(4,128)S(1)} %add_add_fusion.2.tab_ref, s32[2560,1]{1,0:T(8,128)S(1)} %copy-done.3, s32[1,2560]{1,0:T(1,128)S(1)} %fusion.45.qseg_ref, ...), custom_call_target="tpu_custom_call" | custom-call | flops 1024 | bytes 1024 | tf_op jit(solution)/shard_map/attend_forward/pallas_call | solution.py:301
  109.6 12.5 %attend_forward.5 = (bf16[1280,512]{1,0:T(8,128)(2,1)S(1)}, bf16[1280,512]{1,0:T(8,128)(2,1)S(1)}, bf16[512,2560]{1,0:T(8,128)(2,1)S(1)}, f32[4,2,2560]{2,1,0:T(2,128)S(1)}) custom-call(s32[3,10]{1,0:T(4,128)S(1)} %add_add_fusion.2.tab_ref, s32[2560,1]{1,0:T(8,128)S(1)} %copy-done.3, ...), custom_call_target="tpu_custom_call", output_to_operand_aliasing={{0}: (5, {}), {1}: (6, {}), {2}: (7, {}), {3}: (8, {})} | custom-call | flops 1024 | bytes 1024 | tf_op jit(solution)/shard_map/attend_forward/pallas_call | solution.py:301
  122.1 12.5 %attend_forward.6 = (bf16[1280,512]{1,0:T(8,128)(2,1)S(1)}, bf16[1280,512]{1,0:T(8,128)(2,1)S(1)}, bf16[512,2560]{1,0:T(8,128)(2,1)S(1)}, f32[4,2,2560]{2,1,0:T(2,128)S(1)}) custom-call(s32[3,10]{1,0:T(4,128)S(1)} %add_add_fusion.2.tab_ref, s32[2560,1]{1,0:T(8,128)S(1)} %copy-done.3, ...), custom_call_target="tpu_custom_call", output_to_operand_aliasing={{0}: (5, {}), {1}: (6, {}), {2}: (7, {}), {3}: (8, {})} | custom-call | flops 1024 | bytes 1024 | tf_op jit(solution)/shard_map/attend_forward/pallas_call | solution.py:301
  134.7 12.7 %attend_forward.7 = (bf16[1280,512]{1,0:T(8,128)(2,1)S(1)}, bf16[1280,512]{1,0:T(8,128)(2,1)S(1)}, bf16[512,2560]{1,0:T(8,128)(2,1)S(1)}, f32[4,2,2560]{2,1,0:T(2,128)S(1)}) custom-call(s32[3,10]{1,0:T(4,128)S(1)} %add_add_fusion.2.tab_ref, s32[2560,1]{1,0:T(8,128)S(1)} %copy-done.3, ...), custom_call_target="tpu_custom_call", output_to_operand_aliasing={{0}: (5, {}), {1}: (6, {}), {2}: (7, {}), {3}: (8, {})} | custom-call | flops 1024 | bytes 1024 | tf_op jit(solution)/shard_map/attend_forward/pallas_call | solution.py:301
  152.5 25.4 %collective-permute-start.10 = (bf16[1280,1024]{1,0:T(8,128)(2,1)S(1)}, bf16[1280,1024]{1,0:T(8,128)(2,1)S(1)}, u32[]{:S(2)}, u32[]{:S(2)}) collective-permute-start(bf16[1280,1024]{1,0:T(8,128)(2,1)S(1)} %convolution_convert_fusion.1), channel_id=1, source_target_pairs={{0,2},{2,0},{1,3},{3,1},{4,6},{6,4},{5,7},{7,5},{8,10},{10,8},{9,1... | collective-permute-start | bytes 7864328 | tf_op jit(solution)/shard_map/ppermute | solution.py:675
  178.9 4.6 broadcast_select_fusion.2.up_ref
  194.8 3.4 collective-permute-start.11
  198.2 3.7 maximum_select_fusion.down_ref
  202.3 17.7 %feed_forward.2 = (bf16[2560,1024]{1,0:T(8,128)(2,1)}, bf16[2560,2048]{1,0:T(8,128)(2,1)}, bf16[2560,2048]{1,0:T(8,128)(2,1)}, bf16[1280,1024]{1,0:T(8,128)(2,1)S(1)}) custom-call(bf16[1280,1024]{1,0:T(8,128)(2,1)S(1)} %add_convert_fusion.1.x_ref, bf16[1024,2048]{1,0:T(8,128)(2,1)} %broadcast_select_fusion.2.up_ref, f32[1,2048]{1,0:T(1,128)S(1)} %bitcast.52, ...), custom_call_target="tpu_custom_call" | custom-call | flops 16106127360 | bytes 16777216 | tf_op jit(solution)/shard_map/feed_forward/pallas_call | solution.py:411
  220.0 17.9 %feed_forward.3 = (bf16[2560,1024]{1,0:T(8,128)(2,1)}, bf16[2560,2048]{1,0:T(8,128)(2,1)}, bf16[2560,2048]{1,0:T(8,128)(2,1)}, bf16[1280,1024]{1,0:T(8,128)(2,1)S(1)}) custom-call(bf16[1280,1024]{1,0:T(8,128)(2,1)S(1)} %collective-permute-done.11.x_ref, ...), custom_call_target="tpu_custom_call", output_to_operand_aliasing={{0}: (4, {}), {1}: (5, {}), {2}: (6, {})} | custom-call | flops 16106127360 | bytes 16777216 | tf_op jit(solution)/shard_map/feed_forward/pallas_call | solution.py:411
  237.9 9.6 %collective-permute-start.13 = (bf16[1280,1024]{1,0:T(8,128)(2,1)S(1)}, bf16[1280,1024]{1,0:T(8,128)(2,1)S(1)}, u32[]{:S(2)}, u32[]{:S(2)}) collective-permute-start(bf16[1280,1024]{1,0:T(8,128)(2,1)S(1)} %get-tuple-element.129), channel_id=1, source_target_pairs={{0,2},{2,0},{1,3},{3,1},{4,6},{6,4},{5,7},{7,5},{8,10},{10,8},{9,1... | collective-permute-start | bytes 7864328 | tf_op jit(solution)/shard_map/ppermute | solution.py:675
  247.4 4.5 collective-permute-done.13
  254.3 3.6 fusion.26
  257.9 4.9 convert_reduce_fusion.2
  263.2 16.1 %feed_back.2 = (bf16[2560,2048]{1,0:T(8,128)(2,1)}, f32[1,2048]{1,0:T(1,128)S(1)}, bf16[1280,1024]{1,0:T(8,128)(2,1)S(1)}) custom-call(bf16[1280,1024]{1,0:T(8,128)(2,1)S(1)} %get-tuple-element.193.g_ref, bf16[2560,2048]{1,0:T(8,128)(2,1)} %get-tuple-element.135.slope_ref, bf16[2048,1024]{1,0:T(8,128)(2,1)} %maximum_select_fusion.down_ref, ...), custom_call_target="tpu_custom_call" | custom-call | flops 1024 | bytes 1024 | tf_op jit(solution)/shard_map/feed_back/pallas_call | solution.py:473
  279.3 15.3 %fusion.38 = bf16[2048,1024]{1,0:T(8,128)(2,1)} fusion(bf16[2560,2048]{1,0:T(8,128)(2,1)} %get-tuple-element.131, bf16[1280,1024]{1,0:T(8,128)(2,1)S(1)} %collective-permute-done.14.g_ref, bf16[1280,1024]{1,0:T(8,128)(2,1)S(1)} %get-tuple-element.193.g_ref), kind=kOutput, calls=%fused_computation.72 | convolution fusion | flops 10750001152 | bytes 19922944 | tf_op jit(solution)/shard_map/dot_general | solution.py:35
  294.6 15.9 %feed_back.3 = (bf16[2560,2048]{1,0:T(8,128)(2,1)}, f32[1,2048]{1,0:T(1,128)S(1)}, bf16[1280,1024]{1,0:T(8,128)(2,1)S(1)}) custom-call(bf16[1280,1024]{1,0:T(8,128)(2,1)S(1)} %collective-permute-done.14.g_ref, bf16[2560,2048]{1,0:T(8,128)(2,1)} %get-tuple-element.135.slope_ref, ...), custom_call_target="tpu_custom_call", output_to_operand_aliasing={{0}: (4, {})} | custom-call | flops 1024 | bytes 1024 | tf_op jit(solution)/shard_map/feed_back/pallas_call | solution.py:473
  311.6 3.9 collective-permute-done.16
  315.4 4.9 multiply_reduce_fusion
  320.3 8.6 %multiply_reduce_fusion.1 = (f32[1024]{0:T(1024)S(1)}, f32[1280]{0:T(1024)S(1)}, f32[1280]{0:T(1024)S(1)}, f32[1024]{0:T(1024)}, f32[1280,1024]{1,0:T(8,128)S(1)}) fusion(f32[1280,1024]{1,0:T(8,128)} %copy-done.27, f32[1280]{0:T(1024)S(1)} %add_rsqrt_fusion.2, f32[1280]{0:T(1024)S(1)} %broadcast_multiply_fusion.10, f32[1024]{0:T(1024)S(1)} %copy-done.58, ...), kind=kLoop, calls=%fused_computation.42 | loop fusion | flops 27520512 | bytes 23650304 | tf_op jit(solution)/shard_map/reduce_sum | solution.py:932
  331.5 16.9 %convolution_convert_fusion = bf16[1024,2048]{1,0:T(8,128)(2,1)} fusion(bf16[2560,1024]{1,0:T(8,128)(2,1)} %get-tuple-element.133, bf16[2560,2048]{1,0:T(8,128)(2,1)} %get-tuple-element.137), kind=kOutput, calls=%fused_computation.71 | convolution fusion | flops 10739515392 | bytes 19922944 | tf_op jit(solution)/shard_map/dot_general | solution.py:35
  366.2 36.7 %attend_backward.3 = (bf16[1280,768]{1,0:T(8,128)(2,1)S(1)}, bf16[1280,768]{1,0:T(8,128)(2,1)}) custom-call(s32[3,10]{1,0:T(4,128)S(1)} %add_add_fusion.2.tab_ref, s32[2560,1]{1,0:T(8,128)S(1)} %copy-done.4, s32[1,2560]{1,0:T(1,128)S(1)} %fusion.45.qseg_ref, bf16[1280,1536]{1,0:T(8,128)(2,1)} %copy-done, bf16[1280,1536]{1,0:T(8,128)(2,1)} %copy-done.1, ...), custom_call_target="tpu_custom_call" | custom-call | flops 1024 | bytes 1024 | tf_op jit(solution)/shard_map/attend_backward/pallas_call | solution.py:335
  405.2 8.9 %weight_grad.2 = (bf16[1024,768]{1,0:T(8,128)(2,1)}, f32[1,768]{1,0:T(1,128)S(1)}) custom-call(bf16[1280,1024]{1,0:T(8,128)(2,1)S(1)} %copy-done.6, bf16[1280,1024]{1,0:T(8,128)(2,1)} %collective-permute-done.6.refs_1_, bf16[1280,768]{1,0:T(8,128)(2,1)S(1)} %get-tuple-element.146.refs_2_.refs_0_, bf16[1280,768]{1,0:T(8,128)(2,1)S(1)} %copy-done.22), custom_call_target="tpu_custom_call" | custom-call | flops 1024 | bytes 1024 | tf_op jit(solution)/shard_map/weight_grad/pallas_call | solution.py:513
  416.2 19.9 %attend_backward.4 = (bf16[1280,768]{1,0:T(8,128)(2,1)S(1)}, bf16[1280,768]{1,0:T(8,128)(2,1)}) custom-call(s32[3,10]{1,0:T(4,128)S(1)} %add_add_fusion.2.tab_ref, s32[2560,1]{1,0:T(8,128)S(1)} %copy-done.4, s32[1,2560]{1,0:T(1,128)S(1)} %fusion.45.qseg_ref, bf16[1280,1536]{1,0:T(8,128)(2,1)} %copy-done, bf16[1280,1536]{1,0:T(8,128)(2,1)} %copy-done.1, ...), custom_call_target="tpu_custom_call" | custom-call | flops 1024 | bytes 1024 | tf_op jit(solution)/shard_map/attend_backward/pallas_call | solution.py:335
  438.5 4.6 broadcast_select_fusion.1
  443.1 40.8 %all-reduce.4.cloned.1.call-done = bf16[2048,1024]{1,0:T(8,128)(2,1)} async-done(((bf16[2048,1024]{1,0:T(8,128)(2,1)}), bf16[2048,1024]{1,0:T(8,128)(2,1)}) %all-reduce.4.cloned.1.call-update) | async-done | bytes 4194320 | tf_op jit(solution)/shard_map/psum | solution.py:699
  486.5 20.0 %attend_backward.5 = (bf16[1280,768]{1,0:T(8,128)(2,1)S(1)}, bf16[1280,768]{1,0:T(8,128)(2,1)}) custom-call(s32[3,10]{1,0:T(4,128)S(1)} %add_add_fusion.2.tab_ref, s32[2560,1]{1,0:T(8,128)S(1)} %copy-done.4, s32[1,2560]{1,0:T(1,128)S(1)} %fusion.45.qseg_ref, bf16[1280,1536]{1,0:T(8,128)(2,1)} %copy-done, ...), custom_call_target="tpu_custom_call", output_to_operand_aliasing={{0}: (9, {}), {1}: (10, {})} | custom-call | flops 1024 | bytes 1024 | tf_op jit(solution)/shard_map/attend_backward/pallas_call | solution.py:335
  508.8 8.7 %weight_grad.3 = (bf16[1024,768]{1,0:T(8,128)(2,1)}, f32[1,768]{1,0:T(1,128)S(1)}) custom-call(bf16[1280,1024]{1,0:T(8,128)(2,1)S(1)} %copy-done.7, bf16[1280,1024]{1,0:T(8,128)(2,1)} %collective-permute-done.6.refs_1_, bf16[1280,768]{1,0:T(8,128)(2,1)S(1)} %get-tuple-element.161.refs_1_.refs_2_, bf16[1280,768]{1,0:T(8,128)(2,1)S(1)} %copy-done.12), custom_call_target="tpu_custom_call" | custom-call | flops 1024 | bytes 1024 | tf_op jit(solution)/shard_map/weight_grad/pallas_call | solution.py:513
  522.5 3.2 copy.81.w_ref
  528.8 5.5 input_grad.3
  538.7 3.3 collective-permute-start.32
  548.4 4.5 input_grad.2
  560.0 10.9 %collective-permute-start.40 = (bf16[128,768]{1,0:T(8,128)(2,1)}, bf16[128,768]{1,0:T(8,128)(2,1)}, u32[]{:S(2)}, u32[]{:S(2)}) collective-permute-start(bf16[128,768]{1,0:T(8,128)(2,1)} %constant_dynamic-slice_fusion.2), channel_id=1, source_target_pairs={{8,0},{9,1},{10,2},{11,3},{12,4},{13,5},{14,6},{15,7},{0,8},{1,9},... | collective-permute-start | bytes 589832 | tf_op jit(solution)/shard_map/ppermute | solution.py:644
  580.8 5.5 fusion.20
  590.2 6.5 fusion.19
  599.0 7.2 collective-permute-done.25
  613.3 13.0 %collective-permute-done.34 = bf16[128,768]{1,0:T(8,128)(2,1)S(1)} collective-permute-done((bf16[128,768]{1,0:T(8,128)(2,1)S(1)}, bf16[128,768]{1,0:T(8,128)(2,1)S(1)}, u32[]{:S(2)}, u32[]{:S(2)}) %collective-permute-start.34) | collective-permute-done | bytes 196640 | tf_op jit(solution)/shard_map/ppermute | solution.py:644
  635.9 3.6 collective-permute-done.43
  641.0 8.3 %collective-permute-done.37 = bf16[128,768]{1,0:T(8,128)(2,1)S(1)} collective-permute-done((bf16[128,768]{1,0:T(8,128)(2,1)S(1)}, bf16[128,768]{1,0:T(8,128)(2,1)S(1)}, u32[]{:S(2)}, u32[]{:S(2)}) %collective-permute-start.37) | collective-permute-done | bytes 196640 | tf_op jit(solution)/shard_map/ppermute | solution.py:644
  649.4 6.7 convert_element_type.231
  656.2 63.9 %all-reduce.6.cloned.1.call-done = (bf16[512,1024]{1,0:T(8,128)(2,1)}, bf16[1024,2048]{1,0:T(8,128)(2,1)}) async-done(((bf16[512,1024]{1,0:T(8,128)(2,1)}, bf16[1024,2048]{1,0:T(8,128)(2,1)}), (bf16[512,1024]{1,0:T(8,128)(2,1)}, bf16[1024,2048]{1,0:T(8,128)(2,1)})) %all-reduce.6.cloned.1.call-update) | async-done | bytes 5242896 | tf_op jit(solution)/shard_map/psum | solution.py:699
  722.9 6.7 convert_element_type.230
  742.4 4.4 select_convert_fusion
  (358 shorter events, 158.0 us)
Async XLA Ops:
  7.2 476.6 %all-reduce.4.cloned.1.call-start = ((), (), s32[]{:S(2)}) async-start(), calls=%async_computation | async-start | bytes 8388608 | tf_op jit(solution)/shard_map/psum | solution.py:699
  10.7 0.8 collective-permute-start
  12.4 0.7 collective-permute-start.1
  13.1 15.6 %collective-permute-start.2 = (bf16[1280,1024]{1,0:T(8,128)(2,1)}, bf16[1280,1024]{1,0:T(8,128)(2,1)}, u32[]{:S(2)}, u32[]{:S(2)}) collective-permute-start(bf16[1280,1024]{1,0:T(8,128)(2,1)} %param.20), channel_id=1, source_target_pairs={{1,2},{2,1},{5,6},{6,5},{9,10},{10,9},{13,14},{14,13},{17,18},{18,... | collective-permute-start | bytes 7864328 | tf_op jit(solution)/shard_map/ppermute | solution.py:625
  15.3 8.5 %collective-permute-start.4 = (bf16[256,3,512]{0,2,1:T(8,128)(2,1)}, bf16[256,3,512]{0,2,1:T(8,128)(2,1)}, u32[]{:S(2)}, u32[]{:S(2)}) collective-permute-start(bf16[256,3,512]{0,2,1:T(8,128)(2,1)} %copy-done.52), channel_id=1, source_target_pairs={{9,1},{10,2},{13,5},{14,6},{1,9},{2,10},{5,13},{6,14},{25,17},{26,... | collective-permute-start | bytes 2359304 | tf_op jit(solution)/shard_map/ppermute | solution.py:644
  26.7 49.5 %collective-permute-start.5 = (bf16[512,3,512]{0,2,1:T(8,128)(2,1)}, bf16[512,3,512]{0,2,1:T(8,128)(2,1)}, u32[]{:S(2)}, u32[]{:S(2)}) collective-permute-start(bf16[512,3,512]{0,2,1:T(8,128)(2,1)} %pad_maximum_fusion), channel_id=1, source_target_pairs={{5,1},{6,2},{1,5},{2,6},{13,9},{14,10},{9,13},{10,14},{21,17},{22,... | collective-permute-start | bytes 4718600 | tf_op jit(solution)/shard_map/ppermute | solution.py:644
  29.6 92.5 %collective-permute-start.3 = (bf16[1024,2048]{1,0:T(8,128)(2,1)}, bf16[1024,2048]{1,0:T(8,128)(2,1)}, u32[]{:S(2)}, u32[]{:S(2)}) collective-permute-start(bf16[1024,2048]{1,0:T(8,128)(2,1)} %param.31), channel_id=1, source_target_pairs={{1,2},{2,1},{5,6},{6,5},{9,10},{10,9},{13,14},{14,13},{17,18},{18,... | collective-permute-start | bytes 12582920 | tf_op jit(solution)/shard_map/ppermute | solution.py:625
  34.6 54.7 %collective-permute-start.6 = (bf16[1280,1024]{1,0:T(8,128)(2,1)S(1)}, bf16[1280,1024]{1,0:T(8,128)(2,1)}, u32[]{:S(2)}, u32[]{:S(2)}) collective-permute-start(bf16[1280,1024]{1,0:T(8,128)(2,1)S(1)} %fusion.14.refs_0_), channel_id=1, source_target_pairs={{0,2},{2,0},{1,3},{3,1},{4,6},{6,4},{5,7},{7,5},{8,10},{10,8},{9,1... | collective-permute-start | bytes 7864328 | tf_op jit(solution)/shard_map/ppermute | solution.py:675
  78.9 68.5 %collective-permute-start.8 = (bf16[1024,1024]{1,0:T(8,128)(2,1)}, bf16[1024,1024]{1,0:T(8,128)(2,1)S(1)}, u32[]{:S(2)}, u32[]{:S(2)}) collective-permute-start(bf16[1024,1024]{1,0:T(8,128)(2,1)} %get-tuple-element.115), channel_id=1, source_target_pairs={{1,2},{2,1},{5,6},{6,5},{9,10},{10,9},{13,14},{14,13},{17,18},{18,... | collective-permute-start | bytes 6291464 | tf_op jit(solution)/shard_map/ppermute | solution.py:625
  79.7 67.7 %collective-permute-start.9 = (bf16[1024,1024]{1,0:T(8,128)(2,1)S(1)}, bf16[1024,1024]{1,0:T(8,128)(2,1)S(1)}, u32[]{:S(2)}, u32[]{:S(2)}) collective-permute-start(bf16[1024,1024]{1,0:T(8,128)(2,1)S(1)} %copy-done.46), channel_id=1, source_target_pairs={{1,2},{2,1},{5,6},{6,5},{9,10},{10,9},{13,14},{14,13},{17,18},{18,... | collective-permute-start | bytes 6291464 | tf_op jit(solution)/shard_map/ppermute | solution.py:625
  82.2 65.2 %collective-permute-start.7 = (bf16[512,1024]{1,0:T(8,128)(2,1)}, bf16[512,1024]{1,0:T(8,128)(2,1)}, u32[]{:S(2)}, u32[]{:S(2)}) collective-permute-start(bf16[512,1024]{1,0:T(8,128)(2,1)} %param.25), channel_id=1, source_target_pairs={{1,2},{2,1},{5,6},{6,5},{9,10},{10,9},{13,14},{14,13},{17,18},{18,... | collective-permute-start | bytes 3145736 | tf_op jit(solution)/shard_map/ppermute | solution.py:625
  152.5 31.0 %collective-permute-start.10 = (bf16[1280,1024]{1,0:T(8,128)(2,1)S(1)}, bf16[1280,1024]{1,0:T(8,128)(2,1)S(1)}, u32[]{:S(2)}, u32[]{:S(2)}) collective-permute-start(bf16[1280,1024]{1,0:T(8,128)(2,1)S(1)} %convolution_convert_fusion.1), channel_id=1, source_target_pairs={{0,2},{2,0},{1,3},{3,1},{4,6},{6,4},{5,7},{7,5},{8,10},{10,8},{9,1... | collective-permute-start | bytes 7864328 | tf_op jit(solution)/shard_map/ppermute | solution.py:675
  177.9 24.0 %collective-permute-start.12 = (bf16[1280,1024]{1,0:T(8,128)(2,1)S(1)}, bf16[1280,1024]{1,0:T(8,128)(2,1)S(1)}, u32[]{:S(2)}, u32[]{:S(2)}) collective-permute-start(bf16[1280,1024]{1,0:T(8,128)(2,1)S(1)} %copy-done.41), channel_id=1, source_target_pairs={{1,2},{2,1},{5,6},{6,5},{9,10},{10,9},{13,14},{14,13},{17,18},{18,... | collective-permute-start | bytes 7864328 | tf_op jit(solution)/shard_map/ppermute | solution.py:625
  194.8 25.2 %collective-permute-start.11 = (bf16[1280,1024]{1,0:T(8,128)(2,1)S(1)}, bf16[1280,1024]{1,0:T(8,128)(2,1)S(1)}, u32[]{:S(2)}, u32[]{:S(2)}) collective-permute-start(bf16[1280,1024]{1,0:T(8,128)(2,1)S(1)} %add_convert_fusion.1.x_ref), channel_id=1, source_target_pairs={{0,2},{2,0},{1,3},{3,1},{4,6},{6,4},{5,7},{7,5},{8,10},{10,8},{9,1... | collective-permute-start | bytes 7864328 | tf_op jit(solution)/shard_map/ppermute | solution.py:675
  237.9 14.1 %collective-permute-start.13 = (bf16[1280,1024]{1,0:T(8,128)(2,1)S(1)}, bf16[1280,1024]{1,0:T(8,128)(2,1)S(1)}, u32[]{:S(2)}, u32[]{:S(2)}) collective-permute-start(bf16[1280,1024]{1,0:T(8,128)(2,1)S(1)} %get-tuple-element.129), channel_id=1, source_target_pairs={{0,2},{2,0},{1,3},{3,1},{4,6},{6,4},{5,7},{7,5},{8,10},{10,8},{9,1... | collective-permute-start | bytes 7864328 | tf_op jit(solution)/shard_map/ppermute | solution.py:675
  262.8 16.5 %collective-permute-start.14 = (bf16[1280,1024]{1,0:T(8,128)(2,1)S(1)}, bf16[1280,1024]{1,0:T(8,128)(2,1)S(1)}, u32[]{:S(2)}, u32[]{:S(2)}) collective-permute-start(bf16[1280,1024]{1,0:T(8,128)(2,1)S(1)} %get-tuple-element.193.g_ref), channel_id=1, source_target_pairs={{0,2},{2,0},{1,3},{3,1},{4,6},{6,4},{5,7},{7,5},{8,10},{10,8},{9,1... | collective-permute-start | bytes 7864328 | tf_op jit(solution)/shard_map/ppermute | solution.py:675
  310.4 5.0 collective-permute-start.16
  310.6 44.8 %collective-permute-start.15 = (bf16[2048,1024]{1,0:T(8,128)(2,1)}, bf16[2048,1024]{1,0:T(8,128)(2,1)S(1)}, u32[]{:S(2)}, u32[]{:S(2)}) collective-permute-start(bf16[2048,1024]{1,0:T(8,128)(2,1)} %fusion.38), channel_id=1, source_target_pairs={{2,1},{1,2},{6,5},{5,6},{10,9},{9,10},{14,13},{13,14},{18,17},{17,... | collective-permute-start | bytes 12582920 | tf_op jit(solution)/shard_map/ppermute | solution.py:625
  331.3 21.4 %collective-permute-start.17 = (bf16[1280,1024]{1,0:T(8,128)(2,1)S(1)}, bf16[1280,1024]{1,0:T(8,128)(2,1)S(1)}, u32[]{:S(2)}, u32[]{:S(2)}) collective-permute-start(bf16[1280,1024]{1,0:T(8,128)(2,1)S(1)} %get-tuple-element.195), channel_id=1, source_target_pairs={{0,2},{2,0},{1,3},{3,1},{4,6},{6,4},{5,7},{7,5},{8,10},{10,8},{9,1... | collective-permute-start | bytes 7864328 | tf_op jit(solution)/shard_map/ppermute | solution.py:675
  348.3 87.8 %collective-permute-start.21 = (bf16[1024,2048]{1,0:T(8,128)(2,1)}, bf16[1024,2048]{1,0:T(8,128)(2,1)}, u32[]{:S(2)}, u32[]{:S(2)}) collective-permute-start(bf16[1024,2048]{1,0:T(8,128)(2,1)} %convolution_convert_fusion), channel_id=1, source_target_pairs={{2,1},{1,2},{6,5},{5,6},{10,9},{9,10},{14,13},{13,14},{18,17},{17,... | collective-permute-start | bytes 12582920 | tf_op jit(solution)/shard_map/ppermute | solution.py:625
  359.5 76.7 %collective-permute-start.22 = (bf16[512,1024]{1,0:T(8,128)(2,1)}, bf16[512,1024]{1,0:T(8,128)(2,1)}, u32[]{:S(2)}, u32[]{:S(2)}) collective-permute-start(bf16[512,1024]{1,0:T(8,128)(2,1)} %add_convert_fusion.2), channel_id=1, source_target_pairs={{2,1},{1,2},{6,5},{5,6},{10,9},{9,10},{14,13},{13,14},{18,17},{17,... | collective-permute-start | bytes 3145736 | tf_op jit(solution)/shard_map/ppermute | solution.py:625
  363.6 356.5 %all-reduce.6.cloned.1.call-start = ((), (), s32[]{:S(2)}) async-start(), calls=%async_computation.1 | async-start | bytes 10485760 | tf_op jit(solution)/shard_map/psum | solution.py:699
  414.0 105.5 %collective-permute-start.18 = (bf16[1024,768]{1,0:T(8,128)(2,1)}, bf16[1024,768]{1,0:T(8,128)(2,1)}, u32[]{:S(2)}, u32[]{:S(2)}) collective-permute-start(bf16[1024,768]{1,0:T(8,128)(2,1)} %get-tuple-element.149), channel_id=1, source_target_pairs={{2,1},{1,2},{6,5},{5,6},{10,9},{9,10},{14,13},{13,14},{18,17},{17,... | collective-permute-start | bytes 4718600 | tf_op jit(solution)/shard_map/ppermute | solution.py:625
  517.5 17.4 %collective-permute-start.31 = (bf16[1024,768]{1,0:T(8,128)(2,1)}, bf16[1024,768]{1,0:T(8,128)(2,1)}, u32[]{:S(2)}, u32[]{:S(2)}) collective-permute-start(bf16[1024,768]{1,0:T(8,128)(2,1)} %get-tuple-element.168), channel_id=1, source_target_pairs={{2,1},{1,2},{6,5},{5,6},{10,9},{9,10},{14,13},{13,14},{18,17},{17,... | collective-permute-start | bytes 4718600 | tf_op jit(solution)/shard_map/ppermute | solution.py:625
  522.5 19.4 %collective-permute-start.19 = (bf16[512,768]{1,0:T(8,128)(2,1)}, bf16[512,768]{1,0:T(8,128)(2,1)}, u32[]{:S(2)}, u32[]{:S(2)}) collective-permute-start(bf16[512,768]{1,0:T(8,128)(2,1)} %constant_dynamic-slice_fusion.8), channel_id=1, source_target_pairs={{2,0},{3,1},{0,2},{1,3},{6,4},{7,5},{4,6},{5,7},{10,8},{11,9},{8,1... | collective-permute-start | bytes 2359304 | tf_op jit(solution)/shard_map/ppermute | solution.py:644
  534.4 46.4 %collective-permute-start.23 = (bf16[1280,1024]{1,0:T(8,128)(2,1)}, bf16[1280,1024]{1,0:T(8,128)(2,1)}, u32[]{:S(2)}, u32[]{:S(2)}) collective-permute-start(bf16[1280,1024]{1,0:T(8,128)(2,1)} %input_grad.3), channel_id=1, source_target_pairs={{0,2},{2,0},{1,3},{3,1},{4,6},{6,4},{5,7},{7,5},{8,10},{10,8},{9,1... | collective-permute-start | bytes 7864328 | tf_op jit(solution)/shard_map/ppermute | solution.py:675
  538.7 18.8 %collective-permute-start.32 = (bf16[512,768]{1,0:T(8,128)(2,1)}, bf16[512,768]{1,0:T(8,128)(2,1)}, u32[]{:S(2)}, u32[]{:S(2)}) collective-permute-start(bf16[512,768]{1,0:T(8,128)(2,1)} %constant_dynamic-slice_fusion.6), channel_id=1, source_target_pairs={{2,0},{3,1},{0,2},{1,3},{6,4},{7,5},{4,6},{5,7},{10,8},{11,9},{8,1... | collective-permute-start | bytes 2359304 | tf_op jit(solution)/shard_map/ppermute | solution.py:644
  545.0 11.3 %collective-permute-start.30 = (bf16[256,768]{1,0:T(8,128)(2,1)}, bf16[256,768]{1,0:T(8,128)(2,1)}, u32[]{:S(2)}, u32[]{:S(2)}) collective-permute-start(bf16[256,768]{1,0:T(8,128)(2,1)} %constant_dynamic-slice_fusion.7), channel_id=1, source_target_pairs={{4,0},{5,1},{6,2},{7,3},{0,4},{1,5},{2,6},{3,7},{12,8},{13,9},{14,... | collective-permute-start | bytes 1179656 | tf_op jit(solution)/shard_map/ppermute | solution.py:644
  560.0 15.8 %collective-permute-start.40 = (bf16[128,768]{1,0:T(8,128)(2,1)}, bf16[128,768]{1,0:T(8,128)(2,1)}, u32[]{:S(2)}, u32[]{:S(2)}) collective-permute-start(bf16[128,768]{1,0:T(8,128)(2,1)} %constant_dynamic-slice_fusion.2), channel_id=1, source_target_pairs={{8,0},{9,1},{10,2},{11,3},{12,4},{13,5},{14,6},{15,7},{0,8},{1,9},... | collective-permute-start | bytes 589832 | tf_op jit(solution)/shard_map/ppermute | solution.py:644
  571.0 161.9 %collective-permute-start.20 = (bf16[1280,1024]{1,0:T(8,128)(2,1)}, bf16[1280,1024]{1,0:T(8,128)(2,1)}, u32[]{:S(2)}, u32[]{:S(2)}) collective-permute-start(bf16[1280,1024]{1,0:T(8,128)(2,1)} %get-tuple-element.150), channel_id=1, source_target_pairs={{2,1},{1,2},{6,5},{5,6},{10,9},{9,10},{14,13},{13,14},{18,17},{17,... | collective-permute-start | bytes 7864328 | tf_op jit(solution)/shard_map/ppermute | solution.py:625
  573.9 32.4 %collective-permute-start.33 = (bf16[256,768]{1,0:T(8,128)(2,1)}, bf16[256,768]{1,0:T(8,128)(2,1)}, u32[]{:S(2)}, u32[]{:S(2)}) collective-permute-start(bf16[256,768]{1,0:T(8,128)(2,1)} %constant_dynamic-slice_fusion.5), channel_id=1, source_target_pairs={{8,0},{9,1},{10,2},{11,3},{12,4},{13,5},{14,6},{15,7},{0,8},{1,9},... | collective-permute-start | bytes 1179656 | tf_op jit(solution)/shard_map/ppermute | solution.py:644
  578.4 30.3 %collective-permute-start.41 = (bf16[64,768]{1,0:T(8,128)(2,1)}, bf16[64,768]{1,0:T(8,128)(2,1)}, u32[]{:S(2)}, u32[]{:S(2)}) collective-permute-start(bf16[64,768]{1,0:T(8,128)(2,1)} %constant_dynamic-slice_fusion.1), channel_id=1, source_target_pairs={{16,0},{17,1},{18,2},{19,3},{20,4},{21,5},{22,6},{23,7},{24,8},{25... | collective-permute-start | bytes 294920 | tf_op jit(solution)/shard_map/ppermute | solution.py:644
  588.4 17.8 %collective-permute-start.25 = (f32[16384]{0:T(1024)S(1)}, f32[16384]{0:T(1024)S(1)}, u32[]{:S(2)}, u32[]{:S(2)}) collective-permute-start(f32[16384]{0:T(1024)S(1)} %pad_maximum_fusion.7), channel_id=1, source_target_pairs={{0,1},{1,0},{2,3},{3,2},{4,5},{5,4},{6,7},{7,6},{8,9},{9,8},{10,11... | collective-permute-start | bytes 196616 | tf_op jit(solution)/shard_map/ppermute | solution.py:694
  596.7 145.7 %collective-permute-start.24 = (bf16[1280,1024]{1,0:T(8,128)(2,1)}, bf16[1280,1024]{1,0:T(8,128)(2,1)}, u32[]{:S(2)}, u32[]{:S(2)}) collective-permute-start(bf16[1280,1024]{1,0:T(8,128)(2,1)} %fusion.19), channel_id=1, source_target_pairs={{2,1},{1,2},{6,5},{5,6},{10,9},{9,10},{14,13},{13,14},{18,17},{17,... | collective-permute-start | bytes 7864328 | tf_op jit(solution)/shard_map/ppermute | solution.py:625
  606.2 5.2 collective-permute-start.26
  607.5 18.8 %collective-permute-start.34 = (bf16[128,768]{1,0:T(8,128)(2,1)S(1)}, bf16[128,768]{1,0:T(8,128)(2,1)S(1)}, u32[]{:S(2)}, u32[]{:S(2)}) collective-permute-start(bf16[128,768]{1,0:T(8,128)(2,1)S(1)} %constant_dynamic-slice_fusion.4), channel_id=1, source_target_pairs={{16,0},{17,1},{18,2},{19,3},{20,4},{21,5},{22,6},{23,7},{24,8},{25... | collective-permute-start | bytes 589832 | tf_op jit(solution)/shard_map/ppermute | solution.py:644
  609.7 20.7 %collective-permute-start.42 = (bf16[64,768]{1,0:T(8,128)(2,1)S(1)}, bf16[64,768]{1,0:T(8,128)(2,1)S(1)}, u32[]{:S(2)}, u32[]{:S(2)}) collective-permute-start(bf16[64,768]{1,0:T(8,128)(2,1)S(1)} %add_convert_fusion.9), channel_id=1, source_target_pairs={{16,0},{17,1},{18,2},{19,3},{20,4},{21,5},{22,6},{23,7},{24,8},{25... | collective-permute-start | bytes 294920 | tf_op jit(solution)/shard_map/ppermute | solution.py:644
  611.5 28.3 %collective-permute-start.27 = (f32[16384]{0:T(1024)S(1)}, f32[16384]{0:T(1024)S(1)}, u32[]{:S(2)}, u32[]{:S(2)}) collective-permute-start(f32[16384]{0:T(1024)S(1)} %add.382), channel_id=1, source_target_pairs={{0,4},{1,5},{2,6},{3,7},{4,0},{5,1},{6,2},{7,3},{8,12},{9,13},{10,... | collective-permute-start | bytes 196616 | tf_op jit(solution)/shard_map/ppermute | solution.py:694
  626.4 4.7 collective-permute-start.35
  631.1 4.7 collective-permute-start.36
  632.8 6.7 collective-permute-start.43
  635.8 13.4 %collective-permute-start.37 = (bf16[128,768]{1,0:T(8,128)(2,1)S(1)}, bf16[128,768]{1,0:T(8,128)(2,1)S(1)}, u32[]{:S(2)}, u32[]{:S(2)}) collective-permute-start(bf16[128,768]{1,0:T(8,128)(2,1)S(1)} %pad_maximum_fusion.5), channel_id=1, source_target_pairs={{16,0},{17,1},{18,2},{19,3},{20,4},{21,5},{22,6},{23,7},{24,8},{25... | collective-permute-start | bytes 589832 | tf_op jit(solution)/shard_map/ppermute | solution.py:644
  639.6 92.1 %collective-permute-start.44 = (bf16[256,768]{1,0:T(8,128)(2,1)S(1)}, bf16[256,768]{1,0:T(8,128)(2,1)S(1)}, u32[]{:S(2)}, u32[]{:S(2)}) collective-permute-start(bf16[256,768]{1,0:T(8,128)(2,1)S(1)} %pad_maximum_fusion.4), channel_id=1, source_target_pairs={{4,0},{5,1},{6,2},{7,3},{0,4},{1,5},{2,6},{3,7},{12,8},{13,9},{14,... | collective-permute-start | bytes 1179656 | tf_op jit(solution)/shard_map/ppermute | solution.py:644
  639.7 89.8 %collective-permute-start.28 = (f32[16384]{0:T(1024)S(1)}, f32[16384]{0:T(1024)S(1)}, u32[]{:S(2)}, u32[]{:S(2)}) collective-permute-start(f32[16384]{0:T(1024)S(1)} %add.383), channel_id=1, source_target_pairs={{0,8},{1,9},{2,10},{3,11},{4,12},{5,13},{6,14},{7,15},{8,0},{9,1},... | collective-permute-start | bytes 196616 | tf_op jit(solution)/shard_map/ppermute | solution.py:694
  649.4 82.7 %collective-permute-start.38 = (bf16[256,768]{1,0:T(8,128)(2,1)S(1)}, bf16[256,768]{1,0:T(8,128)(2,1)S(1)}, u32[]{:S(2)}, u32[]{:S(2)}) collective-permute-start(bf16[256,768]{1,0:T(8,128)(2,1)S(1)} %pad_maximum_fusion.3), channel_id=1, source_target_pairs={{8,0},{9,1},{10,2},{11,3},{12,4},{13,5},{14,6},{15,7},{0,8},{1,9},... | collective-permute-start | bytes 1179656 | tf_op jit(solution)/shard_map/ppermute | solution.py:644
  729.6 6.4 collective-permute-start.29
  732.0 5.9 collective-permute-start.45
  732.3 7.8 %collective-permute-start.39 = (bf16[512,768]{1,0:T(8,128)(2,1)S(1)}, bf16[512,768]{1,0:T(8,128)(2,1)S(1)}, u32[]{:S(2)}, u32[]{:S(2)}) collective-permute-start(bf16[512,768]{1,0:T(8,128)(2,1)S(1)} %pad_maximum_fusion.1.a), channel_id=1, source_target_pairs={{2,0},{3,1},{0,2},{1,3},{6,4},{7,5},{4,6},{5,7},{10,8},{11,9},{8,1... | collective-permute-start | bytes 2359304 | tf_op jit(solution)/shard_map/ppermute | solution.py:644
  (77 other events, 726.2 us)
Sparse Core Ops, SparseCore 0:
  363.7 120.1 all-reduce.3
  571.1 148.9 all-reduce.5

commit v11 on v10

--- a/solution.py
+++ b/solution.py
@@ -904,7 +904,8 @@
         g_w_up = jnp.where(stays, g_w_up, g_w_up_far)
         g_w_out = jnp.where(stays, g_w_out, g_w_out_far)
     g_w_up = layout.sum_dp(g_w_up, 0)
-    g_w_out = layout.sum_dp(g_w_out, 0)
+    bits = [-1, *layout.order(2 % len(layout.order(0)))]
+    g_w_out = layout.halved_by(g_w_out, bits)
     layer_out = layout.give_back(after(layer_out, g_w_qkv[0]))
     sums = jnp.concatenate(sums, 1)
     grad_a1 = [input_grad(d, w_qkv) for d in zip(*done)]
@@ -913,7 +914,8 @@
     grad_input = grad_input.astype(bf16)
     steps = [layout.order(k) for k in range(chunks)]
     g_w_qkv[0] = layout.halved(g_w_qkv[0], steps[0].pop(0))
-    g_w_qkv = list(lax.optimization_barrier(tuple(g_w_qkv)))
+    g_w_out, *g_w_qkv = lax.optimization_barrier((g_w_out, *g_w_qkv))
+    g_w_out = layout.joined_by(g_w_out, bits)
     g_w_qkv = [layout.halved_by(g, s) for g, s in zip(g_w_qkv, steps)]
     g_w_qkv = [layout.joined_by(g, layout.order(k)) for k, g in enumerate(g_w_qkv)]
     begun = ()

time: 763 us -> 816 us (1.069)
  Pallas kernels: 227 us -> 286 us
  starting transfers between devices: 138 us -> 117 us
    pallas_call x3, Pallas kernels: 76.6 us -> 114 us  [attend_backward(): pl.pallas_call(functools.partial(backward_kernel, parts), grid_spec=pltpu...]
    ppermute x18 -> x26, waiting for transfers between devices: 34.5 us -> 65.2 us  [partner(): return lax.ppermute(value, self.axes, moves)]
    pallas_call x4, Pallas kernels: 50.3 us -> 72.8 us  [attend_forward(): pl.pallas_call(functools.partial(forward_kernel, parts), grid_spec=pltpu....]
    ppermute x8, starting transfers between devices: 78.1 us -> 56.5 us  [to_rank(): return lax.ppermute(value, self.axes, moves)]
    psum x2, waiting for transfers between devices: 105 us -> 84.7 us  [sum_dp(): return lax.psum(value, 'dp', axis_index_groups=[order])]
    ppermute x5, waiting for transfers between devices: 8.5 us -> 0.01 us  [sum_all(): lax.ppermute(value, self.axes, [(i, i ^ step) for i in range(devices)])]
    ppermute x18 -> x26, starting transfers between devices: 27.5 us -> 29.7 us  [partner(): return lax.ppermute(value, self.axes, moves)]
    unnamed x157 -> x167, local copies, waits for them, and re-layouts: 31.1 us -> 30.4 us
  transfers between devices with their start and end apart: 48 -> 56, of which waited for: 14 -> 16; matrix products, arithmetic and copies ran while one was open for 20% -> 20% of each run, Pallas kernels for 26% -> 31%
where the time goes in v11:
time: 816 us; the launch traced here: 802 us
  Pallas kernels  286 us (35%)
  waiting for transfers between devices  158 us (19%)
  starting transfers between devices  117 us (14%)
  other arithmetic  115 us (14%)
  matrix products  56 us (7%)
  local copies, waits for them, and re-layouts  52.6 us (6%)
  between operations  17.4 us (2%)
    pallas_call x3, Pallas kernels, attend_backward(): pl.pallas_call(functools.partial(backward_kernel, parts), grid_spec=pltpu...  114 us
    psum x2, waiting for transfers between devices, sum_dp(): return lax.psum(value, 'dp', axis_index_groups=[order])  84.7 us
    pallas_call x4, Pallas kernels, attend_forward(): pl.pallas_call(functools.partial(forward_kernel, parts), grid_spec=pltpu....  72.8 us
    ppermute x26, waiting for transfers between devices, partner(): return lax.ppermute(value, self.axes, moves)  65.2 us
    ppermute x8, starting transfers between devices, to_rank(): return lax.ppermute(value, self.axes, moves)  56.5 us
    dot_general x4, matrix products, contract_rows(): lax.dot_general(left, right, (((0,), (0,)), ((), ())), preferred_element_...  36.1 us
    pallas_call x2, Pallas kernels, feed_forward(): pl.pallas_call(functools.partial(feed_kernel, min(units, FEED)), grid=(st...  35.6 us
    pallas_call x2, Pallas kernels, feed_back(): pl.pallas_call(functools.partial(feed_back_kernel, min(units, FEED)), gri...  32 us
  transfers between devices with their start and end apart: 56, of which 16 were waited for; matrix products, arithmetic and copies ran while one was open for 20% of the time, Pallas kernels for 31%

profile of v11, /device:TPU:0, one launch (start us, length us, event | category | flops | bytes accessed | tf_op | source)
XLA Modules:
  0.0 802.4 jit_solution(17580449490935598582)
XLA Ops:
  16.9 4.7 fusion.52
  34.6 38.5 %collective-permute-start.6 = (bf16[1280,1024]{1,0:T(8,128)(2,1)S(1)}, bf16[1280,1024]{1,0:T(8,128)(2,1)}, u32[]{:S(2)}, u32[]{:S(2)}) collective-permute-start(bf16[1280,1024]{1,0:T(8,128)(2,1)S(1)} %fusion.14.refs_0_), channel_id=1, source_target_pairs={{0,2},{2,0},{1,3},{3,1},{4,6},{6,4},{5,7},{7,5},{8,10},{10,8},{9,1... | collective-permute-start | bytes 7864328 | tf_op jit(solution)/shard_map/ppermute | solution.py:675
  84.3 4.5 fusion.2.refs_0_
  88.9 7.7 fusion.3.refs_1_
  96.7 18.1 %attend_forward.4 = (bf16[1280,512]{1,0:T(8,128)(2,1)S(1)}, bf16[1280,512]{1,0:T(8,128)(2,1)S(1)}, bf16[512,2560]{1,0:T(8,128)(2,1)S(1)}, f32[4,2,2560]{2,1,0:T(2,128)S(1)}) custom-call(s32[3,10]{1,0:T(4,128)S(1)} %add_add_fusion.2.tab_ref, s32[2560,1]{1,0:T(8,128)S(1)} %copy-done.3, s32[1,2560]{1,0:T(1,128)S(1)} %fusion.45.qseg_ref, ...), custom_call_target="tpu_custom_call" | custom-call | flops 1024 | bytes 1024 | tf_op jit(solution)/shard_map/attend_forward/pallas_call | solution.py:301
  114.8 18.1 %attend_forward.5 = (bf16[1280,512]{1,0:T(8,128)(2,1)S(1)}, bf16[1280,512]{1,0:T(8,128)(2,1)S(1)}, bf16[512,2560]{1,0:T(8,128)(2,1)S(1)}, f32[4,2,2560]{2,1,0:T(2,128)S(1)}) custom-call(s32[3,10]{1,0:T(4,128)S(1)} %add_add_fusion.2.tab_ref, s32[2560,1]{1,0:T(8,128)S(1)} %copy-done.3, ...), custom_call_target="tpu_custom_call", output_to_operand_aliasing={{0}: (5, {}), {1}: (6, {}), {2}: (7, {}), {3}: (8, {})} | custom-call | flops 1024 | bytes 1024 | tf_op jit(solution)/shard_map/attend_forward/pallas_call | solution.py:301
  132.9 18.1 %attend_forward.6 = (bf16[1280,512]{1,0:T(8,128)(2,1)S(1)}, bf16[1280,512]{1,0:T(8,128)(2,1)S(1)}, bf16[512,2560]{1,0:T(8,128)(2,1)S(1)}, f32[4,2,2560]{2,1,0:T(2,128)S(1)}) custom-call(s32[3,10]{1,0:T(4,128)S(1)} %add_add_fusion.2.tab_ref, s32[2560,1]{1,0:T(8,128)S(1)} %copy-done.3, ...), custom_call_target="tpu_custom_call", output_to_operand_aliasing={{0}: (5, {}), {1}: (6, {}), {2}: (7, {}), {3}: (8, {})} | custom-call | flops 1024 | bytes 1024 | tf_op jit(solution)/shard_map/attend_forward/pallas_call | solution.py:301
  151.1 18.5 %attend_forward.7 = (bf16[1280,512]{1,0:T(8,128)(2,1)S(1)}, bf16[1280,512]{1,0:T(8,128)(2,1)S(1)}, bf16[512,2560]{1,0:T(8,128)(2,1)S(1)}, f32[4,2,2560]{2,1,0:T(2,128)S(1)}) custom-call(s32[3,10]{1,0:T(4,128)S(1)} %add_add_fusion.2.tab_ref, s32[2560,1]{1,0:T(8,128)S(1)} %copy-done.3, ...), custom_call_target="tpu_custom_call", output_to_operand_aliasing={{0}: (5, {}), {1}: (6, {}), {2}: (7, {}), {3}: (8, {})} | custom-call | flops 1024 | bytes 1024 | tf_op jit(solution)/shard_map/attend_forward/pallas_call | solution.py:301
  174.7 4.1 collective-permute-start.10
  179.8 4.6 broadcast_select_fusion.2.up_ref
  198.2 3.7 maximum_select_fusion.down_ref
  202.2 17.7 %feed_forward.2 = (bf16[2560,1024]{1,0:T(8,128)(2,1)}, bf16[2560,2048]{1,0:T(8,128)(2,1)}, bf16[2560,2048]{1,0:T(8,128)(2,1)}, bf16[1280,1024]{1,0:T(8,128)(2,1)S(1)}) custom-call(bf16[1280,1024]{1,0:T(8,128)(2,1)S(1)} %add_convert_fusion.1.x_ref, bf16[1024,2048]{1,0:T(8,128)(2,1)} %broadcast_select_fusion.2.up_ref, f32[1,2048]{1,0:T(1,128)S(1)} %bitcast.52, ...), custom_call_target="tpu_custom_call" | custom-call | flops 16106127360 | bytes 16777216 | tf_op jit(solution)/shard_map/feed_forward/pallas_call | solution.py:411
  220.0 17.8 %feed_forward.3 = (bf16[2560,1024]{1,0:T(8,128)(2,1)}, bf16[2560,2048]{1,0:T(8,128)(2,1)}, bf16[2560,2048]{1,0:T(8,128)(2,1)}, bf16[1280,1024]{1,0:T(8,128)(2,1)S(1)}) custom-call(bf16[1280,1024]{1,0:T(8,128)(2,1)S(1)} %collective-permute-done.11.x_ref, ...), custom_call_target="tpu_custom_call", output_to_operand_aliasing={{0}: (4, {}), {1}: (5, {}), {2}: (6, {})} | custom-call | flops 16106127360 | bytes 16777216 | tf_op jit(solution)/shard_map/feed_forward/pallas_call | solution.py:411
  237.8 10.5 %collective-permute-start.13 = (bf16[1280,1024]{1,0:T(8,128)(2,1)S(1)}, bf16[1280,1024]{1,0:T(8,128)(2,1)S(1)}, u32[]{:S(2)}, u32[]{:S(2)}) collective-permute-start(bf16[1280,1024]{1,0:T(8,128)(2,1)S(1)} %get-tuple-element.130), channel_id=1, source_target_pairs={{0,2},{2,0},{1,3},{3,1},{4,6},{6,4},{5,7},{7,5},{8,10},{10,8},{9,1... | collective-permute-start | bytes 7864328 | tf_op jit(solution)/shard_map/ppermute | solution.py:675
  248.4 4.5 collective-permute-done.13
  255.2 4.2 fusion.26
  259.4 4.9 convert_reduce_fusion.2
  264.6 15.9 %feed_back.2 = (bf16[2560,2048]{1,0:T(8,128)(2,1)}, f32[1,2048]{1,0:T(1,128)S(1)}, bf16[1280,1024]{1,0:T(8,128)(2,1)S(1)}) custom-call(bf16[1280,1024]{1,0:T(8,128)(2,1)S(1)} %get-tuple-element.193.g_ref, bf16[2560,2048]{1,0:T(8,128)(2,1)} %get-tuple-element.136.slope_ref, bf16[2048,1024]{1,0:T(8,128)(2,1)} %maximum_select_fusion.down_ref, ...), custom_call_target="tpu_custom_call" | custom-call | flops 1024 | bytes 1024 | tf_op jit(solution)/shard_map/feed_back/pallas_call | solution.py:473
  280.5 15.3 %fusion.38 = bf16[2048,1024]{1,0:T(8,128)(2,1)} fusion(bf16[2560,2048]{1,0:T(8,128)(2,1)} %get-tuple-element.132, bf16[1280,1024]{1,0:T(8,128)(2,1)S(1)} %collective-permute-done.14.g_ref, bf16[1280,1024]{1,0:T(8,128)(2,1)S(1)} %get-tuple-element.193.g_ref), kind=kOutput, calls=%fused_computation.72 | convolution fusion | flops 10750001152 | bytes 19922944 | tf_op jit(solution)/shard_map/dot_general | solution.py:35
  295.8 16.1 %feed_back.3 = (bf16[2560,2048]{1,0:T(8,128)(2,1)}, f32[1,2048]{1,0:T(1,128)S(1)}, bf16[1280,1024]{1,0:T(8,128)(2,1)S(1)}) custom-call(bf16[1280,1024]{1,0:T(8,128)(2,1)S(1)} %collective-permute-done.14.g_ref, bf16[2560,2048]{1,0:T(8,128)(2,1)} %get-tuple-element.136.slope_ref, ...), custom_call_target="tpu_custom_call", output_to_operand_aliasing={{0}: (4, {})} | custom-call | flops 1024 | bytes 1024 | tf_op jit(solution)/shard_map/feed_back/pallas_call | solution.py:473
  313.0 3.8 collective-permute-done.16
  316.9 5.5 multiply_reduce_fusion
  322.4 8.6 %multiply_reduce_fusion.1 = (f32[1024]{0:T(1024)}, f32[1280]{0:T(1024)S(1)}, f32[1280]{0:T(1024)S(1)}, f32[1024]{0:T(1024)}, f32[1280,1024]{1,0:T(8,128)S(1)}) fusion(f32[1280,1024]{1,0:T(8,128)} %copy-done.28, f32[1280]{0:T(1024)S(1)} %add_rsqrt_fusion.2, f32[1280]{0:T(1024)S(1)} %broadcast_multiply_fusion.10, f32[1024]{0:T(1024)S(1)} %copy-done.64, ...), kind=kLoop, calls=%fused_computation.42 | loop fusion | flops 27520512 | bytes 23650304 | tf_op jit(solution)/shard_map/reduce_sum | solution.py:934
  333.5 16.8 %convolution_convert_fusion = bf16[1024,2048]{1,0:T(8,128)(2,1)} fusion(bf16[2560,1024]{1,0:T(8,128)(2,1)} %get-tuple-element.134, bf16[2560,2048]{1,0:T(8,128)(2,1)} %get-tuple-element.138), kind=kOutput, calls=%fused_computation.71 | convolution fusion | flops 10739515392 | bytes 19922944 | tf_op jit(solution)/shard_map/dot_general | solution.py:35
  368.2 55.4 %attend_backward.3 = (bf16[1280,768]{1,0:T(8,128)(2,1)S(1)}, bf16[1280,768]{1,0:T(8,128)(2,1)}) custom-call(s32[3,10]{1,0:T(4,128)S(1)} %add_add_fusion.2.tab_ref, s32[2560,1]{1,0:T(8,128)S(1)} %copy-done.4, s32[1,2560]{1,0:T(1,128)S(1)} %fusion.45.qseg_ref, bf16[1280,1536]{1,0:T(8,128)(2,1)} %copy-done, bf16[1280,1536]{1,0:T(8,128)(2,1)} %copy-done.1, ...), custom_call_target="tpu_custom_call" | custom-call | flops 1024 | bytes 1024 | tf_op jit(solution)/shard_map/attend_backward/pallas_call | solution.py:335
  425.8 8.7 %weight_grad.2 = (bf16[1024,768]{1,0:T(8,128)(2,1)}, f32[1,768]{1,0:T(1,128)S(1)}) custom-call(bf16[1280,1024]{1,0:T(8,128)(2,1)S(1)} %copy-done.6, bf16[1280,1024]{1,0:T(8,128)(2,1)} %collective-permute-done.6.refs_1_, bf16[1280,768]{1,0:T(8,128)(2,1)S(1)} %get-tuple-element.147.refs_2_.refs_0_, bf16[1280,768]{1,0:T(8,128)(2,1)S(1)} %copy-done.22), custom_call_target="tpu_custom_call" | custom-call | flops 1024 | bytes 1024 | tf_op jit(solution)/shard_map/weight_grad/pallas_call | solution.py:513
  439.2 29.2 %attend_backward.4 = (bf16[1280,768]{1,0:T(8,128)(2,1)S(1)}, bf16[1280,768]{1,0:T(8,128)(2,1)}) custom-call(s32[3,10]{1,0:T(4,128)S(1)} %add_add_fusion.2.tab_ref, s32[2560,1]{1,0:T(8,128)S(1)} %copy-done.4, s32[1,2560]{1,0:T(1,128)S(1)} %fusion.45.qseg_ref, bf16[1280,1536]{1,0:T(8,128)(2,1)} %copy-done, bf16[1280,1536]{1,0:T(8,128)(2,1)} %copy-done.1, ...), custom_call_target="tpu_custom_call" | custom-call | flops 1024 | bytes 1024 | tf_op jit(solution)/shard_map/attend_backward/pallas_call | solution.py:335
  470.7 4.7 broadcast_select_fusion.1
  478.1 5.3 all-reduce.3.cloned.1.call-done
  488.9 29.2 %attend_backward.5 = (bf16[1280,768]{1,0:T(8,128)(2,1)S(1)}, bf16[1280,768]{1,0:T(8,128)(2,1)}) custom-call(s32[3,10]{1,0:T(4,128)S(1)} %add_add_fusion.2.tab_ref, s32[2560,1]{1,0:T(8,128)S(1)} %copy-done.4, s32[1,2560]{1,0:T(1,128)S(1)} %fusion.45.qseg_ref, bf16[1280,1536]{1,0:T(8,128)(2,1)} %copy-done, ...), custom_call_target="tpu_custom_call", output_to_operand_aliasing={{0}: (9, {}), {1}: (10, {})} | custom-call | flops 1024 | bytes 1024 | tf_op jit(solution)/shard_map/attend_backward/pallas_call | solution.py:335
  520.4 8.8 %weight_grad.3 = (bf16[1024,768]{1,0:T(8,128)(2,1)}, f32[1,768]{1,0:T(1,128)S(1)}) custom-call(bf16[1280,1024]{1,0:T(8,128)(2,1)S(1)} %copy-done.7, bf16[1280,1024]{1,0:T(8,128)(2,1)} %collective-permute-done.6.refs_1_, bf16[1280,768]{1,0:T(8,128)(2,1)S(1)} %get-tuple-element.162.refs_1_.refs_2_, bf16[1280,768]{1,0:T(8,128)(2,1)S(1)} %copy-done.12), custom_call_target="tpu_custom_call" | custom-call | flops 1024 | bytes 1024 | tf_op jit(solution)/shard_map/weight_grad/pallas_call | solution.py:513
  539.2 5.5 input_grad.3
  544.8 4.5 input_grad.2
  554.7 4.2 collective-permute-start.34
  558.9 12.0 %collective-permute-done.31 = bf16[128,1024]{1,0:T(8,128)(2,1)S(1)} collective-permute-done((bf16[128,1024]{1,0:T(8,128)(2,1)S(1)}, bf16[128,1024]{1,0:T(8,128)(2,1)S(1)}, u32[]{:S(2)}, u32[]{:S(2)}) %collective-permute-start.31) | collective-permute-done | bytes 262176 | tf_op jit(solution)/shard_map/ppermute | solution.py:644
  580.5 3.6 collective-permute-done.33
  586.5 4.4 convert_element_type.279
  593.2 79.5 %all-reduce.5.cloned.1.call-done = bf16[1024,2048]{1,0:T(8,128)(2,1)} async-done(((bf16[1024,2048]{1,0:T(8,128)(2,1)}), bf16[1024,2048]{1,0:T(8,128)(2,1)}) %all-reduce.5.cloned.1.call-update) | async-done | bytes 4194320 | tf_op jit(solution)/shard_map/psum | solution.py:699
  672.7 6.8 convert_element_type.278
  687.6 13.6 %collective-permute-done.44 = bf16[128,768]{1,0:T(8,128)(2,1)S(1)} collective-permute-done((bf16[128,768]{1,0:T(8,128)(2,1)S(1)}, bf16[128,768]{1,0:T(8,128)(2,1)S(1)}, u32[]{:S(2)}, u32[]{:S(2)}) %collective-permute-start.44) | collective-permute-done | bytes 196640 | tf_op jit(solution)/shard_map/ppermute | solution.py:644
  704.4 5.3 fusion.20
  717.5 6.5 fusion.19
  732.0 4.0 collective-permute-done.46
  736.0 9.2 %collective-permute-done.38 = bf16[128,768]{1,0:T(8,128)(2,1)S(1)} collective-permute-done((bf16[128,768]{1,0:T(8,128)(2,1)S(1)}, bf16[128,768]{1,0:T(8,128)(2,1)S(1)}, u32[]{:S(2)}, u32[]{:S(2)}) %collective-permute-start.38) | collective-permute-done | bytes 196640 | tf_op jit(solution)/shard_map/ppermute | solution.py:644
  746.4 3.6 collective-permute-done.39
  759.4 6.1 collective-permute-done.41
  770.0 7.3 collective-permute-done.42
  790.9 4.4 select_convert_fusion
  (399 shorter events, 181.1 us)
Async XLA Ops:
  7.2 476.2 %all-reduce.3.cloned.1.call-start = ((), (), s32[]{:S(2)}) async-start(), calls=%async_computation | async-start | bytes 8388608 | tf_op jit(solution)/shard_map/psum | solution.py:699
  13.1 15.6 %collective-permute-start.2 = (bf16[1280,1024]{1,0:T(8,128)(2,1)}, bf16[1280,1024]{1,0:T(8,128)(2,1)}, u32[]{:S(2)}, u32[]{:S(2)}) collective-permute-start(bf16[1280,1024]{1,0:T(8,128)(2,1)} %param.20), channel_id=1, source_target_pairs={{1,2},{2,1},{5,6},{6,5},{9,10},{10,9},{13,14},{14,13},{17,18},{18,... | collective-permute-start | bytes 7864328 | tf_op jit(solution)/shard_map/ppermute | solution.py:625
  15.3 8.5 %collective-permute-start.4 = (bf16[256,3,512]{0,2,1:T(8,128)(2,1)}, bf16[256,3,512]{0,2,1:T(8,128)(2,1)}, u32[]{:S(2)}, u32[]{:S(2)}) collective-permute-start(bf16[256,3,512]{0,2,1:T(8,128)(2,1)} %copy-done.54), channel_id=1, source_target_pairs={{9,1},{10,2},{13,5},{14,6},{1,9},{2,10},{5,13},{6,14},{25,17},{26,... | collective-permute-start | bytes 2359304 | tf_op jit(solution)/shard_map/ppermute | solution.py:644
  26.7 49.5 %collective-permute-start.5 = (bf16[512,3,512]{0,2,1:T(8,128)(2,1)}, bf16[512,3,512]{0,2,1:T(8,128)(2,1)}, u32[]{:S(2)}, u32[]{:S(2)}) collective-permute-start(bf16[512,3,512]{0,2,1:T(8,128)(2,1)} %pad_maximum_fusion), channel_id=1, source_target_pairs={{5,1},{6,2},{1,5},{2,6},{13,9},{14,10},{9,13},{10,14},{21,17},{22,... | collective-permute-start | bytes 4718600 | tf_op jit(solution)/shard_map/ppermute | solution.py:644
  29.6 103.3 %collective-permute-start.3 = (bf16[1024,2048]{1,0:T(8,128)(2,1)}, bf16[1024,2048]{1,0:T(8,128)(2,1)}, u32[]{:S(2)}, u32[]{:S(2)}) collective-permute-start(bf16[1024,2048]{1,0:T(8,128)(2,1)} %param.31), channel_id=1, source_target_pairs={{1,2},{2,1},{5,6},{6,5},{9,10},{10,9},{13,14},{14,13},{17,18},{18,... | collective-permute-start | bytes 12582920 | tf_op jit(solution)/shard_map/ppermute | solution.py:625
  34.6 54.3 %collective-permute-start.6 = (bf16[1280,1024]{1,0:T(8,128)(2,1)S(1)}, bf16[1280,1024]{1,0:T(8,128)(2,1)}, u32[]{:S(2)}, u32[]{:S(2)}) collective-permute-start(bf16[1280,1024]{1,0:T(8,128)(2,1)S(1)} %fusion.14.refs_0_), channel_id=1, source_target_pairs={{0,2},{2,0},{1,3},{3,1},{4,6},{6,4},{5,7},{7,5},{8,10},{10,8},{9,1... | collective-permute-start | bytes 7864328 | tf_op jit(solution)/shard_map/ppermute | solution.py:675
  78.9 90.7 %collective-permute-start.8 = (bf16[1024,1024]{1,0:T(8,128)(2,1)}, bf16[1024,1024]{1,0:T(8,128)(2,1)S(1)}, u32[]{:S(2)}, u32[]{:S(2)}) collective-permute-start(bf16[1024,1024]{1,0:T(8,128)(2,1)} %get-tuple-element.116), channel_id=1, source_target_pairs={{1,2},{2,1},{5,6},{6,5},{9,10},{10,9},{13,14},{14,13},{17,18},{18,... | collective-permute-start | bytes 6291464 | tf_op jit(solution)/shard_map/ppermute | solution.py:625
  79.7 89.9 %collective-permute-start.9 = (bf16[1024,1024]{1,0:T(8,128)(2,1)S(1)}, bf16[1024,1024]{1,0:T(8,128)(2,1)S(1)}, u32[]{:S(2)}, u32[]{:S(2)}) collective-permute-start(bf16[1024,1024]{1,0:T(8,128)(2,1)S(1)} %copy-done.47), channel_id=1, source_target_pairs={{1,2},{2,1},{5,6},{6,5},{9,10},{10,9},{13,14},{14,13},{17,18},{18,... | collective-permute-start | bytes 6291464 | tf_op jit(solution)/shard_map/ppermute | solution.py:625
  82.2 87.4 %collective-permute-start.7 = (bf16[512,1024]{1,0:T(8,128)(2,1)}, bf16[512,1024]{1,0:T(8,128)(2,1)}, u32[]{:S(2)}, u32[]{:S(2)}) collective-permute-start(bf16[512,1024]{1,0:T(8,128)(2,1)} %param.25), channel_id=1, source_target_pairs={{1,2},{2,1},{5,6},{6,5},{9,10},{10,9},{13,14},{14,13},{17,18},{18,... | collective-permute-start | bytes 3145736 | tf_op jit(solution)/shard_map/ppermute | solution.py:625
  174.7 9.7 %collective-permute-start.10 = (bf16[1280,1024]{1,0:T(8,128)(2,1)S(1)}, bf16[1280,1024]{1,0:T(8,128)(2,1)S(1)}, u32[]{:S(2)}, u32[]{:S(2)}) collective-permute-start(bf16[1280,1024]{1,0:T(8,128)(2,1)S(1)} %convolution_convert_fusion.1), channel_id=1, source_target_pairs={{0,2},{2,0},{1,3},{3,1},{4,6},{6,4},{5,7},{7,5},{8,10},{10,8},{9,1... | collective-permute-start | bytes 7864328 | tf_op jit(solution)/shard_map/ppermute | solution.py:675
  178.9 23.0 %collective-permute-start.12 = (bf16[1280,1024]{1,0:T(8,128)(2,1)S(1)}, bf16[1280,1024]{1,0:T(8,128)(2,1)S(1)}, u32[]{:S(2)}, u32[]{:S(2)}) collective-permute-start(bf16[1280,1024]{1,0:T(8,128)(2,1)S(1)} %copy-done.41), channel_id=1, source_target_pairs={{1,2},{2,1},{5,6},{6,5},{9,10},{10,9},{13,14},{14,13},{17,18},{18,... | collective-permute-start | bytes 7864328 | tf_op jit(solution)/shard_map/ppermute | solution.py:625
  195.8 24.2 %collective-permute-start.11 = (bf16[1280,1024]{1,0:T(8,128)(2,1)S(1)}, bf16[1280,1024]{1,0:T(8,128)(2,1)S(1)}, u32[]{:S(2)}, u32[]{:S(2)}) collective-permute-start(bf16[1280,1024]{1,0:T(8,128)(2,1)S(1)} %add_convert_fusion.1.x_ref), channel_id=1, source_target_pairs={{0,2},{2,0},{1,3},{3,1},{4,6},{6,4},{5,7},{7,5},{8,10},{10,8},{9,1... | collective-permute-start | bytes 7864328 | tf_op jit(solution)/shard_map/ppermute | solution.py:675
  237.8 15.1 %collective-permute-start.13 = (bf16[1280,1024]{1,0:T(8,128)(2,1)S(1)}, bf16[1280,1024]{1,0:T(8,128)(2,1)S(1)}, u32[]{:S(2)}, u32[]{:S(2)}) collective-permute-start(bf16[1280,1024]{1,0:T(8,128)(2,1)S(1)} %get-tuple-element.130), channel_id=1, source_target_pairs={{0,2},{2,0},{1,3},{3,1},{4,6},{6,4},{5,7},{7,5},{8,10},{10,8},{9,1... | collective-permute-start | bytes 7864328 | tf_op jit(solution)/shard_map/ppermute | solution.py:675
  264.2 16.3 %collective-permute-start.14 = (bf16[1280,1024]{1,0:T(8,128)(2,1)S(1)}, bf16[1280,1024]{1,0:T(8,128)(2,1)S(1)}, u32[]{:S(2)}, u32[]{:S(2)}) collective-permute-start(bf16[1280,1024]{1,0:T(8,128)(2,1)S(1)} %get-tuple-element.193.g_ref), channel_id=1, source_target_pairs={{0,2},{2,0},{1,3},{3,1},{4,6},{6,4},{5,7},{7,5},{8,10},{10,8},{9,1... | collective-permute-start | bytes 7864328 | tf_op jit(solution)/shard_map/ppermute | solution.py:675
  312.1 45.3 %collective-permute-start.15 = (bf16[2048,1024]{1,0:T(8,128)(2,1)}, bf16[2048,1024]{1,0:T(8,128)(2,1)S(1)}, u32[]{:S(2)}, u32[]{:S(2)}) collective-permute-start(bf16[2048,1024]{1,0:T(8,128)(2,1)} %fusion.38), channel_id=1, source_target_pairs={{2,1},{1,2},{6,5},{5,6},{10,9},{9,10},{14,13},{13,14},{18,17},{17,... | collective-permute-start | bytes 12582920 | tf_op jit(solution)/shard_map/ppermute | solution.py:625
  333.3 21.4 %collective-permute-start.17 = (bf16[1280,1024]{1,0:T(8,128)(2,1)S(1)}, bf16[1280,1024]{1,0:T(8,128)(2,1)S(1)}, u32[]{:S(2)}, u32[]{:S(2)}) collective-permute-start(bf16[1280,1024]{1,0:T(8,128)(2,1)S(1)} %get-tuple-element.195), channel_id=1, source_target_pairs={{0,2},{2,0},{1,3},{3,1},{4,6},{6,4},{5,7},{7,5},{8,10},{10,8},{9,1... | collective-permute-start | bytes 7864328 | tf_op jit(solution)/shard_map/ppermute | solution.py:675
  350.3 118.0 %collective-permute-start.21 = (bf16[1024,2048]{1,0:T(8,128)(2,1)}, bf16[1024,2048]{1,0:T(8,128)(2,1)}, u32[]{:S(2)}, u32[]{:S(2)}) collective-permute-start(bf16[1024,2048]{1,0:T(8,128)(2,1)} %convolution_convert_fusion), channel_id=1, source_target_pairs={{2,1},{1,2},{6,5},{5,6},{10,9},{9,10},{14,13},{13,14},{18,17},{17,... | collective-permute-start | bytes 12582920 | tf_op jit(solution)/shard_map/ppermute | solution.py:625
  361.5 106.9 %collective-permute-start.22 = (bf16[512,1024]{1,0:T(8,128)(2,1)}, bf16[512,1024]{1,0:T(8,128)(2,1)}, u32[]{:S(2)}, u32[]{:S(2)}) collective-permute-start(bf16[512,1024]{1,0:T(8,128)(2,1)} %add_convert_fusion.2), channel_id=1, source_target_pairs={{2,1},{1,2},{6,5},{5,6},{10,9},{9,10},{14,13},{13,14},{18,17},{17,... | collective-permute-start | bytes 3145736 | tf_op jit(solution)/shard_map/ppermute | solution.py:625
  365.6 307.1 %all-reduce.5.cloned.1.call-start = ((), (), s32[]{:S(2)}) async-start(), calls=%async_computation.1 | async-start | bytes 8388608 | tf_op jit(solution)/shard_map/psum | solution.py:699
  434.5 40.9 %collective-permute-start.18 = (bf16[1024,768]{1,0:T(8,128)(2,1)}, bf16[1024,768]{1,0:T(8,128)(2,1)}, u32[]{:S(2)}, u32[]{:S(2)}) collective-permute-start(bf16[1024,768]{1,0:T(8,128)(2,1)} %get-tuple-element.150), channel_id=1, source_target_pairs={{2,1},{1,2},{6,5},{5,6},{10,9},{9,10},{14,13},{13,14},{18,17},{17,... | collective-permute-start | bytes 4718600 | tf_op jit(solution)/shard_map/ppermute | solution.py:625
  485.3 65.7 %collective-permute-start.30 = (bf16[256,1024]{1,0:T(8,128)(2,1)}, bf16[256,1024]{1,0:T(8,128)(2,1)}, u32[]{:S(2)}, u32[]{:S(2)}) collective-permute-start(bf16[256,1024]{1,0:T(8,128)(2,1)} %constant_dynamic-slice_fusion.11), channel_id=1, source_target_pairs={{2,0},{3,1},{0,2},{1,3},{6,4},{7,5},{4,6},{5,7},{10,8},{11,9},{8,1... | collective-permute-start | bytes 1572872 | tf_op jit(solution)/shard_map/ppermute | solution.py:644
  529.1 44.8 %collective-permute-start.35 = (bf16[1024,768]{1,0:T(8,128)(2,1)}, bf16[1024,768]{1,0:T(8,128)(2,1)}, u32[]{:S(2)}, u32[]{:S(2)}) collective-permute-start(bf16[1024,768]{1,0:T(8,128)(2,1)} %get-tuple-element.170), channel_id=1, source_target_pairs={{2,1},{1,2},{6,5},{5,6},{10,9},{9,10},{14,13},{13,14},{18,17},{17,... | collective-permute-start | bytes 4718600 | tf_op jit(solution)/shard_map/ppermute | solution.py:625
  532.3 21.0 %collective-permute-start.19 = (bf16[512,768]{1,0:T(8,128)(2,1)}, bf16[512,768]{1,0:T(8,128)(2,1)}, u32[]{:S(2)}, u32[]{:S(2)}) collective-permute-start(bf16[512,768]{1,0:T(8,128)(2,1)} %constant_dynamic-slice_fusion.12), channel_id=1, source_target_pairs={{2,0},{3,1},{0,2},{1,3},{6,4},{7,5},{4,6},{5,7},{10,8},{11,9},{8,1... | collective-permute-start | bytes 2359304 | tf_op jit(solution)/shard_map/ppermute | solution.py:644
  550.7 153.6 %collective-permute-start.23 = (bf16[1280,1024]{1,0:T(8,128)(2,1)}, bf16[1280,1024]{1,0:T(8,128)(2,1)}, u32[]{:S(2)}, u32[]{:S(2)}) collective-permute-start(bf16[1280,1024]{1,0:T(8,128)(2,1)} %input_grad.3), channel_id=1, source_target_pairs={{0,2},{2,0},{1,3},{3,1},{4,6},{6,4},{5,7},{7,5},{8,10},{10,8},{9,1... | collective-permute-start | bytes 7864328 | tf_op jit(solution)/shard_map/ppermute | solution.py:675
  553.2 17.7 %collective-permute-start.31 = (bf16[128,1024]{1,0:T(8,128)(2,1)S(1)}, bf16[128,1024]{1,0:T(8,128)(2,1)S(1)}, u32[]{:S(2)}, u32[]{:S(2)}) collective-permute-start(bf16[128,1024]{1,0:T(8,128)(2,1)S(1)} %constant_dynamic-slice_fusion.10), channel_id=1, source_target_pairs={{16,0},{17,1},{18,2},{19,3},{20,4},{21,5},{22,6},{23,7},{24,8},{25... | collective-permute-start | bytes 786440 | tf_op jit(solution)/shard_map/ppermute | solution.py:644
  554.7 24.9 %collective-permute-start.34 = (bf16[256,768]{1,0:T(8,128)(2,1)S(1)}, bf16[256,768]{1,0:T(8,128)(2,1)S(1)}, u32[]{:S(2)}, u32[]{:S(2)}) collective-permute-start(bf16[256,768]{1,0:T(8,128)(2,1)S(1)} %constant_dynamic-slice_fusion.7), channel_id=1, source_target_pairs={{4,0},{5,1},{6,2},{7,3},{0,4},{1,5},{2,6},{3,7},{12,8},{13,9},{14,... | collective-permute-start | bytes 1179656 | tf_op jit(solution)/shard_map/ppermute | solution.py:644
  571.0 7.0 collective-permute-start.32
  575.5 8.6 %collective-permute-start.36 = (bf16[512,768]{1,0:T(8,128)(2,1)S(1)}, bf16[512,768]{1,0:T(8,128)(2,1)S(1)}, u32[]{:S(2)}, u32[]{:S(2)}) collective-permute-start(bf16[512,768]{1,0:T(8,128)(2,1)S(1)} %constant_dynamic-slice_fusion.6), channel_id=1, source_target_pairs={{2,0},{3,1},{0,2},{1,3},{6,4},{7,5},{4,6},{5,7},{10,8},{11,9},{8,1... | collective-permute-start | bytes 2359304 | tf_op jit(solution)/shard_map/ppermute | solution.py:644
  584.4 95.2 %collective-permute-start.50 = (bf16[32,1024]{1,0:T(8,128)(2,1)S(1)}, bf16[32,1024]{1,0:T(8,128)(2,1)S(1)}, u32[]{:S(2)}, u32[]{:S(2)}) collective-permute-start(bf16[32,1024]{1,0:T(8,128)(2,1)S(1)} %add_convert_fusion.14), channel_id=1, source_target_pairs={{8,0},{9,1},{10,2},{11,3},{12,4},{13,5},{14,6},{15,7},{0,8},{1,9},... | collective-permute-start | bytes 196616 | tf_op jit(solution)/shard_map/ppermute | solution.py:644
  591.0 186.5 %collective-permute-start.20 = (bf16[1280,1024]{1,0:T(8,128)(2,1)}, bf16[1280,1024]{1,0:T(8,128)(2,1)}, u32[]{:S(2)}, u32[]{:S(2)}) collective-permute-start(bf16[1280,1024]{1,0:T(8,128)(2,1)} %get-tuple-element.151), channel_id=1, source_target_pairs={{2,1},{1,2},{6,5},{5,6},{10,9},{9,10},{14,13},{13,14},{18,17},{17,... | collective-permute-start | bytes 7864328 | tf_op jit(solution)/shard_map/ppermute | solution.py:625
  681.5 48.6 %collective-permute-start.37 = (bf16[256,768]{1,0:T(8,128)(2,1)}, bf16[256,768]{1,0:T(8,128)(2,1)}, u32[]{:S(2)}, u32[]{:S(2)}) collective-permute-start(bf16[256,768]{1,0:T(8,128)(2,1)} %constant_dynamic-slice_fusion.5), channel_id=1, source_target_pairs={{8,0},{9,1},{10,2},{11,3},{12,4},{13,5},{14,6},{15,7},{0,8},{1,9},... | collective-permute-start | bytes 1179656 | tf_op jit(solution)/shard_map/ppermute | solution.py:644
  683.5 17.7 %collective-permute-start.44 = (bf16[128,768]{1,0:T(8,128)(2,1)S(1)}, bf16[128,768]{1,0:T(8,128)(2,1)S(1)}, u32[]{:S(2)}, u32[]{:S(2)}) collective-permute-start(bf16[128,768]{1,0:T(8,128)(2,1)S(1)} %constant_dynamic-slice_fusion.2), channel_id=1, source_target_pairs={{8,0},{9,1},{10,2},{11,3},{12,4},{13,5},{14,6},{15,7},{0,8},{1,9},... | collective-permute-start | bytes 589832 | tf_op jit(solution)/shard_map/ppermute | solution.py:644
  686.0 64.3 %collective-permute-start.52 = (bf16[128,1024]{1,0:T(8,128)(2,1)}, bf16[128,1024]{1,0:T(8,128)(2,1)}, u32[]{:S(2)}, u32[]{:S(2)}) collective-permute-start(bf16[128,1024]{1,0:T(8,128)(2,1)} %pad_maximum_fusion.6), channel_id=1, source_target_pairs={{16,0},{17,1},{18,2},{19,3},{20,4},{21,5},{22,6},{23,7},{24,8},{25... | collective-permute-start | bytes 786440 | tf_op jit(solution)/shard_map/ppermute | solution.py:644
  703.5 23.0 %collective-permute-start.45 = (bf16[64,768]{1,0:T(8,128)(2,1)}, bf16[64,768]{1,0:T(8,128)(2,1)}, u32[]{:S(2)}, u32[]{:S(2)}) collective-permute-start(bf16[64,768]{1,0:T(8,128)(2,1)} %constant_dynamic-slice_fusion.1), channel_id=1, source_target_pairs={{16,0},{17,1},{18,2},{19,3},{20,4},{21,5},{22,6},{23,7},{24,8},{25... | collective-permute-start | bytes 294920 | tf_op jit(solution)/shard_map/ppermute | solution.py:644
  715.9 8.0 collective-permute-start.25
  723.9 66.9 %collective-permute-start.24 = (bf16[1280,1024]{1,0:T(8,128)(2,1)}, bf16[1280,1024]{1,0:T(8,128)(2,1)}, u32[]{:S(2)}, u32[]{:S(2)}) collective-permute-start(bf16[1280,1024]{1,0:T(8,128)(2,1)} %fusion.19), channel_id=1, source_target_pairs={{2,1},{1,2},{6,5},{5,6},{10,9},{9,10},{14,13},{13,14},{18,17},{17,... | collective-permute-start | bytes 7864328 | tf_op jit(solution)/shard_map/ppermute | solution.py:625
  727.9 8.0 %collective-permute-start.46 = (bf16[64,768]{1,0:T(8,128)(2,1)S(1)}, bf16[64,768]{1,0:T(8,128)(2,1)S(1)}, u32[]{:S(2)}, u32[]{:S(2)}) collective-permute-start(bf16[64,768]{1,0:T(8,128)(2,1)S(1)} %add_convert_fusion.12), channel_id=1, source_target_pairs={{16,0},{17,1},{18,2},{19,3},{20,4},{21,5},{22,6},{23,7},{24,8},{25... | collective-permute-start | bytes 294920 | tf_op jit(solution)/shard_map/ppermute | solution.py:644
  730.1 15.6 %collective-permute-start.27 = (f32[16384]{0:T(1024)S(1)}, f32[16384]{0:T(1024)S(1)}, u32[]{:S(2)}, u32[]{:S(2)}) collective-permute-start(f32[16384]{0:T(1024)S(1)} %add.416), channel_id=1, source_target_pairs={{0,4},{1,5},{2,6},{3,7},{4,0},{5,1},{6,2},{7,3},{8,12},{9,13},{10,... | collective-permute-start | bytes 196616 | tf_op jit(solution)/shard_map/ppermute | solution.py:694
  735.9 9.3 %collective-permute-start.38 = (bf16[128,768]{1,0:T(8,128)(2,1)S(1)}, bf16[128,768]{1,0:T(8,128)(2,1)S(1)}, u32[]{:S(2)}, u32[]{:S(2)}) collective-permute-start(bf16[128,768]{1,0:T(8,128)(2,1)S(1)} %constant_dynamic-slice_fusion.4), channel_id=1, source_target_pairs={{16,0},{17,1},{18,2},{19,3},{20,4},{21,5},{22,6},{23,7},{24,8},{25... | collective-permute-start | bytes 589832 | tf_op jit(solution)/shard_map/ppermute | solution.py:644
  745.7 12.8 %collective-permute-start.47 = (bf16[128,768]{1,0:T(8,128)(2,1)S(1)}, bf16[128,768]{1,0:T(8,128)(2,1)S(1)}, u32[]{:S(2)}, u32[]{:S(2)}) collective-permute-start(bf16[128,768]{1,0:T(8,128)(2,1)S(1)} %pad_maximum_fusion.8), channel_id=1, source_target_pairs={{8,0},{9,1},{10,2},{11,3},{12,4},{13,5},{14,6},{15,7},{0,8},{1,9},... | collective-permute-start | bytes 589832 | tf_op jit(solution)/shard_map/ppermute | solution.py:644
  749.9 16.5 %collective-permute-start.28 = (f32[16384]{0:T(1024)S(1)}, f32[16384]{0:T(1024)S(1)}, u32[]{:S(2)}, u32[]{:S(2)}) collective-permute-start(f32[16384]{0:T(1024)S(1)} %add.417), channel_id=1, source_target_pairs={{0,8},{1,9},{2,10},{3,11},{4,12},{5,13},{6,14},{7,15},{8,0},{9,1},... | collective-permute-start | bytes 196616 | tf_op jit(solution)/shard_map/ppermute | solution.py:694
  755.0 10.5 %collective-permute-start.41 = (bf16[128,768]{1,0:T(8,128)(2,1)S(1)}, bf16[128,768]{1,0:T(8,128)(2,1)S(1)}, u32[]{:S(2)}, u32[]{:S(2)}) collective-permute-start(bf16[128,768]{1,0:T(8,128)(2,1)S(1)} %pad_maximum_fusion.7), channel_id=1, source_target_pairs={{16,0},{17,1},{18,2},{19,3},{20,4},{21,5},{22,6},{23,7},{24,8},{25... | collective-permute-start | bytes 589832 | tf_op jit(solution)/shard_map/ppermute | solution.py:644
  758.6 8.5 %collective-permute-start.48 = (bf16[256,768]{1,0:T(8,128)(2,1)S(1)}, bf16[256,768]{1,0:T(8,128)(2,1)S(1)}, u32[]{:S(2)}, u32[]{:S(2)}) collective-permute-start(bf16[256,768]{1,0:T(8,128)(2,1)S(1)} %pad_maximum_fusion.5), channel_id=1, source_target_pairs={{4,0},{5,1},{6,2},{7,3},{0,4},{1,5},{2,6},{3,7},{12,8},{13,9},{14,... | collective-permute-start | bytes 1179656 | tf_op jit(solution)/shard_map/ppermute | solution.py:644
  765.6 11.7 %collective-permute-start.42 = (bf16[256,768]{1,0:T(8,128)(2,1)S(1)}, bf16[256,768]{1,0:T(8,128)(2,1)S(1)}, u32[]{:S(2)}, u32[]{:S(2)}) collective-permute-start(bf16[256,768]{1,0:T(8,128)(2,1)S(1)} %pad_maximum_fusion.4), channel_id=1, source_target_pairs={{8,0},{9,1},{10,2},{11,3},{12,4},{13,5},{14,6},{15,7},{0,8},{1,9},... | collective-permute-start | bytes 1179656 | tf_op jit(solution)/shard_map/ppermute | solution.py:644
  766.5 17.0 %collective-permute-start.53 = (bf16[256,1024]{1,0:T(8,128)(2,1)}, bf16[256,1024]{1,0:T(8,128)(2,1)}, u32[]{:S(2)}, u32[]{:S(2)}) collective-permute-start(bf16[256,1024]{1,0:T(8,128)(2,1)} %pad_maximum_fusion.3), channel_id=1, source_target_pairs={{2,0},{3,1},{0,2},{1,3},{6,4},{7,5},{4,6},{5,7},{10,8},{11,9},{8,1... | collective-permute-start | bytes 1572872 | tf_op jit(solution)/shard_map/ppermute | solution.py:644
  767.1 14.5 %collective-permute-start.29 = (f32[16384]{0:T(1024)S(1)}, f32[16384]{0:T(1024)S(1)}, u32[]{:S(2)}, u32[]{:S(2)}) collective-permute-start(f32[16384]{0:T(1024)S(1)} %add.418), channel_id=1, source_target_pairs={{0,16},{1,17},{2,18},{3,19},{4,20},{5,21},{6,22},{7,23},{8,24},{9,... | collective-permute-start | bytes 196616 | tf_op jit(solution)/shard_map/ppermute | solution.py:694
  777.3 9.1 %collective-permute-start.49 = (bf16[512,768]{1,0:T(8,128)(2,1)S(1)}, bf16[512,768]{1,0:T(8,128)(2,1)S(1)}, u32[]{:S(2)}, u32[]{:S(2)}) collective-permute-start(bf16[512,768]{1,0:T(8,128)(2,1)S(1)} %pad_maximum_fusion.2.a), channel_id=1, source_target_pairs={{2,0},{3,1},{0,2},{1,3},{6,4},{7,5},{4,6},{5,7},{10,8},{11,9},{8,1... | collective-permute-start | bytes 2359304 | tf_op jit(solution)/shard_map/ppermute | solution.py:644
  777.5 11.1 %collective-permute-start.43 = (bf16[512,768]{1,0:T(8,128)(2,1)S(1)}, bf16[512,768]{1,0:T(8,128)(2,1)S(1)}, u32[]{:S(2)}, u32[]{:S(2)}) collective-permute-start(bf16[512,768]{1,0:T(8,128)(2,1)S(1)} %pad_maximum_fusion.1.a), channel_id=1, source_target_pairs={{2,0},{3,1},{0,2},{1,3},{6,4},{7,5},{4,6},{5,7},{10,8},{11,9},{8,1... | collective-permute-start | bytes 2359304 | tf_op jit(solution)/shard_map/ppermute | solution.py:644
  (90 other events, 1050.1 us)
Sparse Core Ops, SparseCore 0:
  365.7 117.6 all-reduce.2
  551.1 121.5 all-reduce.4

commit v12 on v11

--- a/solution.py
+++ b/solution.py
@@ -918,6 +918,7 @@
     g_w_out = layout.joined_by(g_w_out, bits)
     g_w_qkv = [layout.halved_by(g, s) for g, s in zip(g_w_qkv, steps)]
     g_w_qkv = [layout.joined_by(g, layout.order(k)) for k, g in enumerate(g_w_qkv)]
+    g_w_up, *g_w_qkv = lax.optimization_barrier((g_w_up, *g_w_qkv))
     begun = ()
     for chunk, mine in enumerate(g_w_qkv):
         theirs = layout.partner(mine, -1)

time: 816 us -> 759 us (0.930)
  Pallas kernels: 286 us -> 194 us
  starting transfers between devices: 117 us -> 177 us
  waiting for transfers between devices: 158 us -> 142 us
    pallas_call x3, Pallas kernels: 114 us -> 55.9 us  [attend_backward(): pl.pallas_call(functools.partial(backward_kernel, parts), grid_spec=pltpu...]
    pallas_call x4, Pallas kernels: 72.8 us -> 38.7 us  [attend_forward(): pl.pallas_call(functools.partial(forward_kernel, parts), grid_spec=pltpu....]
    ppermute x8, starting transfers between devices: 56.5 us -> 90.5 us  [to_rank(): return lax.ppermute(value, self.axes, moves)]
    ppermute x26, starting transfers between devices: 29.7 us -> 50.3 us  [partner(): return lax.ppermute(value, self.axes, moves)]
    psum x2, waiting for transfers between devices: 84.7 us -> 69.8 us  [sum_dp(): return lax.psum(value, 'dp', axis_index_groups=[order])]
  transfers between devices with their start and end apart: 56 -> 56, of which waited for: 16 -> 16; matrix products, arithmetic and copies ran while one was open for 20% -> 21% of each run, Pallas kernels for 31% -> 21%
where the time goes in v12:
time: 759 us; the launch traced here: 751 us
  Pallas kernels  194 us (26%)
  starting transfers between devices  177 us (23%)
  waiting for transfers between devices  142 us (19%)
  other arithmetic  115 us (15%)
  matrix products  55.9 us (7%)
  local copies, waits for them, and re-layouts  49.7 us (7%)
  between operations  17.4 us (2%)
    ppermute x8, starting transfers between devices, to_rank(): return lax.ppermute(value, self.axes, moves)  90.5 us
    psum x2, waiting for transfers between devices, sum_dp(): return lax.psum(value, 'dp', axis_index_groups=[order])  69.8 us
    ppermute x26, waiting for transfers between devices, partner(): return lax.ppermute(value, self.axes, moves)  63.3 us
    pallas_call x3, Pallas kernels, attend_backward(): pl.pallas_call(functools.partial(backward_kernel, parts), grid_spec=pltpu...  55.9 us
    ppermute x26, starting transfers between devices, partner(): return lax.ppermute(value, self.axes, moves)  50.3 us
    pallas_call x4, Pallas kernels, attend_forward(): pl.pallas_call(functools.partial(forward_kernel, parts), grid_spec=pltpu....  38.7 us
    dot_general x4, matrix products, contract_rows(): lax.dot_general(left, right, (((0,), (0,)), ((), ())), preferred_element_...  36.1 us
    pallas_call x2, Pallas kernels, feed_forward(): pl.pallas_call(functools.partial(feed_kernel, min(units, FEED)), grid=(st...  35.6 us
  transfers between devices with their start and end apart: 56, of which 16 were waited for; matrix products, arithmetic and copies ran while one was open for 21% of the time, Pallas kernels for 21%

profile of v12, /device:TPU:0, one launch (start us, length us, event | category | flops | bytes accessed | tf_op | source)
XLA Modules:
  0.0 750.5 jit_solution(7129142909202309436)
XLA Ops:
  16.9 4.7 fusion.52
  34.6 38.5 %collective-permute-start.6 = (bf16[1280,1024]{1,0:T(8,128)(2,1)S(1)}, bf16[1280,1024]{1,0:T(8,128)(2,1)}, u32[]{:S(2)}, u32[]{:S(2)}) collective-permute-start(bf16[1280,1024]{1,0:T(8,128)(2,1)S(1)} %fusion.14.refs_0_), channel_id=1, source_target_pairs={{0,2},{2,0},{1,3},{3,1},{4,6},{6,4},{5,7},{7,5},{8,10},{10,8},{9,1... | collective-permute-start | bytes 7864328 | tf_op jit(solution)/shard_map/ppermute | solution.py:675
  84.3 4.5 fusion.2.refs_0_
  88.9 7.7 %fusion.3.refs_1_ = bf16[1280,1536]{1,0:T(8,128)(2,1)S(1)} fusion(bf16[1280,1024]{1,0:T(8,128)(2,1)} %collective-permute-done.6.refs_1_, bf16[1024,1536]{0,1:T(8,128)(2,1)S(1)} %bitcast.60, f32[1536]{0:T(1024)S(1)} %copy-done.77, f32[1536]{0:T(1024)S(1)} %add.383), kind=kOutput, calls=%fused_computation.12 | convolution fusion | flops 4032430080 | bytes 9711616 | tf_op jit(solution)/shard_map/dot_general | solution.py:57
  96.7 9.6 %attend_forward.4 = (bf16[1280,512]{1,0:T(8,128)(2,1)S(1)}, bf16[1280,512]{1,0:T(8,128)(2,1)S(1)}, bf16[512,2560]{1,0:T(8,128)(2,1)S(1)}, f32[4,2,2560]{2,1,0:T(2,128)S(1)}) custom-call(s32[3,10]{1,0:T(4,128)S(1)} %add_add_fusion.2.tab_ref, s32[2560,1]{1,0:T(8,128)S(1)} %copy-done.3, s32[1,2560]{1,0:T(1,128)S(1)} %fusion.45.qseg_ref, ...), custom_call_target="tpu_custom_call" | custom-call | flops 1024 | bytes 1024 | tf_op jit(solution)/shard_map/attend_forward/pallas_call | solution.py:301
  106.3 9.6 %attend_forward.5 = (bf16[1280,512]{1,0:T(8,128)(2,1)S(1)}, bf16[1280,512]{1,0:T(8,128)(2,1)S(1)}, bf16[512,2560]{1,0:T(8,128)(2,1)S(1)}, f32[4,2,2560]{2,1,0:T(2,128)S(1)}) custom-call(s32[3,10]{1,0:T(4,128)S(1)} %add_add_fusion.2.tab_ref, s32[2560,1]{1,0:T(8,128)S(1)} %copy-done.3, ...), custom_call_target="tpu_custom_call", output_to_operand_aliasing={{0}: (5, {}), {1}: (6, {}), {2}: (7, {}), {3}: (8, {})} | custom-call | flops 1024 | bytes 1024 | tf_op jit(solution)/shard_map/attend_forward/pallas_call | solution.py:301
  115.9 9.6 %attend_forward.6 = (bf16[1280,512]{1,0:T(8,128)(2,1)S(1)}, bf16[1280,512]{1,0:T(8,128)(2,1)S(1)}, bf16[512,2560]{1,0:T(8,128)(2,1)S(1)}, f32[4,2,2560]{2,1,0:T(2,128)S(1)}) custom-call(s32[3,10]{1,0:T(4,128)S(1)} %add_add_fusion.2.tab_ref, s32[2560,1]{1,0:T(8,128)S(1)} %copy-done.3, ...), custom_call_target="tpu_custom_call", output_to_operand_aliasing={{0}: (5, {}), {1}: (6, {}), {2}: (7, {}), {3}: (8, {})} | custom-call | flops 1024 | bytes 1024 | tf_op jit(solution)/shard_map/attend_forward/pallas_call | solution.py:301
  125.5 10.0 %attend_forward.7 = (bf16[1280,512]{1,0:T(8,128)(2,1)S(1)}, bf16[1280,512]{1,0:T(8,128)(2,1)S(1)}, bf16[512,2560]{1,0:T(8,128)(2,1)S(1)}, f32[4,2,2560]{2,1,0:T(2,128)S(1)}) custom-call(s32[3,10]{1,0:T(4,128)S(1)} %add_add_fusion.2.tab_ref, s32[2560,1]{1,0:T(8,128)S(1)} %copy-done.3, ...), custom_call_target="tpu_custom_call", output_to_operand_aliasing={{0}: (5, {}), {1}: (6, {}), {2}: (7, {}), {3}: (8, {})} | custom-call | flops 1024 | bytes 1024 | tf_op jit(solution)/shard_map/attend_forward/pallas_call | solution.py:301
  140.6 37.3 %collective-permute-start.10 = (bf16[1280,1024]{1,0:T(8,128)(2,1)S(1)}, bf16[1280,1024]{1,0:T(8,128)(2,1)S(1)}, u32[]{:S(2)}, u32[]{:S(2)}) collective-permute-start(bf16[1280,1024]{1,0:T(8,128)(2,1)S(1)} %convolution_convert_fusion.1), channel_id=1, source_target_pairs={{0,2},{2,0},{1,3},{3,1},{4,6},{6,4},{5,7},{7,5},{8,10},{10,8},{9,1... | collective-permute-start | bytes 7864328 | tf_op jit(solution)/shard_map/ppermute | solution.py:675
  178.9 4.6 broadcast_select_fusion.2.up_ref
  194.8 4.3 collective-permute-start.11
  199.1 3.7 maximum_select_fusion.down_ref
  203.2 17.7 %feed_forward.2 = (bf16[2560,1024]{1,0:T(8,128)(2,1)}, bf16[2560,2048]{1,0:T(8,128)(2,1)}, bf16[2560,2048]{1,0:T(8,128)(2,1)}, bf16[1280,1024]{1,0:T(8,128)(2,1)S(1)}) custom-call(bf16[1280,1024]{1,0:T(8,128)(2,1)S(1)} %add_convert_fusion.1.x_ref, bf16[1024,2048]{1,0:T(8,128)(2,1)} %broadcast_select_fusion.2.up_ref, f32[1,2048]{1,0:T(1,128)S(1)} %bitcast.52, ...), custom_call_target="tpu_custom_call" | custom-call | flops 16106127360 | bytes 16777216 | tf_op jit(solution)/shard_map/feed_forward/pallas_call | solution.py:411
  220.9 17.8 %feed_forward.3 = (bf16[2560,1024]{1,0:T(8,128)(2,1)}, bf16[2560,2048]{1,0:T(8,128)(2,1)}, bf16[2560,2048]{1,0:T(8,128)(2,1)}, bf16[1280,1024]{1,0:T(8,128)(2,1)S(1)}) custom-call(bf16[1280,1024]{1,0:T(8,128)(2,1)S(1)} %collective-permute-done.11.x_ref, ...), custom_call_target="tpu_custom_call", output_to_operand_aliasing={{0}: (4, {}), {1}: (5, {}), {2}: (6, {})} | custom-call | flops 16106127360 | bytes 16777216 | tf_op jit(solution)/shard_map/feed_forward/pallas_call | solution.py:411
  238.8 9.6 %collective-permute-start.13 = (bf16[1280,1024]{1,0:T(8,128)(2,1)S(1)}, bf16[1280,1024]{1,0:T(8,128)(2,1)S(1)}, u32[]{:S(2)}, u32[]{:S(2)}) collective-permute-start(bf16[1280,1024]{1,0:T(8,128)(2,1)S(1)} %get-tuple-element.133), channel_id=1, source_target_pairs={{0,2},{2,0},{1,3},{3,1},{4,6},{6,4},{5,7},{7,5},{8,10},{10,8},{9,1... | collective-permute-start | bytes 7864328 | tf_op jit(solution)/shard_map/ppermute | solution.py:675
  248.4 4.5 collective-permute-done.13
  255.2 4.2 fusion.26
  259.4 4.9 convert_reduce_fusion.2
  264.7 15.9 %feed_back.2 = (bf16[2560,2048]{1,0:T(8,128)(2,1)}, f32[1,2048]{1,0:T(1,128)S(1)}, bf16[1280,1024]{1,0:T(8,128)(2,1)S(1)}) custom-call(bf16[1280,1024]{1,0:T(8,128)(2,1)S(1)} %get-tuple-element.199.g_ref, bf16[2560,2048]{1,0:T(8,128)(2,1)} %get-tuple-element.139.slope_ref, bf16[2048,1024]{1,0:T(8,128)(2,1)} %maximum_select_fusion.down_ref, ...), custom_call_target="tpu_custom_call" | custom-call | flops 1024 | bytes 1024 | tf_op jit(solution)/shard_map/feed_back/pallas_call | solution.py:473
  280.6 15.3 %fusion.38 = bf16[2048,1024]{1,0:T(8,128)(2,1)} fusion(bf16[2560,2048]{1,0:T(8,128)(2,1)} %get-tuple-element.135, bf16[1280,1024]{1,0:T(8,128)(2,1)S(1)} %collective-permute-done.14.g_ref, bf16[1280,1024]{1,0:T(8,128)(2,1)S(1)} %get-tuple-element.199.g_ref), kind=kOutput, calls=%fused_computation.72 | convolution fusion | flops 10750001152 | bytes 19922944 | tf_op jit(solution)/shard_map/dot_general | solution.py:35
  295.8 16.1 %feed_back.3 = (bf16[2560,2048]{1,0:T(8,128)(2,1)}, f32[1,2048]{1,0:T(1,128)S(1)}, bf16[1280,1024]{1,0:T(8,128)(2,1)S(1)}) custom-call(bf16[1280,1024]{1,0:T(8,128)(2,1)S(1)} %collective-permute-done.14.g_ref, bf16[2560,2048]{1,0:T(8,128)(2,1)} %get-tuple-element.139.slope_ref, ...), custom_call_target="tpu_custom_call", output_to_operand_aliasing={{0}: (4, {})} | custom-call | flops 1024 | bytes 1024 | tf_op jit(solution)/shard_map/feed_back/pallas_call | solution.py:473
  313.1 3.8 collective-permute-done.16
  316.9 5.5 multiply_reduce_fusion
  322.4 8.6 %multiply_reduce_fusion.1 = (f32[1024]{0:T(1024)}, f32[1280]{0:T(1024)S(1)}, f32[1280]{0:T(1024)S(1)}, f32[1024]{0:T(1024)}, f32[1280,1024]{1,0:T(8,128)S(1)}) fusion(f32[1280,1024]{1,0:T(8,128)} %copy-done.28, f32[1280]{0:T(1024)S(1)} %add_rsqrt_fusion.2, f32[1280]{0:T(1024)S(1)} %broadcast_multiply_fusion.10, f32[1024]{0:T(1024)S(1)} %copy-done.63, ...), kind=kLoop, calls=%fused_computation.42 | loop fusion | flops 27520512 | bytes 23650304 | tf_op jit(solution)/shard_map/reduce_sum | solution.py:935
  333.5 16.8 %convolution_convert_fusion = bf16[1024,2048]{1,0:T(8,128)(2,1)} fusion(bf16[2560,1024]{1,0:T(8,128)(2,1)} %get-tuple-element.137, bf16[2560,2048]{1,0:T(8,128)(2,1)} %get-tuple-element.141), kind=kOutput, calls=%fused_computation.71 | convolution fusion | flops 10739515392 | bytes 19922944 | tf_op jit(solution)/shard_map/dot_general | solution.py:35
  368.2 26.4 %attend_backward.3 = (bf16[1280,768]{1,0:T(8,128)(2,1)S(1)}, bf16[1280,768]{1,0:T(8,128)(2,1)}) custom-call(s32[3,10]{1,0:T(4,128)S(1)} %add_add_fusion.2.tab_ref, s32[2560,1]{1,0:T(8,128)S(1)} %copy-done.4, s32[1,2560]{1,0:T(1,128)S(1)} %fusion.45.qseg_ref, bf16[1280,1536]{1,0:T(8,128)(2,1)} %copy-done, bf16[1280,1536]{1,0:T(8,128)(2,1)} %copy-done.1, ...), custom_call_target="tpu_custom_call" | custom-call | flops 1024 | bytes 1024 | tf_op jit(solution)/shard_map/attend_backward/pallas_call | solution.py:335
  397.0 8.7 %weight_grad.2 = (bf16[1024,768]{1,0:T(8,128)(2,1)}, f32[1,768]{1,0:T(1,128)S(1)}) custom-call(bf16[1280,1024]{1,0:T(8,128)(2,1)S(1)} %copy-done.6, bf16[1280,1024]{1,0:T(8,128)(2,1)} %collective-permute-done.6.refs_1_, bf16[1280,768]{1,0:T(8,128)(2,1)S(1)} %get-tuple-element.150.refs_2_.refs_0_, bf16[1280,768]{1,0:T(8,128)(2,1)S(1)} %copy-done.22), custom_call_target="tpu_custom_call" | custom-call | flops 1024 | bytes 1024 | tf_op jit(solution)/shard_map/weight_grad/pallas_call | solution.py:513
  410.3 14.7 %attend_backward.4 = (bf16[1280,768]{1,0:T(8,128)(2,1)S(1)}, bf16[1280,768]{1,0:T(8,128)(2,1)}) custom-call(s32[3,10]{1,0:T(4,128)S(1)} %add_add_fusion.2.tab_ref, s32[2560,1]{1,0:T(8,128)S(1)} %copy-done.4, s32[1,2560]{1,0:T(1,128)S(1)} %fusion.45.qseg_ref, bf16[1280,1536]{1,0:T(8,128)(2,1)} %copy-done, bf16[1280,1536]{1,0:T(8,128)(2,1)} %copy-done.1, ...), custom_call_target="tpu_custom_call" | custom-call | flops 1024 | bytes 1024 | tf_op jit(solution)/shard_map/attend_backward/pallas_call | solution.py:335
  427.4 4.6 broadcast_select_fusion.1
  434.8 48.5 %all-reduce.3.cloned.1.call-done = bf16[2048,1024]{1,0:T(8,128)(2,1)} async-done(((bf16[2048,1024]{1,0:T(8,128)(2,1)}), bf16[2048,1024]{1,0:T(8,128)(2,1)}) %all-reduce.3.cloned.1.call-update) | async-done | bytes 4194320 | tf_op jit(solution)/shard_map/psum | solution.py:699
  488.0 14.7 %attend_backward.5 = (bf16[1280,768]{1,0:T(8,128)(2,1)S(1)}, bf16[1280,768]{1,0:T(8,128)(2,1)}) custom-call(s32[3,10]{1,0:T(4,128)S(1)} %add_add_fusion.2.tab_ref, s32[2560,1]{1,0:T(8,128)S(1)} %copy-done.4, s32[1,2560]{1,0:T(1,128)S(1)} %fusion.45.qseg_ref, bf16[1280,1536]{1,0:T(8,128)(2,1)} %copy-done, ...), custom_call_target="tpu_custom_call", output_to_operand_aliasing={{0}: (9, {}), {1}: (10, {})} | custom-call | flops 1024 | bytes 1024 | tf_op jit(solution)/shard_map/attend_backward/pallas_call | solution.py:335
  505.0 8.9 %weight_grad.3 = (bf16[1024,768]{1,0:T(8,128)(2,1)}, f32[1,768]{1,0:T(1,128)S(1)}) custom-call(bf16[1280,1024]{1,0:T(8,128)(2,1)S(1)} %copy-done.7, bf16[1280,1024]{1,0:T(8,128)(2,1)} %collective-permute-done.6.refs_1_, bf16[1280,768]{1,0:T(8,128)(2,1)S(1)} %get-tuple-element.165.refs_1_.refs_2_, bf16[1280,768]{1,0:T(8,128)(2,1)S(1)} %copy-done.12), custom_call_target="tpu_custom_call" | custom-call | flops 1024 | bytes 1024 | tf_op jit(solution)/shard_map/weight_grad/pallas_call | solution.py:513
  517.1 16.6 %collective-permute-start.19 = (bf16[512,768]{1,0:T(8,128)(2,1)}, bf16[512,768]{1,0:T(8,128)(2,1)}, u32[]{:S(2)}, u32[]{:S(2)}) collective-permute-start(bf16[512,768]{1,0:T(8,128)(2,1)} %constant_dynamic-slice_fusion.12), channel_id=1, source_target_pairs={{2,0},{3,1},{0,2},{1,3},{6,4},{7,5},{4,6},{5,7},{10,8},{11,9},{8,1... | collective-permute-start | bytes 2359304 | tf_op jit(solution)/shard_map/ppermute | solution.py:644
  540.3 5.5 input_grad.3
  545.9 4.5 input_grad.2
  558.5 10.2 %collective-permute-done.31 = bf16[128,1024]{1,0:T(8,128)(2,1)S(1)} collective-permute-done((bf16[128,1024]{1,0:T(8,128)(2,1)S(1)}, bf16[128,1024]{1,0:T(8,128)(2,1)S(1)}, u32[]{:S(2)}, u32[]{:S(2)}) %collective-permute-start.31) | collective-permute-done | bytes 262176 | tf_op jit(solution)/shard_map/ppermute | solution.py:644
  580.7 6.8 convert_element_type.279
  593.0 4.8 collective-permute-done.51
  606.0 5.3 fusion.20
  618.0 6.5 fusion.19
  631.7 5.1 collective-permute-start.27
  639.5 13.8 %collective-permute-done.43 = bf16[128,768]{1,0:T(8,128)(2,1)S(1)} collective-permute-done((bf16[128,768]{1,0:T(8,128)(2,1)S(1)}, bf16[128,768]{1,0:T(8,128)(2,1)S(1)}, u32[]{:S(2)}, u32[]{:S(2)}) %collective-permute-start.43) | collective-permute-done | bytes 196640 | tf_op jit(solution)/shard_map/ppermute | solution.py:644
  664.3 5.0 collective-permute-start.46
  672.0 8.9 %collective-permute-done.46 = bf16[128,768]{1,0:T(8,128)(2,1)S(1)} collective-permute-done((bf16[128,768]{1,0:T(8,128)(2,1)S(1)}, bf16[128,768]{1,0:T(8,128)(2,1)S(1)}, u32[]{:S(2)}, u32[]{:S(2)}) %collective-permute-start.46) | collective-permute-done | bytes 196640 | tf_op jit(solution)/shard_map/ppermute | solution.py:644
  684.4 14.6 %collective-permute-done.47 = bf16[256,768]{1,0:T(8,128)(2,1)S(1)} collective-permute-done((bf16[256,768]{1,0:T(8,128)(2,1)S(1)}, bf16[256,768]{1,0:T(8,128)(2,1)S(1)}, u32[]{:S(2)}, u32[]{:S(2)}) %collective-permute-start.47) | collective-permute-done | bytes 393248 | tf_op jit(solution)/shard_map/ppermute | solution.py:644
  699.1 21.3 %all-reduce.5.cloned.1.call-done = bf16[1024,2048]{1,0:T(8,128)(2,1)} async-done(((bf16[1024,2048]{1,0:T(8,128)(2,1)}), bf16[1024,2048]{1,0:T(8,128)(2,1)}) %all-reduce.5.cloned.1.call-update) | async-done | bytes 4194320 | tf_op jit(solution)/shard_map/psum | solution.py:699
  730.1 4.4 convert_element_type.278
  739.1 4.4 select_convert_fusion
  (399 shorter events, 183.7 us)
Async XLA Ops:
  7.2 476.1 %all-reduce.3.cloned.1.call-start = ((), (), s32[]{:S(2)}) async-start(), calls=%async_computation | async-start | bytes 8388608 | tf_op jit(solution)/shard_map/psum | solution.py:699
  13.1 15.6 %collective-permute-start.2 = (bf16[1280,1024]{1,0:T(8,128)(2,1)}, bf16[1280,1024]{1,0:T(8,128)(2,1)}, u32[]{:S(2)}, u32[]{:S(2)}) collective-permute-start(bf16[1280,1024]{1,0:T(8,128)(2,1)} %param.20), channel_id=1, source_target_pairs={{1,2},{2,1},{5,6},{6,5},{9,10},{10,9},{13,14},{14,13},{17,18},{18,... | collective-permute-start | bytes 7864328 | tf_op jit(solution)/shard_map/ppermute | solution.py:625
  15.3 8.5 %collective-permute-start.4 = (bf16[256,3,512]{0,2,1:T(8,128)(2,1)}, bf16[256,3,512]{0,2,1:T(8,128)(2,1)}, u32[]{:S(2)}, u32[]{:S(2)}) collective-permute-start(bf16[256,3,512]{0,2,1:T(8,128)(2,1)} %copy-done.53), channel_id=1, source_target_pairs={{9,1},{10,2},{13,5},{14,6},{1,9},{2,10},{5,13},{6,14},{25,17},{26,... | collective-permute-start | bytes 2359304 | tf_op jit(solution)/shard_map/ppermute | solution.py:644
  26.7 49.5 %collective-permute-start.5 = (bf16[512,3,512]{0,2,1:T(8,128)(2,1)}, bf16[512,3,512]{0,2,1:T(8,128)(2,1)}, u32[]{:S(2)}, u32[]{:S(2)}) collective-permute-start(bf16[512,3,512]{0,2,1:T(8,128)(2,1)} %pad_maximum_fusion), channel_id=1, source_target_pairs={{5,1},{6,2},{1,5},{2,6},{13,9},{14,10},{9,13},{10,14},{21,17},{22,... | collective-permute-start | bytes 4718600 | tf_op jit(solution)/shard_map/ppermute | solution.py:644
  29.6 86.3 %collective-permute-start.3 = (bf16[1024,2048]{1,0:T(8,128)(2,1)}, bf16[1024,2048]{1,0:T(8,128)(2,1)}, u32[]{:S(2)}, u32[]{:S(2)}) collective-permute-start(bf16[1024,2048]{1,0:T(8,128)(2,1)} %param.31), channel_id=1, source_target_pairs={{1,2},{2,1},{5,6},{6,5},{9,10},{10,9},{13,14},{14,13},{17,18},{18,... | collective-permute-start | bytes 12582920 | tf_op jit(solution)/shard_map/ppermute | solution.py:625
  34.6 54.3 %collective-permute-start.6 = (bf16[1280,1024]{1,0:T(8,128)(2,1)S(1)}, bf16[1280,1024]{1,0:T(8,128)(2,1)}, u32[]{:S(2)}, u32[]{:S(2)}) collective-permute-start(bf16[1280,1024]{1,0:T(8,128)(2,1)S(1)} %fusion.14.refs_0_), channel_id=1, source_target_pairs={{0,2},{2,0},{1,3},{3,1},{4,6},{6,4},{5,7},{7,5},{8,10},{10,8},{9,1... | collective-permute-start | bytes 7864328 | tf_op jit(solution)/shard_map/ppermute | solution.py:675
  78.9 56.6 %collective-permute-start.8 = (bf16[1024,1024]{1,0:T(8,128)(2,1)}, bf16[1024,1024]{1,0:T(8,128)(2,1)S(1)}, u32[]{:S(2)}, u32[]{:S(2)}) collective-permute-start(bf16[1024,1024]{1,0:T(8,128)(2,1)} %get-tuple-element.119), channel_id=1, source_target_pairs={{1,2},{2,1},{5,6},{6,5},{9,10},{10,9},{13,14},{14,13},{17,18},{18,... | collective-permute-start | bytes 6291464 | tf_op jit(solution)/shard_map/ppermute | solution.py:625
  79.7 55.8 %collective-permute-start.9 = (bf16[1024,1024]{1,0:T(8,128)(2,1)S(1)}, bf16[1024,1024]{1,0:T(8,128)(2,1)S(1)}, u32[]{:S(2)}, u32[]{:S(2)}) collective-permute-start(bf16[1024,1024]{1,0:T(8,128)(2,1)S(1)} %copy-done.45), channel_id=1, source_target_pairs={{1,2},{2,1},{5,6},{6,5},{9,10},{10,9},{13,14},{14,13},{17,18},{18,... | collective-permute-start | bytes 6291464 | tf_op jit(solution)/shard_map/ppermute | solution.py:625
  82.2 53.2 %collective-permute-start.7 = (bf16[512,1024]{1,0:T(8,128)(2,1)}, bf16[512,1024]{1,0:T(8,128)(2,1)}, u32[]{:S(2)}, u32[]{:S(2)}) collective-permute-start(bf16[512,1024]{1,0:T(8,128)(2,1)} %param.25), channel_id=1, source_target_pairs={{1,2},{2,1},{5,6},{6,5},{9,10},{10,9},{13,14},{14,13},{17,18},{18,... | collective-permute-start | bytes 3145736 | tf_op jit(solution)/shard_map/ppermute | solution.py:625
  140.6 42.9 %collective-permute-start.10 = (bf16[1280,1024]{1,0:T(8,128)(2,1)S(1)}, bf16[1280,1024]{1,0:T(8,128)(2,1)S(1)}, u32[]{:S(2)}, u32[]{:S(2)}) collective-permute-start(bf16[1280,1024]{1,0:T(8,128)(2,1)S(1)} %convolution_convert_fusion.1), channel_id=1, source_target_pairs={{0,2},{2,0},{1,3},{3,1},{4,6},{6,4},{5,7},{7,5},{8,10},{10,8},{9,1... | collective-permute-start | bytes 7864328 | tf_op jit(solution)/shard_map/ppermute | solution.py:675
  177.9 24.9 %collective-permute-start.12 = (bf16[1280,1024]{1,0:T(8,128)(2,1)S(1)}, bf16[1280,1024]{1,0:T(8,128)(2,1)S(1)}, u32[]{:S(2)}, u32[]{:S(2)}) collective-permute-start(bf16[1280,1024]{1,0:T(8,128)(2,1)S(1)} %copy-done.39), channel_id=1, source_target_pairs={{1,2},{2,1},{5,6},{6,5},{9,10},{10,9},{13,14},{14,13},{17,18},{18,... | collective-permute-start | bytes 7864328 | tf_op jit(solution)/shard_map/ppermute | solution.py:625
  194.8 26.1 %collective-permute-start.11 = (bf16[1280,1024]{1,0:T(8,128)(2,1)S(1)}, bf16[1280,1024]{1,0:T(8,128)(2,1)S(1)}, u32[]{:S(2)}, u32[]{:S(2)}) collective-permute-start(bf16[1280,1024]{1,0:T(8,128)(2,1)S(1)} %add_convert_fusion.1.x_ref), channel_id=1, source_target_pairs={{0,2},{2,0},{1,3},{3,1},{4,6},{6,4},{5,7},{7,5},{8,10},{10,8},{9,1... | collective-permute-start | bytes 7864328 | tf_op jit(solution)/shard_map/ppermute | solution.py:675
  238.8 14.2 %collective-permute-start.13 = (bf16[1280,1024]{1,0:T(8,128)(2,1)S(1)}, bf16[1280,1024]{1,0:T(8,128)(2,1)S(1)}, u32[]{:S(2)}, u32[]{:S(2)}) collective-permute-start(bf16[1280,1024]{1,0:T(8,128)(2,1)S(1)} %get-tuple-element.133), channel_id=1, source_target_pairs={{0,2},{2,0},{1,3},{3,1},{4,6},{6,4},{5,7},{7,5},{8,10},{10,8},{9,1... | collective-permute-start | bytes 7864328 | tf_op jit(solution)/shard_map/ppermute | solution.py:675
  264.3 16.3 %collective-permute-start.14 = (bf16[1280,1024]{1,0:T(8,128)(2,1)S(1)}, bf16[1280,1024]{1,0:T(8,128)(2,1)S(1)}, u32[]{:S(2)}, u32[]{:S(2)}) collective-permute-start(bf16[1280,1024]{1,0:T(8,128)(2,1)S(1)} %get-tuple-element.199.g_ref), channel_id=1, source_target_pairs={{0,2},{2,0},{1,3},{3,1},{4,6},{6,4},{5,7},{7,5},{8,10},{10,8},{9,1... | collective-permute-start | bytes 7864328 | tf_op jit(solution)/shard_map/ppermute | solution.py:675
  312.1 45.3 %collective-permute-start.15 = (bf16[2048,1024]{1,0:T(8,128)(2,1)}, bf16[2048,1024]{1,0:T(8,128)(2,1)S(1)}, u32[]{:S(2)}, u32[]{:S(2)}) collective-permute-start(bf16[2048,1024]{1,0:T(8,128)(2,1)} %fusion.38), channel_id=1, source_target_pairs={{2,1},{1,2},{6,5},{5,6},{10,9},{9,10},{14,13},{13,14},{18,17},{17,... | collective-permute-start | bytes 12582920 | tf_op jit(solution)/shard_map/ppermute | solution.py:625
  333.4 21.4 %collective-permute-start.17 = (bf16[1280,1024]{1,0:T(8,128)(2,1)S(1)}, bf16[1280,1024]{1,0:T(8,128)(2,1)S(1)}, u32[]{:S(2)}, u32[]{:S(2)}) collective-permute-start(bf16[1280,1024]{1,0:T(8,128)(2,1)S(1)} %get-tuple-element.201), channel_id=1, source_target_pairs={{0,2},{2,0},{1,3},{3,1},{4,6},{6,4},{5,7},{7,5},{8,10},{10,8},{9,1... | collective-permute-start | bytes 7864328 | tf_op jit(solution)/shard_map/ppermute | solution.py:675
  350.4 74.7 %collective-permute-start.21 = (bf16[1024,2048]{1,0:T(8,128)(2,1)}, bf16[1024,2048]{1,0:T(8,128)(2,1)}, u32[]{:S(2)}, u32[]{:S(2)}) collective-permute-start(bf16[1024,2048]{1,0:T(8,128)(2,1)} %convolution_convert_fusion), channel_id=1, source_target_pairs={{2,1},{1,2},{6,5},{5,6},{10,9},{9,10},{14,13},{13,14},{18,17},{17,... | collective-permute-start | bytes 12582920 | tf_op jit(solution)/shard_map/ppermute | solution.py:625
  361.5 63.5 %collective-permute-start.22 = (bf16[512,1024]{1,0:T(8,128)(2,1)}, bf16[512,1024]{1,0:T(8,128)(2,1)}, u32[]{:S(2)}, u32[]{:S(2)}) collective-permute-start(bf16[512,1024]{1,0:T(8,128)(2,1)} %add_convert_fusion.2), channel_id=1, source_target_pairs={{2,1},{1,2},{6,5},{5,6},{10,9},{9,10},{14,13},{13,14},{18,17},{17,... | collective-permute-start | bytes 3145736 | tf_op jit(solution)/shard_map/ppermute | solution.py:625
  365.6 354.8 %all-reduce.5.cloned.1.call-start = ((), (), s32[]{:S(2)}) async-start(), calls=%async_computation.1 | async-start | bytes 8388608 | tf_op jit(solution)/shard_map/psum | solution.py:699
  405.7 26.4 %collective-permute-start.18 = (bf16[1024,768]{1,0:T(8,128)(2,1)}, bf16[1024,768]{1,0:T(8,128)(2,1)}, u32[]{:S(2)}, u32[]{:S(2)}) collective-permute-start(bf16[1024,768]{1,0:T(8,128)(2,1)} %get-tuple-element.153), channel_id=1, source_target_pairs={{2,1},{1,2},{6,5},{5,6},{10,9},{9,10},{14,13},{13,14},{18,17},{17,... | collective-permute-start | bytes 4718600 | tf_op jit(solution)/shard_map/ppermute | solution.py:625
  485.2 66.7 %collective-permute-start.30 = (bf16[256,1024]{1,0:T(8,128)(2,1)}, bf16[256,1024]{1,0:T(8,128)(2,1)}, u32[]{:S(2)}, u32[]{:S(2)}) collective-permute-start(bf16[256,1024]{1,0:T(8,128)(2,1)} %constant_dynamic-slice_fusion.11), channel_id=1, source_target_pairs={{2,0},{3,1},{0,2},{1,3},{6,4},{7,5},{4,6},{5,7},{10,8},{11,9},{8,1... | collective-permute-start | bytes 1572872 | tf_op jit(solution)/shard_map/ppermute | solution.py:644
  513.9 55.0 %collective-permute-start.35 = (bf16[1024,768]{1,0:T(8,128)(2,1)}, bf16[1024,768]{1,0:T(8,128)(2,1)}, u32[]{:S(2)}, u32[]{:S(2)}) collective-permute-start(bf16[1024,768]{1,0:T(8,128)(2,1)} %get-tuple-element.174), channel_id=1, source_target_pairs={{2,1},{1,2},{6,5},{5,6},{10,9},{9,10},{14,13},{13,14},{18,17},{17,... | collective-permute-start | bytes 4718600 | tf_op jit(solution)/shard_map/ppermute | solution.py:625
  517.1 39.0 %collective-permute-start.19 = (bf16[512,768]{1,0:T(8,128)(2,1)}, bf16[512,768]{1,0:T(8,128)(2,1)}, u32[]{:S(2)}, u32[]{:S(2)}) collective-permute-start(bf16[512,768]{1,0:T(8,128)(2,1)} %constant_dynamic-slice_fusion.12), channel_id=1, source_target_pairs={{2,0},{3,1},{0,2},{1,3},{6,4},{7,5},{4,6},{5,7},{10,8},{11,9},{8,1... | collective-permute-start | bytes 2359304 | tf_op jit(solution)/shard_map/ppermute | solution.py:644
  551.9 54.0 %collective-permute-start.23 = (bf16[1280,1024]{1,0:T(8,128)(2,1)}, bf16[1280,1024]{1,0:T(8,128)(2,1)}, u32[]{:S(2)}, u32[]{:S(2)}) collective-permute-start(bf16[1280,1024]{1,0:T(8,128)(2,1)} %input_grad.3), channel_id=1, source_target_pairs={{0,2},{2,0},{1,3},{3,1},{4,6},{6,4},{5,7},{7,5},{8,10},{10,8},{9,1... | collective-permute-start | bytes 7864328 | tf_op jit(solution)/shard_map/ppermute | solution.py:675
  553.4 15.3 %collective-permute-start.31 = (bf16[128,1024]{1,0:T(8,128)(2,1)S(1)}, bf16[128,1024]{1,0:T(8,128)(2,1)S(1)}, u32[]{:S(2)}, u32[]{:S(2)}) collective-permute-start(bf16[128,1024]{1,0:T(8,128)(2,1)S(1)} %constant_dynamic-slice_fusion.10), channel_id=1, source_target_pairs={{16,0},{17,1},{18,2},{19,3},{20,4},{21,5},{22,6},{23,7},{24,8},{25... | collective-permute-start | bytes 786440 | tf_op jit(solution)/shard_map/ppermute | solution.py:644
  557.6 17.8 %collective-permute-start.34 = (bf16[256,768]{1,0:T(8,128)(2,1)S(1)}, bf16[256,768]{1,0:T(8,128)(2,1)S(1)}, u32[]{:S(2)}, u32[]{:S(2)}) collective-permute-start(bf16[256,768]{1,0:T(8,128)(2,1)S(1)} %constant_dynamic-slice_fusion.7), channel_id=1, source_target_pairs={{4,0},{5,1},{6,2},{7,3},{0,4},{1,5},{2,6},{3,7},{12,8},{13,9},{14,... | collective-permute-start | bytes 1179656 | tf_op jit(solution)/shard_map/ppermute | solution.py:644
  570.5 7.9 %collective-permute-start.36 = (bf16[512,768]{1,0:T(8,128)(2,1)S(1)}, bf16[512,768]{1,0:T(8,128)(2,1)S(1)}, u32[]{:S(2)}, u32[]{:S(2)}) collective-permute-start(bf16[512,768]{1,0:T(8,128)(2,1)S(1)} %constant_dynamic-slice_fusion.6), channel_id=1, source_target_pairs={{2,0},{3,1},{0,2},{1,3},{6,4},{7,5},{4,6},{5,7},{10,8},{11,9},{8,1... | collective-permute-start | bytes 2359304 | tf_op jit(solution)/shard_map/ppermute | solution.py:644
  578.6 11.1 %collective-permute-start.50 = (bf16[32,1024]{1,0:T(8,128)(2,1)S(1)}, bf16[32,1024]{1,0:T(8,128)(2,1)S(1)}, u32[]{:S(2)}, u32[]{:S(2)}) collective-permute-start(bf16[32,1024]{1,0:T(8,128)(2,1)S(1)} %add_convert_fusion.14), channel_id=1, source_target_pairs={{8,0},{9,1},{10,2},{11,3},{12,4},{13,5},{14,6},{15,7},{0,8},{1,9},... | collective-permute-start | bytes 196616 | tf_op jit(solution)/shard_map/ppermute | solution.py:644
  587.5 133.1 %collective-permute-start.20 = (bf16[1280,1024]{1,0:T(8,128)(2,1)}, bf16[1280,1024]{1,0:T(8,128)(2,1)}, u32[]{:S(2)}, u32[]{:S(2)}) collective-permute-start(bf16[1280,1024]{1,0:T(8,128)(2,1)} %get-tuple-element.154), channel_id=1, source_target_pairs={{2,1},{1,2},{6,5},{5,6},{10,9},{9,10},{14,13},{13,14},{18,17},{17,... | collective-permute-start | bytes 7864328 | tf_op jit(solution)/shard_map/ppermute | solution.py:625
  589.8 8.0 %collective-permute-start.51 = (bf16[64,1024]{1,0:T(8,128)(2,1)S(1)}, bf16[64,1024]{1,0:T(8,128)(2,1)S(1)}, u32[]{:S(2)}, u32[]{:S(2)}) collective-permute-start(bf16[64,1024]{1,0:T(8,128)(2,1)S(1)} %pad_maximum_fusion.9), channel_id=1, source_target_pairs={{4,0},{5,1},{6,2},{7,3},{0,4},{1,5},{2,6},{3,7},{12,8},{13,9},{14,... | collective-permute-start | bytes 393224 | tf_op jit(solution)/shard_map/ppermute | solution.py:644
  590.1 12.0 %collective-permute-start.37 = (bf16[128,768]{1,0:T(8,128)(2,1)S(1)}, bf16[128,768]{1,0:T(8,128)(2,1)S(1)}, u32[]{:S(2)}, u32[]{:S(2)}) collective-permute-start(bf16[128,768]{1,0:T(8,128)(2,1)S(1)} %constant_dynamic-slice_fusion.5), channel_id=1, source_target_pairs={{8,0},{9,1},{10,2},{11,3},{12,4},{13,5},{14,6},{15,7},{0,8},{1,9},... | collective-permute-start | bytes 589832 | tf_op jit(solution)/shard_map/ppermute | solution.py:644
  591.7 40.0 %collective-permute-start.42 = (bf16[256,768]{1,0:T(8,128)(2,1)}, bf16[256,768]{1,0:T(8,128)(2,1)}, u32[]{:S(2)}, u32[]{:S(2)}) collective-permute-start(bf16[256,768]{1,0:T(8,128)(2,1)} %constant_dynamic-slice_fusion.3), channel_id=1, source_target_pairs={{8,0},{9,1},{10,2},{11,3},{12,4},{13,5},{14,6},{15,7},{0,8},{1,9},... | collective-permute-start | bytes 1179656 | tf_op jit(solution)/shard_map/ppermute | solution.py:644
  598.6 60.9 %collective-permute-start.52 = (bf16[128,1024]{1,0:T(8,128)(2,1)}, bf16[128,1024]{1,0:T(8,128)(2,1)}, u32[]{:S(2)}, u32[]{:S(2)}) collective-permute-start(bf16[128,1024]{1,0:T(8,128)(2,1)} %pad_maximum_fusion.6), channel_id=1, source_target_pairs={{16,0},{17,1},{18,2},{19,3},{20,4},{21,5},{22,6},{23,7},{24,8},{25... | collective-permute-start | bytes 786440 | tf_op jit(solution)/shard_map/ppermute | solution.py:644
  602.9 24.1 %collective-permute-start.38 = (bf16[64,768]{1,0:T(8,128)(2,1)}, bf16[64,768]{1,0:T(8,128)(2,1)}, u32[]{:S(2)}, u32[]{:S(2)}) collective-permute-start(bf16[64,768]{1,0:T(8,128)(2,1)} %constant_dynamic-slice_fusion.4), channel_id=1, source_target_pairs={{16,0},{17,1},{18,2},{19,3},{20,4},{21,5},{22,6},{23,7},{24,8},{25... | collective-permute-start | bytes 294920 | tf_op jit(solution)/shard_map/ppermute | solution.py:644
  617.6 6.9 collective-permute-start.25
  624.5 114.6 %collective-permute-start.24 = (bf16[1280,1024]{1,0:T(8,128)(2,1)}, bf16[1280,1024]{1,0:T(8,128)(2,1)}, u32[]{:S(2)}, u32[]{:S(2)}) collective-permute-start(bf16[1280,1024]{1,0:T(8,128)(2,1)} %fusion.19), channel_id=1, source_target_pairs={{2,1},{1,2},{6,5},{5,6},{10,9},{9,10},{14,13},{13,14},{18,17},{17,... | collective-permute-start | bytes 7864328 | tf_op jit(solution)/shard_map/ppermute | solution.py:625
  629.5 9.9 %collective-permute-start.39 = (bf16[64,768]{1,0:T(8,128)(2,1)S(1)}, bf16[64,768]{1,0:T(8,128)(2,1)S(1)}, u32[]{:S(2)}, u32[]{:S(2)}) collective-permute-start(bf16[64,768]{1,0:T(8,128)(2,1)S(1)} %add_convert_fusion.13), channel_id=1, source_target_pairs={{16,0},{17,1},{18,2},{19,3},{20,4},{21,5},{22,6},{23,7},{24,8},{25... | collective-permute-start | bytes 294920 | tf_op jit(solution)/shard_map/ppermute | solution.py:644
  631.7 23.9 %collective-permute-start.27 = (f32[16384]{0:T(1024)S(1)}, f32[16384]{0:T(1024)S(1)}, u32[]{:S(2)}, u32[]{:S(2)}) collective-permute-start(f32[16384]{0:T(1024)S(1)} %add.416), channel_id=1, source_target_pairs={{0,4},{1,5},{2,6},{3,7},{4,0},{5,1},{6,2},{7,3},{8,12},{9,13},{10,... | collective-permute-start | bytes 196616 | tf_op jit(solution)/shard_map/ppermute | solution.py:694
  639.5 13.8 %collective-permute-start.43 = (bf16[128,768]{1,0:T(8,128)(2,1)S(1)}, bf16[128,768]{1,0:T(8,128)(2,1)S(1)}, u32[]{:S(2)}, u32[]{:S(2)}) collective-permute-start(bf16[128,768]{1,0:T(8,128)(2,1)S(1)} %constant_dynamic-slice_fusion.2), channel_id=1, source_target_pairs={{16,0},{17,1},{18,2},{19,3},{20,4},{21,5},{22,6},{23,7},{24,8},{25... | collective-permute-start | bytes 589832 | tf_op jit(solution)/shard_map/ppermute | solution.py:644
  655.6 13.7 %collective-permute-start.40 = (bf16[128,768]{1,0:T(8,128)(2,1)S(1)}, bf16[128,768]{1,0:T(8,128)(2,1)S(1)}, u32[]{:S(2)}, u32[]{:S(2)}) collective-permute-start(bf16[128,768]{1,0:T(8,128)(2,1)S(1)} %pad_maximum_fusion.7), channel_id=1, source_target_pairs={{8,0},{9,1},{10,2},{11,3},{12,4},{13,5},{14,6},{15,7},{0,8},{1,9},... | collective-permute-start | bytes 589832 | tf_op jit(solution)/shard_map/ppermute | solution.py:644
  658.2 23.8 %collective-permute-start.28 = (f32[16384]{0:T(1024)S(1)}, f32[16384]{0:T(1024)S(1)}, u32[]{:S(2)}, u32[]{:S(2)}) collective-permute-start(f32[16384]{0:T(1024)S(1)} %add.417), channel_id=1, source_target_pairs={{0,8},{1,9},{2,10},{3,11},{4,12},{5,13},{6,14},{7,15},{8,0},{9,1},... | collective-permute-start | bytes 196616 | tf_op jit(solution)/shard_map/ppermute | solution.py:694
  664.3 16.6 %collective-permute-start.46 = (bf16[128,768]{1,0:T(8,128)(2,1)S(1)}, bf16[128,768]{1,0:T(8,128)(2,1)S(1)}, u32[]{:S(2)}, u32[]{:S(2)}) collective-permute-start(bf16[128,768]{1,0:T(8,128)(2,1)S(1)} %pad_maximum_fusion.8), channel_id=1, source_target_pairs={{16,0},{17,1},{18,2},{19,3},{20,4},{21,5},{22,6},{23,7},{24,8},{25... | collective-permute-start | bytes 589832 | tf_op jit(solution)/shard_map/ppermute | solution.py:644
  669.4 12.5 %collective-permute-start.41 = (bf16[256,768]{1,0:T(8,128)(2,1)S(1)}, bf16[256,768]{1,0:T(8,128)(2,1)S(1)}, u32[]{:S(2)}, u32[]{:S(2)}) collective-permute-start(bf16[256,768]{1,0:T(8,128)(2,1)S(1)} %pad_maximum_fusion.4), channel_id=1, source_target_pairs={{4,0},{5,1},{6,2},{7,3},{0,4},{1,5},{2,6},{3,7},{12,8},{13,9},{14,... | collective-permute-start | bytes 1179656 | tf_op jit(solution)/shard_map/ppermute | solution.py:644
  681.0 17.9 %collective-permute-start.47 = (bf16[256,768]{1,0:T(8,128)(2,1)S(1)}, bf16[256,768]{1,0:T(8,128)(2,1)S(1)}, u32[]{:S(2)}, u32[]{:S(2)}) collective-permute-start(bf16[256,768]{1,0:T(8,128)(2,1)S(1)} %pad_maximum_fusion.5), channel_id=1, source_target_pairs={{8,0},{9,1},{10,2},{11,3},{12,4},{13,5},{14,6},{15,7},{0,8},{1,9},... | collective-permute-start | bytes 1179656 | tf_op jit(solution)/shard_map/ppermute | solution.py:644
  681.9 45.2 %collective-permute-start.53 = (bf16[256,1024]{1,0:T(8,128)(2,1)}, bf16[256,1024]{1,0:T(8,128)(2,1)}, u32[]{:S(2)}, u32[]{:S(2)}) collective-permute-start(bf16[256,1024]{1,0:T(8,128)(2,1)} %pad_maximum_fusion.3), channel_id=1, source_target_pairs={{2,0},{3,1},{0,2},{1,3},{6,4},{7,5},{4,6},{5,7},{10,8},{11,9},{8,1... | collective-permute-start | bytes 1572872 | tf_op jit(solution)/shard_map/ppermute | solution.py:644
  682.0 42.5 %collective-permute-start.29 = (f32[16384]{0:T(1024)S(1)}, f32[16384]{0:T(1024)}, u32[]{:S(2)}, u32[]{:S(2)}) collective-permute-start(f32[16384]{0:T(1024)S(1)} %add.418), channel_id=1, source_target_pairs={{0,16},{1,17},{2,18},{3,19},{4,20},{5,21},{6,22},{7,23},{8,24},{9,... | collective-permute-start | bytes 196616 | tf_op jit(solution)/shard_map/ppermute | solution.py:694
  720.4 16.4 %collective-permute-start.48 = (bf16[512,768]{1,0:T(8,128)(2,1)S(1)}, bf16[512,768]{1,0:T(8,128)(2,1)S(1)}, u32[]{:S(2)}, u32[]{:S(2)}) collective-permute-start(bf16[512,768]{1,0:T(8,128)(2,1)S(1)} %pad_maximum_fusion.2.a), channel_id=1, source_target_pairs={{2,0},{3,1},{0,2},{1,3},{6,4},{7,5},{4,6},{5,7},{10,8},{11,9},{8,1... | collective-permute-start | bytes 2359304 | tf_op jit(solution)/shard_map/ppermute | solution.py:644
  720.5 14.0 %collective-permute-start.49 = (bf16[512,768]{1,0:T(8,128)(2,1)S(1)}, bf16[512,768]{1,0:T(8,128)(2,1)S(1)}, u32[]{:S(2)}, u32[]{:S(2)}) collective-permute-start(bf16[512,768]{1,0:T(8,128)(2,1)S(1)} %pad_maximum_fusion.1.a), channel_id=1, source_target_pairs={{2,0},{3,1},{0,2},{1,3},{6,4},{7,5},{4,6},{5,7},{10,8},{11,9},{8,1... | collective-permute-start | bytes 2359304 | tf_op jit(solution)/shard_map/ppermute | solution.py:644
  (90 other events, 871.6 us)
Sparse Core Ops, SparseCore 0:
  365.7 117.5 all-reduce.2
  580.7 139.6 all-reduce.4
